TPU v7x, 32 devices: a whole 2x2x4 slice. The times are simulated.
32 devices in a mesh: seq: 8 (over z, x), head: 4 (over y, core).
Axes of the slice: x: 2, y: 2, z: 4, core: 2. Of those that a mesh axis runs over, the one named last changes fastest.
Arguments:
- ref_audio: bfloat16 [1024, 1024], P('seq', 'head'), may hold values from -32 to 32
- val_audio: bfloat16 [1024, 1024], P('seq', 'head'), may hold values from -6 to 6
- ref_video: bfloat16 [192, 1024], P('seq', 'head'), may hold values from -32 to 32
- val_video: bfloat16 [192, 1024], P('seq', 'head'), may hold values from -6 to 6
- audio_proj: bfloat16 [1024, 1024], P('head'), may hold values from -1.25 to 1.25
- video_proj: bfloat16 [1024, 1024], P('head'), may hold values from -1.25 to 1.25
Outputs:
- audio_out: bfloat16 [1024, 1024], P('seq', 'head')
- video_out: bfloat16 [192, 1024], P('seq', 'head')
All inputs are finite; a program needn't handle non-finite values.
Results may differ from a plain program's by a relative error of at most 0.012.
Values may be sent and summed in bfloat16 or wider, within the bound.
No kernel may reach another device: no remote copies, remote signals or barrier semaphores. Data moves between devices by JAX's collectives and lax.ppermute only.
A program may use at most 64 MiB of HBM per device.

v0:
```python
import math

import jax
import jax.numpy as jnp
from jax import lax
from jax.sharding import PartitionSpec as P

HEAD_DIM = 64


def shifted(block, axis, distance):
    devices = range(lax.axis_size(axis))
    route = [((i - distance) % len(devices), i) for i in devices]
    return lax.ppermute(block, axis, route)


def visit_tile(row_state, kv_block, col_state, aud_ref, aud_val):
    vid_ref, vid_val = kv_block
    row_top, row_total, row_acc = row_state
    col_top, col_total, col_acc = col_state
    scores = jnp.einsum(
        "vhd,ahd->hva", vid_ref, aud_ref, preferred_element_type=jnp.float32
    ) * HEAD_DIM ** (-0.5)
    row_new = jnp.maximum(row_top, jnp.max(scores, axis=1))
    row_probs = jnp.exp(scores - row_new[:, None, :])
    row_fade = jnp.exp(row_top - row_new)
    row_total = row_total * row_fade + jnp.sum(row_probs, axis=1)
    row_acc = row_acc * row_fade.T[:, :, None] + jnp.einsum(
        "hva,vhd->ahd", row_probs.astype(jnp.bfloat16), vid_val, preferred_element_type=jnp.float32
    )
    col_new = jnp.maximum(col_top, jnp.max(scores, axis=2))
    col_probs = jnp.exp(scores - col_new[:, :, None])
    col_fade = jnp.exp(col_top - col_new)
    col_total = col_total * col_fade + jnp.sum(col_probs, axis=2)
    col_acc = col_acc * col_fade.T[:, :, None] + jnp.einsum(
        "hva,ahd->vhd", col_probs.astype(jnp.bfloat16), aud_val, preferred_element_type=jnp.float32
    )
    return ((row_new, row_total, row_acc), (col_new, col_total, col_acc))


def fresh_state(local_heads, token_rows):
    return (
        jnp.full((local_heads, token_rows), -jnp.inf, jnp.float32),
        jnp.zeros((local_heads, token_rows), jnp.float32),
        jnp.zeros((token_rows, local_heads, HEAD_DIM), jnp.float32),
    )


def per_device(ref_audio, val_audio, ref_video, val_video, audio_proj, video_proj):
    aud_rows = ref_audio.shape[0]
    vid_rows = ref_video.shape[0]
    local_heads = ref_audio.shape[1] // HEAD_DIM
    aud_ref = ref_audio.reshape(aud_rows, local_heads, HEAD_DIM)
    aud_val = val_audio.reshape(aud_rows, local_heads, HEAD_DIM)
    kv_block = (
        ref_video.reshape(vid_rows, local_heads, HEAD_DIM),
        val_video.reshape(vid_rows, local_heads, HEAD_DIM),
    )
    row_state = fresh_state(local_heads, aud_rows)
    cycle_size = lax.axis_size("seq")
    unroll_by = math.gcd(8, cycle_size)

    def one_turn(turn_index, loop_state):
        row_state, moving_block, col_state = loop_state
        for inner_step in range(unroll_by):
            row_state, col_state = visit_tile(row_state, moving_block, col_state, aud_ref, aud_val)
            moving_block = shifted((moving_block[0], moving_block[1]), "seq", 1)
            col_state = shifted((col_state[0], col_state[1], col_state[2]), "seq", 1)
        return (row_state, moving_block, col_state)

    row_state, moving_block, col_state = lax.fori_loop(
        0,
        cycle_size // unroll_by,
        one_turn,
        (row_state, kv_block, fresh_state(local_heads, vid_rows)),
    )
    col_total = col_state[1].T
    col_acc = col_state[2]
    aud_mix = (
        (row_state[2] / row_state[1].T[:, :, None])
        .reshape(aud_rows, local_heads * HEAD_DIM)
        .astype(jnp.bfloat16)
    )
    vid_mix = (
        (col_acc / col_total[:, :, None])
        .reshape(vid_rows, local_heads * HEAD_DIM)
        .astype(jnp.bfloat16)
    )
    aud_term = jnp.dot(aud_mix, audio_proj, preferred_element_type=jnp.float32)
    vid_term = jnp.dot(vid_mix, video_proj, preferred_element_type=jnp.float32)
    audio_sum, video_sum = (
        lax.psum_scatter(
            aud_term.astype(jnp.bfloat16), "head", scatter_dimension=1, tiled=True
        ).astype(jnp.float32),
        lax.psum_scatter(
            vid_term.astype(jnp.bfloat16), "head", scatter_dimension=1, tiled=True
        ).astype(jnp.float32),
    )
    return (audio_sum.astype(jnp.bfloat16), video_sum.astype(jnp.bfloat16))


def solution(mesh):
    in_specs = (
        P("seq", "head"),
        P("seq", "head"),
        P("seq", "head"),
        P("seq", "head"),
        P("head", None),
        P("head", None),
    )
    out_specs = (P("seq", "head"), P("seq", "head"))
    return jax.shard_map(
        per_device, mesh=mesh, in_specs=in_specs, out_specs=out_specs, check_vma=False
    )
```

profile of v0, /device:TPU:0, one launch (start us, length us, event | category | flops | bytes accessed | tf_op | source)
XLA Modules:
  0.0 156.3 jit_solution(3897405797656208397)
XLA Ops:
  8.1 3.0 %collective-permute-start = (bf16[24,4,64]{2,0,1:T(8,128)(2,1)S(1)}, bf16[24,4,64]{2,0,1:T(8,128)(2,1)S(1)}, u32[]{:S(2)}, u32[]{:S(2)}) collective-permute-start(bf16[24,4,64]{2,0,1:T(8,128)(2,1)S(1)} %copy.25), channel_id=1, source_target_pairs={{28,0},{0,4},{4,8},{8,12},{12,16},{16,20},{20,24},{24,28},{29,1},{... | collective-permute-start | bytes 36872 | tf_op jit(solution)/shard_map/while/body/eval_jaxpr/ppermute | solution.py:14
  11.4 1.6 %collective-permute-start.15 = (f32[4,24]{1,0:T(4,128)S(1)}, f32[4,24]{1,0:T(4,128)S(1)}, u32[]{:S(2)}, u32[]{:S(2)}) collective-permute-start(f32[4,24]{1,0:T(4,128)S(1)} %get-tuple-element.65), channel_id=1, source_target_pairs={{28,0},{0,4},{4,8},{8,12},{12,16},{16,20},{20,24},{24,28},{29,1},{... | collective-permute-start | bytes 1160 | tf_op jit(solution)/shard_map/while/body/eval_jaxpr/ppermute | solution.py:14
  15.1 1.6 %collective-permute-start.14 = (f32[24,4,64]{2,0,1:T(8,128)S(1)}, f32[24,4,64]{2,0,1:T(8,128)S(1)}, u32[]{:S(2)}, u32[]{:S(2)}) collective-permute-start(f32[24,4,64]{2,0,1:T(8,128)S(1)} %fusion.17), channel_id=1, source_target_pairs={{28,0},{0,4},{4,8},{8,12},{12,16},{16,20},{20,24},{24,28},{29,1},{... | collective-permute-start | bytes 73736 | tf_op jit(solution)/shard_map/while/body/eval_jaxpr/ppermute | solution.py:14
  21.7 1.7 %collective-permute-done.1 = bf16[24,4,64]{2,0,1:T(8,128)(2,1)S(1)} collective-permute-done((bf16[24,4,64]{2,0,1:T(8,128)(2,1)S(1)}, bf16[24,4,64]{2,0,1:T(8,128)(2,1)S(1)}, u32[]{:S(2)}, u32[]{:S(2)}) %collective-permute-start.1) | collective-permute-done | bytes 12320 | tf_op jit(solution)/shard_map/while/body/eval_jaxpr/ppermute | solution.py:14
  27.2 2.7 %collective-permute-done.3 = bf16[24,4,64]{2,0,1:T(8,128)(2,1)S(1)} collective-permute-done((bf16[24,4,64]{2,0,1:T(8,128)(2,1)S(1)}, bf16[24,4,64]{2,0,1:T(8,128)(2,1)S(1)}, u32[]{:S(2)}, u32[]{:S(2)}) %collective-permute-start.3) | collective-permute-done | bytes 12320 | tf_op jit(solution)/shard_map/while/body/eval_jaxpr/ppermute | solution.py:14
  30.0 3.2 %collective-permute-done.4 = bf16[24,4,64]{2,0,1:T(8,128)(2,1)S(1)} collective-permute-done((bf16[24,4,64]{2,0,1:T(8,128)(2,1)S(1)}, bf16[24,4,64]{2,0,1:T(8,128)(2,1)S(1)}, u32[]{:S(2)}, u32[]{:S(2)}) %collective-permute-start.4) | collective-permute-done | bytes 12320 | tf_op jit(solution)/shard_map/while/body/eval_jaxpr/ppermute | solution.py:14
  33.4 3.0 %collective-permute-done.5 = bf16[24,4,64]{2,0,1:T(8,128)(2,1)S(1)} collective-permute-done((bf16[24,4,64]{2,0,1:T(8,128)(2,1)S(1)}, bf16[24,4,64]{2,0,1:T(8,128)(2,1)S(1)}, u32[]{:S(2)}, u32[]{:S(2)}) %collective-permute-start.5) | collective-permute-done | bytes 12320 | tf_op jit(solution)/shard_map/while/body/eval_jaxpr/ppermute | solution.py:14
  36.5 3.2 %collective-permute-done.6 = bf16[24,4,64]{2,0,1:T(8,128)(2,1)S(1)} collective-permute-done((bf16[24,4,64]{2,0,1:T(8,128)(2,1)S(1)}, bf16[24,4,64]{2,0,1:T(8,128)(2,1)S(1)}, u32[]{:S(2)}, u32[]{:S(2)}) %collective-permute-start.6) | collective-permute-done | bytes 12320 | tf_op jit(solution)/shard_map/while/body/eval_jaxpr/ppermute | solution.py:14
  43.2 4.1 %collective-permute-done.8 = bf16[24,4,64]{2,0,1:T(8,128)(2,1)S(1)} collective-permute-done((bf16[24,4,64]{2,0,1:T(8,128)(2,1)S(1)}, bf16[24,4,64]{2,0,1:T(8,128)(2,1)S(1)}, u32[]{:S(2)}, u32[]{:S(2)}) %collective-permute-start.8) | collective-permute-done | bytes 12320 | tf_op jit(solution)/shard_map/while/body/eval_jaxpr/ppermute | solution.py:14
  47.9 1.8 %collective-permute-done.9 = bf16[24,4,64]{2,0,1:T(8,128)(2,1)S(1)} collective-permute-done((bf16[24,4,64]{2,0,1:T(8,128)(2,1)S(1)}, bf16[24,4,64]{2,0,1:T(8,128)(2,1)S(1)}, u32[]{:S(2)}, u32[]{:S(2)}) %collective-permute-start.9) | collective-permute-done | bytes 12320 | tf_op jit(solution)/shard_map/while/body/eval_jaxpr/ppermute | solution.py:14
  49.7 4.1 %collective-permute-done.10 = bf16[24,4,64]{2,0,1:T(8,128)(2,1)S(1)} collective-permute-done((bf16[24,4,64]{2,0,1:T(8,128)(2,1)S(1)}, bf16[24,4,64]{2,0,1:T(8,128)(2,1)S(1)}, u32[]{:S(2)}, u32[]{:S(2)}) %collective-permute-start.10) | collective-permute-done | bytes 12320 | tf_op jit(solution)/shard_map/while/body/eval_jaxpr/ppermute | solution.py:14
  54.4 2.2 %collective-permute-start.20 = (f32[24,4,64]{2,0,1:T(8,128)S(1)}, f32[24,4,64]{2,0,1:T(8,128)S(1)}, u32[]{:S(2)}, u32[]{:S(2)}) collective-permute-start(f32[24,4,64]{2,0,1:T(8,128)S(1)} %multiply_add_fusion.4), channel_id=1, source_target_pairs={{28,0},{0,4},{4,8},{8,12},{12,16},{16,20},{20,24},{24,28},{29,1},{... | collective-permute-start | bytes 73736 | tf_op jit(solution)/shard_map/while/body/eval_jaxpr/ppermute | solution.py:14
  57.6 3.1 %collective-permute-done.12 = bf16[24,4,64]{2,0,1:T(8,128)(2,1)S(1)} collective-permute-done((bf16[24,4,64]{2,0,1:T(8,128)(2,1)S(1)}, bf16[24,4,64]{2,0,1:T(8,128)(2,1)S(1)}, u32[]{:S(2)}, u32[]{:S(2)}) %collective-permute-start.12) | collective-permute-done | bytes 12320 | tf_op jit(solution)/shard_map/while/body/eval_jaxpr/ppermute | solution.py:14
  63.4 4.1 %collective-permute-done.30 = f32[4,24]{1,0:T(4,128)S(1)} collective-permute-done((f32[4,24]{1,0:T(4,128)S(1)}, f32[4,24]{1,0:T(4,128)S(1)}, u32[]{:S(2)}, u32[]{:S(2)}) %collective-permute-start.30) | collective-permute-done | bytes 416 | tf_op jit(solution)/shard_map/while/body/eval_jaxpr/ppermute | solution.py:14
  67.7 6.1 %collective-permute-done.31 = f32[4,24]{1,0:T(4,128)S(1)} collective-permute-done((f32[4,24]{1,0:T(4,128)S(1)}, f32[4,24]{1,0:T(4,128)S(1)}, u32[]{:S(2)}, u32[]{:S(2)}) %collective-permute-start.31) | collective-permute-done | bytes 416 | tf_op jit(solution)/shard_map/while/body/eval_jaxpr/ppermute | solution.py:14
  74.0 6.1 %collective-permute-done.32 = f32[4,24]{1,0:T(4,128)S(1)} collective-permute-done((f32[4,24]{1,0:T(4,128)S(1)}, f32[4,24]{1,0:T(4,128)S(1)}, u32[]{:S(2)}, u32[]{:S(2)}) %collective-permute-start.32) | collective-permute-done | bytes 416 | tf_op jit(solution)/shard_map/while/body/eval_jaxpr/ppermute | solution.py:14
  80.4 6.0 %collective-permute-done.33 = f32[4,24]{1,0:T(4,128)S(1)} collective-permute-done((f32[4,24]{1,0:T(4,128)S(1)}, f32[4,24]{1,0:T(4,128)S(1)}, u32[]{:S(2)}, u32[]{:S(2)}) %collective-permute-start.33) | collective-permute-done | bytes 416 | tf_op jit(solution)/shard_map/while/body/eval_jaxpr/ppermute | solution.py:14
  87.4 5.2 %collective-permute-done.34 = f32[4,24]{1,0:T(4,128)S(1)} collective-permute-done((f32[4,24]{1,0:T(4,128)S(1)}, f32[4,24]{1,0:T(4,128)S(1)}, u32[]{:S(2)}, u32[]{:S(2)}) %collective-permute-start.34) | collective-permute-done | bytes 416 | tf_op jit(solution)/shard_map/while/body/eval_jaxpr/ppermute | solution.py:14
  94.5 4.5 %collective-permute-done.35 = f32[4,24]{1,0:T(4,128)S(1)} collective-permute-done((f32[4,24]{1,0:T(4,128)S(1)}, f32[4,24]{1,0:T(4,128)S(1)}, u32[]{:S(2)}, u32[]{:S(2)}) %collective-permute-start.35) | collective-permute-done | bytes 416 | tf_op jit(solution)/shard_map/while/body/eval_jaxpr/ppermute | solution.py:14
  99.0 2.3 %collective-permute-done.26 = f32[24,4,64]{2,0,1:T(8,128)S(1)} collective-permute-done((f32[24,4,64]{2,0,1:T(8,128)S(1)}, f32[24,4,64]{2,0,1:T(8,128)S(1)}, u32[]{:S(2)}, u32[]{:S(2)}) %collective-permute-start.26) | collective-permute-done | bytes 24608 | tf_op jit(solution)/shard_map/while/body/eval_jaxpr/ppermute | solution.py:14
  101.8 3.5 %collective-permute-done.36 = f32[4,24]{1,0:T(4,128)S(1)} collective-permute-done((f32[4,24]{1,0:T(4,128)S(1)}, f32[4,24]{1,0:T(4,128)S(1)}, u32[]{:S(2)}, u32[]{:S(2)}) %collective-permute-start.36) | collective-permute-done | bytes 416 | tf_op jit(solution)/shard_map/while/body/eval_jaxpr/ppermute | solution.py:14
  105.3 3.0 %collective-permute-done.28 = f32[24,4,64]{2,0,1:T(8,128)S(1)} collective-permute-done((f32[24,4,64]{2,0,1:T(8,128)S(1)}, f32[24,4,64]{2,0,1:T(8,128)S(1)}, u32[]{:S(2)}, u32[]{:S(2)}) %collective-permute-start.28) | collective-permute-done | bytes 24608 | tf_op jit(solution)/shard_map/while/body/eval_jaxpr/ppermute | solution.py:14
  110.4 15.8 %reduce-scatter.5.cloned.1.call-done = bf16[24,256]{1,0:T(8,128)(2,1)} async-done(((bf16[24,1024]{1,0:T(8,128)(2,1)}), bf16[24,256]{1,0:T(8,128)(2,1)}) %reduce-scatter.5.cloned.1.call-update) | async-done | bytes 12304 | tf_op jit(solution)/shard_map/reduce_scatter | solution.py:95
  126.2 23.2 %reduce-scatter.3.cloned.1.call-done = bf16[128,256]{1,0:T(8,128)(2,1)} async-done(((bf16[128,1024]{1,0:T(8,128)(2,1)}), bf16[128,256]{1,0:T(8,128)(2,1)}) %reduce-scatter.3.cloned.1.call-update) | async-done | bytes 65552 | tf_op jit(solution)/shard_map/reduce_scatter | solution.py:92
  (127 shorter events, 26.8 us)
Async XLA Ops:
  7.2 119.0 %reduce-scatter.5.cloned.1.call-start = ((), (), s32[]{:S(2)}) async-start(), calls=%async_computation.3 | async-start | bytes 61440 | tf_op jit(solution)/shard_map/reduce_scatter | solution.py:95
  8.1 10.3 %collective-permute-start = (bf16[24,4,64]{2,0,1:T(8,128)(2,1)S(1)}, bf16[24,4,64]{2,0,1:T(8,128)(2,1)S(1)}, u32[]{:S(2)}, u32[]{:S(2)}) collective-permute-start(bf16[24,4,64]{2,0,1:T(8,128)(2,1)S(1)} %copy.25), channel_id=1, source_target_pairs={{28,0},{0,4},{4,8},{8,12},{12,16},{16,20},{20,24},{24,28},{29,1},{... | collective-permute-start | bytes 36872 | tf_op jit(solution)/shard_map/while/body/eval_jaxpr/ppermute | solution.py:14
  11.4 8.7 %collective-permute-start.15 = (f32[4,24]{1,0:T(4,128)S(1)}, f32[4,24]{1,0:T(4,128)S(1)}, u32[]{:S(2)}, u32[]{:S(2)}) collective-permute-start(f32[4,24]{1,0:T(4,128)S(1)} %get-tuple-element.65), channel_id=1, source_target_pairs={{28,0},{0,4},{4,8},{8,12},{12,16},{16,20},{20,24},{24,28},{29,1},{... | collective-permute-start | bytes 1160 | tf_op jit(solution)/shard_map/while/body/eval_jaxpr/ppermute | solution.py:14
  13.2 47.9 %collective-permute-start.29 = (f32[4,24]{1,0:T(4,128)S(1)}, f32[4,24]{1,0:T(4,128)S(1)}, u32[]{:S(2)}, u32[]{:S(2)}) collective-permute-start(f32[4,24]{1,0:T(4,128)S(1)} %get-tuple-element.98), channel_id=1, source_target_pairs={{28,0},{0,4},{4,8},{8,12},{12,16},{16,20},{20,24},{24,28},{29,1},{... | collective-permute-start | bytes 1160 | tf_op jit(solution)/shard_map/while/body/eval_jaxpr/ppermute | solution.py:14
  15.1 11.5 %collective-permute-start.14 = (f32[24,4,64]{2,0,1:T(8,128)S(1)}, f32[24,4,64]{2,0,1:T(8,128)S(1)}, u32[]{:S(2)}, u32[]{:S(2)}) collective-permute-start(f32[24,4,64]{2,0,1:T(8,128)S(1)} %fusion.17), channel_id=1, source_target_pairs={{28,0},{0,4},{4,8},{8,12},{12,16},{16,20},{20,24},{24,28},{29,1},{... | collective-permute-start | bytes 73736 | tf_op jit(solution)/shard_map/while/body/eval_jaxpr/ppermute | solution.py:14
  16.8 6.6 %collective-permute-start.1 = (bf16[24,4,64]{2,0,1:T(8,128)(2,1)S(1)}, bf16[24,4,64]{2,0,1:T(8,128)(2,1)S(1)}, u32[]{:S(2)}, u32[]{:S(2)}) collective-permute-start(bf16[24,4,64]{2,0,1:T(8,128)(2,1)S(1)} %copy.26), channel_id=1, source_target_pairs={{28,0},{0,4},{4,8},{8,12},{12,16},{16,20},{20,24},{24,28},{29,1},{... | collective-permute-start | bytes 36872 | tf_op jit(solution)/shard_map/while/body/eval_jaxpr/ppermute | solution.py:14
  23.4 6.5 %collective-permute-start.3 = (bf16[24,4,64]{2,0,1:T(8,128)(2,1)S(1)}, bf16[24,4,64]{2,0,1:T(8,128)(2,1)S(1)}, u32[]{:S(2)}, u32[]{:S(2)}) collective-permute-start(bf16[24,4,64]{2,0,1:T(8,128)(2,1)S(1)} %collective-permute-done.1), channel_id=1, source_target_pairs={{28,0},{0,4},{4,8},{8,12},{12,16},{16,20},{20,24},{24,28},{29,1},{... | collective-permute-start | bytes 36872 | tf_op jit(solution)/shard_map/while/body/eval_jaxpr/ppermute | solution.py:14
  26.5 6.8 %collective-permute-start.19 = (f32[4,24]{1,0:T(4,128)S(1)}, f32[4,24]{1,0:T(4,128)S(1)}, u32[]{:S(2)}, u32[]{:S(2)}) collective-permute-start(f32[4,24]{1,0:T(4,128)S(1)} %get-tuple-element.78), channel_id=1, source_target_pairs={{28,0},{0,4},{4,8},{8,12},{12,16},{16,20},{20,24},{24,28},{29,1},{... | collective-permute-start | bytes 1160 | tf_op jit(solution)/shard_map/while/body/eval_jaxpr/ppermute | solution.py:14
  26.5 6.6 %collective-permute-start.4 = (bf16[24,4,64]{2,0,1:T(8,128)(2,1)S(1)}, bf16[24,4,64]{2,0,1:T(8,128)(2,1)S(1)}, u32[]{:S(2)}, u32[]{:S(2)}) collective-permute-start(bf16[24,4,64]{2,0,1:T(8,128)(2,1)S(1)} %collective-permute-done.2), channel_id=1, source_target_pairs={{28,0},{0,4},{4,8},{8,12},{12,16},{16,20},{20,24},{24,28},{29,1},{... | collective-permute-start | bytes 36872 | tf_op jit(solution)/shard_map/while/body/eval_jaxpr/ppermute | solution.py:14
  26.8 13.1 %collective-permute-start.16 = (f32[24,4,64]{2,0,1:T(8,128)S(1)}, f32[24,4,64]{2,0,1:T(8,128)S(1)}, u32[]{:S(2)}, u32[]{:S(2)}) collective-permute-start(f32[24,4,64]{2,0,1:T(8,128)S(1)} %multiply_add_fusion.6), channel_id=1, source_target_pairs={{28,0},{0,4},{4,8},{8,12},{12,16},{16,20},{20,24},{24,28},{29,1},{... | collective-permute-start | bytes 73736 | tf_op jit(solution)/shard_map/while/body/eval_jaxpr/ppermute | solution.py:14
  36.5 6.7 %collective-permute-start.7 = (bf16[24,4,64]{2,0,1:T(8,128)(2,1)S(1)}, bf16[24,4,64]{2,0,1:T(8,128)(2,1)S(1)}, u32[]{:S(2)}, u32[]{:S(2)}) collective-permute-start(bf16[24,4,64]{2,0,1:T(8,128)(2,1)S(1)} %collective-permute-done.5), channel_id=1, source_target_pairs={{28,0},{0,4},{4,8},{8,12},{12,16},{16,20},{20,24},{24,28},{29,1},{... | collective-permute-start | bytes 36872 | tf_op jit(solution)/shard_map/while/body/eval_jaxpr/ppermute | solution.py:14
  39.9 7.6 %collective-permute-start.23 = (f32[4,24]{1,0:T(4,128)S(1)}, f32[4,24]{1,0:T(4,128)S(1)}, u32[]{:S(2)}, u32[]{:S(2)}) collective-permute-start(f32[4,24]{1,0:T(4,128)S(1)} %get-tuple-element.74), channel_id=1, source_target_pairs={{28,0},{0,4},{4,8},{8,12},{12,16},{16,20},{20,24},{24,28},{29,1},{... | collective-permute-start | bytes 1160 | tf_op jit(solution)/shard_map/while/body/eval_jaxpr/ppermute | solution.py:14
  40.2 14.0 %collective-permute-start.18 = (f32[24,4,64]{2,0,1:T(8,128)S(1)}, f32[24,4,64]{2,0,1:T(8,128)S(1)}, u32[]{:S(2)}, u32[]{:S(2)}) collective-permute-start(f32[24,4,64]{2,0,1:T(8,128)S(1)} %multiply_add_fusion.5), channel_id=1, source_target_pairs={{28,0},{0,4},{4,8},{8,12},{12,16},{16,20},{20,24},{24,28},{29,1},{... | collective-permute-start | bytes 73736 | tf_op jit(solution)/shard_map/while/body/eval_jaxpr/ppermute | solution.py:14
  40.2 7.0 %collective-permute-start.8 = (bf16[24,4,64]{2,0,1:T(8,128)(2,1)S(1)}, bf16[24,4,64]{2,0,1:T(8,128)(2,1)S(1)}, u32[]{:S(2)}, u32[]{:S(2)}) collective-permute-start(bf16[24,4,64]{2,0,1:T(8,128)(2,1)S(1)} %collective-permute-done.6), channel_id=1, source_target_pairs={{28,0},{0,4},{4,8},{8,12},{12,16},{16,20},{20,24},{24,28},{29,1},{... | collective-permute-start | bytes 36872 | tf_op jit(solution)/shard_map/while/body/eval_jaxpr/ppermute | solution.py:14
  49.7 6.9 %collective-permute-start.11 = (bf16[24,4,64]{2,0,1:T(8,128)(2,1)S(1)}, bf16[24,4,64]{2,0,1:T(8,128)(2,1)S(1)}, u32[]{:S(2)}, u32[]{:S(2)}) collective-permute-start(bf16[24,4,64]{2,0,1:T(8,128)(2,1)S(1)} %collective-permute-done.9), channel_id=1, source_target_pairs={{28,0},{0,4},{4,8},{8,12},{12,16},{16,20},{20,24},{24,28},{29,1},{... | collective-permute-start | bytes 36872 | tf_op jit(solution)/shard_map/while/body/eval_jaxpr/ppermute | solution.py:14
  54.0 8.0 %collective-permute-start.27 = (f32[4,24]{1,0:T(4,128)S(1)}, f32[4,24]{1,0:T(4,128)S(1)}, u32[]{:S(2)}, u32[]{:S(2)}) collective-permute-start(f32[4,24]{1,0:T(4,128)S(1)} %get-tuple-element.70), channel_id=1, source_target_pairs={{28,0},{0,4},{4,8},{8,12},{12,16},{16,20},{20,24},{24,28},{29,1},{... | collective-permute-start | bytes 1160 | tf_op jit(solution)/shard_map/while/body/eval_jaxpr/ppermute | solution.py:14
  54.1 6.6 %collective-permute-start.12 = (bf16[24,4,64]{2,0,1:T(8,128)(2,1)S(1)}, bf16[24,4,64]{2,0,1:T(8,128)(2,1)S(1)}, u32[]{:S(2)}, u32[]{:S(2)}) collective-permute-start(bf16[24,4,64]{2,0,1:T(8,128)(2,1)S(1)} %collective-permute-done.10), channel_id=1, source_target_pairs={{28,0},{0,4},{4,8},{8,12},{12,16},{16,20},{20,24},{24,28},{29,1},{... | collective-permute-start | bytes 36872 | tf_op jit(solution)/shard_map/while/body/eval_jaxpr/ppermute | solution.py:14
  54.4 25.7 %collective-permute-start.20 = (f32[24,4,64]{2,0,1:T(8,128)S(1)}, f32[24,4,64]{2,0,1:T(8,128)S(1)}, u32[]{:S(2)}, u32[]{:S(2)}) collective-permute-start(f32[24,4,64]{2,0,1:T(8,128)S(1)} %multiply_add_fusion.4), channel_id=1, source_target_pairs={{28,0},{0,4},{4,8},{8,12},{12,16},{16,20},{20,24},{24,28},{29,1},{... | collective-permute-start | bytes 73736 | tf_op jit(solution)/shard_map/while/body/eval_jaxpr/ppermute | solution.py:14
  56.6 44.9 %collective-permute-start.13 = (bf16[24,4,64]{2,0,1:T(8,128)(2,1)S(1)}, bf16[24,4,64]{2,0,1:T(8,128)(2,1)S(1)}, u32[]{:S(2)}, u32[]{:S(2)}) collective-permute-start(bf16[24,4,64]{2,0,1:T(8,128)(2,1)S(1)} %collective-permute-done.11), channel_id=1, source_target_pairs={{28,0},{0,4},{4,8},{8,12},{12,16},{16,20},{20,24},{24,28},{29,1},{... | collective-permute-start | bytes 36872 | tf_op jit(solution)/shard_map/while/body/eval_jaxpr/ppermute | solution.py:14
  80.3 6.8 %collective-permute-start.22 = (f32[24,4,64]{2,0,1:T(8,128)S(1)}, f32[24,4,64]{2,0,1:T(8,128)S(1)}, u32[]{:S(2)}, u32[]{:S(2)}) collective-permute-start(f32[24,4,64]{2,0,1:T(8,128)S(1)} %multiply_add_fusion.3), channel_id=1, source_target_pairs={{28,0},{0,4},{4,8},{8,12},{12,16},{16,20},{20,24},{24,28},{29,1},{... | collective-permute-start | bytes 73736 | tf_op jit(solution)/shard_map/while/body/eval_jaxpr/ppermute | solution.py:14
  87.4 6.8 %collective-permute-start.24 = (f32[24,4,64]{2,0,1:T(8,128)S(1)}, f32[24,4,64]{2,0,1:T(8,128)S(1)}, u32[]{:S(2)}, u32[]{:S(2)}) collective-permute-start(f32[24,4,64]{2,0,1:T(8,128)S(1)} %multiply_add_fusion.2), channel_id=1, source_target_pairs={{28,0},{0,4},{4,8},{8,12},{12,16},{16,20},{20,24},{24,28},{29,1},{... | collective-permute-start | bytes 73736 | tf_op jit(solution)/shard_map/while/body/eval_jaxpr/ppermute | solution.py:14
  94.4 6.8 %collective-permute-start.26 = (f32[24,4,64]{2,0,1:T(8,128)S(1)}, f32[24,4,64]{2,0,1:T(8,128)S(1)}, u32[]{:S(2)}, u32[]{:S(2)}) collective-permute-start(f32[24,4,64]{2,0,1:T(8,128)S(1)} %multiply_add_fusion.1), channel_id=1, source_target_pairs={{28,0},{0,4},{4,8},{8,12},{12,16},{16,20},{20,24},{24,28},{29,1},{... | collective-permute-start | bytes 73736 | tf_op jit(solution)/shard_map/while/body/eval_jaxpr/ppermute | solution.py:14
  101.5 6.8 %collective-permute-start.28 = (f32[24,4,64]{2,0,1:T(8,128)S(1)}, f32[24,4,64]{2,0,1:T(8,128)S(1)}, u32[]{:S(2)}, u32[]{:S(2)}) collective-permute-start(f32[24,4,64]{2,0,1:T(8,128)S(1)} %multiply_add_fusion), channel_id=1, source_target_pairs={{28,0},{0,4},{4,8},{8,12},{12,16},{16,20},{20,24},{24,28},{29,1},{... | collective-permute-start | bytes 73736 | tf_op jit(solution)/shard_map/while/body/eval_jaxpr/ppermute | solution.py:14
  109.3 40.1 %reduce-scatter.3.cloned.1.call-start = ((), (), s32[]{:S(2)}) async-start(), calls=%async_computation.2 | async-start | bytes 327680 | tf_op jit(solution)/shard_map/reduce_scatter | solution.py:92
  (20 other events, 221.7 us)
Sparse Core Ops, SparseCore 0:
  109.5 16.6 reduce-scatter.4
  129.4 20.0 reduce-scatter.2
where the time goes:
time: 157 us; the launch traced here: 156 us
  waiting for transfers between devices  113 us (72%)
  starting transfers between devices  18.7 us (12%)
  between operations  14.5 us (9%)
  matrix products  6.93 us (4%)
  other arithmetic  1.61 us (1%)
    ppermute x37, waiting for transfers between devices, shifted(): return lax.ppermute(block, axis, route)  74.2 us
    reduce_scatter x1, waiting for transfers between devices, per_device(): lax.psum_scatter(aud_term.astype(jnp.bfloat16), 'head', scatter_dimension...  23.2 us
    ppermute x37, starting transfers between devices, shifted(): return lax.ppermute(block, axis, route)  18.6 us
    reduce_scatter x1, waiting for transfers between devices, per_device(): lax.psum_scatter(vid_term.astype(jnp.bfloat16), 'head', scatter_dimension...  15.8 us
  transfers between devices with their start and end apart: 39, of which 25 were waited for; matrix products, arithmetic and copies ran while one was open for 5% of the time, Pallas kernels for 0%

commit v1 on v0

v1 whole, which is shorter than its diff:
```python
import jax
import jax.numpy as jnp
from jax import lax
from jax.experimental import pallas as pl
from jax.experimental.pallas import tpu as pltpu
from jax.sharding import PartitionSpec as P

HEAD_DIM = 64
LANES = 128
SCALE = HEAD_DIM ** (-0.5)
VMEM_LIMIT = 48 * 1024 * 1024


def dot(a, b, dims=((1,), (0,))):
    return lax.dot_general(a, b, (dims, ((), ())), preferred_element_type=jnp.float32)


def normalised(ref, other, values):
    scores = dot(ref, other, ((1,), (1,)))
    top = jnp.max(scores, axis=1, keepdims=True)
    probs = jnp.exp((scores - top) * SCALE)
    total = jnp.sum(probs, axis=1, keepdims=True)
    mix = dot(probs.astype(jnp.bfloat16), values) / total
    return mix, top * SCALE + jnp.log(total)


def attend(aud_ref, aud_val, video, proj, aud_out, col_out):
    width = aud_ref.shape[1]
    heads = width // HEAD_DIM
    vid_rows = video.shape[0]
    lane = lax.broadcasted_iota(jnp.int32, (vid_rows, LANES), 1)
    stats = jnp.zeros((vid_rows, LANES), jnp.float32)
    aud_mix, col_mix = [], []
    for h in range(heads):
        cols = slice(h * HEAD_DIM, (h + 1) * HEAD_DIM)
        vals = slice(width + h * HEAD_DIM, width + (h + 1) * HEAD_DIM)
        q, a, k, v = aud_ref[:, cols], aud_val[:, cols], video[:, cols], video[:, vals]
        aud_mix.append(normalised(q, k, v)[0])
        mix, logsum = normalised(k, q, a)
        col_mix.append(mix)
        for part in range(3):
            piece = logsum.astype(jnp.bfloat16).astype(jnp.float32)
            stats = jnp.where(lane == part * heads + h, piece, stats)
            logsum = logsum - piece
    col_out[:, :width] = jnp.concatenate(col_mix, axis=1).astype(jnp.bfloat16)
    col_out[:, width:] = stats.astype(jnp.bfloat16)
    mixed = jnp.concatenate(aud_mix, axis=1).astype(jnp.bfloat16)
    peers = aud_out.shape[0]
    step = aud_out.shape[2]
    for p in range(peers):
        aud_out[p] = dot(mixed, proj[:, p * step : (p + 1) * step]).astype(jnp.bfloat16)


def combine(state, proj, vid_out):
    blocks, rows, _ = state.shape
    width = proj.shape[0]
    heads = width // HEAD_DIM
    source = lax.broadcasted_iota(jnp.int32, (LANES, width), 0)
    target = lax.broadcasted_iota(jnp.int32, (LANES, width), 1)
    spread = ((source < 3 * heads) & (source % heads == target // HEAD_DIM)).astype(jnp.bfloat16)
    logsums = [dot(state[b, :, width:], spread) for b in range(blocks)]
    top = logsums[0]
    for b in range(1, blocks):
        top = jnp.maximum(top, logsums[b])
    total = jnp.zeros((rows, width), jnp.float32)
    mix = jnp.zeros((rows, width), jnp.float32)
    for b in range(blocks):
        weight = jnp.exp(logsums[b] - top)
        total += weight
        mix += weight * state[b, :, :width].astype(jnp.float32)
    mixed = (mix / total).astype(jnp.bfloat16)
    step = vid_out.shape[2]
    for p in range(vid_out.shape[0]):
        vid_out[p] = dot(mixed, proj[:, p * step : (p + 1) * step]).astype(jnp.bfloat16)


def call(body, out_shape, *args):
    vmem = pl.BlockSpec(memory_space=pltpu.VMEM)
    return pl.pallas_call(
        body,
        out_shape=out_shape,
        in_specs=[vmem] * len(args),
        out_specs=jax.tree.map(lambda _: vmem, out_shape),
        compiler_params=pltpu.CompilerParams(vmem_limit_bytes=VMEM_LIMIT),
    )(*args)


def exchange(blocks, axis):
    return lax.all_to_all(blocks, axis, split_axis=0, concat_axis=0, tiled=True)


def per_device(ref_audio, val_audio, ref_video, val_video, audio_proj, video_proj):
    blocks = lax.axis_size("seq")
    peers = lax.axis_size("head")
    aud_rows, width = ref_audio.shape
    vid_rows = ref_video.shape[0]
    model = audio_proj.shape[1]
    bf16 = jnp.bfloat16
    mine = jnp.concatenate([ref_video, val_video], axis=1)
    video = exchange(jnp.broadcast_to(mine[None], (blocks,) + mine.shape), "seq")
    aud_term, col_state = call(
        attend,
        (
            jax.ShapeDtypeStruct((peers, aud_rows, model // peers), bf16),
            jax.ShapeDtypeStruct((blocks * vid_rows, width + LANES), bf16),
        ),
        ref_audio,
        val_audio,
        video.reshape(blocks * vid_rows, 2 * width),
        audio_proj,
    )
    col_state = exchange(col_state.reshape(blocks, vid_rows, width + LANES), "seq")
    vid_term = call(
        combine,
        jax.ShapeDtypeStruct((peers, vid_rows, model // peers), bf16),
        col_state,
        video_proj,
    )
    aud_sum = jnp.sum(exchange(aud_term, "head").astype(jnp.float32), axis=0)
    vid_sum = jnp.sum(exchange(vid_term, "head").astype(jnp.float32), axis=0)
    return aud_sum.astype(bf16), vid_sum.astype(bf16)


def solution(mesh):
    in_specs = (
        P("seq", "head"),
        P("seq", "head"),
        P("seq", "head"),
        P("seq", "head"),
        P("head", None),
        P("head", None),
    )
    out_specs = (P("seq", "head"), P("seq", "head"))
    return jax.shard_map(
        per_device, mesh=mesh, in_specs=in_specs, out_specs=out_specs, check_vma=False
    )
```

time: 157 us -> 47.4 us (0.30)
  waiting for transfers between devices: 113 us -> 8.33 us
  blocking collectives: 0 us -> 25.7 us
  between operations: 14.5 us -> 0.69 us
  starting transfers between devices: 18.7 us -> 6.68 us
  matrix products: 6.93 us -> 0 us
  Pallas kernels: 0 us -> 3.52 us
    ppermute x37 -> x0, waiting for transfers between devices: 74.2 us -> none  [shifted(): return lax.ppermute(block, axis, route)]
    reduce_scatter x2 -> x0, waiting for transfers between devices: 39.1 us -> none  [the longest x1 23.2 us: per_device(): lax.psum_scatter(aud_term.astype(jnp.bfloat16), 'head', scatter_dimension...]
    all_to_all x0 -> x2, blocking collectives: none -> 25.7 us  [exchange(): return lax.all_to_all(blocks, axis, split_axis=0, concat_axis=0, tiled=True)]
    ppermute x37 -> x0, starting transfers between devices: 18.6 us -> none  [shifted(): return lax.ppermute(block, axis, route)]
    all_to_all x0 -> x2, waiting for transfers between devices: none -> 8.33 us  [exchange(): return lax.all_to_all(blocks, axis, split_axis=0, concat_axis=0, tiled=True)]
    dot_general x26 -> x0, matrix products: 6.93 us -> none  [the longest x8 1.73 us: visit_tile(): jnp.einsum('vhd,ahd->hva', vid_ref, aud_ref, preferred_element_type=jnp.f...]
    all_to_all x0 -> x2, starting transfers between devices: none -> 6.68 us  [exchange(): return lax.all_to_all(blocks, axis, split_axis=0, concat_axis=0, tiled=True)]
    pallas_call x0 -> x2, Pallas kernels: none -> 3.52 us  [call(): pl.pallas_call(body, out_shape=out_shape, in_specs=[vmem] * len(args), ou...]
  transfers between devices with their start and end apart: 39 -> 2, of which waited for: 25 -> 2; matrix products, arithmetic and copies ran while one was open for 5% -> 1% of each run, Pallas kernels for 0% -> 2%
where the time goes in v1:
time: 47.4 us; the launch traced here: 47 us
  blocking collectives  25.7 us (54%)
  waiting for transfers between devices  8.33 us (18%)
  starting transfers between devices  6.68 us (14%)
  Pallas kernels  3.52 us (7%)
  other arithmetic  2.07 us (4%)
  between operations  0.69 us (1%)
    all_to_all x2, blocking collectives, exchange(): return lax.all_to_all(blocks, axis, split_axis=0, concat_axis=0, tiled=True)  25.7 us
    all_to_all x2, waiting for transfers between devices, exchange(): return lax.all_to_all(blocks, axis, split_axis=0, concat_axis=0, tiled=True)  8.33 us
    all_to_all x2, starting transfers between devices, exchange(): return lax.all_to_all(blocks, axis, split_axis=0, concat_axis=0, tiled=True)  6.68 us
    pallas_call x2, Pallas kernels, call(): pl.pallas_call(body, out_shape=out_shape, in_specs=[vmem] * len(args), ou...  3.52 us
  transfers between devices with their start and end apart: 2, of which 2 were waited for; matrix products, arithmetic and copies ran while one was open for 1% of the time, Pallas kernels for 2%

profile of v1, /device:TPU:0, one launch (start us, length us, event | category | flops | bytes accessed | tf_op | source)
XLA Modules:
  0.0 47.0 jit_solution(2562500697641363857)
XLA Ops:
  0.6 0.0 copy-start.1
  0.6 0.8 %pad_maximum_fusion = bf16[24,512]{1,0:T(8,128)(2,1)S(1)} fusion(bf16[24,256]{1,0:T(8,128)(2,1)} %param.9, bf16[24,256]{1,0:T(8,128)(2,1)} %param.8), kind=kLoop, calls=%fused_computation | loop fusion | flops 49152 | bytes 49152 | tf_op jit(solution)/shard_map/concatenate | solution.py:99
  1.4 0.0 copy-start.2
  1.5 0.0 copy-start.3
  1.5 15.1 %all_to_all.20 = bf16[8,24,512]{2,1,0:T(8,128)(2,1)S(1)} all-to-all(bf16[8,24,512]{2,1,0:T(8,128)(2,1)S(1)} %broadcast_in_dim.2), channel_id=1, replica_groups=mesh['seq'=8,'head'=4] {'seq'}, dimensions={0} | all-to-all | bytes 393216 | tf_op jit(solution)/shard_map/all_to_all | solution.py:89
  16.6 0.0 copy-done.1
  16.6 0.0 copy-done.2
  16.6 0.0 copy-done.3
  16.6 2.5 %shard_map.77 = (bf16[4,128,256]{2,1,0:T(8,128)(2,1)}, bf16[192,384]{1,0:T(8,128)(2,1)S(1)}) custom-call(bf16[128,256]{1,0:T(8,128)(2,1)S(1)} %copy-done.2, bf16[128,256]{1,0:T(8,128)(2,1)S(1)} %copy-done.3, bf16[192,512]{1,0:T(8,128)(2,1)S(1)} %bitcast.2, bf16[256,1024]{1,0:T(8,128)(2,1)S(1)} %copy-done.1), custom_call_target="tpu_custom_call" | custom-call | tf_op jit(solution)/shard_map/pallas_call | solution.py:79
  19.2 0.0 copy-start
  19.2 10.5 %all_to_all.21.state = bf16[8,24,384]{2,1,0:T(8,128)(2,1)S(1)} all-to-all(bf16[8,24,384]{2,1,0:T(8,128)(2,1)S(1)} %bitcast.3), channel_id=1, replica_groups=mesh['seq'=8,'head'=4] {'seq'}, dimensions={0} | all-to-all | bytes 294912 | tf_op jit(solution)/shard_map/all_to_all | solution.py:89
  29.7 3.4 %all-to-all-start.1 = ((bf16[4,128,256]{2,1,0:T(8,128)(2,1)}), bf16[4,128,256]{2,1,0:T(8,128)(2,1)S(1)}, u32[]{:S(2)}, u32[]{:S(2)}) async-start(bf16[4,128,256]{2,1,0:T(8,128)(2,1)} %get-tuple-element.4), calls=%async_computation.1 | async-start | bytes 524288 | tf_op jit(solution)/shard_map/all_to_all | solution.py:89
  33.1 0.0 copy-done
  33.1 1.0 %shard_map.78 = bf16[4,24,256]{2,1,0:T(8,128)(2,1)} custom-call(bf16[8,24,384]{2,1,0:T(8,128)(2,1)S(1)} %all_to_all.21.state, bf16[256,1024]{1,0:T(8,128)(2,1)S(1)} %copy-done), custom_call_target="tpu_custom_call" | custom-call | tf_op jit(solution)/shard_map/pallas_call | solution.py:79
  34.1 5.0 %all-to-all-done.1 = bf16[4,128,256]{2,1,0:T(8,128)(2,1)S(1)} async-done(((bf16[4,128,256]{2,1,0:T(8,128)(2,1)}), bf16[4,128,256]{2,1,0:T(8,128)(2,1)S(1)}, u32[]{:S(2)}, u32[]{:S(2)}) %all-to-all-start.1) | async-done | bytes 262176 | tf_op jit(solution)/shard_map/all_to_all | solution.py:89
  39.1 3.3 %all-to-all-start.3 = ((bf16[4,24,256]{2,1,0:T(8,128)(2,1)}), bf16[4,24,256]{2,1,0:T(8,128)(2,1)S(1)}, u32[]{:S(2)}, u32[]{:S(2)}) async-start(bf16[4,24,256]{2,1,0:T(8,128)(2,1)} %shard_map.78), calls=%async_computation.3 | async-start | bytes 98304 | tf_op jit(solution)/shard_map/all_to_all | solution.py:89
  42.4 0.7 %reduce_sum.24 = bf16[128,256]{1,0:T(8,128)(2,1)} reduce(bf16[4,128,256]{2,1,0:T(8,128)(2,1)S(1)} %all-to-all-done.1, bf16[]{:T(256)} %constant.3.clone.1), dimensions={0}, to_apply=%region_0.0 | reduce | flops 98304 | bytes 327682 | tf_op jit(solution)/shard_map/reduce_sum | solution.py:119
  43.0 3.3 %all-to-all-done.3 = bf16[4,24,256]{2,1,0:T(8,128)(2,1)S(1)} async-done(((bf16[4,24,256]{2,1,0:T(8,128)(2,1)}), bf16[4,24,256]{2,1,0:T(8,128)(2,1)S(1)}, u32[]{:S(2)}, u32[]{:S(2)}) %all-to-all-start.3) | async-done | bytes 49184 | tf_op jit(solution)/shard_map/all_to_all | solution.py:89
  46.4 0.6 %reduce_sum.25 = bf16[24,256]{1,0:T(8,128)(2,1)} reduce(bf16[4,24,256]{2,1,0:T(8,128)(2,1)S(1)} %all-to-all-done.3, bf16[]{:T(256)} %constant.3.clone.1), dimensions={0}, to_apply=%region_1.0 | reduce | flops 18432 | bytes 61442 | tf_op jit(solution)/shard_map/reduce_sum | solution.py:120
  (1 shorter events, 0.0 us)
Async XLA Ops:
  0.6 16.0 %copy-start.1 = (bf16[256,1024]{1,0:T(8,128)(2,1)S(1)}, bf16[256,1024]{1,0:T(8,128)(2,1)}, u32[]{:S(2)}) copy-start(bf16[256,1024]{1,0:T(8,128)(2,1)} %proj.2) | copy-start | bytes 1572868
  1.4 15.2 %copy-start.2 = (bf16[128,256]{1,0:T(8,128)(2,1)S(1)}, bf16[128,256]{1,0:T(8,128)(2,1)}, u32[]{:S(2)}) copy-start(bf16[128,256]{1,0:T(8,128)(2,1)} %aud_ref.1) | copy-start | bytes 196612
  1.5 15.2 %copy-start.3 = (bf16[128,256]{1,0:T(8,128)(2,1)S(1)}, bf16[128,256]{1,0:T(8,128)(2,1)}, u32[]{:S(2)}) copy-start(bf16[128,256]{1,0:T(8,128)(2,1)} %aud_val.1) | copy-start | bytes 196612
  19.2 13.9 %copy-start = (bf16[256,1024]{1,0:T(8,128)(2,1)S(1)}, bf16[256,1024]{1,0:T(8,128)(2,1)}, u32[]{:S(2)}) copy-start(bf16[256,1024]{1,0:T(8,128)(2,1)} %proj.3) | copy-start | bytes 1572868
  29.7 9.4 %all-to-all-start.1 = ((bf16[4,128,256]{2,1,0:T(8,128)(2,1)}), bf16[4,128,256]{2,1,0:T(8,128)(2,1)S(1)}, u32[]{:S(2)}, u32[]{:S(2)}) async-start(bf16[4,128,256]{2,1,0:T(8,128)(2,1)} %get-tuple-element.4), calls=%async_computation.1 | async-start | bytes 524288 | tf_op jit(solution)/shard_map/all_to_all | solution.py:89
  39.1 7.3 %all-to-all-start.3 = ((bf16[4,24,256]{2,1,0:T(8,128)(2,1)}), bf16[4,24,256]{2,1,0:T(8,128)(2,1)S(1)}, u32[]{:S(2)}, u32[]{:S(2)}) async-start(bf16[4,24,256]{2,1,0:T(8,128)(2,1)} %shard_map.78), calls=%async_computation.3 | async-start | bytes 98304 | tf_op jit(solution)/shard_map/all_to_all | solution.py:89

commit v2 on v1

v2 whole, which is shorter than its diff:
```python
import jax
import jax.numpy as jnp
from jax import lax
from jax.experimental import pallas as pl
from jax.experimental.pallas import tpu as pltpu
from jax.sharding import PartitionSpec as P

HEAD_DIM = 64
LANES = 128
PIECES = 3
SCALE = HEAD_DIM ** (-0.5)
VMEM_LIMIT = 48 * 1024 * 1024
BF16 = jnp.bfloat16
F32 = jnp.float32


def dot(a, b, contract_a=1, contract_b=0):
    dims = (((contract_a,), (contract_b,)), ((), ()))
    return lax.dot_general(a, b, dims, preferred_element_type=F32)


def split_pieces(value):
    pieces = []
    for _ in range(PIECES):
        piece = value.astype(BF16).astype(F32)
        pieces.append(piece)
        value = value - piece
    return pieces


def head_lanes(rows, width, head):
    return lax.broadcasted_iota(jnp.int32, (rows, width), 1) // HEAD_DIM == head


def pack(aud_ref, aud_val, vid_ref, vid_val, aud, vid, sems):
    width = aud_ref.shape[1]
    copies = [
        pltpu.make_async_copy(source, target.at[:, start : start + width], sems.at[i])
        for i, (source, target, start) in enumerate(
            ((aud_ref, aud, 0), (aud_val, aud, width), (vid_ref, vid, 0), (vid_val, vid, width))
        )
    ]
    for copy in copies:
        copy.start()
    for copy in copies:
        copy.wait()


def attend(aud_count, vid_count, *refs):
    auds, vids = refs[:aud_count], refs[aud_count : aud_count + vid_count]
    outs = refs[aud_count + vid_count :]
    row_outs, col_outs = outs[:aud_count], outs[aud_count:]
    width = auds[0].shape[1] // 2
    heads = width // HEAD_DIM
    aud_rows, vid_rows = auds[0].shape[0], vids[0].shape[0]
    aud = jnp.concatenate([ref[...] for ref in auds], axis=0)
    vid = jnp.concatenate([ref[...].astype(F32) for ref in vids], axis=0)
    queries, aud_vals = aud[:, :width], aud[:, width:]
    total_aud, total_vid = aud.shape[0], vid.shape[0]
    masks = [head_lanes(total_vid, width, h) for h in range(heads)]
    keys = jnp.concatenate([jnp.where(m, vid[:, :width], 0.0) for m in masks], axis=0)
    vals = jnp.concatenate([jnp.where(m, vid[:, width:], 0.0) for m in masks], axis=0)
    scores = dot(keys.astype(BF16), queries, 1, 1).reshape(heads, total_vid, total_aud)

    row_top = jnp.max(scores, axis=1, keepdims=True)
    row_probs = jnp.exp((scores - row_top) * SCALE)
    row_total = jnp.sum(row_probs, axis=1, keepdims=True)
    row_probs = row_probs.reshape(heads * total_vid, total_aud).astype(BF16)
    row_mix = dot(vals.astype(BF16), row_probs, 0, 0).reshape(heads, HEAD_DIM, total_aud)
    row_mix = (row_mix / row_total).reshape(width, total_aud)
    row_log = (row_top * SCALE + jnp.log(row_total)).reshape(heads, total_aud)
    row_log = jnp.concatenate(split_pieces(row_log), axis=0)
    for i in range(aud_count):
        cols = slice(i * aud_rows, (i + 1) * aud_rows)
        row_outs[i][:width, :] = row_mix[:, cols].astype(BF16)
        row_outs[i][width:, :] = jnp.concatenate(
            [row_log[:, cols], jnp.zeros((row_outs[i].shape[0] - width - PIECES * heads, aud_rows), F32)], axis=0
        ).astype(BF16)

    col_top = jnp.max(scores, axis=2, keepdims=True)
    col_probs = jnp.exp((scores - col_top) * SCALE)
    col_total = jnp.sum(col_probs, axis=2, keepdims=True)
    col_probs = col_probs.reshape(heads * total_vid, total_aud).astype(BF16)
    every = dot(col_probs, aud_vals).reshape(heads, total_vid, width)
    col_log = col_top * SCALE + jnp.log(col_total)
    lane = lax.broadcasted_iota(jnp.int32, (total_vid, LANES), 1)
    col_mix, divisor = every[0], jnp.broadcast_to(col_total[0], (total_vid, width))
    stats = jnp.zeros((total_vid, LANES), F32)
    for h in range(heads):
        if h:
            col_mix = jnp.where(masks[h], every[h], col_mix)
            divisor = jnp.where(masks[h], col_total[h], divisor)
        for i, piece in enumerate(split_pieces(col_log[h])):
            stats = jnp.where(lane == i * heads + h, piece, stats)
    col_mix = col_mix / divisor
    for i in range(vid_count):
        rows = slice(i * vid_rows, (i + 1) * vid_rows)
        col_outs[i][:, :width] = col_mix[rows].astype(BF16)
        col_outs[i][:, width:] = stats[rows].astype(BF16)


def merged(mixes, logs):
    top = logs[0]
    for log in logs[1:]:
        top = jnp.maximum(top, log)
    weights = [jnp.exp(log - top) for log in logs]
    total = sum(weights[1:], weights[0])
    mix = weights[0] * mixes[0]
    for weight, part in zip(weights[1:], mixes[1:]):
        mix += weight * part
    return mix / total


def project(aud_count, vid_count, aud_me, *refs):
    rows, cols = refs[:aud_count], refs[aud_count : aud_count + vid_count]
    aud_proj, vid_proj = refs[aud_count + vid_count : aud_count + vid_count + 2]
    outs = refs[aud_count + vid_count + 2 :]
    width = aud_proj.shape[0]
    heads = width // HEAD_DIM
    aud_rows, vid_rows = rows[0].shape[1], cols[0].shape[0]

    logs, mixes = [], []
    for ref in rows:
        pieces = ref[width:, :].astype(F32)
        log = pieces[:heads]
        for i in range(1, PIECES):
            log = log + pieces[i * heads : (i + 1) * heads]
        logs.append(log.reshape(heads, 1, aud_rows))
        mixes.append(ref[:width, :].astype(F32).reshape(heads, HEAD_DIM, aud_rows))
    aud_mix = merged(mixes, logs).reshape(width, aud_rows).astype(BF16)

    source = lax.broadcasted_iota(jnp.int32, (LANES, width), 0)
    target = lax.broadcasted_iota(jnp.int32, (LANES, width), 1)
    spread = ((source < PIECES * heads) & (source % heads == target // HEAD_DIM)).astype(BF16)
    logs = [dot(ref[:, width:], spread) for ref in cols]
    vid_mix = merged([ref[:, :width].astype(F32) for ref in cols], logs).astype(BF16)

    step = outs[0].shape[1]
    me = aud_me[0]
    for i, out in enumerate(outs):
        block = pl.ds(pl.multiple_of(partner(me, i, len(outs)) * step, step), step)
        out[:aud_rows, :] = dot(aud_mix, aud_proj[:, block], 0, 0).astype(out.dtype)
        out[aud_rows:, :] = dot(vid_mix, vid_proj[:, block]).astype(out.dtype)


def add(*refs):
    terms, (aud_out, vid_out) = refs[:-2], refs[-2:]
    aud_rows = aud_out.shape[0]
    for out, rows in ((aud_out, slice(0, aud_rows)), (vid_out, slice(aud_rows, None))):
        total = terms[0][rows, :].astype(F32)
        for term in terms[1:]:
            total += term[rows, :].astype(F32)
        out[...] = total.astype(BF16)


def call(body, out_shape, args, in_specs=None, scratch=()):
    vmem = pl.BlockSpec(memory_space=pltpu.VMEM)
    return pl.pallas_call(
        body,
        out_shape=out_shape,
        in_specs=in_specs or [vmem] * len(args),
        out_specs=[vmem] * len(out_shape),
        scratch_shapes=scratch,
        compiler_params=pltpu.CompilerParams(vmem_limit_bytes=VMEM_LIMIT),
    )(*args)


def is_power(n):
    return n & (n - 1) == 0


def partner(index, k, size):
    return index ^ k if is_power(size) else (index + k) % size


def factors(size):
    aud = 1
    while size % (aud * 2) == 0 and (aud * 2) ** 2 <= size:
        aud *= 2
    return aud, size // aud


def route(size, inner, count, k):
    pairs = []
    for i in range(size):
        here = i // inner % count
        pairs.append((i, i + (partner(here, k, count) - here) * inner))
    return pairs


def per_device(ref_audio, val_audio, ref_video, val_video, audio_proj, video_proj):
    seq, peers = lax.axis_size("seq"), lax.axis_size("head")
    aud_count, vid_count = factors(seq)
    aud_rows, width = ref_audio.shape
    vid_rows = ref_video.shape[0]
    heads = width // HEAD_DIM
    step = audio_proj.shape[1] // peers
    shape = jax.ShapeDtypeStruct

    def send(block, inner, count, k, back=False):
        if k == 0:
            return block
        pairs = route(seq, inner, count, k)
        return lax.ppermute(block, "seq", [(b, a) for a, b in pairs] if back else pairs)

    aud, vid = call(
        pack,
        (shape((aud_rows, 2 * width), BF16), shape((vid_rows, 2 * width), BF16)),
        (ref_audio, val_audio, ref_video, val_video),
        in_specs=[pl.BlockSpec(memory_space=pl.ANY)] * 4,
        scratch=[pltpu.SemaphoreType.DMA((4,))],
    )
    auds = [send(aud, 1, aud_count, k) for k in range(aud_count)]
    vids = [send(vid, aud_count, vid_count, k) for k in range(vid_count)]
    log_rows = -(-PIECES * heads // 16) * 16
    states = call(
        lambda *refs: attend(aud_count, vid_count, *refs),
        [shape((width + log_rows, aud_rows), BF16)] * aud_count
        + [shape((vid_rows, width + LANES), BF16)] * vid_count,
        auds + vids,
    )
    rows = [send(states[k], 1, aud_count, k, True) for k in range(aud_count)]
    cols = [send(states[aud_count + k], aud_count, vid_count, k, True) for k in range(vid_count)]
    me = lax.axis_index("head").astype(jnp.int32).reshape(1)
    vmem = pl.BlockSpec(memory_space=pltpu.VMEM)
    terms = call(
        lambda *refs: project(aud_count, vid_count, *refs),
        [shape((aud_rows + vid_rows, step), F32)]
        + [shape((aud_rows + vid_rows, step), BF16)] * (peers - 1),
        [me] + rows + cols + [audio_proj, video_proj],
        in_specs=[pl.BlockSpec(memory_space=pltpu.SMEM)] + [vmem] * (seq_terms(aud_count, vid_count)),
    )
    got = [terms[0]] + [
        lax.ppermute(terms[k], "head", route(peers, 1, peers, k)) for k in range(1, peers)
    ]
    aud_out, vid_out = call(
        add, (shape((aud_rows, step), BF16), shape((vid_rows, step), BF16)), got
    )
    return aud_out, vid_out


def seq_terms(aud_count, vid_count):
    return aud_count + vid_count + 2


def solution(mesh):
    in_specs = (
        P("seq", "head"),
        P("seq", "head"),
        P("seq", "head"),
        P("seq", "head"),
        P("head", None),
        P("head", None),
    )
    out_specs = (P("seq", "head"), P("seq", "head"))
    return jax.shard_map(
        per_device, mesh=mesh, in_specs=in_specs, out_specs=out_specs, check_vma=False
    )
```

time: 47.4 us -> 32.7 us (0.69)
  blocking collectives: 25.7 us -> 0 us
  starting transfers between devices: 6.68 us -> 14.3 us
  local copies, waits for them, and re-layouts: 0.04 us -> 4.13 us
  waiting for transfers between devices: 8.33 us -> 11.5 us
  other arithmetic: 2.07 us -> 0 us
  Pallas kernels: 3.52 us -> 1.76 us
    all_to_all x2 -> x0, blocking collectives: 25.7 us -> none  [exchange(): return lax.all_to_all(blocks, axis, split_axis=0, concat_axis=0, tiled=True)]
    ppermute x0 -> x11, starting transfers between devices: none -> 14.3 us  [the longest x8 12.4 us: send(): lax.ppermute(block, 'seq', [(b, a) for a, b in pairs] if back else pairs)]
    ppermute x0 -> x11, waiting for transfers between devices: none -> 11.5 us  [the longest x8 7.14 us: send(): lax.ppermute(block, 'seq', [(b, a) for a, b in pairs] if back else pairs)]
    all_to_all x2 -> x0, waiting for transfers between devices: 8.33 us -> none  [exchange(): return lax.all_to_all(blocks, axis, split_axis=0, concat_axis=0, tiled=True)]
    all_to_all x2 -> x0, starting transfers between devices: 6.68 us -> none  [exchange(): return lax.all_to_all(blocks, axis, split_axis=0, concat_axis=0, tiled=True)]
    unnamed x8 -> x12, local copies, waits for them, and re-layouts: 0.02 us -> 4.13 us
    pallas_call x2 -> x4, Pallas kernels: 3.52 us -> 1.76 us  [call(): pl.pallas_call(body, out_shape=out_shape, in_specs=in_specs or [vmem] * l...]
    reduce_sum x2 -> x0, other arithmetic: 1.28 us -> none  [the longest x1 0.67 us: per_device(): aud_sum = jnp.sum(exchange(aud_term, 'head').astype(jnp.float32), axis=0)]
  transfers between devices with their start and end apart: 2 -> 11, of which waited for: 2 -> 6; matrix products, arithmetic and copies ran while one was open for 1% -> 0% of each run, Pallas kernels for 2% -> 0%
where the time goes in v2:
time: 32.7 us; the launch traced here: 32.4 us
  starting transfers between devices  14.3 us (44%)
  waiting for transfers between devices  11.5 us (35%)
  local copies, waits for them, and re-layouts  4.13 us (13%)
  Pallas kernels  1.76 us (5%)
  between operations  0.68 us (2%)
    ppermute x8, starting transfers between devices, send(): lax.ppermute(block, 'seq', [(b, a) for a, b in pairs] if back else pairs)  12.4 us
    ppermute x8, waiting for transfers between devices, send(): lax.ppermute(block, 'seq', [(b, a) for a, b in pairs] if back else pairs)  7.14 us
    ppermute x3, waiting for transfers between devices, per_device(): lax.ppermute(terms[k], 'head', route(peers, 1, peers, k))  4.36 us
    unnamed x12, local copies, waits for them, and re-layouts  4.13 us
    ppermute x3, starting transfers between devices, per_device(): lax.ppermute(terms[k], 'head', route(peers, 1, peers, k))  1.92 us
    pallas_call x4, Pallas kernels, call(): pl.pallas_call(body, out_shape=out_shape, in_specs=in_specs or [vmem] * l...  1.76 us
  transfers between devices with their start and end apart: 11, of which 6 were waited for; matrix products, arithmetic and copies ran while one was open for 0% of the time, Pallas kernels for 0%

profile of v2, /device:TPU:0, one launch (start us, length us, event | category | flops | bytes accessed | tf_op | source)
XLA Modules:
  0.0 32.4 jit_solution(7761591990311884939)
XLA Ops:
  0.6 0.8 %copy-done.2 = bf16[128,256]{1,0:T(8,128)(2,1)S(1)} copy-done((bf16[128,256]{1,0:T(8,128)(2,1)S(1)}, bf16[128,256]{1,0:T(8,128)(2,1)}, u32[]{:S(2)}) %copy-start.2) | copy-done | bytes 65560
  1.5 0.8 %copy-done.3 = bf16[128,256]{1,0:T(8,128)(2,1)S(1)} copy-done((bf16[128,256]{1,0:T(8,128)(2,1)S(1)}, bf16[128,256]{1,0:T(8,128)(2,1)}, u32[]{:S(2)}) %copy-start.3) | copy-done | bytes 65560
  2.3 0.7 %copy-done.4 = bf16[24,256]{1,0:T(8,128)(2,1)S(1)} copy-done((bf16[24,256]{1,0:T(8,128)(2,1)S(1)}, bf16[24,256]{1,0:T(8,128)(2,1)}, u32[]{:S(2)}) %copy-start.4) | copy-done | bytes 12312
  3.0 0.7 %copy-done.5 = bf16[24,256]{1,0:T(8,128)(2,1)S(1)} copy-done((bf16[24,256]{1,0:T(8,128)(2,1)S(1)}, bf16[24,256]{1,0:T(8,128)(2,1)}, u32[]{:S(2)}) %copy-start.5) | copy-done | bytes 12312
  3.7 0.1 shard_map.77
  3.8 3.0 %collective-permute-start = (bf16[128,512]{1,0:T(8,128)(2,1)S(1)}, bf16[128,512]{1,0:T(8,128)(2,1)S(1)}, u32[]{:S(2)}, u32[]{:S(2)}) collective-permute-start(bf16[128,512]{1,0:T(8,128)(2,1)S(1)} %get-tuple-element.14.refs_0_), channel_id=1, source_target_pairs={{0,4},{4,0},{8,12},{12,8},{16,20},{20,16},{24,28},{28,24},{1,5},{5... | collective-permute-start | bytes 393224 | tf_op jit(solution)/shard_map/ppermute | solution.py:204
  6.8 3.6 %collective-permute-start.3 = (bf16[24,512]{1,0:T(8,128)(2,1)S(1)}, bf16[24,512]{1,0:T(8,128)(2,1)S(1)}, u32[]{:S(2)}, u32[]{:S(2)}) collective-permute-start(bf16[24,512]{1,0:T(8,128)(2,1)S(1)} %get-tuple-element.15.refs_2_), channel_id=1, source_target_pairs={{0,24},{4,28},{8,16},{12,20},{16,8},{20,12},{24,0},{28,4},{1,25},{... | collective-permute-start | bytes 73736 | tf_op jit(solution)/shard_map/ppermute | solution.py:204
  10.4 0.8 %collective-permute-start.1 = (bf16[24,512]{1,0:T(8,128)(2,1)S(1)}, bf16[24,512]{1,0:T(8,128)(2,1)S(1)}, u32[]{:S(2)}, u32[]{:S(2)}) collective-permute-start(bf16[24,512]{1,0:T(8,128)(2,1)S(1)} %get-tuple-element.15.refs_2_), channel_id=1, source_target_pairs={{0,8},{4,12},{8,0},{12,4},{16,24},{20,28},{24,16},{28,20},{1,9},{5... | collective-permute-start | bytes 73736 | tf_op jit(solution)/shard_map/ppermute | solution.py:204
  11.2 1.5 %collective-permute-done.3.refs_5_ = bf16[24,512]{1,0:T(8,128)(2,1)S(1)} collective-permute-done((bf16[24,512]{1,0:T(8,128)(2,1)S(1)}, bf16[24,512]{1,0:T(8,128)(2,1)S(1)}, u32[]{:S(2)}, u32[]{:S(2)}) %collective-permute-start.3) | collective-permute-done | bytes 24608 | tf_op jit(solution)/shard_map/ppermute | solution.py:204
  12.7 2.4 %collective-permute-done.2.refs_4_ = bf16[24,512]{1,0:T(8,128)(2,1)S(1)} collective-permute-done((bf16[24,512]{1,0:T(8,128)(2,1)S(1)}, bf16[24,512]{1,0:T(8,128)(2,1)S(1)}, u32[]{:S(2)}, u32[]{:S(2)}) %collective-permute-start.2) | collective-permute-done | bytes 24608 | tf_op jit(solution)/shard_map/ppermute | solution.py:204
  15.1 0.6 %shard_map.78 = (bf16[272,128]{1,0:T(8,128)(2,1)S(1)}, bf16[272,128]{1,0:T(8,128)(2,1)S(1)}, bf16[24,384]{1,0:T(8,128)(2,1)S(1)}, bf16[24,384]{1,0:T(8,128)(2,1)...) custom-call(bf16[128,512]{1,0:T(8,128)(2,1)S(1)} %get-tuple-element.14.refs_0_, ...), custom_call_target="tpu_custom_call" | custom-call | tf_op jit(solution)/shard_map/pallas_call | solution.py:158
  15.8 0.6 %collective-permute-start.4 = (bf16[272,128]{1,0:T(8,128)(2,1)S(1)}, bf16[272,128]{1,0:T(8,128)(2,1)S(1)}, u32[]{:S(2)}, u32[]{:S(2)}) collective-permute-start(bf16[272,128]{1,0:T(8,128)(2,1)S(1)} %get-tuple-element.17), channel_id=1, source_target_pairs={{4,0},{0,4},{12,8},{8,12},{20,16},{16,20},{28,24},{24,28},{5,1},{1... | collective-permute-start | bytes 208904 | tf_op jit(solution)/shard_map/ppermute | solution.py:204
  16.4 2.0 %collective-permute-start.6 = (bf16[24,384]{1,0:T(8,128)(2,1)S(1)}, bf16[24,384]{1,0:T(8,128)(2,1)S(1)}, u32[]{:S(2)}, u32[]{:S(2)}) collective-permute-start(bf16[24,384]{1,0:T(8,128)(2,1)S(1)} %get-tuple-element.20), channel_id=1, source_target_pairs={{16,0},{20,4},{24,8},{28,12},{0,16},{4,20},{8,24},{12,28},{17,1},{... | collective-permute-start | bytes 55304 | tf_op jit(solution)/shard_map/ppermute | solution.py:204
  18.4 2.4 %collective-permute-start.7 = (bf16[24,384]{1,0:T(8,128)(2,1)S(1)}, bf16[24,384]{1,0:T(8,128)(2,1)S(1)}, u32[]{:S(2)}, u32[]{:S(2)}) collective-permute-start(bf16[24,384]{1,0:T(8,128)(2,1)S(1)} %get-tuple-element.21), channel_id=1, source_target_pairs={{24,0},{28,4},{16,8},{20,12},{8,16},{12,20},{0,24},{4,28},{25,1},{... | collective-permute-start | bytes 55304 | tf_op jit(solution)/shard_map/ppermute | solution.py:204
  20.8 0.3 collective-permute-done.6.refs_5_
  21.0 2.9 %collective-permute-done.7.refs_6_ = bf16[24,384]{1,0:T(8,128)(2,1)S(1)} collective-permute-done((bf16[24,384]{1,0:T(8,128)(2,1)S(1)}, bf16[24,384]{1,0:T(8,128)(2,1)S(1)}, u32[]{:S(2)}, u32[]{:S(2)}) %collective-permute-start.7) | collective-permute-done | bytes 18464 | tf_op jit(solution)/shard_map/ppermute | solution.py:204
  24.0 1.0 %copy-done.1 = bf16[256,1024]{1,0:T(8,128)(2,1)S(1)} copy-done((bf16[256,1024]{1,0:T(8,128)(2,1)S(1)}, bf16[256,1024]{1,0:T(8,128)(2,1)}, u32[]{:S(2)}) %copy-start.1) | copy-done | bytes 524312
  25.0 0.4 %shard_map.79 = (f32[152,256]{1,0:T(8,128)S(1)}, bf16[152,256]{1,0:T(8,128)(2,1)S(1)}, bf16[152,256]{1,0:T(8,128)(2,1)S(1)}, bf16[152,256]{1,0:T(8,128)(2,1)S(1)}) custom-call(s32[1]{0:T(128)} %bitcast.refs_0_, bf16[272,128]{1,0:T(8,128)(2,1)S(1)} %get-tuple-element.16.refs_1_, bf16[272,128]{1,0:T(8,128)(2,1)S(1)} %collective-permute-done.4.refs_2_, ...), custom_call_target="tpu_custom_call" | custom-call | tf_op jit(solution)/shard_map/pallas_call | solution.py:158
  25.4 0.1 collective-permute-start.8
  25.5 1.6 %collective-permute-start.9 = (bf16[152,256]{1,0:T(8,128)(2,1)S(1)}, bf16[152,256]{1,0:T(8,128)(2,1)S(1)}, u32[]{:S(2)}, u32[]{:S(2)}) collective-permute-start(bf16[152,256]{1,0:T(8,128)(2,1)S(1)} %get-tuple-element.24), channel_id=1, source_target_pairs={{0,2},{1,3},{2,0},{3,1},{4,6},{5,7},{6,4},{7,5},{8,10},{9,11},{10,... | collective-permute-start | bytes 233480 | tf_op jit(solution)/shard_map/ppermute | solution.py:234
  27.1 0.3 collective-permute-start.10
  27.3 3.1 %collective-permute-done.9.refs_2_ = bf16[152,256]{1,0:T(8,128)(2,1)S(1)} collective-permute-done((bf16[152,256]{1,0:T(8,128)(2,1)S(1)}, bf16[152,256]{1,0:T(8,128)(2,1)S(1)}, u32[]{:S(2)}, u32[]{:S(2)}) %collective-permute-start.9) | collective-permute-done | bytes 77856 | tf_op jit(solution)/shard_map/ppermute | solution.py:234
  30.5 1.2 %collective-permute-done.10.refs_3_ = bf16[152,256]{1,0:T(8,128)(2,1)S(1)} collective-permute-done((bf16[152,256]{1,0:T(8,128)(2,1)S(1)}, bf16[152,256]{1,0:T(8,128)(2,1)S(1)}, u32[]{:S(2)}, u32[]{:S(2)}) %collective-permute-start.10) | collective-permute-done | bytes 77856 | tf_op jit(solution)/shard_map/ppermute | solution.py:234
  31.7 0.7 %shard_map.80 = (bf16[128,256]{1,0:T(8,128)(2,1)}, bf16[24,256]{1,0:T(8,128)(2,1)}) custom-call(f32[152,256]{1,0:T(8,128)S(1)} %get-tuple-element.22.refs_0_, bf16[152,256]{1,0:T(8,128)(2,1)S(1)} %collective-permute-done.8.refs_1_, bf16[152,256]{1,0:T(8,128)(2,1)S(1)} %collective-permute-done.9.refs_2_, bf16[152,256]{1,0:T(8,128)(2,1)S(1)} %collective-permute-done.10.refs_3_), custom_call_target="tpu_custom_call" | custom-call | tf_op jit(solution)/shard_map/pallas_call | solution.py:158
  (14 shorter events, 0.0 us)
Async XLA Ops:
  0.6 0.8 %copy-start.2 = (bf16[128,256]{1,0:T(8,128)(2,1)S(1)}, bf16[128,256]{1,0:T(8,128)(2,1)}, u32[]{:S(2)}) copy-start(bf16[128,256]{1,0:T(8,128)(2,1)} %aud_ref.1) | copy-start | bytes 196612
  1.5 0.8 %copy-start.3 = (bf16[128,256]{1,0:T(8,128)(2,1)S(1)}, bf16[128,256]{1,0:T(8,128)(2,1)}, u32[]{:S(2)}) copy-start(bf16[128,256]{1,0:T(8,128)(2,1)} %aud_val.1) | copy-start | bytes 196612
  2.3 0.7 %copy-start.4 = (bf16[24,256]{1,0:T(8,128)(2,1)S(1)}, bf16[24,256]{1,0:T(8,128)(2,1)}, u32[]{:S(2)}) copy-start(bf16[24,256]{1,0:T(8,128)(2,1)} %vid_ref.1) | copy-start | bytes 36868
  3.0 0.7 %copy-start.5 = (bf16[24,256]{1,0:T(8,128)(2,1)S(1)}, bf16[24,256]{1,0:T(8,128)(2,1)}, u32[]{:S(2)}) copy-start(bf16[24,256]{1,0:T(8,128)(2,1)} %vid_val.1) | copy-start | bytes 36868
  3.7 20.2 %copy-start = (bf16[256,1024]{1,0:T(8,128)(2,1)S(1)}, bf16[256,1024]{1,0:T(8,128)(2,1)}, u32[]{:S(2)}) copy-start(bf16[256,1024]{1,0:T(8,128)(2,1)} %refs_7_.1) | copy-start | bytes 1572868
  3.8 11.3 %collective-permute-start = (bf16[128,512]{1,0:T(8,128)(2,1)S(1)}, bf16[128,512]{1,0:T(8,128)(2,1)S(1)}, u32[]{:S(2)}, u32[]{:S(2)}) collective-permute-start(bf16[128,512]{1,0:T(8,128)(2,1)S(1)} %get-tuple-element.14.refs_0_), channel_id=1, source_target_pairs={{0,4},{4,0},{8,12},{12,8},{16,20},{20,16},{24,28},{28,24},{1,5},{5... | collective-permute-start | bytes 393224 | tf_op jit(solution)/shard_map/ppermute | solution.py:204
  6.8 5.9 %collective-permute-start.3 = (bf16[24,512]{1,0:T(8,128)(2,1)S(1)}, bf16[24,512]{1,0:T(8,128)(2,1)S(1)}, u32[]{:S(2)}, u32[]{:S(2)}) collective-permute-start(bf16[24,512]{1,0:T(8,128)(2,1)S(1)} %get-tuple-element.15.refs_2_), channel_id=1, source_target_pairs={{0,24},{4,28},{8,16},{12,20},{16,8},{20,12},{24,0},{28,4},{1,25},{... | collective-permute-start | bytes 73736 | tf_op jit(solution)/shard_map/ppermute | solution.py:204
  10.4 4.7 %collective-permute-start.2 = (bf16[24,512]{1,0:T(8,128)(2,1)S(1)}, bf16[24,512]{1,0:T(8,128)(2,1)S(1)}, u32[]{:S(2)}, u32[]{:S(2)}) collective-permute-start(bf16[24,512]{1,0:T(8,128)(2,1)S(1)} %get-tuple-element.15.refs_2_), channel_id=1, source_target_pairs={{0,16},{4,20},{8,24},{12,28},{16,0},{20,4},{24,8},{28,12},{1,17},{... | collective-permute-start | bytes 73736 | tf_op jit(solution)/shard_map/ppermute | solution.py:204
  10.4 4.7 %collective-permute-start.1 = (bf16[24,512]{1,0:T(8,128)(2,1)S(1)}, bf16[24,512]{1,0:T(8,128)(2,1)S(1)}, u32[]{:S(2)}, u32[]{:S(2)}) collective-permute-start(bf16[24,512]{1,0:T(8,128)(2,1)S(1)} %get-tuple-element.15.refs_2_), channel_id=1, source_target_pairs={{0,8},{4,12},{8,0},{12,4},{16,24},{20,28},{24,16},{28,20},{1,9},{5... | collective-permute-start | bytes 73736 | tf_op jit(solution)/shard_map/ppermute | solution.py:204
  15.8 8.2 %collective-permute-start.4 = (bf16[272,128]{1,0:T(8,128)(2,1)S(1)}, bf16[272,128]{1,0:T(8,128)(2,1)S(1)}, u32[]{:S(2)}, u32[]{:S(2)}) collective-permute-start(bf16[272,128]{1,0:T(8,128)(2,1)S(1)} %get-tuple-element.17), channel_id=1, source_target_pairs={{4,0},{0,4},{12,8},{8,12},{20,16},{16,20},{28,24},{24,28},{5,1},{1... | collective-permute-start | bytes 208904 | tf_op jit(solution)/shard_map/ppermute | solution.py:204
  16.4 4.4 %collective-permute-start.5 = (bf16[24,384]{1,0:T(8,128)(2,1)S(1)}, bf16[24,384]{1,0:T(8,128)(2,1)S(1)}, u32[]{:S(2)}, u32[]{:S(2)}) collective-permute-start(bf16[24,384]{1,0:T(8,128)(2,1)S(1)} %get-tuple-element.19), channel_id=1, source_target_pairs={{8,0},{12,4},{0,8},{4,12},{24,16},{28,20},{16,24},{20,28},{9,1},{1... | collective-permute-start | bytes 55304 | tf_op jit(solution)/shard_map/ppermute | solution.py:204
  16.4 4.7 %collective-permute-start.6 = (bf16[24,384]{1,0:T(8,128)(2,1)S(1)}, bf16[24,384]{1,0:T(8,128)(2,1)S(1)}, u32[]{:S(2)}, u32[]{:S(2)}) collective-permute-start(bf16[24,384]{1,0:T(8,128)(2,1)S(1)} %get-tuple-element.20), channel_id=1, source_target_pairs={{16,0},{20,4},{24,8},{28,12},{0,16},{4,20},{8,24},{12,28},{17,1},{... | collective-permute-start | bytes 55304 | tf_op jit(solution)/shard_map/ppermute | solution.py:204
  18.4 5.6 %collective-permute-start.7 = (bf16[24,384]{1,0:T(8,128)(2,1)S(1)}, bf16[24,384]{1,0:T(8,128)(2,1)S(1)}, u32[]{:S(2)}, u32[]{:S(2)}) collective-permute-start(bf16[24,384]{1,0:T(8,128)(2,1)S(1)} %get-tuple-element.21), channel_id=1, source_target_pairs={{24,0},{28,4},{16,8},{20,12},{8,16},{12,20},{0,24},{4,28},{25,1},{... | collective-permute-start | bytes 55304 | tf_op jit(solution)/shard_map/ppermute | solution.py:204
  24.0 1.0 %copy-start.1 = (bf16[256,1024]{1,0:T(8,128)(2,1)S(1)}, bf16[256,1024]{1,0:T(8,128)(2,1)}, u32[]{:S(2)}) copy-start(bf16[256,1024]{1,0:T(8,128)(2,1)} %refs_8_.1) | copy-start | bytes 1572868
  25.4 1.9 %collective-permute-start.8 = (bf16[152,256]{1,0:T(8,128)(2,1)S(1)}, bf16[152,256]{1,0:T(8,128)(2,1)S(1)}, u32[]{:S(2)}, u32[]{:S(2)}) collective-permute-start(bf16[152,256]{1,0:T(8,128)(2,1)S(1)} %get-tuple-element.23), channel_id=1, source_target_pairs={{0,1},{1,0},{2,3},{3,2},{4,5},{5,4},{6,7},{7,6},{8,9},{9,8},{10,11... | collective-permute-start | bytes 233480 | tf_op jit(solution)/shard_map/ppermute | solution.py:234
  25.5 5.0 %collective-permute-start.9 = (bf16[152,256]{1,0:T(8,128)(2,1)S(1)}, bf16[152,256]{1,0:T(8,128)(2,1)S(1)}, u32[]{:S(2)}, u32[]{:S(2)}) collective-permute-start(bf16[152,256]{1,0:T(8,128)(2,1)S(1)} %get-tuple-element.24), channel_id=1, source_target_pairs={{0,2},{1,3},{2,0},{3,1},{4,6},{5,7},{6,4},{7,5},{8,10},{9,11},{10,... | collective-permute-start | bytes 233480 | tf_op jit(solution)/shard_map/ppermute | solution.py:234
  27.1 4.6 %collective-permute-start.10 = (bf16[152,256]{1,0:T(8,128)(2,1)S(1)}, bf16[152,256]{1,0:T(8,128)(2,1)S(1)}, u32[]{:S(2)}, u32[]{:S(2)}) collective-permute-start(bf16[152,256]{1,0:T(8,128)(2,1)S(1)} %get-tuple-element.25), channel_id=1, source_target_pairs={{0,3},{1,2},{2,1},{3,0},{4,7},{5,6},{6,5},{7,4},{8,11},{9,10},{10,... | collective-permute-start | bytes 233480 | tf_op jit(solution)/shard_map/ppermute | solution.py:234

commit v3 on v2

--- a/solution.py
+++ b/solution.py
@@ -111,14 +111,18 @@
     return mix / total
 
 
-def project(aud_count, vid_count, aud_me, *refs):
-    rows, cols = refs[:aud_count], refs[aud_count : aud_count + vid_count]
-    aud_proj, vid_proj = refs[aud_count + vid_count : aud_count + vid_count + 2]
-    outs = refs[aud_count + vid_count + 2 :]
-    width = aud_proj.shape[0]
-    heads = width // HEAD_DIM
-    aud_rows, vid_rows = rows[0].shape[1], cols[0].shape[0]
-
+def project(mix, proj, me, outs):
+    step = outs[0].shape[1]
+    for i, out in enumerate(outs):
+        block = pl.ds(pl.multiple_of(partner(me, i, len(outs)) * step, step), step)
+        out[...] = dot(mix, proj[:, block]).astype(out.dtype)
+
+
+def project_audio(count, me, *refs):
+    rows, proj, outs = refs[:count], refs[count], refs[count + 1 :]
+    width = proj.shape[0]
+    heads = width // HEAD_DIM
+    aud_rows = rows[0].shape[1]
     logs, mixes = [], []
     for ref in rows:
         pieces = ref[width:, :].astype(F32)
@@ -127,30 +131,28 @@
             log = log + pieces[i * heads : (i + 1) * heads]
         logs.append(log.reshape(heads, 1, aud_rows))
         mixes.append(ref[:width, :].astype(F32).reshape(heads, HEAD_DIM, aud_rows))
-    aud_mix = merged(mixes, logs).reshape(width, aud_rows).astype(BF16)
-
+    mix = merged(mixes, logs).reshape(width, aud_rows)
+    project(mix.T.astype(BF16), proj, me[0], outs)
+
+
+def project_video(count, me, *refs):
+    cols, proj, outs = refs[:count], refs[count], refs[count + 1 :]
+    width = proj.shape[0]
+    heads = width // HEAD_DIM
     source = lax.broadcasted_iota(jnp.int32, (LANES, width), 0)
     target = lax.broadcasted_iota(jnp.int32, (LANES, width), 1)
     spread = ((source < PIECES * heads) & (source % heads == target // HEAD_DIM)).astype(BF16)
     logs = [dot(ref[:, width:], spread) for ref in cols]
-    vid_mix = merged([ref[:, :width].astype(F32) for ref in cols], logs).astype(BF16)
-
-    step = outs[0].shape[1]
-    me = aud_me[0]
-    for i, out in enumerate(outs):
-        block = pl.ds(pl.multiple_of(partner(me, i, len(outs)) * step, step), step)
-        out[:aud_rows, :] = dot(aud_mix, aud_proj[:, block], 0, 0).astype(out.dtype)
-        out[aud_rows:, :] = dot(vid_mix, vid_proj[:, block]).astype(out.dtype)
+    mix = merged([ref[:, :width].astype(F32) for ref in cols], logs)
+    project(mix.astype(BF16), proj, me[0], outs)
 
 
 def add(*refs):
-    terms, (aud_out, vid_out) = refs[:-2], refs[-2:]
-    aud_rows = aud_out.shape[0]
-    for out, rows in ((aud_out, slice(0, aud_rows)), (vid_out, slice(aud_rows, None))):
-        total = terms[0][rows, :].astype(F32)
-        for term in terms[1:]:
-            total += term[rows, :].astype(F32)
-        out[...] = total.astype(BF16)
+    terms, out = refs[:-1], refs[-1]
+    total = terms[0][...].astype(F32)
+    for term in terms[1:]:
+        total += term[...].astype(F32)
+    out[...] = total.astype(BF16)
 
 
 def call(body, out_shape, args, in_specs=None, scratch=()):
@@ -206,8 +208,11 @@
     aud, vid = call(
         pack,
         (shape((aud_rows, 2 * width), BF16), shape((vid_rows, 2 * width), BF16)),
-        (ref_audio, val_audio, ref_video, val_video),
-        in_specs=[pl.BlockSpec(memory_space=pl.ANY)] * 4,
+        [
+            pltpu.with_memory_space_constraint(x, pltpu.HBM)
+            for x in (ref_audio, val_audio, ref_video, val_video)
+        ],
+        in_specs=[pl.BlockSpec(memory_space=pltpu.HBM)] * 4,
         scratch=[pltpu.SemaphoreType.DMA((4,))],
     )
     auds = [send(aud, 1, aud_count, k) for k in range(aud_count)]
@@ -220,27 +225,29 @@
         auds + vids,
     )
     rows = [send(states[k], 1, aud_count, k, True) for k in range(aud_count)]
-    cols = [send(states[aud_count + k], aud_count, vid_count, k, True) for k in range(vid_count)]
+    cols = [
+        send(states[aud_count + k], aud_count, vid_count, k, True) for k in reversed(range(vid_count))
+    ]
     me = lax.axis_index("head").astype(jnp.int32).reshape(1)
     vmem = pl.BlockSpec(memory_space=pltpu.VMEM)
-    terms = call(
-        lambda *refs: project(aud_count, vid_count, *refs),
-        [shape((aud_rows + vid_rows, step), F32)]
-        + [shape((aud_rows + vid_rows, step), BF16)] * (peers - 1),
-        [me] + rows + cols + [audio_proj, video_proj],
-        in_specs=[pl.BlockSpec(memory_space=pltpu.SMEM)] + [vmem] * (seq_terms(aud_count, vid_count)),
-    )
-    got = [terms[0]] + [
-        lax.ppermute(terms[k], "head", route(peers, 1, peers, k)) for k in range(1, peers)
-    ]
-    aud_out, vid_out = call(
-        add, (shape((aud_rows, step), BF16), shape((vid_rows, step), BF16)), got
-    )
-    return aud_out, vid_out
-
-
-def seq_terms(aud_count, vid_count):
-    return aud_count + vid_count + 2
+
+    def head_sum(body, states, proj, count):
+        terms = call(
+            lambda *refs: body(len(states), *refs),
+            [shape((count, step), F32)] + [shape((count, step), BF16)] * (peers - 1),
+            [me] + states + [proj],
+            in_specs=[pl.BlockSpec(memory_space=pltpu.SMEM)] + [vmem] * (len(states) + 1),
+        )
+        got = [
+            lax.ppermute(terms[k], "head", route(peers, 1, peers, k))
+            for k in reversed(range(1, peers))
+        ]
+        return call(add, [shape((count, step), BF16)], [terms[0]] + got)[0]
+
+    return (
+        head_sum(project_audio, rows, audio_proj, aud_rows),
+        head_sum(project_video, cols, video_proj, vid_rows),
+    )
 
 
 def solution(mesh):

time: 32.7 us -> 36.3 us (1.11)
  waiting for transfers between devices: 11.5 us -> 19.7 us
  local copies, waits for them, and re-layouts: 4.13 us -> 0.01 us
  starting transfers between devices: 14.3 us -> 12.2 us
  Pallas kernels: 1.76 us -> 3.49 us
    ppermute x8, waiting for transfers between devices: 7.14 us -> 17 us  [send(): lax.ppermute(block, 'seq', [(b, a) for a, b in pairs] if back else pairs)]
    unnamed x12 -> x4, local copies, waits for them, and re-layouts: 4.13 us -> 0.01 us
    ppermute x8, starting transfers between devices: 12.4 us -> 8.56 us  [send(): lax.ppermute(block, 'seq', [(b, a) for a, b in pairs] if back else pairs)]
    ppermute x3 -> x6, starting transfers between devices: 1.92 us -> 3.67 us  [head_sum(): lax.ppermute(terms[k], 'head', route(peers, 1, peers, k))]
    pallas_call x4 -> x6, Pallas kernels: 1.76 us -> 3.49 us  [call(): pl.pallas_call(body, out_shape=out_shape, in_specs=in_specs or [vmem] * l...]
    ppermute x3 -> x6, waiting for transfers between devices: 4.36 us -> 2.65 us  [head_sum(): lax.ppermute(terms[k], 'head', route(peers, 1, peers, k))]
  transfers between devices with their start and end apart: 11 -> 14, of which waited for: 6 -> 9; matrix products, arithmetic and copies ran while one was open for 0% -> 0% of each run, Pallas kernels for 0% -> 3%
where the time goes in v3:
time: 36.3 us; the launch traced here: 36.1 us
  waiting for transfers between devices  19.7 us (54%)
  starting transfers between devices  12.2 us (34%)
  Pallas kernels  3.49 us (10%)
  between operations  0.69 us (2%)
    ppermute x8, waiting for transfers between devices, send(): lax.ppermute(block, 'seq', [(b, a) for a, b in pairs] if back else pairs)  17 us
    ppermute x8, starting transfers between devices, send(): lax.ppermute(block, 'seq', [(b, a) for a, b in pairs] if back else pairs)  8.56 us
    ppermute x6, starting transfers between devices, head_sum(): lax.ppermute(terms[k], 'head', route(peers, 1, peers, k))  3.67 us
    pallas_call x6, Pallas kernels, call(): pl.pallas_call(body, out_shape=out_shape, in_specs=in_specs or [vmem] * l...  3.49 us
    ppermute x6, waiting for transfers between devices, head_sum(): lax.ppermute(terms[k], 'head', route(peers, 1, peers, k))  2.65 us
  transfers between devices with their start and end apart: 14, of which 9 were waited for; matrix products, arithmetic and copies ran while one was open for 0% of the time, Pallas kernels for 3%

profile of v3, /device:TPU:0, one launch (start us, length us, event | category | flops | bytes accessed | tf_op | source)
XLA Modules:
  0.0 36.1 jit_solution(13031340055474942175)
XLA Ops:
  0.6 1.0 %shard_map.77 = (bf16[128,512]{1,0:T(8,128)(2,1)S(1)}, bf16[24,512]{1,0:T(8,128)(2,1)S(1)}) custom-call(bf16[128,256]{1,0:T(8,128)(2,1)} %aud_ref.1, bf16[128,256]{1,0:T(8,128)(2,1)} %aud_val.1, bf16[24,256]{1,0:T(8,128)(2,1)} %vid_ref.1, bf16[24,256]{1,0:T(8,128)(2,1)} %vid_val.1), custom_call_target="tpu_custom_call" | custom-call | tf_op jit(solution)/shard_map/pallas_call | solution.py:160
  1.6 3.0 %collective-permute-start = (bf16[128,512]{1,0:T(8,128)(2,1)S(1)}, bf16[128,512]{1,0:T(8,128)(2,1)S(1)}, u32[]{:S(2)}, u32[]{:S(2)}) collective-permute-start(bf16[128,512]{1,0:T(8,128)(2,1)S(1)} %get-tuple-element.18.refs_0_), channel_id=1, source_target_pairs={{0,4},{4,0},{8,12},{12,8},{16,20},{20,16},{24,28},{28,24},{1,5},{5... | collective-permute-start | bytes 393224 | tf_op jit(solution)/shard_map/ppermute | solution.py:206
  4.6 1.6 %collective-permute-start.1 = (bf16[24,512]{1,0:T(8,128)(2,1)S(1)}, bf16[24,512]{1,0:T(8,128)(2,1)S(1)}, u32[]{:S(2)}, u32[]{:S(2)}) collective-permute-start(bf16[24,512]{1,0:T(8,128)(2,1)S(1)} %get-tuple-element.19.refs_2_), channel_id=1, source_target_pairs={{0,8},{4,12},{8,0},{12,4},{16,24},{20,28},{24,16},{28,20},{1,9},{5... | collective-permute-start | bytes 73736 | tf_op jit(solution)/shard_map/ppermute | solution.py:206
  6.2 2.6 %collective-permute-start.2 = (bf16[24,512]{1,0:T(8,128)(2,1)S(1)}, bf16[24,512]{1,0:T(8,128)(2,1)S(1)}, u32[]{:S(2)}, u32[]{:S(2)}) collective-permute-start(bf16[24,512]{1,0:T(8,128)(2,1)S(1)} %get-tuple-element.19.refs_2_), channel_id=1, source_target_pairs={{0,16},{4,20},{8,24},{12,28},{16,0},{20,4},{24,8},{28,12},{1,17},{... | collective-permute-start | bytes 73736 | tf_op jit(solution)/shard_map/ppermute | solution.py:206
  8.8 0.2 collective-permute-start.3
  9.0 2.1 %collective-permute-done.2.refs_4_ = bf16[24,512]{1,0:T(8,128)(2,1)S(1)} collective-permute-done((bf16[24,512]{1,0:T(8,128)(2,1)S(1)}, bf16[24,512]{1,0:T(8,128)(2,1)S(1)}, u32[]{:S(2)}, u32[]{:S(2)}) %collective-permute-start.2) | collective-permute-done | bytes 24608 | tf_op jit(solution)/shard_map/ppermute | solution.py:206
  11.1 3.3 %collective-permute-done.3.refs_5_ = bf16[24,512]{1,0:T(8,128)(2,1)S(1)} collective-permute-done((bf16[24,512]{1,0:T(8,128)(2,1)S(1)}, bf16[24,512]{1,0:T(8,128)(2,1)S(1)}, u32[]{:S(2)}, u32[]{:S(2)}) %collective-permute-start.3) | collective-permute-done | bytes 24608 | tf_op jit(solution)/shard_map/ppermute | solution.py:206
  14.4 0.6 %shard_map.78 = (bf16[272,128]{1,0:T(8,128)(2,1)S(1)}, bf16[272,128]{1,0:T(8,128)(2,1)S(1)}, bf16[24,384]{1,0:T(8,128)(2,1)S(1)}, bf16[24,384]{1,0:T(8,128)(2,1)...) custom-call(bf16[128,512]{1,0:T(8,128)(2,1)S(1)} %get-tuple-element.18.refs_0_, ...), custom_call_target="tpu_custom_call" | custom-call | tf_op jit(solution)/shard_map/pallas_call | solution.py:160
  15.1 0.6 %collective-permute-start.4 = (bf16[272,128]{1,0:T(8,128)(2,1)S(1)}, bf16[272,128]{1,0:T(8,128)(2,1)S(1)}, u32[]{:S(2)}, u32[]{:S(2)}) collective-permute-start(bf16[272,128]{1,0:T(8,128)(2,1)S(1)} %get-tuple-element.21), channel_id=1, source_target_pairs={{4,0},{0,4},{12,8},{8,12},{20,16},{16,20},{28,24},{24,28},{5,1},{1... | collective-permute-start | bytes 208904 | tf_op jit(solution)/shard_map/ppermute | solution.py:206
  15.7 3.8 %collective-permute-done.4.refs_2_ = bf16[272,128]{1,0:T(8,128)(2,1)S(1)} collective-permute-done((bf16[272,128]{1,0:T(8,128)(2,1)S(1)}, bf16[272,128]{1,0:T(8,128)(2,1)S(1)}, u32[]{:S(2)}, u32[]{:S(2)}) %collective-permute-start.4) | collective-permute-done | bytes 69664 | tf_op jit(solution)/shard_map/ppermute | solution.py:206
  19.4 0.3 shard_map.79
  19.8 1.6 %collective-permute-start.6 = (bf16[128,256]{1,0:T(8,128)(2,1)S(1)}, bf16[128,256]{1,0:T(8,128)(2,1)S(1)}, u32[]{:S(2)}, u32[]{:S(2)}) collective-permute-start(bf16[128,256]{1,0:T(8,128)(2,1)S(1)} %get-tuple-element.24), channel_id=1, source_target_pairs={{0,2},{1,3},{2,0},{3,1},{4,6},{5,7},{6,4},{7,5},{8,10},{9,11},{10,... | collective-permute-start | bytes 196616 | tf_op jit(solution)/shard_map/ppermute | solution.py:242
  21.4 0.3 collective-permute-start.7
  21.7 0.6 %collective-permute-start.8 = (bf16[24,384]{1,0:T(8,128)(2,1)S(1)}, bf16[24,384]{1,0:T(8,128)(2,1)S(1)}, u32[]{:S(2)}, u32[]{:S(2)}) collective-permute-start(bf16[24,384]{1,0:T(8,128)(2,1)S(1)} %get-tuple-element.26), channel_id=1, source_target_pairs={{24,0},{28,4},{16,8},{20,12},{8,16},{12,20},{0,24},{4,28},{25,1},{... | collective-permute-start | bytes 55304 | tf_op jit(solution)/shard_map/ppermute | solution.py:206
  22.2 3.2 %collective-permute-done.10.refs_3_ = bf16[24,384]{1,0:T(8,128)(2,1)S(1)} collective-permute-done((bf16[24,384]{1,0:T(8,128)(2,1)S(1)}, bf16[24,384]{1,0:T(8,128)(2,1)S(1)}, u32[]{:S(2)}, u32[]{:S(2)}) %collective-permute-start.10) | collective-permute-done | bytes 18464 | tf_op jit(solution)/shard_map/ppermute | solution.py:206
  25.4 1.8 %collective-permute-done.8.refs_1_ = bf16[24,384]{1,0:T(8,128)(2,1)S(1)} collective-permute-done((bf16[24,384]{1,0:T(8,128)(2,1)S(1)}, bf16[24,384]{1,0:T(8,128)(2,1)S(1)}, u32[]{:S(2)}, u32[]{:S(2)}) %collective-permute-start.8) | collective-permute-done | bytes 18464 | tf_op jit(solution)/shard_map/ppermute | solution.py:206
  27.2 2.9 %collective-permute-done.9.refs_2_ = bf16[24,384]{1,0:T(8,128)(2,1)S(1)} collective-permute-done((bf16[24,384]{1,0:T(8,128)(2,1)S(1)}, bf16[24,384]{1,0:T(8,128)(2,1)S(1)}, u32[]{:S(2)}, u32[]{:S(2)}) %collective-permute-start.9) | collective-permute-done | bytes 18464 | tf_op jit(solution)/shard_map/ppermute | solution.py:206
  30.1 0.3 shard_map.81
  30.5 1.6 %collective-permute-start.12 = (bf16[24,256]{1,0:T(8,128)(2,1)S(1)}, bf16[24,256]{1,0:T(8,128)(2,1)S(1)}, u32[]{:S(2)}, u32[]{:S(2)}) collective-permute-start(bf16[24,256]{1,0:T(8,128)(2,1)S(1)} %get-tuple-element.32), channel_id=1, source_target_pairs={{0,2},{1,3},{2,0},{3,1},{4,6},{5,7},{6,4},{7,5},{8,10},{9,11},{10,... | collective-permute-start | bytes 36872 | tf_op jit(solution)/shard_map/ppermute | solution.py:242
  32.1 1.6 %collective-permute-done.11.refs_1_ = bf16[24,256]{1,0:T(8,128)(2,1)S(1)} collective-permute-done((bf16[24,256]{1,0:T(8,128)(2,1)S(1)}, bf16[24,256]{1,0:T(8,128)(2,1)S(1)}, u32[]{:S(2)}, u32[]{:S(2)}) %collective-permute-start.11) | collective-permute-done | bytes 12320 | tf_op jit(solution)/shard_map/ppermute | solution.py:242
  33.7 0.5 %collective-permute-done.12.refs_2_ = bf16[24,256]{1,0:T(8,128)(2,1)S(1)} collective-permute-done((bf16[24,256]{1,0:T(8,128)(2,1)S(1)}, bf16[24,256]{1,0:T(8,128)(2,1)S(1)}, u32[]{:S(2)}, u32[]{:S(2)}) %collective-permute-start.12) | collective-permute-done | bytes 12320 | tf_op jit(solution)/shard_map/ppermute | solution.py:242
  34.2 0.6 %collective-permute-done.13.refs_3_ = bf16[24,256]{1,0:T(8,128)(2,1)S(1)} collective-permute-done((bf16[24,256]{1,0:T(8,128)(2,1)S(1)}, bf16[24,256]{1,0:T(8,128)(2,1)S(1)}, u32[]{:S(2)}, u32[]{:S(2)}) %collective-permute-start.13) | collective-permute-done | bytes 12320 | tf_op jit(solution)/shard_map/ppermute | solution.py:242
  34.8 0.6 %shard_map.82 = bf16[24,256]{1,0:T(8,128)(2,1)} custom-call(f32[24,256]{1,0:T(8,128)S(1)} %get-tuple-element.30.refs_0_, bf16[24,256]{1,0:T(8,128)(2,1)S(1)} %collective-permute-done.11.refs_1_, bf16[24,256]{1,0:T(8,128)(2,1)S(1)} %collective-permute-done.12.refs_2_, bf16[24,256]{1,0:T(8,128)(2,1)S(1)} %collective-permute-done.13.refs_3_), custom_call_target="tpu_custom_call" | custom-call | tf_op jit(solution)/shard_map/pallas_call | solution.py:160
  35.4 0.7 %shard_map.80 = bf16[128,256]{1,0:T(8,128)(2,1)} custom-call(f32[128,256]{1,0:T(8,128)S(1)} %get-tuple-element.22.refs_0_, bf16[128,256]{1,0:T(8,128)(2,1)S(1)} %collective-permute-done.5.refs_1_, bf16[128,256]{1,0:T(8,128)(2,1)S(1)} %collective-permute-done.6.refs_2_, bf16[128,256]{1,0:T(8,128)(2,1)S(1)} %collective-permute-done.7.refs_3_), custom_call_target="tpu_custom_call" | custom-call | tf_op jit(solution)/shard_map/pallas_call | solution.py:160
  (14 shorter events, 0.3 us)
Async XLA Ops:
  0.6 18.8 %copy-start = (bf16[256,1024]{1,0:T(8,128)(2,1)S(1)}, bf16[256,1024]{1,0:T(8,128)(2,1)}, u32[]{:S(2)}) copy-start(bf16[256,1024]{1,0:T(8,128)(2,1)} %refs_3_.1) | copy-start | bytes 1572868
  1.6 12.8 %collective-permute-start = (bf16[128,512]{1,0:T(8,128)(2,1)S(1)}, bf16[128,512]{1,0:T(8,128)(2,1)S(1)}, u32[]{:S(2)}, u32[]{:S(2)}) collective-permute-start(bf16[128,512]{1,0:T(8,128)(2,1)S(1)} %get-tuple-element.18.refs_0_), channel_id=1, source_target_pairs={{0,4},{4,0},{8,12},{12,8},{16,20},{20,16},{24,28},{28,24},{1,5},{5... | collective-permute-start | bytes 393224 | tf_op jit(solution)/shard_map/ppermute | solution.py:206
  4.6 25.5 %copy-start.1 = (bf16[256,1024]{1,0:T(8,128)(2,1)S(1)}, bf16[256,1024]{1,0:T(8,128)(2,1)}, u32[]{:S(2)}) copy-start(bf16[256,1024]{1,0:T(8,128)(2,1)} %refs_5_.1) | copy-start | bytes 1572868
  4.6 4.4 %collective-permute-start.1 = (bf16[24,512]{1,0:T(8,128)(2,1)S(1)}, bf16[24,512]{1,0:T(8,128)(2,1)S(1)}, u32[]{:S(2)}, u32[]{:S(2)}) collective-permute-start(bf16[24,512]{1,0:T(8,128)(2,1)S(1)} %get-tuple-element.19.refs_2_), channel_id=1, source_target_pairs={{0,8},{4,12},{8,0},{12,4},{16,24},{20,28},{24,16},{28,20},{1,9},{5... | collective-permute-start | bytes 73736 | tf_op jit(solution)/shard_map/ppermute | solution.py:206
  6.2 4.9 %collective-permute-start.2 = (bf16[24,512]{1,0:T(8,128)(2,1)S(1)}, bf16[24,512]{1,0:T(8,128)(2,1)S(1)}, u32[]{:S(2)}, u32[]{:S(2)}) collective-permute-start(bf16[24,512]{1,0:T(8,128)(2,1)S(1)} %get-tuple-element.19.refs_2_), channel_id=1, source_target_pairs={{0,16},{4,20},{8,24},{12,28},{16,0},{20,4},{24,8},{28,12},{1,17},{... | collective-permute-start | bytes 73736 | tf_op jit(solution)/shard_map/ppermute | solution.py:206
  8.8 5.6 %collective-permute-start.3 = (bf16[24,512]{1,0:T(8,128)(2,1)S(1)}, bf16[24,512]{1,0:T(8,128)(2,1)S(1)}, u32[]{:S(2)}, u32[]{:S(2)}) collective-permute-start(bf16[24,512]{1,0:T(8,128)(2,1)S(1)} %get-tuple-element.19.refs_2_), channel_id=1, source_target_pairs={{0,24},{4,28},{8,16},{12,20},{16,8},{20,12},{24,0},{28,4},{1,25},{... | collective-permute-start | bytes 73736 | tf_op jit(solution)/shard_map/ppermute | solution.py:206
  15.1 4.4 %collective-permute-start.4 = (bf16[272,128]{1,0:T(8,128)(2,1)S(1)}, bf16[272,128]{1,0:T(8,128)(2,1)S(1)}, u32[]{:S(2)}, u32[]{:S(2)}) collective-permute-start(bf16[272,128]{1,0:T(8,128)(2,1)S(1)} %get-tuple-element.21), channel_id=1, source_target_pairs={{4,0},{0,4},{12,8},{8,12},{20,16},{16,20},{28,24},{24,28},{5,1},{1... | collective-permute-start | bytes 208904 | tf_op jit(solution)/shard_map/ppermute | solution.py:206
  19.7 15.7 %collective-permute-start.5 = (bf16[128,256]{1,0:T(8,128)(2,1)S(1)}, bf16[128,256]{1,0:T(8,128)(2,1)S(1)}, u32[]{:S(2)}, u32[]{:S(2)}) collective-permute-start(bf16[128,256]{1,0:T(8,128)(2,1)S(1)} %get-tuple-element.23), channel_id=1, source_target_pairs={{0,3},{1,2},{2,1},{3,0},{4,7},{5,6},{6,5},{7,4},{8,11},{9,10},{10,... | collective-permute-start | bytes 196616 | tf_op jit(solution)/shard_map/ppermute | solution.py:242
  19.8 15.6 %collective-permute-start.6 = (bf16[128,256]{1,0:T(8,128)(2,1)S(1)}, bf16[128,256]{1,0:T(8,128)(2,1)S(1)}, u32[]{:S(2)}, u32[]{:S(2)}) collective-permute-start(bf16[128,256]{1,0:T(8,128)(2,1)S(1)} %get-tuple-element.24), channel_id=1, source_target_pairs={{0,2},{1,3},{2,0},{3,1},{4,6},{5,7},{6,4},{7,5},{8,10},{9,11},{10,... | collective-permute-start | bytes 196616 | tf_op jit(solution)/shard_map/ppermute | solution.py:242
  21.4 14.0 %collective-permute-start.7 = (bf16[128,256]{1,0:T(8,128)(2,1)S(1)}, bf16[128,256]{1,0:T(8,128)(2,1)S(1)}, u32[]{:S(2)}, u32[]{:S(2)}) collective-permute-start(bf16[128,256]{1,0:T(8,128)(2,1)S(1)} %get-tuple-element.25), channel_id=1, source_target_pairs={{0,1},{1,0},{2,3},{3,2},{4,5},{5,4},{6,7},{7,6},{8,9},{9,8},{10,11... | collective-permute-start | bytes 196616 | tf_op jit(solution)/shard_map/ppermute | solution.py:242
  21.7 3.8 %collective-permute-start.10 = (bf16[24,384]{1,0:T(8,128)(2,1)S(1)}, bf16[24,384]{1,0:T(8,128)(2,1)S(1)}, u32[]{:S(2)}, u32[]{:S(2)}) collective-permute-start(bf16[24,384]{1,0:T(8,128)(2,1)S(1)} %get-tuple-element.28), channel_id=1, source_target_pairs={{8,0},{12,4},{0,8},{4,12},{24,16},{28,20},{16,24},{20,28},{9,1},{1... | collective-permute-start | bytes 55304 | tf_op jit(solution)/shard_map/ppermute | solution.py:206
  21.7 5.6 %collective-permute-start.8 = (bf16[24,384]{1,0:T(8,128)(2,1)S(1)}, bf16[24,384]{1,0:T(8,128)(2,1)S(1)}, u32[]{:S(2)}, u32[]{:S(2)}) collective-permute-start(bf16[24,384]{1,0:T(8,128)(2,1)S(1)} %get-tuple-element.26), channel_id=1, source_target_pairs={{24,0},{28,4},{16,8},{20,12},{8,16},{12,20},{0,24},{4,28},{25,1},{... | collective-permute-start | bytes 55304 | tf_op jit(solution)/shard_map/ppermute | solution.py:206
  25.4 4.7 %collective-permute-start.9 = (bf16[24,384]{1,0:T(8,128)(2,1)S(1)}, bf16[24,384]{1,0:T(8,128)(2,1)S(1)}, u32[]{:S(2)}, u32[]{:S(2)}) collective-permute-start(bf16[24,384]{1,0:T(8,128)(2,1)S(1)} %get-tuple-element.27), channel_id=1, source_target_pairs={{16,0},{20,4},{24,8},{28,12},{0,16},{4,20},{8,24},{12,28},{17,1},{... | collective-permute-start | bytes 55304 | tf_op jit(solution)/shard_map/ppermute | solution.py:206
  30.4 3.2 %collective-permute-start.11 = (bf16[24,256]{1,0:T(8,128)(2,1)S(1)}, bf16[24,256]{1,0:T(8,128)(2,1)S(1)}, u32[]{:S(2)}, u32[]{:S(2)}) collective-permute-start(bf16[24,256]{1,0:T(8,128)(2,1)S(1)} %get-tuple-element.31), channel_id=1, source_target_pairs={{0,3},{1,2},{2,1},{3,0},{4,7},{5,6},{6,5},{7,4},{8,11},{9,10},{10,... | collective-permute-start | bytes 36872 | tf_op jit(solution)/shard_map/ppermute | solution.py:242
  30.5 3.8 %collective-permute-start.12 = (bf16[24,256]{1,0:T(8,128)(2,1)S(1)}, bf16[24,256]{1,0:T(8,128)(2,1)S(1)}, u32[]{:S(2)}, u32[]{:S(2)}) collective-permute-start(bf16[24,256]{1,0:T(8,128)(2,1)S(1)} %get-tuple-element.32), channel_id=1, source_target_pairs={{0,2},{1,3},{2,0},{3,1},{4,6},{5,7},{6,4},{7,5},{8,10},{9,11},{10,... | collective-permute-start | bytes 36872 | tf_op jit(solution)/shard_map/ppermute | solution.py:242
  33.6 1.2 %collective-permute-start.13 = (bf16[24,256]{1,0:T(8,128)(2,1)S(1)}, bf16[24,256]{1,0:T(8,128)(2,1)S(1)}, u32[]{:S(2)}, u32[]{:S(2)}) collective-permute-start(bf16[24,256]{1,0:T(8,128)(2,1)S(1)} %get-tuple-element.33), channel_id=1, source_target_pairs={{0,1},{1,0},{2,3},{3,2},{4,5},{5,4},{6,7},{7,6},{8,9},{9,8},{10,11... | collective-permute-start | bytes 36872 | tf_op jit(solution)/shard_map/ppermute | solution.py:242

commit v4 on v3

v4 whole, which is shorter than its diff:
```python
import functools

import jax
import jax.numpy as jnp
from jax import lax
from jax.experimental import pallas as pl
from jax.experimental.pallas import tpu as pltpu
from jax.sharding import PartitionSpec as P

HEAD_DIM = 64
LANES = 128
PIECES = 3
SCALE = HEAD_DIM ** (-0.5)
VMEM_LIMIT = 48 * 1024 * 1024
COST = 5 * 10**9
BF16 = jnp.bfloat16
F32 = jnp.float32


def dot(a, b, contract_a=1, contract_b=0):
    dims = (((contract_a,), (contract_b,)), ((), ()))
    return lax.dot_general(a, b, dims, preferred_element_type=F32)


def split_pieces(value):
    pieces = []
    for _ in range(PIECES):
        piece = value.astype(BF16).astype(F32)
        pieces.append(piece)
        value = value - piece
    return pieces


def head_lanes(rows, width, head):
    return lax.broadcasted_iota(jnp.int32, (rows, width), 1) // HEAD_DIM == head


def pack(aud_ref, aud_val, vid_ref, vid_val, aud, vid, sems):
    width = aud_ref.shape[1]
    copies = [
        pltpu.make_async_copy(source, target.at[:, start : start + width], sems.at[i])
        for i, (source, target, start) in enumerate(
            ((aud_ref, aud, 0), (aud_val, aud, width), (vid_ref, vid, 0), (vid_val, vid, width))
        )
    ]
    for copy in copies:
        copy.start()
    for copy in copies:
        copy.wait()


def in_order(blocks):
    order = [0]
    bit = len(blocks) // 2
    while bit:
        order += [k + bit for k in order]
        bit //= 2
    return [blocks[len(blocks) - 1 - k] for k in order]


def attend(aud_count, *refs):
    auds, vids, (row_keep, row_give, col_keep, col_give) = refs[:aud_count], refs[aud_count:-4], refs[-4:]
    auds, vids = in_order(auds), in_order(vids)
    width = auds[0].shape[1] // 2
    heads = width // HEAD_DIM
    aud = jnp.concatenate([ref[...] for ref in auds], axis=0)
    vid = jnp.concatenate([ref[...] for ref in vids], axis=0).astype(F32)
    queries, aud_vals = aud[:, :width], aud[:, width:]
    total_aud, total_vid = aud.shape[0], vid.shape[0]
    masks = [head_lanes(total_vid, width, h) for h in range(heads)]
    keys = jnp.concatenate([jnp.where(m, vid[:, :width], 0.0) for m in masks], axis=0)
    vals = jnp.concatenate([jnp.where(m, vid[:, width:], 0.0) for m in masks], axis=0)
    scores = dot(keys.astype(BF16), queries, 1, 1).reshape(heads, total_vid, total_aud)

    row_top = jnp.max(scores, axis=1, keepdims=True)
    row_probs = jnp.exp((scores - row_top) * SCALE)
    row_total = jnp.sum(row_probs, axis=1, keepdims=True)
    row_probs = row_probs.reshape(heads * total_vid, total_aud).astype(BF16)
    row_mix = dot(vals.astype(BF16), row_probs, 0, 0).reshape(heads, HEAD_DIM, total_aud)
    row_mix = (row_mix / row_total).reshape(width, total_aud)
    row_log = (row_top * SCALE + jnp.log(row_total)).reshape(heads, total_aud)
    for i, out in enumerate((row_keep, row_give)):
        cols = slice(i * out.shape[1], (i + 1) * out.shape[1])
        put_rows(out, row_mix[:, cols], row_log[:, cols])

    col_top = jnp.max(scores, axis=2, keepdims=True)
    col_probs = jnp.exp((scores - col_top) * SCALE)
    col_total = jnp.sum(col_probs, axis=2, keepdims=True)
    col_probs = col_probs.reshape(heads * total_vid, total_aud).astype(BF16)
    every = dot(col_probs, aud_vals).reshape(heads, total_vid, width)
    col_log = col_top * SCALE + jnp.log(col_total)
    col_mix, divisor = every[0], jnp.broadcast_to(col_total[0], (total_vid, width))
    for h in range(1, heads):
        col_mix = jnp.where(masks[h], every[h], col_mix)
        divisor = jnp.where(masks[h], col_total[h], divisor)
    col_mix = col_mix / divisor
    lane = lax.broadcasted_iota(jnp.int32, (total_vid, LANES), 1) % heads
    logs = jnp.broadcast_to(col_log[0], (total_vid, LANES))
    for h in range(1, heads):
        logs = jnp.where(lane == h, col_log[h], logs)
    for i, out in enumerate((col_keep, col_give)):
        rows = slice(i * out.shape[0], (i + 1) * out.shape[0])
        put_cols(out, col_mix[rows], logs[rows])


def put_rows(out, mix, log):
    width, tokens = mix.shape
    pad = jnp.zeros((out.shape[0] - width - PIECES * log.shape[0], tokens), F32)
    out[:width, :] = mix.astype(BF16)
    out[width:, :] = jnp.concatenate(split_pieces(log) + [pad], axis=0).astype(BF16)


def get_rows(ref, width):
    heads, tokens = width // HEAD_DIM, ref.shape[1]
    pieces = ref[width:, :].astype(F32)
    log = pieces[:heads]
    for i in range(1, PIECES):
        log = log + pieces[i * heads : (i + 1) * heads]
    mix = ref[:width, :].astype(F32).reshape(heads, HEAD_DIM, tokens)
    return mix, log.reshape(heads, 1, tokens)


def put_cols(out, mix, logs):
    width = mix.shape[1]
    heads = width // HEAD_DIM
    lane = lax.broadcasted_iota(jnp.int32, logs.shape, 1)
    pieces = split_pieces(logs)
    stats = jnp.zeros_like(logs)
    for i, piece in enumerate(pieces):
        stats = jnp.where(lane // heads == i, piece, stats)
    out[:, :width] = mix.astype(BF16)
    out[:, width:] = stats.astype(BF16)


def get_cols(ref, width, log_width, lane_heads):
    heads = width // HEAD_DIM
    source = lax.broadcasted_iota(jnp.int32, (LANES, log_width), 0)
    target = lax.broadcasted_iota(jnp.int32, (LANES, log_width), 1)
    spread = (source < PIECES * heads) & (source % heads == lane_heads(target))
    return ref[:, :width].astype(F32), dot(ref[:, width:], spread.astype(BF16))


def merge_weights(logs):
    top = jnp.maximum(logs[0], logs[1])
    weights = [jnp.exp(log - top) for log in logs]
    total = weights[0] + weights[1]
    return [weight / total for weight in weights], top + jnp.log(total)


def merge_rows(mine, got, keep, give):
    width = mine.shape[0] // HEAD_DIM * HEAD_DIM
    states = [get_rows(ref, width) for ref in (mine, got)]
    weights, logs = merge_weights([log for _, log in states])
    mix = weights[0] * states[0][0] + weights[1] * states[1][0]
    mix, logs = mix.reshape(width, -1), logs.reshape(width // HEAD_DIM, -1)
    for i, out in enumerate((keep, give)):
        cols = slice(i * out.shape[1], (i + 1) * out.shape[1])
        put_rows(out, mix[:, cols], logs[:, cols])


def merge_cols(mine, got, keep, give):
    width = mine.shape[1] - LANES
    heads = width // HEAD_DIM
    wide = [get_cols(ref, width, width, lambda lane: lane // HEAD_DIM) for ref in (mine, got)]
    slim = [get_cols(ref, width, LANES, lambda lane: lane % heads)[1] for ref in (mine, got)]
    weights, _ = merge_weights([log for _, log in wide])
    _, logs = merge_weights(slim)
    mix = weights[0] * wide[0][0] + weights[1] * wide[1][0]
    for i, out in enumerate((keep, give)):
        rows = slice(i * out.shape[0], (i + 1) * out.shape[0])
        put_cols(out, mix[rows], logs[rows])


def project(mix, proj, me, outs):
    step = outs[0].shape[1]
    for i, out in enumerate(outs):
        block = pl.ds(pl.multiple_of(partner(me, i, len(outs)) * step, step), step)
        out[...] = dot(mix, proj[:, block]).astype(out.dtype)


def project_audio(me, mine, got, proj, *outs):
    width = proj.shape[0]
    states = [get_rows(ref, width) for ref in (mine, got)]
    weights, _ = merge_weights([log for _, log in states])
    mix = weights[0] * states[0][0] + weights[1] * states[1][0]
    project(mix.reshape(width, -1).T.astype(BF16), proj, me[0], outs)


def project_video(me, mine, got, proj, *outs):
    width = proj.shape[0]
    states = [get_cols(ref, width, width, lambda lane: lane // HEAD_DIM) for ref in (mine, got)]
    weights, _ = merge_weights([log for _, log in states])
    mix = weights[0] * states[0][0] + weights[1] * states[1][0]
    project(mix.astype(BF16), proj, me[0], outs)


def add(*refs):
    terms, outs = refs[:-2], refs[-2:]
    count = len(terms) // 2
    for out, group in zip(outs, (terms[:count], terms[count:])):
        total = group[0][...].astype(F32)
        for term in group[1:]:
            total += term[...].astype(F32)
        out[...] = total.astype(BF16)


def call(body, out_shape, args, in_specs=None, scratch=()):
    vmem = pl.BlockSpec(memory_space=pltpu.VMEM)
    return pl.pallas_call(
        body,
        out_shape=out_shape,
        in_specs=in_specs or [vmem] * len(args),
        out_specs=[vmem] * len(out_shape),
        scratch_shapes=scratch,
        compiler_params=pltpu.CompilerParams(vmem_limit_bytes=VMEM_LIMIT),
        cost_estimate=pl.CostEstimate(flops=COST, bytes_accessed=0, transcendentals=0),
    )(*args)


def partner(index, k, size):
    return index ^ k


def swap(block, axis, distance):
    return lax.ppermute(block, axis, [(i, i ^ distance) for i in range(lax.axis_size(axis))])


def factors(size):
    bits = size.bit_length() - 1
    assert size == 1 << bits
    return 1 << (bits // 2), 1 << (bits - bits // 2)


def bits_of(inner, count):
    return [inner << i for i in reversed(range(count.bit_length() - 1))]


def per_device(ref_audio, val_audio, ref_video, val_video, audio_proj, video_proj):
    seq, peers = lax.axis_size("seq"), lax.axis_size("head")
    aud_count, vid_count = factors(seq)
    aud_rows, width = ref_audio.shape
    vid_rows = ref_video.shape[0]
    heads = width // HEAD_DIM
    step = audio_proj.shape[1] // peers
    aud_bits, vid_bits = bits_of(1, aud_count), bits_of(aud_count, vid_count)
    log_rows = -(-PIECES * heads // 16) * 16

    def shape(rows, cols, dtype=BF16):
        return jax.ShapeDtypeStruct((rows, cols), dtype)

    def gather(block, distances):
        count = 1 << len(distances)
        return [swap(block, "seq", k * distances[-1]) for k in reversed(range(1, count))] + [block]

    def scatter(keep, give, distances, merge, axis):
        for distance in reversed(distances[1:]):
            got = swap(give, "seq", distance)
            half = list(keep.shape)
            half[axis] //= 2
            keep, give = call(merge, [shape(*half)] * 2, [keep, got])
        return keep, swap(give, "seq", distances[0])

    aud, vid = call(
        pack,
        [shape(aud_rows, 2 * width), shape(vid_rows, 2 * width)],
        [
            pltpu.with_memory_space_constraint(x, pltpu.HBM)
            for x in (ref_audio, val_audio, ref_video, val_video)
        ],
        in_specs=[pl.BlockSpec(memory_space=pltpu.HBM)] * 4,
        scratch=[pltpu.SemaphoreType.DMA((4,))],
    )
    auds = gather(aud, aud_bits)
    vids = gather(vid, vid_bits)
    rows_shape = shape(width + log_rows, aud_rows * aud_count // 2)
    cols_shape = shape(vid_rows * vid_count // 2, width + LANES)
    row_keep, row_give, col_keep, col_give = call(
        functools.partial(attend, aud_count),
        [rows_shape, rows_shape, cols_shape, cols_shape],
        [*auds, *vids],
    )
    rows = scatter(row_keep, row_give, aud_bits, merge_rows, 1)
    cols = scatter(col_keep, col_give, vid_bits, merge_cols, 0)

    me = lax.axis_index("head").astype(jnp.int32).reshape(1)
    vmem = pl.BlockSpec(memory_space=pltpu.VMEM)
    smem = pl.BlockSpec(memory_space=pltpu.SMEM)
    hbm = pl.BlockSpec(memory_space=pl.ANY)

    def head_terms(body, states, proj, count, after=()):
        return call(
            lambda *refs: body(*refs[:4], *refs[4 + len(after) :]),
            [shape(count, step, F32)] + [shape(count, step)] * (peers - 1),
            [me, *states, proj, *after],
            in_specs=[smem, vmem, vmem, vmem] + [hbm] * len(after),
        )

    def exchange(terms):
        return [terms[0]] + [swap(terms[k], "head", k) for k in range(1, peers)]

    aud_got = exchange(head_terms(project_audio, rows, audio_proj, aud_rows, cols[:1]))
    vid_got = exchange(head_terms(project_video, cols, video_proj, vid_rows, aud_got[1:2]))
    return tuple(call(add, [shape(aud_rows, step), shape(vid_rows, step)], aud_got + vid_got))


def solution(mesh):
    in_specs = (
        P("seq", "head"),
        P("seq", "head"),
        P("seq", "head"),
        P("seq", "head"),
        P("head", None),
        P("head", None),
    )
    out_specs = (P("seq", "head"), P("seq", "head"))
    return jax.shard_map(
        per_device, mesh=mesh, in_specs=in_specs, out_specs=out_specs, check_vma=False
    )
```

time: 36.3 us -> 29.7 us (0.82)
  waiting for transfers between devices: 19.7 us -> 11.5 us
  starting transfers between devices: 12.2 us -> 13.7 us
  local copies, waits for them, and re-layouts: 0.01 us -> 0.61 us
  Pallas kernels: 3.49 us -> 3 us
    ppermute x14 -> x13, waiting for transfers between devices: 19.7 us -> 11.5 us  [swap(): lax.ppermute(block, axis, [(i, i ^ distance) for i in range(lax.axis_size...]
    ppermute x14 -> x13, starting transfers between devices: 12.2 us -> 13.7 us  [swap(): lax.ppermute(block, axis, [(i, i ^ distance) for i in range(lax.axis_size...]
    unnamed x4, local copies, waits for them, and re-layouts: 0.01 us -> 0.61 us
    pallas_call x6, Pallas kernels: 3.49 us -> 3 us  [call(): pl.pallas_call(body, out_shape=out_shape, in_specs=in_specs or [vmem] * l...]
  transfers between devices with their start and end apart: 14 -> 13, of which waited for: 9 -> 8; matrix products, arithmetic and copies ran while one was open for 0% -> 0% of each run, Pallas kernels for 3% -> 2%
where the time goes in v4:
time: 29.7 us; the launch traced here: 29.4 us
  starting transfers between devices  13.7 us (46%)
  waiting for transfers between devices  11.5 us (39%)
  Pallas kernels  3 us (10%)
  between operations  0.7 us (2%)
  local copies, waits for them, and re-layouts  0.61 us (2%)
    ppermute x13, starting transfers between devices, swap(): lax.ppermute(block, axis, [(i, i ^ distance) for i in range(lax.axis_size...  13.7 us
    ppermute x13, waiting for transfers between devices, swap(): lax.ppermute(block, axis, [(i, i ^ distance) for i in range(lax.axis_size...  11.5 us
    pallas_call x6, Pallas kernels, call(): pl.pallas_call(body, out_shape=out_shape, in_specs=in_specs or [vmem] * l...  3 us
    unnamed x4, local copies, waits for them, and re-layouts  0.61 us
  transfers between devices with their start and end apart: 13, of which 8 were waited for; matrix products, arithmetic and copies ran while one was open for 0% of the time, Pallas kernels for 2%

profile of v4, /device:TPU:0, one launch (start us, length us, event | category | flops | bytes accessed | tf_op | source)
XLA Modules:
  0.0 29.4 jit_solution(2405965501348571932)
XLA Ops:
  0.6 0.9 %shard_map.77 = (bf16[128,512]{1,0:T(8,128)(2,1)S(1)}, bf16[24,512]{1,0:T(8,128)(2,1)S(1)}) custom-call(bf16[128,256]{1,0:T(8,128)(2,1)} %aud_ref.1, bf16[128,256]{1,0:T(8,128)(2,1)} %aud_val.1, bf16[24,256]{1,0:T(8,128)(2,1)} %vid_ref.1, bf16[24,256]{1,0:T(8,128)(2,1)} %vid_val.1), custom_call_target="tpu_custom_call" | custom-call | flops 5000000000 | tf_op jit(solution)/shard_map/pallas_call | solution.py:209
  1.5 3.0 %collective-permute-start = (bf16[128,512]{1,0:T(8,128)(2,1)S(1)}, bf16[128,512]{1,0:T(8,128)(2,1)S(1)}, u32[]{:S(2)}, u32[]{:S(2)}) collective-permute-start(bf16[128,512]{1,0:T(8,128)(2,1)S(1)} %get-tuple-element.18.refs_1_), channel_id=1, source_target_pairs={{0,4},{4,0},{8,12},{12,8},{16,20},{20,16},{24,28},{28,24},{1,5},{5... | collective-permute-start | bytes 393224 | tf_op jit(solution)/shard_map/ppermute | solution.py:225
  4.6 3.6 %collective-permute-start.1 = (bf16[24,512]{1,0:T(8,128)(2,1)S(1)}, bf16[24,512]{1,0:T(8,128)(2,1)S(1)}, u32[]{:S(2)}, u32[]{:S(2)}) collective-permute-start(bf16[24,512]{1,0:T(8,128)(2,1)S(1)} %get-tuple-element.19.refs_5_), channel_id=1, source_target_pairs={{0,24},{4,28},{8,16},{12,20},{16,8},{20,12},{24,0},{28,4},{1,25},{... | collective-permute-start | bytes 73736 | tf_op jit(solution)/shard_map/ppermute | solution.py:225
  8.2 0.8 %collective-permute-start.3 = (bf16[24,512]{1,0:T(8,128)(2,1)S(1)}, bf16[24,512]{1,0:T(8,128)(2,1)S(1)}, u32[]{:S(2)}, u32[]{:S(2)}) collective-permute-start(bf16[24,512]{1,0:T(8,128)(2,1)S(1)} %get-tuple-element.19.refs_5_), channel_id=1, source_target_pairs={{0,8},{4,12},{8,0},{12,4},{16,24},{20,28},{24,16},{28,20},{1,9},{5... | collective-permute-start | bytes 73736 | tf_op jit(solution)/shard_map/ppermute | solution.py:225
  8.9 1.5 %collective-permute-done.1.refs_2_ = bf16[24,512]{1,0:T(8,128)(2,1)S(1)} collective-permute-done((bf16[24,512]{1,0:T(8,128)(2,1)S(1)}, bf16[24,512]{1,0:T(8,128)(2,1)S(1)}, u32[]{:S(2)}, u32[]{:S(2)}) %collective-permute-start.1) | collective-permute-done | bytes 24608 | tf_op jit(solution)/shard_map/ppermute | solution.py:225
  10.4 2.4 %collective-permute-done.2.refs_3_ = bf16[24,512]{1,0:T(8,128)(2,1)S(1)} collective-permute-done((bf16[24,512]{1,0:T(8,128)(2,1)S(1)}, bf16[24,512]{1,0:T(8,128)(2,1)S(1)}, u32[]{:S(2)}, u32[]{:S(2)}) %collective-permute-start.2) | collective-permute-done | bytes 24608 | tf_op jit(solution)/shard_map/ppermute | solution.py:225
  12.9 0.6 %shard_map.78 = (bf16[272,128]{1,0:T(8,128)(2,1)S(1)}, bf16[272,128]{1,0:T(8,128)(2,1)S(1)}, bf16[48,384]{1,0:T(8,128)(2,1)S(1)}, bf16[48,384]{1,0:T(8,128)(2,1)S(1)}) custom-call(bf16[128,512]{1,0:T(8,128)(2,1)S(1)} %collective-permute-done.refs_0_, bf16[128,512]{1,0:T(8,128)(2,1)S(1)} %get-tuple-element.18.refs_1_, ...), custom_call_target="tpu_custom_call" | custom-call | flops 5000000000 | tf_op jit(solution)/shard_map/pallas_call | solution.py:209
  13.5 0.1 collective-permute-start.5
  13.6 0.6 %collective-permute-start.4 = (bf16[272,128]{1,0:T(8,128)(2,1)S(1)}, bf16[272,128]{1,0:T(8,128)(2,1)S(1)}, u32[]{:S(2)}, u32[]{:S(2)}) collective-permute-start(bf16[272,128]{1,0:T(8,128)(2,1)S(1)} %get-tuple-element.21), channel_id=1, source_target_pairs={{0,4},{4,0},{8,12},{12,8},{16,20},{20,16},{24,28},{28,24},{1,5},{5... | collective-permute-start | bytes 208904 | tf_op jit(solution)/shard_map/ppermute | solution.py:225
  14.2 3.3 %collective-permute-done.5.got = bf16[48,384]{1,0:T(8,128)(2,1)S(1)} collective-permute-done((bf16[48,384]{1,0:T(8,128)(2,1)S(1)}, bf16[48,384]{1,0:T(8,128)(2,1)S(1)}, u32[]{:S(2)}, u32[]{:S(2)}) %collective-permute-start.5) | collective-permute-done | bytes 36896 | tf_op jit(solution)/shard_map/ppermute | solution.py:225
  17.6 0.2 shard_map.79
  17.7 0.2 collective-permute-done.4.refs_2_
  18.0 0.6 %copy-done = bf16[256,1024]{1,0:T(8,128)(2,1)S(1)} copy-done((bf16[256,1024]{1,0:T(8,128)(2,1)S(1)}, bf16[256,1024]{1,0:T(8,128)(2,1)}, u32[]{:S(2)}) %copy-start) | copy-done | bytes 524312
  18.6 0.3 %shard_map.80 = (f32[128,256]{1,0:T(8,128)S(1)}, bf16[128,256]{1,0:T(8,128)(2,1)S(1)}, bf16[128,256]{1,0:T(8,128)(2,1)S(1)}, bf16[128,256]{1,0:T(8,128)(2,1)S(1)}) custom-call(s32[1]{0:T(128)} %bitcast.refs_0_, bf16[272,128]{1,0:T(8,128)(2,1)S(1)} %get-tuple-element.20.refs_1_, bf16[272,128]{1,0:T(8,128)(2,1)S(1)} %collective-permute-done.4.refs_2_, ...), custom_call_target="tpu_custom_call" | custom-call | flops 5000000000 | tf_op jit(solution)/shard_map/pallas_call | solution.py:209
  19.0 2.1 %collective-permute-start.9 = (bf16[24,384]{1,0:T(8,128)(2,1)S(1)}, bf16[24,384]{1,0:T(8,128)(2,1)S(1)}, u32[]{:S(2)}, u32[]{:S(2)}) collective-permute-start(bf16[24,384]{1,0:T(8,128)(2,1)S(1)} %get-tuple-element.29), channel_id=1, source_target_pairs={{0,16},{4,20},{8,24},{12,28},{16,0},{20,4},{24,8},{28,12},{1,17},{... | collective-permute-start | bytes 55304 | tf_op jit(solution)/shard_map/ppermute | solution.py:225
  21.1 1.6 %collective-permute-start.7 = (bf16[128,256]{1,0:T(8,128)(2,1)S(1)}, bf16[128,256]{1,0:T(8,128)(2,1)S(1)}, u32[]{:S(2)}, u32[]{:S(2)}) collective-permute-start(bf16[128,256]{1,0:T(8,128)(2,1)S(1)} %get-tuple-element.27), channel_id=1, source_target_pairs={{0,2},{1,3},{2,0},{3,1},{4,6},{5,7},{6,4},{7,5},{8,10},{9,11},{10,... | collective-permute-start | bytes 196616 | tf_op jit(solution)/shard_map/ppermute | solution.py:225
  22.6 1.1 %collective-permute-done.9.refs_2_ = bf16[24,384]{1,0:T(8,128)(2,1)S(1)} collective-permute-done((bf16[24,384]{1,0:T(8,128)(2,1)S(1)}, bf16[24,384]{1,0:T(8,128)(2,1)S(1)}, u32[]{:S(2)}, u32[]{:S(2)}) %collective-permute-start.9) | collective-permute-done | bytes 18464 | tf_op jit(solution)/shard_map/ppermute | solution.py:225
  23.7 0.3 %shard_map.81 = (f32[24,256]{1,0:T(8,128)S(1)}, bf16[24,256]{1,0:T(8,128)(2,1)S(1)}, bf16[24,256]{1,0:T(8,128)(2,1)S(1)}, bf16[24,256]{1,0:T(8,128)(2,1)S(1)}) custom-call(s32[1]{0:T(128)} %bitcast.refs_0_, bf16[24,384]{1,0:T(8,128)(2,1)S(1)} %get-tuple-element.24.refs_4_.refs_1_, bf16[24,384]{1,0:T(8,128)(2,1)S(1)} %collective-permute-done.9.refs_2_, ...), custom_call_target="tpu_custom_call" | custom-call | flops 5000000000 | tf_op jit(solution)/shard_map/pallas_call | solution.py:209
  24.1 1.6 %collective-permute-start.11 = (bf16[24,256]{1,0:T(8,128)(2,1)S(1)}, bf16[24,256]{1,0:T(8,128)(2,1)S(1)}, u32[]{:S(2)}, u32[]{:S(2)}) collective-permute-start(bf16[24,256]{1,0:T(8,128)(2,1)S(1)} %get-tuple-element.32), channel_id=1, source_target_pairs={{0,2},{1,3},{2,0},{3,1},{4,6},{5,7},{6,4},{7,5},{8,10},{9,11},{10,... | collective-permute-start | bytes 36872 | tf_op jit(solution)/shard_map/ppermute | solution.py:225
  25.7 0.3 collective-permute-start.12
  25.9 1.0 %collective-permute-done.8.refs_3_ = bf16[128,256]{1,0:T(8,128)(2,1)S(1)} collective-permute-done((bf16[128,256]{1,0:T(8,128)(2,1)S(1)}, bf16[128,256]{1,0:T(8,128)(2,1)S(1)}, u32[]{:S(2)}, u32[]{:S(2)}) %collective-permute-start.8) | collective-permute-done | bytes 65568 | tf_op jit(solution)/shard_map/ppermute | solution.py:225
  27.0 0.8 %collective-permute-done.11.refs_6_ = bf16[24,256]{1,0:T(8,128)(2,1)S(1)} collective-permute-done((bf16[24,256]{1,0:T(8,128)(2,1)S(1)}, bf16[24,256]{1,0:T(8,128)(2,1)S(1)}, u32[]{:S(2)}, u32[]{:S(2)}) %collective-permute-start.11) | collective-permute-done | bytes 12320 | tf_op jit(solution)/shard_map/ppermute | solution.py:225
  27.8 0.9 %collective-permute-done.12.refs_7_ = bf16[24,256]{1,0:T(8,128)(2,1)S(1)} collective-permute-done((bf16[24,256]{1,0:T(8,128)(2,1)S(1)}, bf16[24,256]{1,0:T(8,128)(2,1)S(1)}, u32[]{:S(2)}, u32[]{:S(2)}) %collective-permute-start.12) | collective-permute-done | bytes 12320 | tf_op jit(solution)/shard_map/ppermute | solution.py:225
  28.8 0.7 %shard_map.82 = (bf16[128,256]{1,0:T(8,128)(2,1)}, bf16[24,256]{1,0:T(8,128)(2,1)}) custom-call(f32[128,256]{1,0:T(8,128)S(1)} %get-tuple-element.25.refs_0_, bf16[128,256]{1,0:T(8,128)(2,1)S(1)} %collective-permute-done.6.refs_4_.refs_1_, bf16[128,256]{1,0:T(8,128)(2,1)S(1)} %collective-permute-done.7.refs_2_, ...), custom_call_target="tpu_custom_call" | custom-call | flops 5000000000 | tf_op jit(solution)/shard_map/pallas_call | solution.py:209
  (12 shorter events, 0.1 us)
Async XLA Ops:
  1.5 11.3 %collective-permute-start = (bf16[128,512]{1,0:T(8,128)(2,1)S(1)}, bf16[128,512]{1,0:T(8,128)(2,1)S(1)}, u32[]{:S(2)}, u32[]{:S(2)}) collective-permute-start(bf16[128,512]{1,0:T(8,128)(2,1)S(1)} %get-tuple-element.18.refs_1_), channel_id=1, source_target_pairs={{0,4},{4,0},{8,12},{12,8},{16,20},{20,16},{24,28},{28,24},{1,5},{5... | collective-permute-start | bytes 393224 | tf_op jit(solution)/shard_map/ppermute | solution.py:225
  4.6 5.9 %collective-permute-start.1 = (bf16[24,512]{1,0:T(8,128)(2,1)S(1)}, bf16[24,512]{1,0:T(8,128)(2,1)S(1)}, u32[]{:S(2)}, u32[]{:S(2)}) collective-permute-start(bf16[24,512]{1,0:T(8,128)(2,1)S(1)} %get-tuple-element.19.refs_5_), channel_id=1, source_target_pairs={{0,24},{4,28},{8,16},{12,20},{16,8},{20,12},{24,0},{28,4},{1,25},{... | collective-permute-start | bytes 73736 | tf_op jit(solution)/shard_map/ppermute | solution.py:225
  8.2 4.7 %collective-permute-start.2 = (bf16[24,512]{1,0:T(8,128)(2,1)S(1)}, bf16[24,512]{1,0:T(8,128)(2,1)S(1)}, u32[]{:S(2)}, u32[]{:S(2)}) collective-permute-start(bf16[24,512]{1,0:T(8,128)(2,1)S(1)} %get-tuple-element.19.refs_5_), channel_id=1, source_target_pairs={{0,16},{4,20},{8,24},{12,28},{16,0},{20,4},{24,8},{28,12},{1,17},{... | collective-permute-start | bytes 73736 | tf_op jit(solution)/shard_map/ppermute | solution.py:225
  8.2 4.7 %collective-permute-start.3 = (bf16[24,512]{1,0:T(8,128)(2,1)S(1)}, bf16[24,512]{1,0:T(8,128)(2,1)S(1)}, u32[]{:S(2)}, u32[]{:S(2)}) collective-permute-start(bf16[24,512]{1,0:T(8,128)(2,1)S(1)} %get-tuple-element.19.refs_5_), channel_id=1, source_target_pairs={{0,8},{4,12},{8,0},{12,4},{16,24},{20,28},{24,16},{28,20},{1,9},{5... | collective-permute-start | bytes 73736 | tf_op jit(solution)/shard_map/ppermute | solution.py:225
  13.5 4.0 %collective-permute-start.5 = (bf16[48,384]{1,0:T(8,128)(2,1)S(1)}, bf16[48,384]{1,0:T(8,128)(2,1)S(1)}, u32[]{:S(2)}, u32[]{:S(2)}) collective-permute-start(bf16[48,384]{1,0:T(8,128)(2,1)S(1)} %get-tuple-element.23), channel_id=1, source_target_pairs={{0,8},{4,12},{8,0},{12,4},{16,24},{20,28},{24,16},{28,20},{1,9},{5... | collective-permute-start | bytes 110600 | tf_op jit(solution)/shard_map/ppermute | solution.py:225
  13.6 4.4 %collective-permute-start.4 = (bf16[272,128]{1,0:T(8,128)(2,1)S(1)}, bf16[272,128]{1,0:T(8,128)(2,1)S(1)}, u32[]{:S(2)}, u32[]{:S(2)}) collective-permute-start(bf16[272,128]{1,0:T(8,128)(2,1)S(1)} %get-tuple-element.21), channel_id=1, source_target_pairs={{0,4},{4,0},{8,12},{12,8},{16,20},{20,16},{24,28},{28,24},{1,5},{5... | collective-permute-start | bytes 208904 | tf_op jit(solution)/shard_map/ppermute | solution.py:225
  17.5 1.0 %copy-start = (bf16[256,1024]{1,0:T(8,128)(2,1)S(1)}, bf16[256,1024]{1,0:T(8,128)(2,1)}, u32[]{:S(2)}) copy-start(bf16[256,1024]{1,0:T(8,128)(2,1)} %refs_3_.2) | copy-start | bytes 1572868
  18.6 5.1 %copy-start.1 = (bf16[256,1024]{1,0:T(8,128)(2,1)S(1)}, bf16[256,1024]{1,0:T(8,128)(2,1)}, u32[]{:S(2)}) copy-start(bf16[256,1024]{1,0:T(8,128)(2,1)} %refs_3_.3) | copy-start | bytes 1572868
  18.9 4.8 %collective-permute-start.6 = (bf16[128,256]{1,0:T(8,128)(2,1)S(1)}, bf16[128,256]{1,0:T(8,128)(2,1)S(1)}, u32[]{:S(2)}, u32[]{:S(2)}) collective-permute-start(bf16[128,256]{1,0:T(8,128)(2,1)S(1)} %get-tuple-element.26), channel_id=1, source_target_pairs={{0,1},{1,0},{2,3},{3,2},{4,5},{5,4},{6,7},{7,6},{8,9},{9,8},{10,11... | collective-permute-start | bytes 196616 | tf_op jit(solution)/shard_map/ppermute | solution.py:225
  19.0 4.7 %collective-permute-start.9 = (bf16[24,384]{1,0:T(8,128)(2,1)S(1)}, bf16[24,384]{1,0:T(8,128)(2,1)S(1)}, u32[]{:S(2)}, u32[]{:S(2)}) collective-permute-start(bf16[24,384]{1,0:T(8,128)(2,1)S(1)} %get-tuple-element.29), channel_id=1, source_target_pairs={{0,16},{4,20},{8,24},{12,28},{16,0},{20,4},{24,8},{28,12},{1,17},{... | collective-permute-start | bytes 55304 | tf_op jit(solution)/shard_map/ppermute | solution.py:225
  21.1 4.9 %collective-permute-start.7 = (bf16[128,256]{1,0:T(8,128)(2,1)S(1)}, bf16[128,256]{1,0:T(8,128)(2,1)S(1)}, u32[]{:S(2)}, u32[]{:S(2)}) collective-permute-start(bf16[128,256]{1,0:T(8,128)(2,1)S(1)} %get-tuple-element.27), channel_id=1, source_target_pairs={{0,2},{1,3},{2,0},{3,1},{4,6},{5,7},{6,4},{7,5},{8,10},{9,11},{10,... | collective-permute-start | bytes 196616 | tf_op jit(solution)/shard_map/ppermute | solution.py:225
  22.6 4.4 %collective-permute-start.8 = (bf16[128,256]{1,0:T(8,128)(2,1)S(1)}, bf16[128,256]{1,0:T(8,128)(2,1)S(1)}, u32[]{:S(2)}, u32[]{:S(2)}) collective-permute-start(bf16[128,256]{1,0:T(8,128)(2,1)S(1)} %get-tuple-element.28), channel_id=1, source_target_pairs={{0,3},{1,2},{2,1},{3,0},{4,7},{5,6},{6,5},{7,4},{8,11},{9,10},{10,... | collective-permute-start | bytes 196616 | tf_op jit(solution)/shard_map/ppermute | solution.py:225
  24.0 3.0 %collective-permute-start.10 = (bf16[24,256]{1,0:T(8,128)(2,1)S(1)}, bf16[24,256]{1,0:T(8,128)(2,1)S(1)}, u32[]{:S(2)}, u32[]{:S(2)}) collective-permute-start(bf16[24,256]{1,0:T(8,128)(2,1)S(1)} %get-tuple-element.31), channel_id=1, source_target_pairs={{0,1},{1,0},{2,3},{3,2},{4,5},{5,4},{6,7},{7,6},{8,9},{9,8},{10,11... | collective-permute-start | bytes 36872 | tf_op jit(solution)/shard_map/ppermute | solution.py:225
  24.1 3.8 %collective-permute-start.11 = (bf16[24,256]{1,0:T(8,128)(2,1)S(1)}, bf16[24,256]{1,0:T(8,128)(2,1)S(1)}, u32[]{:S(2)}, u32[]{:S(2)}) collective-permute-start(bf16[24,256]{1,0:T(8,128)(2,1)S(1)} %get-tuple-element.32), channel_id=1, source_target_pairs={{0,2},{1,3},{2,0},{3,1},{4,6},{5,7},{6,4},{7,5},{8,10},{9,11},{10,... | collective-permute-start | bytes 36872 | tf_op jit(solution)/shard_map/ppermute | solution.py:225
  25.7 3.1 %collective-permute-start.12 = (bf16[24,256]{1,0:T(8,128)(2,1)S(1)}, bf16[24,256]{1,0:T(8,128)(2,1)S(1)}, u32[]{:S(2)}, u32[]{:S(2)}) collective-permute-start(bf16[24,256]{1,0:T(8,128)(2,1)S(1)} %get-tuple-element.33), channel_id=1, source_target_pairs={{0,3},{1,2},{2,1},{3,0},{4,7},{5,6},{6,5},{7,4},{8,11},{9,10},{10,... | collective-permute-start | bytes 36872 | tf_op jit(solution)/shard_map/ppermute | solution.py:225

commit v5 on v4

v5 whole, which is shorter than its diff:
```python
import functools

import jax
import jax.numpy as jnp
from jax import lax
from jax.experimental import pallas as pl
from jax.experimental.pallas import tpu as pltpu
from jax.sharding import PartitionSpec as P

HEAD_DIM = 64
LANES = 128
PIECES = 3
SCALE = HEAD_DIM ** (-0.5)
VMEM_LIMIT = 48 * 1024 * 1024
COST = 5 * 10**9
BF16 = jnp.bfloat16
F32 = jnp.float32


def dot(a, b, contract_a=1, contract_b=0):
    dims = (((contract_a,), (contract_b,)), ((), ()))
    return lax.dot_general(a, b, dims, preferred_element_type=F32)


def split_pieces(value):
    pieces = []
    for _ in range(PIECES):
        piece = value.astype(BF16).astype(F32)
        pieces.append(piece)
        value = value - piece
    return pieces


def head_lanes(rows, width, head):
    return lax.broadcasted_iota(jnp.int32, (rows, width), 1) // HEAD_DIM == head


def pack(aud_ref, aud_val, vid_ref, vid_val, aud, vid, sems):
    width = aud_ref.shape[1]
    copies = [
        pltpu.make_async_copy(source, target.at[:, start : start + width], sems.at[i])
        for i, (source, target, start) in enumerate(
            ((aud_ref, aud, 0), (aud_val, aud, width), (vid_ref, vid, 0), (vid_val, vid, width))
        )
    ]
    for copy in copies:
        copy.start()
    for copy in copies:
        copy.wait()


def attend(aud_count, vid_count, *refs):
    auds, vids = refs[:aud_count], refs[aud_count : aud_count + vid_count]
    row_outs = refs[aud_count + vid_count : 2 * aud_count + vid_count]
    col_outs = refs[2 * aud_count + vid_count :]
    width = auds[0].shape[1] // 2
    heads = width // HEAD_DIM
    aud = jnp.concatenate([ref[...] for ref in auds], axis=0)
    vid = jnp.concatenate([ref[...] for ref in vids], axis=0).astype(F32)
    queries, aud_vals = aud[:, :width], aud[:, width:]
    total_aud, total_vid = aud.shape[0], vid.shape[0]
    masks = [head_lanes(total_vid, width, h) for h in range(heads)]
    keys = jnp.concatenate([jnp.where(m, vid[:, :width], 0.0) for m in masks], axis=0)
    vals = jnp.concatenate([jnp.where(m, vid[:, width:], 0.0) for m in masks], axis=0)
    scores = dot(keys.astype(BF16), queries, 1, 1).reshape(heads, total_vid, total_aud)

    row_top = jnp.max(scores, axis=1, keepdims=True)
    row_probs = jnp.exp((scores - row_top) * SCALE)
    row_total = jnp.sum(row_probs, axis=1, keepdims=True)
    row_probs = row_probs.reshape(heads * total_vid, total_aud).astype(BF16)
    row_mix = dot(vals.astype(BF16), row_probs, 0, 0).reshape(heads, HEAD_DIM, total_aud)
    row_mix = (row_mix / row_total).reshape(width, total_aud)
    row_log = (row_top * SCALE + jnp.log(row_total)).reshape(heads, total_aud)
    for i, out in enumerate(row_outs):
        cols = slice(i * out.shape[1], (i + 1) * out.shape[1])
        put_rows(out, row_mix[:, cols], row_log[:, cols])

    col_top = jnp.max(scores, axis=2, keepdims=True)
    col_probs = jnp.exp((scores - col_top) * SCALE)
    col_total = jnp.sum(col_probs, axis=2, keepdims=True)
    col_probs = col_probs.reshape(heads * total_vid, total_aud).astype(BF16)
    every = dot(col_probs, aud_vals).reshape(heads, total_vid, width)
    col_log = col_top * SCALE + jnp.log(col_total)
    col_mix, divisor = every[0], jnp.broadcast_to(col_total[0], (total_vid, width))
    for h in range(1, heads):
        col_mix = jnp.where(masks[h], every[h], col_mix)
        divisor = jnp.where(masks[h], col_total[h], divisor)
    col_mix = col_mix / divisor
    lane = lax.broadcasted_iota(jnp.int32, (total_vid, LANES), 1) % heads
    logs = jnp.broadcast_to(col_log[0], (total_vid, LANES))
    for h in range(1, heads):
        logs = jnp.where(lane == h, col_log[h], logs)
    for i, out in enumerate(col_outs):
        rows = slice(i * out.shape[0], (i + 1) * out.shape[0])
        put_cols(out, col_mix[rows], logs[rows])


def put_rows(out, mix, log):
    width, tokens = mix.shape
    pad = jnp.zeros((out.shape[0] - width - PIECES * log.shape[0], tokens), F32)
    out[:width, :] = mix.astype(BF16)
    out[width:, :] = jnp.concatenate(split_pieces(log) + [pad], axis=0).astype(BF16)


def get_rows(ref, width):
    heads, tokens = width // HEAD_DIM, ref.shape[1]
    pieces = ref[width:, :].astype(F32)
    log = pieces[:heads]
    for i in range(1, PIECES):
        log = log + pieces[i * heads : (i + 1) * heads]
    mix = ref[:width, :].astype(F32).reshape(heads, HEAD_DIM, tokens)
    return mix, log.reshape(heads, 1, tokens)


def put_cols(out, mix, logs):
    width = mix.shape[1]
    heads = width // HEAD_DIM
    lane = lax.broadcasted_iota(jnp.int32, logs.shape, 1)
    pieces = split_pieces(logs)
    stats = jnp.zeros_like(logs)
    for i, piece in enumerate(pieces):
        stats = jnp.where(lane // heads == i, piece, stats)
    out[:, :width] = mix.astype(BF16)
    out[:, width:] = stats.astype(BF16)


def get_cols(ref, width):
    heads = width // HEAD_DIM
    source = lax.broadcasted_iota(jnp.int32, (LANES, width), 0)
    target = lax.broadcasted_iota(jnp.int32, (LANES, width), 1)
    spread = (source < PIECES * heads) & (source % heads == target // HEAD_DIM)
    return ref[:, :width].astype(F32), dot(ref[:, width:], spread.astype(BF16))


def merge(states):
    top = states[0][1]
    for _, log in states[1:]:
        top = jnp.maximum(top, log)
    total, mix = 0.0, 0.0
    for part, log in states:
        weight = jnp.exp(log - top)
        total += weight
        mix += weight * part
    return mix / total


def project(mix, proj, me, outs):
    step = outs[0].shape[1]
    for i, out in enumerate(outs):
        block = pl.ds(pl.multiple_of(partner(me, i, len(outs)) * step, step), step)
        out[: mix.shape[0], :] = dot(mix, proj[:, block]).astype(out.dtype)


def project_audio(me, proj, states, outs):
    width = proj.shape[0]
    mix = merge([get_rows(ref, width) for ref in states]).reshape(width, -1)
    project(mix.T.astype(BF16), proj, me[0], outs)


def project_video(me, proj, states, aud_core, outs):
    mix = merge([get_cols(ref, proj.shape[0]) for ref in states])
    aud_rows = aud_core.shape[0]
    outs[1][:aud_rows, :] = aud_core[...]
    project(mix.astype(BF16), proj, me[0], [outs[0], outs[1].at[aud_rows:, :], *outs[2:]])


def add(*refs):
    terms, vid_out, aud_out = refs[:-2], refs[-2], refs[-1]
    count = len(terms) // 2 + 1
    aud_rows = aud_out.shape[0]
    core = terms[1][...].astype(F32)
    vid = terms[0][...] + core[aud_rows:]
    aud = terms[count][...] + core[:aud_rows]
    for vid_term, aud_term in zip(terms[2:count], terms[count + 1 :]):
        vid += vid_term[...].astype(F32)
        aud += aud_term[:aud_rows].astype(F32)
    vid_out[...] = vid.astype(BF16)
    aud_out[...] = aud.astype(BF16)


def call(body, out_shape, args, in_specs=None, scratch=()):
    vmem = pl.BlockSpec(memory_space=pltpu.VMEM)
    return pl.pallas_call(
        body,
        out_shape=out_shape,
        in_specs=in_specs or [vmem] * len(args),
        out_specs=[vmem] * len(out_shape),
        scratch_shapes=scratch,
        compiler_params=pltpu.CompilerParams(vmem_limit_bytes=VMEM_LIMIT),
        cost_estimate=pl.CostEstimate(flops=COST, bytes_accessed=0, transcendentals=0),
    )(*args)


def partner(index, k, size):
    return index ^ k


def swap(block, axis, distance):
    return lax.ppermute(block, axis, [(i, i ^ distance) for i in range(lax.axis_size(axis))])


def factors(size):
    bits = size.bit_length() - 1
    assert size == 1 << bits
    return 1 << (bits // 2), 1 << (bits - bits // 2)


def per_device(ref_audio, val_audio, ref_video, val_video, audio_proj, video_proj):
    seq, peers = lax.axis_size("seq"), lax.axis_size("head")
    aud_count, vid_count = factors(seq)
    aud_rows, width = ref_audio.shape
    vid_rows = ref_video.shape[0]
    heads = width // HEAD_DIM
    step = audio_proj.shape[1] // peers
    log_rows = -(-PIECES * heads // 16) * 16

    def shape(rows, cols, dtype=BF16):
        return jax.ShapeDtypeStruct((rows, cols), dtype)

    def gather(block, stride, count):
        return [swap(block, "seq", k * stride) for k in range(1, count)] + [block]

    def scatter(blocks, stride):
        count = len(blocks)
        return [swap(blocks[k - 1], "seq", k * stride) for k in reversed(range(1, count))] + [blocks[-1]]

    aud, vid = call(
        pack,
        [shape(aud_rows, 2 * width), shape(vid_rows, 2 * width)],
        [
            pltpu.with_memory_space_constraint(x, pltpu.HBM)
            for x in (ref_audio, val_audio, ref_video, val_video)
        ],
        in_specs=[pl.BlockSpec(memory_space=pltpu.HBM)] * 4,
        scratch=[pltpu.SemaphoreType.DMA((4,))],
    )
    auds, vids = gather(aud, 1, aud_count), gather(vid, aud_count, vid_count)
    states = call(
        functools.partial(attend, aud_count, vid_count),
        [shape(width + log_rows, aud_rows)] * aud_count + [shape(vid_rows, width + LANES)] * vid_count,
        [*auds, *vids],
    )
    rows = scatter(states[:aud_count], 1)
    cols = scatter(states[aud_count:], aud_count)

    me = lax.axis_index("head").astype(jnp.int32).reshape(1)
    vmem = pl.BlockSpec(memory_space=pltpu.VMEM)
    smem = pl.BlockSpec(memory_space=pltpu.SMEM)
    hbm = pl.BlockSpec(memory_space=pl.ANY)

    aud_terms = call(
        lambda me, proj, *refs: project_audio(me, proj, refs[:aud_count], refs[aud_count:]),
        [shape(aud_rows, step, F32), shape(aud_rows, step)]
        + [shape(aud_rows + vid_rows + 8, step)] * (peers - 2),
        [me, audio_proj, *rows],
        in_specs=[smem, vmem] + [vmem] * aud_count,
    )
    vid_terms = call(
        lambda me, proj, *refs: project_video(
            me, proj, refs[:vid_count], refs[vid_count], refs[vid_count + 1 :]
        ),
        [shape(vid_rows, step, F32), shape(aud_rows + vid_rows, step)]
        + [shape(vid_rows, step)] * (peers - 2),
        [me, video_proj, *cols, aud_terms[1]],
        in_specs=[smem] + [vmem] * (vid_count + 2),
    )
    vid_got = [vid_terms[0]] + [swap(vid_terms[k], "head", k) for k in range(1, peers)]
    aud_got = [aud_terms[0]] + [swap(aud_terms[k], "head", k) for k in range(2, peers)]
    vid_out, aud_out = call(
        add, [shape(vid_rows, step), shape(aud_rows, step)], vid_got + aud_got
    )
    return aud_out, vid_out


def solution(mesh):
    in_specs = (
        P("seq", "head"),
        P("seq", "head"),
        P("seq", "head"),
        P("seq", "head"),
        P("head", None),
        P("head", None),
    )
    out_specs = (P("seq", "head"), P("seq", "head"))
    return jax.shard_map(
        per_device, mesh=mesh, in_specs=in_specs, out_specs=out_specs, check_vma=False
    )
```

time: 29.7 us -> 27 us (0.909)
  waiting for transfers between devices: 11.5 us -> 7.21 us
  starting transfers between devices: 13.7 us -> 16.1 us
  local copies, waits for them, and re-layouts: 0.61 us -> 0.01 us
    ppermute x13, waiting for transfers between devices: 11.5 us -> 7.21 us  [swap(): lax.ppermute(block, axis, [(i, i ^ distance) for i in range(lax.axis_size...]
    ppermute x13, starting transfers between devices: 13.7 us -> 16.1 us  [swap(): lax.ppermute(block, axis, [(i, i ^ distance) for i in range(lax.axis_size...]
    unnamed x4, local copies, waits for them, and re-layouts: 0.61 us -> 0.01 us
    pallas_call x6 -> x5, Pallas kernels: 3 us -> 2.84 us  [call(): pl.pallas_call(body, out_shape=out_shape, in_specs=in_specs or [vmem] * l...]
  transfers between devices with their start and end apart: 13 -> 13, of which waited for: 8 -> 4; matrix products, arithmetic and copies ran while one was open for 0% -> 0% of each run, Pallas kernels for 2% -> 2%
where the time goes in v5:
time: 27 us; the launch traced here: 26.9 us
  starting transfers between devices  16.1 us (60%)
  waiting for transfers between devices  7.21 us (27%)
  Pallas kernels  2.84 us (11%)
  between operations  0.67 us (2%)
    ppermute x13, starting transfers between devices, swap(): lax.ppermute(block, axis, [(i, i ^ distance) for i in range(lax.axis_size...  16.1 us
    ppermute x13, waiting for transfers between devices, swap(): lax.ppermute(block, axis, [(i, i ^ distance) for i in range(lax.axis_size...  7.21 us
    pallas_call x5, Pallas kernels, call(): pl.pallas_call(body, out_shape=out_shape, in_specs=in_specs or [vmem] * l...  2.84 us
  transfers between devices with their start and end apart: 13, of which 4 were waited for; matrix products, arithmetic and copies ran while one was open for 0% of the time, Pallas kernels for 2%

profile of v5, /device:TPU:0, one launch (start us, length us, event | category | flops | bytes accessed | tf_op | source)
XLA Modules:
  0.0 26.9 jit_solution(6379917996112449535)
XLA Ops:
  0.6 0.9 %shard_map.77 = (bf16[128,512]{1,0:T(8,128)(2,1)S(1)}, bf16[24,512]{1,0:T(8,128)(2,1)S(1)}) custom-call(bf16[128,256]{1,0:T(8,128)(2,1)} %aud_ref.1, bf16[128,256]{1,0:T(8,128)(2,1)} %aud_val.1, bf16[24,256]{1,0:T(8,128)(2,1)} %vid_ref.1, bf16[24,256]{1,0:T(8,128)(2,1)} %vid_val.1), custom_call_target="tpu_custom_call" | custom-call | flops 5000000000 | tf_op jit(solution)/shard_map/pallas_call | solution.py:183
  1.5 3.0 %collective-permute-start = (bf16[128,512]{1,0:T(8,128)(2,1)S(1)}, bf16[128,512]{1,0:T(8,128)(2,1)S(1)}, u32[]{:S(2)}, u32[]{:S(2)}) collective-permute-start(bf16[128,512]{1,0:T(8,128)(2,1)S(1)} %get-tuple-element.20.refs_1_), channel_id=1, source_target_pairs={{0,4},{4,0},{8,12},{12,8},{16,20},{20,16},{24,28},{28,24},{1,5},{5... | collective-permute-start | bytes 393224 | tf_op jit(solution)/shard_map/ppermute | solution.py:199
  4.6 3.6 %collective-permute-start.3 = (bf16[24,512]{1,0:T(8,128)(2,1)S(1)}, bf16[24,512]{1,0:T(8,128)(2,1)S(1)}, u32[]{:S(2)}, u32[]{:S(2)}) collective-permute-start(bf16[24,512]{1,0:T(8,128)(2,1)S(1)} %get-tuple-element.21.refs_5_), channel_id=1, source_target_pairs={{0,24},{4,28},{8,16},{12,20},{16,8},{20,12},{24,0},{28,4},{1,25},{... | collective-permute-start | bytes 73736 | tf_op jit(solution)/shard_map/ppermute | solution.py:199
  8.2 0.8 %collective-permute-start.1 = (bf16[24,512]{1,0:T(8,128)(2,1)S(1)}, bf16[24,512]{1,0:T(8,128)(2,1)S(1)}, u32[]{:S(2)}, u32[]{:S(2)}) collective-permute-start(bf16[24,512]{1,0:T(8,128)(2,1)S(1)} %get-tuple-element.21.refs_5_), channel_id=1, source_target_pairs={{0,8},{4,12},{8,0},{12,4},{16,24},{20,28},{24,16},{28,20},{1,9},{5... | collective-permute-start | bytes 73736 | tf_op jit(solution)/shard_map/ppermute | solution.py:199
  8.9 1.5 %collective-permute-done.3.refs_4_ = bf16[24,512]{1,0:T(8,128)(2,1)S(1)} collective-permute-done((bf16[24,512]{1,0:T(8,128)(2,1)S(1)}, bf16[24,512]{1,0:T(8,128)(2,1)S(1)}, u32[]{:S(2)}, u32[]{:S(2)}) %collective-permute-start.3) | collective-permute-done | bytes 24608 | tf_op jit(solution)/shard_map/ppermute | solution.py:199
  10.4 2.4 %collective-permute-done.2.refs_3_ = bf16[24,512]{1,0:T(8,128)(2,1)S(1)} collective-permute-done((bf16[24,512]{1,0:T(8,128)(2,1)S(1)}, bf16[24,512]{1,0:T(8,128)(2,1)S(1)}, u32[]{:S(2)}, u32[]{:S(2)}) %collective-permute-start.2) | collective-permute-done | bytes 24608 | tf_op jit(solution)/shard_map/ppermute | solution.py:199
  12.9 0.0 collective-permute-done.1.refs_2_
  12.9 0.0 collective-permute-done.refs_0_
  12.9 0.6 %shard_map.78 = (bf16[272,128]{1,0:T(8,128)(2,1)S(1)}, bf16[272,128]{1,0:T(8,128)(2,1)S(1)}, bf16[24,384]{1,0:T(8,128)(2,1)S(1)}, bf16[24,384]{1,0:T(8,128)(2,1)...) custom-call(bf16[128,512]{1,0:T(8,128)(2,1)S(1)} %collective-permute-done.refs_0_, ...), custom_call_target="tpu_custom_call" | custom-call | flops 5000000000 | tf_op jit(solution)/shard_map/pallas_call | solution.py:183
  13.5 0.6 %collective-permute-start.7 = (bf16[272,128]{1,0:T(8,128)(2,1)S(1)}, bf16[272,128]{1,0:T(8,128)(2,1)S(1)}, u32[]{:S(2)}, u32[]{:S(2)}) collective-permute-start(bf16[272,128]{1,0:T(8,128)(2,1)S(1)} %get-tuple-element.26), channel_id=1, source_target_pairs={{0,4},{4,0},{8,12},{12,8},{16,20},{20,16},{24,28},{28,24},{1,5},{5... | collective-permute-start | bytes 208904 | tf_op jit(solution)/shard_map/ppermute | solution.py:199
  14.1 1.5 %collective-permute-start.4 = (bf16[24,384]{1,0:T(8,128)(2,1)S(1)}, bf16[24,384]{1,0:T(8,128)(2,1)S(1)}, u32[]{:S(2)}, u32[]{:S(2)}) collective-permute-start(bf16[24,384]{1,0:T(8,128)(2,1)S(1)} %get-tuple-element.22), channel_id=1, source_target_pairs={{0,24},{4,28},{8,16},{12,20},{16,8},{20,12},{24,0},{28,4},{1,25},{... | collective-permute-start | bytes 55304 | tf_op jit(solution)/shard_map/ppermute | solution.py:199
  15.6 0.6 %collective-permute-start.5 = (bf16[24,384]{1,0:T(8,128)(2,1)S(1)}, bf16[24,384]{1,0:T(8,128)(2,1)S(1)}, u32[]{:S(2)}, u32[]{:S(2)}) collective-permute-start(bf16[24,384]{1,0:T(8,128)(2,1)S(1)} %get-tuple-element.23), channel_id=1, source_target_pairs={{0,16},{4,20},{8,24},{12,28},{16,0},{20,4},{24,8},{28,12},{1,17},{... | collective-permute-start | bytes 55304 | tf_op jit(solution)/shard_map/ppermute | solution.py:199
  16.2 2.4 %collective-permute-start.6 = (bf16[24,384]{1,0:T(8,128)(2,1)S(1)}, bf16[24,384]{1,0:T(8,128)(2,1)S(1)}, u32[]{:S(2)}, u32[]{:S(2)}) collective-permute-start(bf16[24,384]{1,0:T(8,128)(2,1)S(1)} %get-tuple-element.24), channel_id=1, source_target_pairs={{0,8},{4,12},{8,0},{12,4},{16,24},{20,28},{24,16},{28,20},{1,9},{5... | collective-permute-start | bytes 55304 | tf_op jit(solution)/shard_map/ppermute | solution.py:199
  18.5 0.0 collective-permute-done.7.refs_0_
  18.5 0.3 %shard_map.79 = (f32[128,256]{1,0:T(8,128)S(1)}, bf16[128,256]{1,0:T(8,128)(2,1)S(1)}, bf16[160,256]{1,0:T(8,128)(2,1)S(1)}, bf16[160,256]{1,0:T(8,128)(2,1)S(1)}) custom-call(s32[1]{0:T(128)} %bitcast.me, bf16[256,1024]{1,0:T(8,128)(2,1)S(1)} %copy-done, bf16[272,128]{1,0:T(8,128)(2,1)S(1)} %collective-permute-done.7.refs_0_, ...), custom_call_target="tpu_custom_call" | custom-call | flops 5000000000 | tf_op jit(solution)/shard_map/pallas_call | solution.py:183
  18.8 1.6 %collective-permute-start.11 = (bf16[160,256]{1,0:T(8,128)(2,1)S(1)}, bf16[160,256]{1,0:T(8,128)(2,1)S(1)}, u32[]{:S(2)}, u32[]{:S(2)}) collective-permute-start(bf16[160,256]{1,0:T(8,128)(2,1)S(1)} %get-tuple-element.34), channel_id=1, source_target_pairs={{0,2},{1,3},{2,0},{3,1},{4,6},{5,7},{6,4},{7,5},{8,10},{9,11},{10,... | collective-permute-start | bytes 245768 | tf_op jit(solution)/shard_map/ppermute | solution.py:199
  20.4 0.0 collective-permute-done.6.refs_2_
  20.4 0.3 %shard_map.80 = (f32[24,256]{1,0:T(8,128)S(1)}, bf16[152,256]{1,0:T(8,128)(2,1)S(1)}, bf16[24,256]{1,0:T(8,128)(2,1)S(1)}, bf16[24,256]{1,0:T(8,128)(2,1)S(1)}) custom-call(s32[1]{0:T(128)} %bitcast.me, bf16[256,1024]{1,0:T(8,128)(2,1)S(1)} %copy-done.1, bf16[24,384]{1,0:T(8,128)(2,1)S(1)} %collective-permute-done.4.refs_0_, ...), custom_call_target="tpu_custom_call" | custom-call | flops 5000000000 | tf_op jit(solution)/shard_map/pallas_call | solution.py:183
  20.8 0.7 %collective-permute-start.8 = (bf16[152,256]{1,0:T(8,128)(2,1)S(1)}, bf16[152,256]{1,0:T(8,128)(2,1)S(1)}, u32[]{:S(2)}, u32[]{:S(2)}) collective-permute-start(bf16[152,256]{1,0:T(8,128)(2,1)S(1)} %get-tuple-element.30), channel_id=1, source_target_pairs={{0,1},{1,0},{2,3},{3,2},{4,5},{5,4},{6,7},{7,6},{8,9},{9,8},{10,11... | collective-permute-start | bytes 233480 | tf_op jit(solution)/shard_map/ppermute | solution.py:199
  21.4 1.5 %collective-permute-start.9 = (bf16[24,256]{1,0:T(8,128)(2,1)S(1)}, bf16[24,256]{1,0:T(8,128)(2,1)S(1)}, u32[]{:S(2)}, u32[]{:S(2)}) collective-permute-start(bf16[24,256]{1,0:T(8,128)(2,1)S(1)} %get-tuple-element.31), channel_id=1, source_target_pairs={{0,2},{1,3},{2,0},{3,1},{4,6},{5,7},{6,4},{7,5},{8,10},{9,11},{10,... | collective-permute-start | bytes 36872 | tf_op jit(solution)/shard_map/ppermute | solution.py:199
  22.9 0.0 collective-permute-start.10
  22.9 2.3 %collective-permute-done.9.refs_2_ = bf16[24,256]{1,0:T(8,128)(2,1)S(1)} collective-permute-done((bf16[24,256]{1,0:T(8,128)(2,1)S(1)}, bf16[24,256]{1,0:T(8,128)(2,1)S(1)}, u32[]{:S(2)}, u32[]{:S(2)}) %collective-permute-start.9) | collective-permute-done | bytes 12320 | tf_op jit(solution)/shard_map/ppermute | solution.py:199
  25.3 0.9 %collective-permute-done.10.refs_3_ = bf16[24,256]{1,0:T(8,128)(2,1)S(1)} collective-permute-done((bf16[24,256]{1,0:T(8,128)(2,1)S(1)}, bf16[24,256]{1,0:T(8,128)(2,1)S(1)}, u32[]{:S(2)}, u32[]{:S(2)}) %collective-permute-start.10) | collective-permute-done | bytes 12320 | tf_op jit(solution)/shard_map/ppermute | solution.py:199
  26.2 0.7 %shard_map.81 = (bf16[24,256]{1,0:T(8,128)(2,1)}, bf16[128,256]{1,0:T(8,128)(2,1)}) custom-call(f32[24,256]{1,0:T(8,128)S(1)} %get-tuple-element.29.refs_0_, bf16[152,256]{1,0:T(8,128)(2,1)S(1)} %collective-permute-done.8.refs_1_, bf16[24,256]{1,0:T(8,128)(2,1)S(1)} %collective-permute-done.9.refs_2_, bf16[24,256]{1,0:T(8,128)(2,1)S(1)} %collective-permute-done.10.refs_3_, ...), custom_call_target="tpu_custom_call" | custom-call | flops 5000000000 | tf_op jit(solution)/shard_map/pallas_call | solution.py:183
  (11 shorter events, 0.0 us)
Async XLA Ops:
  1.5 11.3 %collective-permute-start = (bf16[128,512]{1,0:T(8,128)(2,1)S(1)}, bf16[128,512]{1,0:T(8,128)(2,1)S(1)}, u32[]{:S(2)}, u32[]{:S(2)}) collective-permute-start(bf16[128,512]{1,0:T(8,128)(2,1)S(1)} %get-tuple-element.20.refs_1_), channel_id=1, source_target_pairs={{0,4},{4,0},{8,12},{12,8},{16,20},{20,16},{24,28},{28,24},{1,5},{5... | collective-permute-start | bytes 393224 | tf_op jit(solution)/shard_map/ppermute | solution.py:199
  4.6 14.0 %copy-start = (bf16[256,1024]{1,0:T(8,128)(2,1)S(1)}, bf16[256,1024]{1,0:T(8,128)(2,1)}, u32[]{:S(2)}) copy-start(bf16[256,1024]{1,0:T(8,128)(2,1)} %proj.2) | copy-start | bytes 1572868
  4.6 5.9 %collective-permute-start.3 = (bf16[24,512]{1,0:T(8,128)(2,1)S(1)}, bf16[24,512]{1,0:T(8,128)(2,1)S(1)}, u32[]{:S(2)}, u32[]{:S(2)}) collective-permute-start(bf16[24,512]{1,0:T(8,128)(2,1)S(1)} %get-tuple-element.21.refs_5_), channel_id=1, source_target_pairs={{0,24},{4,28},{8,16},{12,20},{16,8},{20,12},{24,0},{28,4},{1,25},{... | collective-permute-start | bytes 73736 | tf_op jit(solution)/shard_map/ppermute | solution.py:199
  8.2 4.7 %collective-permute-start.2 = (bf16[24,512]{1,0:T(8,128)(2,1)S(1)}, bf16[24,512]{1,0:T(8,128)(2,1)S(1)}, u32[]{:S(2)}, u32[]{:S(2)}) collective-permute-start(bf16[24,512]{1,0:T(8,128)(2,1)S(1)} %get-tuple-element.21.refs_5_), channel_id=1, source_target_pairs={{0,16},{4,20},{8,24},{12,28},{16,0},{20,4},{24,8},{28,12},{1,17},{... | collective-permute-start | bytes 73736 | tf_op jit(solution)/shard_map/ppermute | solution.py:199
  8.2 4.7 %collective-permute-start.1 = (bf16[24,512]{1,0:T(8,128)(2,1)S(1)}, bf16[24,512]{1,0:T(8,128)(2,1)S(1)}, u32[]{:S(2)}, u32[]{:S(2)}) collective-permute-start(bf16[24,512]{1,0:T(8,128)(2,1)S(1)} %get-tuple-element.21.refs_5_), channel_id=1, source_target_pairs={{0,8},{4,12},{8,0},{12,4},{16,24},{20,28},{24,16},{28,20},{1,9},{5... | collective-permute-start | bytes 73736 | tf_op jit(solution)/shard_map/ppermute | solution.py:199
  13.5 5.0 %collective-permute-start.7 = (bf16[272,128]{1,0:T(8,128)(2,1)S(1)}, bf16[272,128]{1,0:T(8,128)(2,1)S(1)}, u32[]{:S(2)}, u32[]{:S(2)}) collective-permute-start(bf16[272,128]{1,0:T(8,128)(2,1)S(1)} %get-tuple-element.26), channel_id=1, source_target_pairs={{0,4},{4,0},{8,12},{12,8},{16,20},{20,16},{24,28},{28,24},{1,5},{5... | collective-permute-start | bytes 208904 | tf_op jit(solution)/shard_map/ppermute | solution.py:199
  14.1 6.3 %collective-permute-start.4 = (bf16[24,384]{1,0:T(8,128)(2,1)S(1)}, bf16[24,384]{1,0:T(8,128)(2,1)S(1)}, u32[]{:S(2)}, u32[]{:S(2)}) collective-permute-start(bf16[24,384]{1,0:T(8,128)(2,1)S(1)} %get-tuple-element.22), channel_id=1, source_target_pairs={{0,24},{4,28},{8,16},{12,20},{16,8},{20,12},{24,0},{28,4},{1,25},{... | collective-permute-start | bytes 55304 | tf_op jit(solution)/shard_map/ppermute | solution.py:199
  15.6 4.8 %collective-permute-start.5 = (bf16[24,384]{1,0:T(8,128)(2,1)S(1)}, bf16[24,384]{1,0:T(8,128)(2,1)S(1)}, u32[]{:S(2)}, u32[]{:S(2)}) collective-permute-start(bf16[24,384]{1,0:T(8,128)(2,1)S(1)} %get-tuple-element.23), channel_id=1, source_target_pairs={{0,16},{4,20},{8,24},{12,28},{16,0},{20,4},{24,8},{28,12},{1,17},{... | collective-permute-start | bytes 55304 | tf_op jit(solution)/shard_map/ppermute | solution.py:199
  16.2 4.3 %collective-permute-start.6 = (bf16[24,384]{1,0:T(8,128)(2,1)S(1)}, bf16[24,384]{1,0:T(8,128)(2,1)S(1)}, u32[]{:S(2)}, u32[]{:S(2)}) collective-permute-start(bf16[24,384]{1,0:T(8,128)(2,1)S(1)} %get-tuple-element.24), channel_id=1, source_target_pairs={{0,8},{4,12},{8,0},{12,4},{16,24},{20,28},{24,16},{28,20},{1,9},{5... | collective-permute-start | bytes 55304 | tf_op jit(solution)/shard_map/ppermute | solution.py:199
  18.5 1.9 %copy-start.1 = (bf16[256,1024]{1,0:T(8,128)(2,1)S(1)}, bf16[256,1024]{1,0:T(8,128)(2,1)}, u32[]{:S(2)}) copy-start(bf16[256,1024]{1,0:T(8,128)(2,1)} %proj.3) | copy-start | bytes 1572868
  18.8 7.4 %collective-permute-start.11 = (bf16[160,256]{1,0:T(8,128)(2,1)S(1)}, bf16[160,256]{1,0:T(8,128)(2,1)S(1)}, u32[]{:S(2)}, u32[]{:S(2)}) collective-permute-start(bf16[160,256]{1,0:T(8,128)(2,1)S(1)} %get-tuple-element.34), channel_id=1, source_target_pairs={{0,2},{1,3},{2,0},{3,1},{4,6},{5,7},{6,4},{7,5},{8,10},{9,11},{10,... | collective-permute-start | bytes 245768 | tf_op jit(solution)/shard_map/ppermute | solution.py:199
  20.4 5.8 %collective-permute-start.12 = (bf16[160,256]{1,0:T(8,128)(2,1)S(1)}, bf16[160,256]{1,0:T(8,128)(2,1)S(1)}, u32[]{:S(2)}, u32[]{:S(2)}) collective-permute-start(bf16[160,256]{1,0:T(8,128)(2,1)S(1)} %get-tuple-element.35), channel_id=1, source_target_pairs={{0,3},{1,2},{2,1},{3,0},{4,7},{5,6},{6,5},{7,4},{8,11},{9,10},{10,... | collective-permute-start | bytes 245768 | tf_op jit(solution)/shard_map/ppermute | solution.py:199
  20.8 5.4 %collective-permute-start.8 = (bf16[152,256]{1,0:T(8,128)(2,1)S(1)}, bf16[152,256]{1,0:T(8,128)(2,1)S(1)}, u32[]{:S(2)}, u32[]{:S(2)}) collective-permute-start(bf16[152,256]{1,0:T(8,128)(2,1)S(1)} %get-tuple-element.30), channel_id=1, source_target_pairs={{0,1},{1,0},{2,3},{3,2},{4,5},{5,4},{6,7},{7,6},{8,9},{9,8},{10,11... | collective-permute-start | bytes 233480 | tf_op jit(solution)/shard_map/ppermute | solution.py:199
  21.4 3.9 %collective-permute-start.9 = (bf16[24,256]{1,0:T(8,128)(2,1)S(1)}, bf16[24,256]{1,0:T(8,128)(2,1)S(1)}, u32[]{:S(2)}, u32[]{:S(2)}) collective-permute-start(bf16[24,256]{1,0:T(8,128)(2,1)S(1)} %get-tuple-element.31), channel_id=1, source_target_pairs={{0,2},{1,3},{2,0},{3,1},{4,6},{5,7},{6,4},{7,5},{8,10},{9,11},{10,... | collective-permute-start | bytes 36872 | tf_op jit(solution)/shard_map/ppermute | solution.py:199
  22.9 3.2 %collective-permute-start.10 = (bf16[24,256]{1,0:T(8,128)(2,1)S(1)}, bf16[24,256]{1,0:T(8,128)(2,1)S(1)}, u32[]{:S(2)}, u32[]{:S(2)}) collective-permute-start(bf16[24,256]{1,0:T(8,128)(2,1)S(1)} %get-tuple-element.32), channel_id=1, source_target_pairs={{0,3},{1,2},{2,1},{3,0},{4,7},{5,6},{6,5},{7,4},{8,11},{9,10},{10,... | collective-permute-start | bytes 36872 | tf_op jit(solution)/shard_map/ppermute | solution.py:199

commit v6 on v5

--- a/solution.py
+++ b/solution.py
@@ -11,10 +11,25 @@
 LANES = 128
 PIECES = 3
 SCALE = HEAD_DIM ** (-0.5)
+NEVER = -1e30
 VMEM_LIMIT = 48 * 1024 * 1024
 COST = 5 * 10**9
 BF16 = jnp.bfloat16
 F32 = jnp.float32
+
+
+GATHER_4 = [
+    {0: 1, 2: 3},
+    {1: 0, 0: 3, 2: 1, 3: 2},
+    {0: 2, 3: 0, 1: 3},
+    {2: 0, 3: 1, 1: 2},
+]
+SCATTER_4 = [
+    {3: 2, 1: 0},
+    {0: 2, 3: 0, 2: 1, 1: 3},
+    {0: 3, 3: 1, 2: 0},
+    {0: 1, 2: 3, 1: 2},
+]
 
 
 def dot(a, b, contract_a=1, contract_b=0):
@@ -49,14 +64,39 @@
         copy.wait()
 
 
-def attend(aud_count, vid_count, *refs):
-    auds, vids = refs[:aud_count], refs[aud_count : aud_count + vid_count]
-    row_outs = refs[aud_count + vid_count : 2 * aud_count + vid_count]
-    col_outs = refs[2 * aud_count + vid_count :]
+def lookup(table, index):
+    value = jnp.int32(table[0])
+    for i, entry in enumerate(table[1:], 1):
+        value = jnp.where(index == i, entry, value)
+    return value
+
+
+def sources(step, count):
+    back = {target: source for source, target in step.items()}
+    return [back.get(i, -1) for i in range(count)]
+
+
+def targets(step, count):
+    return [step.get(i, -1) for i in range(count)]
+
+
+def attend(aud_count, vid_count, gather, scatter, here, *refs):
+    auds, refs = refs[:aud_count], refs[aud_count:]
+    gots, mine, refs = refs[: len(gather)], refs[len(gather)], refs[len(gather) + 1 :]
+    row_outs, col_outs, (blocks, states) = refs[:aud_count], refs[aud_count:-2], refs[-2:]
+    me = here[0]
+    blocks[me] = mine[...]
+    for step, got in zip(gather, gots):
+        source = lookup(sources(step, vid_count), me)
+
+        @pl.when(source >= 0)
+        def _():
+            blocks[source] = got[...]
+
     width = auds[0].shape[1] // 2
     heads = width // HEAD_DIM
     aud = jnp.concatenate([ref[...] for ref in auds], axis=0)
-    vid = jnp.concatenate([ref[...] for ref in vids], axis=0).astype(F32)
+    vid = blocks[...].astype(F32).reshape(-1, 2 * width)
     queries, aud_vals = aud[:, :width], aud[:, width:]
     total_aud, total_vid = aud.shape[0], vid.shape[0]
     masks = [head_lanes(total_vid, width, h) for h in range(heads)]
@@ -90,9 +130,13 @@
     logs = jnp.broadcast_to(col_log[0], (total_vid, LANES))
     for h in range(1, heads):
         logs = jnp.where(lane == h, col_log[h], logs)
-    for i, out in enumerate(col_outs):
-        rows = slice(i * out.shape[0], (i + 1) * out.shape[0])
-        put_cols(out, col_mix[rows], logs[rows])
+    vid_rows = mine.shape[0]
+    for i in range(vid_count):
+        rows = slice(i * vid_rows, (i + 1) * vid_rows)
+        put_cols(states.at[i], col_mix[rows], logs[rows])
+    for step, out in zip(scatter, col_outs):
+        out[...] = states[jnp.maximum(lookup(targets(step, vid_count), me), 0)]
+    col_outs[-1][...] = states[me]
 
 
 def put_rows(out, mix, log):
@@ -157,8 +201,13 @@
     project(mix.T.astype(BF16), proj, me[0], outs)
 
 
-def project_video(me, proj, states, aud_core, outs):
-    mix = merge([get_cols(ref, proj.shape[0]) for ref in states])
+def project_video(vid_count, scatter, me, here, proj, gots, mine, aud_core, outs):
+    states = [get_cols(mine, proj.shape[0])]
+    for step, got in zip(scatter, gots):
+        mix, log = get_cols(got, proj.shape[0])
+        sent = lookup(sources(step, vid_count), here[0]) >= 0
+        states.append((mix, log + jnp.where(sent, 0.0, NEVER)))
+    mix = merge(states)
     aud_rows = aud_core.shape[0]
     outs[1][:aud_rows, :] = aud_core[...]
     project(mix.astype(BF16), proj, me[0], [outs[0], outs[1].at[aud_rows:, :], *outs[2:]])
@@ -168,10 +217,10 @@
     terms, vid_out, aud_out = refs[:-2], refs[-2], refs[-1]
     count = len(terms) // 2 + 1
     aud_rows = aud_out.shape[0]
-    core = terms[1][...].astype(F32)
+    core = terms[count - 1][...].astype(F32)
     vid = terms[0][...] + core[aud_rows:]
     aud = terms[count][...] + core[:aud_rows]
-    for vid_term, aud_term in zip(terms[2:count], terms[count + 1 :]):
+    for vid_term, aud_term in zip(terms[1 : count - 1], terms[count + 1 :]):
         vid += vid_term[...].astype(F32)
         aud += aud_term[:aud_rows].astype(F32)
     vid_out[...] = vid.astype(BF16)
@@ -205,24 +254,38 @@
     return 1 << (bits // 2), 1 << (bits - bits // 2)
 
 
+def gather_plan(count):
+    if count == 4:
+        return GATHER_4
+    return [{i: i ^ k for i in range(count)} for k in range(1, count)]
+
+
+def scatter_plan(count):
+    if count == 4:
+        return SCATTER_4
+    return [{i: i ^ k for i in range(count)} for k in reversed(range(1, count))]
+
+
+def move(block, axis, stride, count, step):
+    pairs = []
+    for i in range(lax.axis_size(axis)):
+        here = i // stride % count
+        if here in step:
+            pairs.append((i, i + (step[here] - here) * stride))
+    return lax.ppermute(block, axis, pairs)
+
+
 def per_device(ref_audio, val_audio, ref_video, val_video, audio_proj, video_proj):
     seq, peers = lax.axis_size("seq"), lax.axis_size("head")
     aud_count, vid_count = factors(seq)
     aud_rows, width = ref_audio.shape
     vid_rows = ref_video.shape[0]
     heads = width // HEAD_DIM
-    step = audio_proj.shape[1] // peers
+    block = audio_proj.shape[1] // peers
     log_rows = -(-PIECES * heads // 16) * 16
 
     def shape(rows, cols, dtype=BF16):
         return jax.ShapeDtypeStruct((rows, cols), dtype)
-
-    def gather(block, stride, count):
-        return [swap(block, "seq", k * stride) for k in range(1, count)] + [block]
-
-    def scatter(blocks, stride):
-        count = len(blocks)
-        return [swap(blocks[k - 1], "seq", k * stride) for k in reversed(range(1, count))] + [blocks[-1]]
 
     aud, vid = call(
         pack,
@@ -234,40 +297,60 @@
         in_specs=[pl.BlockSpec(memory_space=pltpu.HBM)] * 4,
         scratch=[pltpu.SemaphoreType.DMA((4,))],
     )
-    auds, vids = gather(aud, 1, aud_count), gather(vid, aud_count, vid_count)
-    states = call(
-        functools.partial(attend, aud_count, vid_count),
-        [shape(width + log_rows, aud_rows)] * aud_count + [shape(vid_rows, width + LANES)] * vid_count,
-        [*auds, *vids],
-    )
-    rows = scatter(states[:aud_count], 1)
-    cols = scatter(states[aud_count:], aud_count)
-
-    me = lax.axis_index("head").astype(jnp.int32).reshape(1)
     vmem = pl.BlockSpec(memory_space=pltpu.VMEM)
     smem = pl.BlockSpec(memory_space=pltpu.SMEM)
-    hbm = pl.BlockSpec(memory_space=pl.ANY)
+    here = (lax.axis_index("seq") // aud_count).astype(jnp.int32).reshape(1)
+    gather, scatter = gather_plan(vid_count), scatter_plan(vid_count)
+    auds = [swap(aud, "seq", k) for k in range(1, aud_count)] + [aud]
+    vids = [move(vid, "seq", aud_count, vid_count, step) for step in gather]
+    state = shape(vid_rows, width + LANES)
+    states = call(
+        functools.partial(attend, aud_count, vid_count, gather, scatter),
+        [shape(width + log_rows, aud_rows)] * aud_count + [state] * (len(scatter) + 1),
+        [here, *auds, *vids, vid],
+        in_specs=[smem] + [vmem] * (aud_count + len(gather) + 1),
+        scratch=[
+            pltpu.VMEM((vid_count, *vid.shape), BF16),
+            pltpu.VMEM((vid_count, *state.shape), BF16),
+        ],
+    )
+    rows = [swap(states[k - 1], "seq", k) for k in range(1, aud_count)] + [states[aud_count - 1]]
+    cols = [
+        move(states[aud_count + i], "seq", aud_count, vid_count, step)
+        for i, step in enumerate(scatter)
+    ] + [states[-1]]
+    me = lax.axis_index("head").astype(jnp.int32).reshape(1)
 
     aud_terms = call(
         lambda me, proj, *refs: project_audio(me, proj, refs[:aud_count], refs[aud_count:]),
-        [shape(aud_rows, step, F32), shape(aud_rows, step)]
-        + [shape(aud_rows + vid_rows + 8, step)] * (peers - 2),
+        [shape(aud_rows, block, F32), shape(aud_rows, block)]
+        + [shape(aud_rows + vid_rows + 8, block)] * (peers - 2),
         [me, audio_proj, *rows],
         in_specs=[smem, vmem] + [vmem] * aud_count,
     )
     vid_terms = call(
-        lambda me, proj, *refs: project_video(
-            me, proj, refs[:vid_count], refs[vid_count], refs[vid_count + 1 :]
+        lambda me, here, proj, *refs: project_video(
+            vid_count,
+            scatter,
+            me,
+            here,
+            proj,
+            refs[: len(scatter)],
+            refs[len(scatter)],
+            refs[len(scatter) + 1],
+            refs[len(scatter) + 2 :],
         ),
-        [shape(vid_rows, step, F32), shape(aud_rows + vid_rows, step)]
-        + [shape(vid_rows, step)] * (peers - 2),
-        [me, video_proj, *cols, aud_terms[1]],
-        in_specs=[smem] + [vmem] * (vid_count + 2),
-    )
-    vid_got = [vid_terms[0]] + [swap(vid_terms[k], "head", k) for k in range(1, peers)]
+        [shape(vid_rows, block, F32), shape(aud_rows + vid_rows, block)]
+        + [shape(vid_rows, block)] * (peers - 2),
+        [me, here, video_proj, *cols, aud_terms[1]],
+        in_specs=[smem, smem] + [vmem] * (len(cols) + 2),
+    )
+    vid_got = [vid_terms[0]] + [
+        swap(vid_terms[k], "head", k) for k in reversed(range(1, peers))
+    ]
     aud_got = [aud_terms[0]] + [swap(aud_terms[k], "head", k) for k in range(2, peers)]
     vid_out, aud_out = call(
-        add, [shape(vid_rows, step), shape(aud_rows, step)], vid_got + aud_got
+        add, [shape(vid_rows, block), shape(aud_rows, block)], vid_got + aud_got
     )
     return aud_out, vid_out
 

time: 27 us -> 35.2 us (1.30)
  starting transfers between devices: 16.1 us -> 26.4 us
  waiting for transfers between devices: 7.21 us -> 4.83 us
    ppermute x0 -> x8, starting transfers between devices: none -> 19 us  [move(): return lax.ppermute(block, axis, pairs)]
    ppermute x13 -> x7, starting transfers between devices: 16.1 us -> 7.39 us  [swap(): lax.ppermute(block, axis, [(i, i ^ distance) for i in range(lax.axis_size...]
    ppermute x13 -> x7, waiting for transfers between devices: 7.21 us -> 3.36 us  [swap(): lax.ppermute(block, axis, [(i, i ^ distance) for i in range(lax.axis_size...]
    ppermute x0 -> x8, waiting for transfers between devices: none -> 1.47 us  [move(): return lax.ppermute(block, axis, pairs)]
  transfers between devices with their start and end apart: 13 -> 15, of which waited for: 4 -> 3; matrix products, arithmetic and copies ran while one was open for 0% -> 0% of each run, Pallas kernels for 2% -> 2%
where the time goes in v6:
time: 35.2 us; the launch traced here: 35 us
  starting transfers between devices  26.4 us (75%)
  waiting for transfers between devices  4.83 us (14%)
  Pallas kernels  2.88 us (8%)
  between operations  0.79 us (2%)
    ppermute x8, starting transfers between devices, move(): return lax.ppermute(block, axis, pairs)  19 us
    ppermute x7, starting transfers between devices, swap(): lax.ppermute(block, axis, [(i, i ^ distance) for i in range(lax.axis_size...  7.39 us
    ppermute x7, waiting for transfers between devices, swap(): lax.ppermute(block, axis, [(i, i ^ distance) for i in range(lax.axis_size...  3.36 us
    pallas_call x5, Pallas kernels, call(): pl.pallas_call(body, out_shape=out_shape, in_specs=in_specs or [vmem] * l...  2.88 us
    ppermute x8, waiting for transfers between devices, move(): return lax.ppermute(block, axis, pairs)  1.47 us
  transfers between devices with their start and end apart: 15, of which 3 were waited for; matrix products, arithmetic and copies ran while one was open for 0% of the time, Pallas kernels for 2%

profile of v6, /device:TPU:0, one launch (start us, length us, event | category | flops | bytes accessed | tf_op | source)
XLA Modules:
  0.0 35.0 jit_solution(9787872303207022823)
XLA Ops:
  0.6 0.9 %shard_map.77 = (bf16[128,512]{1,0:T(8,128)(2,1)S(1)}, bf16[24,512]{1,0:T(8,128)(2,1)S(1)}) custom-call(bf16[128,256]{1,0:T(8,128)(2,1)} %aud_ref.1, bf16[128,256]{1,0:T(8,128)(2,1)} %aud_val.1, bf16[24,256]{1,0:T(8,128)(2,1)} %vid_ref.1, bf16[24,256]{1,0:T(8,128)(2,1)} %vid_val.1), custom_call_target="tpu_custom_call" | custom-call | flops 5000000000 | tf_op jit(solution)/shard_map/pallas_call | solution.py:232
  1.5 3.0 %collective-permute-start = (bf16[128,512]{1,0:T(8,128)(2,1)S(1)}, bf16[128,512]{1,0:T(8,128)(2,1)S(1)}, u32[]{:S(2)}, u32[]{:S(2)}) collective-permute-start(bf16[128,512]{1,0:T(8,128)(2,1)S(1)} %get-tuple-element.21.refs_1_), channel_id=1, source_target_pairs={{0,4},{4,0},{8,12},{12,8},{16,20},{20,16},{24,28},{28,24},{1,5},{5... | collective-permute-start | bytes 393224 | tf_op jit(solution)/shard_map/ppermute | solution.py:248
  4.6 1.3 %collective-permute-start.4 = (bf16[24,512]{1,0:T(8,128)(2,1)S(1)}, bf16[24,512]{1,0:T(8,128)(2,1)S(1)}, u32[]{:S(2)}, u32[]{:S(2)}) collective-permute-start(bf16[24,512]{1,0:T(8,128)(2,1)S(1)} %get-tuple-element.22.refs_6_), channel_id=1, source_target_pairs={{8,16},{12,20},{16,0},{20,4},{24,8},{28,12},{9,17},{13,21},{17,1},... | collective-permute-start | bytes 73736 | tf_op jit(solution)/shard_map/ppermute | solution.py:275
  5.8 5.4 %collective-permute-start.3 = (bf16[24,512]{1,0:T(8,128)(2,1)S(1)}, bf16[24,512]{1,0:T(8,128)(2,1)S(1)}, u32[]{:S(2)}, u32[]{:S(2)}) collective-permute-start(bf16[24,512]{1,0:T(8,128)(2,1)S(1)} %get-tuple-element.22.refs_6_), channel_id=1, source_target_pairs={{0,16},{4,20},{8,24},{12,28},{24,0},{28,4},{1,17},{5,21},{9,25},{1... | collective-permute-start | bytes 73736 | tf_op jit(solution)/shard_map/ppermute | solution.py:275
  11.3 1.1 %collective-permute-start.2 = (bf16[24,512]{1,0:T(8,128)(2,1)S(1)}, bf16[24,512]{1,0:T(8,128)(2,1)S(1)}, u32[]{:S(2)}, u32[]{:S(2)}) collective-permute-start(bf16[24,512]{1,0:T(8,128)(2,1)S(1)} %get-tuple-element.22.refs_6_), channel_id=1, source_target_pairs={{0,24},{4,28},{8,0},{12,4},{16,8},{20,12},{24,16},{28,20},{1,25},{... | collective-permute-start | bytes 73736 | tf_op jit(solution)/shard_map/ppermute | solution.py:275
  12.4 2.9 %collective-permute-start.1 = (bf16[24,512]{1,0:T(8,128)(2,1)S(1)}, bf16[24,512]{1,0:T(8,128)(2,1)S(1)}, u32[]{:S(2)}, u32[]{:S(2)}) collective-permute-start(bf16[24,512]{1,0:T(8,128)(2,1)S(1)} %get-tuple-element.22.refs_6_), channel_id=1, source_target_pairs={{0,8},{4,12},{16,24},{20,28},{1,9},{5,13},{17,25},{21,29},{2,10},{... | collective-permute-start | bytes 73736 | tf_op jit(solution)/shard_map/ppermute | solution.py:275
  15.3 0.0 collective-permute-done.3.refs_4_
  15.3 1.5 %collective-permute-done.1.refs_2_ = bf16[24,512]{1,0:T(8,128)(2,1)S(1)} collective-permute-done((bf16[24,512]{1,0:T(8,128)(2,1)S(1)}, bf16[24,512]{1,0:T(8,128)(2,1)S(1)}, u32[]{:S(2)}, u32[]{:S(2)}) %collective-permute-start.1) | collective-permute-done | bytes 24608 | tf_op jit(solution)/shard_map/ppermute | solution.py:275
  16.8 0.7 %shard_map.78 = (bf16[272,128]{1,0:T(8,128)(2,1)S(1)}, bf16[272,128]{1,0:T(8,128)(2,1)S(1)}, bf16[24,384]{1,0:T(8,128)(2,1)S(1)}, bf16[24,384]{1,0:T(8,128)(2,1)...) custom-call(s32[1]{0:T(128)} %bitcast.1.here, ...), custom_call_target="tpu_custom_call" | custom-call | flops 5000000000 | tf_op jit(solution)/shard_map/pallas_call | solution.py:232
  17.4 0.3 collective-permute-start.9
  17.7 1.3 %collective-permute-start.5 = (bf16[24,384]{1,0:T(8,128)(2,1)S(1)}, bf16[24,384]{1,0:T(8,128)(2,1)S(1)}, u32[]{:S(2)}, u32[]{:S(2)}) collective-permute-start(bf16[24,384]{1,0:T(8,128)(2,1)S(1)} %get-tuple-element.23), channel_id=1, source_target_pairs={{8,0},{12,4},{24,16},{28,20},{9,1},{13,5},{25,17},{29,21},{10,2},{... | collective-permute-start | bytes 55304 | tf_op jit(solution)/shard_map/ppermute | solution.py:275
  19.0 0.8 %collective-permute-start.6 = (bf16[24,384]{1,0:T(8,128)(2,1)S(1)}, bf16[24,384]{1,0:T(8,128)(2,1)S(1)}, u32[]{:S(2)}, u32[]{:S(2)}) collective-permute-start(bf16[24,384]{1,0:T(8,128)(2,1)S(1)} %get-tuple-element.24), channel_id=1, source_target_pairs={{0,16},{4,20},{8,24},{12,28},{16,8},{20,12},{24,0},{28,4},{1,17},{... | collective-permute-start | bytes 55304 | tf_op jit(solution)/shard_map/ppermute | solution.py:275
  19.8 5.0 %collective-permute-start.7 = (bf16[24,384]{1,0:T(8,128)(2,1)S(1)}, bf16[24,384]{1,0:T(8,128)(2,1)S(1)}, u32[]{:S(2)}, u32[]{:S(2)}) collective-permute-start(bf16[24,384]{1,0:T(8,128)(2,1)S(1)} %get-tuple-element.25), channel_id=1, source_target_pairs={{0,24},{4,28},{16,0},{20,4},{24,8},{28,12},{1,25},{5,29},{17,1},{2... | collective-permute-start | bytes 55304 | tf_op jit(solution)/shard_map/ppermute | solution.py:275
  24.8 1.3 %collective-permute-start.8 = (bf16[24,384]{1,0:T(8,128)(2,1)S(1)}, bf16[24,384]{1,0:T(8,128)(2,1)S(1)}, u32[]{:S(2)}, u32[]{:S(2)}) collective-permute-start(bf16[24,384]{1,0:T(8,128)(2,1)S(1)} %get-tuple-element.26), channel_id=1, source_target_pairs={{0,8},{4,12},{8,16},{12,20},{16,24},{20,28},{1,9},{5,13},{9,17},{1... | collective-permute-start | bytes 55304 | tf_op jit(solution)/shard_map/ppermute | solution.py:275
  26.1 0.0 copy-start.1
  26.1 0.3 shard_map.79
  26.4 1.9 %collective-permute-start.13 = (bf16[160,256]{1,0:T(8,128)(2,1)S(1)}, bf16[160,256]{1,0:T(8,128)(2,1)S(1)}, u32[]{:S(2)}, u32[]{:S(2)}) collective-permute-start(bf16[160,256]{1,0:T(8,128)(2,1)S(1)} %get-tuple-element.36), channel_id=1, source_target_pairs={{0,2},{1,3},{2,0},{3,1},{4,6},{5,7},{6,4},{7,5},{8,10},{9,11},{10,... | collective-permute-start | bytes 245768 | tf_op jit(solution)/shard_map/ppermute | solution.py:248
  28.4 0.3 shard_map.80
  28.7 0.3 collective-permute-start.12
  29.0 1.5 %collective-permute-start.10 = (bf16[24,256]{1,0:T(8,128)(2,1)S(1)}, bf16[24,256]{1,0:T(8,128)(2,1)S(1)}, u32[]{:S(2)}, u32[]{:S(2)}) collective-permute-start(bf16[24,256]{1,0:T(8,128)(2,1)S(1)} %get-tuple-element.32), channel_id=1, source_target_pairs={{0,3},{1,2},{2,1},{3,0},{4,7},{5,6},{6,5},{7,4},{8,11},{9,10},{10,... | collective-permute-start | bytes 36872 | tf_op jit(solution)/shard_map/ppermute | solution.py:248
  30.6 0.3 %collective-permute-start.11 = (bf16[24,256]{1,0:T(8,128)(2,1)S(1)}, bf16[24,256]{1,0:T(8,128)(2,1)S(1)}, u32[]{:S(2)}, u32[]{:S(2)}) collective-permute-start(bf16[24,256]{1,0:T(8,128)(2,1)S(1)} %get-tuple-element.33), channel_id=1, source_target_pairs={{0,2},{1,3},{2,0},{3,1},{4,6},{5,7},{6,4},{7,5},{8,10},{9,11},{10,... | collective-permute-start | bytes 36872 | tf_op jit(solution)/shard_map/ppermute | solution.py:248
  30.9 2.0 %collective-permute-done.10.refs_1_ = bf16[24,256]{1,0:T(8,128)(2,1)S(1)} collective-permute-done((bf16[24,256]{1,0:T(8,128)(2,1)S(1)}, bf16[24,256]{1,0:T(8,128)(2,1)S(1)}, u32[]{:S(2)}, u32[]{:S(2)}) %collective-permute-start.10) | collective-permute-done | bytes 12320 | tf_op jit(solution)/shard_map/ppermute | solution.py:248
  33.0 1.3 %collective-permute-done.11.refs_2_ = bf16[24,256]{1,0:T(8,128)(2,1)S(1)} collective-permute-done((bf16[24,256]{1,0:T(8,128)(2,1)S(1)}, bf16[24,256]{1,0:T(8,128)(2,1)S(1)}, u32[]{:S(2)}, u32[]{:S(2)}) %collective-permute-start.11) | collective-permute-done | bytes 12320 | tf_op jit(solution)/shard_map/ppermute | solution.py:248
  34.3 0.7 %shard_map.81 = (bf16[24,256]{1,0:T(8,128)(2,1)}, bf16[128,256]{1,0:T(8,128)(2,1)}) custom-call(f32[24,256]{1,0:T(8,128)S(1)} %get-tuple-element.31.refs_0_, bf16[24,256]{1,0:T(8,128)(2,1)S(1)} %collective-permute-done.10.refs_1_, bf16[24,256]{1,0:T(8,128)(2,1)S(1)} %collective-permute-done.11.refs_2_, bf16[152,256]{1,0:T(8,128)(2,1)S(1)} %collective-permute-done.12.refs_3_, ...), custom_call_target="tpu_custom_call" | custom-call | flops 5000000000 | tf_op jit(solution)/shard_map/pallas_call | solution.py:232
  (15 shorter events, 0.0 us)
Async XLA Ops:
  1.5 15.2 %collective-permute-start = (bf16[128,512]{1,0:T(8,128)(2,1)S(1)}, bf16[128,512]{1,0:T(8,128)(2,1)S(1)}, u32[]{:S(2)}, u32[]{:S(2)}) collective-permute-start(bf16[128,512]{1,0:T(8,128)(2,1)S(1)} %get-tuple-element.21.refs_1_), channel_id=1, source_target_pairs={{0,4},{4,0},{8,12},{12,8},{16,20},{20,16},{24,28},{28,24},{1,5},{5... | collective-permute-start | bytes 393224 | tf_op jit(solution)/shard_map/ppermute | solution.py:248
  4.6 10.7 %collective-permute-start.4 = (bf16[24,512]{1,0:T(8,128)(2,1)S(1)}, bf16[24,512]{1,0:T(8,128)(2,1)S(1)}, u32[]{:S(2)}, u32[]{:S(2)}) collective-permute-start(bf16[24,512]{1,0:T(8,128)(2,1)S(1)} %get-tuple-element.22.refs_6_), channel_id=1, source_target_pairs={{8,16},{12,20},{16,0},{20,4},{24,8},{28,12},{9,17},{13,21},{17,1},... | collective-permute-start | bytes 73736 | tf_op jit(solution)/shard_map/ppermute | solution.py:275
  5.8 9.5 %collective-permute-start.3 = (bf16[24,512]{1,0:T(8,128)(2,1)S(1)}, bf16[24,512]{1,0:T(8,128)(2,1)S(1)}, u32[]{:S(2)}, u32[]{:S(2)}) collective-permute-start(bf16[24,512]{1,0:T(8,128)(2,1)S(1)} %get-tuple-element.22.refs_6_), channel_id=1, source_target_pairs={{0,16},{4,20},{8,24},{12,28},{24,0},{28,4},{1,17},{5,21},{9,25},{1... | collective-permute-start | bytes 73736 | tf_op jit(solution)/shard_map/ppermute | solution.py:275
  11.3 4.0 %collective-permute-start.2 = (bf16[24,512]{1,0:T(8,128)(2,1)S(1)}, bf16[24,512]{1,0:T(8,128)(2,1)S(1)}, u32[]{:S(2)}, u32[]{:S(2)}) collective-permute-start(bf16[24,512]{1,0:T(8,128)(2,1)S(1)} %get-tuple-element.22.refs_6_), channel_id=1, source_target_pairs={{0,24},{4,28},{8,0},{12,4},{16,8},{20,12},{24,16},{28,20},{1,25},{... | collective-permute-start | bytes 73736 | tf_op jit(solution)/shard_map/ppermute | solution.py:275
  12.4 4.4 %collective-permute-start.1 = (bf16[24,512]{1,0:T(8,128)(2,1)S(1)}, bf16[24,512]{1,0:T(8,128)(2,1)S(1)}, u32[]{:S(2)}, u32[]{:S(2)}) collective-permute-start(bf16[24,512]{1,0:T(8,128)(2,1)S(1)} %get-tuple-element.22.refs_6_), channel_id=1, source_target_pairs={{0,8},{4,12},{16,24},{20,28},{1,9},{5,13},{17,25},{21,29},{2,10},{... | collective-permute-start | bytes 73736 | tf_op jit(solution)/shard_map/ppermute | solution.py:275
  16.8 9.3 %copy-start = (bf16[256,1024]{1,0:T(8,128)(2,1)S(1)}, bf16[256,1024]{1,0:T(8,128)(2,1)}, u32[]{:S(2)}) copy-start(bf16[256,1024]{1,0:T(8,128)(2,1)} %proj.2) | copy-start | bytes 1572868
  17.4 8.6 %collective-permute-start.9 = (bf16[272,128]{1,0:T(8,128)(2,1)S(1)}, bf16[272,128]{1,0:T(8,128)(2,1)S(1)}, u32[]{:S(2)}, u32[]{:S(2)}) collective-permute-start(bf16[272,128]{1,0:T(8,128)(2,1)S(1)} %get-tuple-element.28), channel_id=1, source_target_pairs={{0,4},{4,0},{8,12},{12,8},{16,20},{20,16},{24,28},{28,24},{1,5},{5... | collective-permute-start | bytes 208904 | tf_op jit(solution)/shard_map/ppermute | solution.py:248
  17.7 10.6 %collective-permute-start.5 = (bf16[24,384]{1,0:T(8,128)(2,1)S(1)}, bf16[24,384]{1,0:T(8,128)(2,1)S(1)}, u32[]{:S(2)}, u32[]{:S(2)}) collective-permute-start(bf16[24,384]{1,0:T(8,128)(2,1)S(1)} %get-tuple-element.23), channel_id=1, source_target_pairs={{8,0},{12,4},{24,16},{28,20},{9,1},{13,5},{25,17},{29,21},{10,2},{... | collective-permute-start | bytes 55304 | tf_op jit(solution)/shard_map/ppermute | solution.py:275
  19.0 9.3 %collective-permute-start.6 = (bf16[24,384]{1,0:T(8,128)(2,1)S(1)}, bf16[24,384]{1,0:T(8,128)(2,1)S(1)}, u32[]{:S(2)}, u32[]{:S(2)}) collective-permute-start(bf16[24,384]{1,0:T(8,128)(2,1)S(1)} %get-tuple-element.24), channel_id=1, source_target_pairs={{0,16},{4,20},{8,24},{12,28},{16,8},{20,12},{24,0},{28,4},{1,17},{... | collective-permute-start | bytes 55304 | tf_op jit(solution)/shard_map/ppermute | solution.py:275
  19.8 8.6 %collective-permute-start.7 = (bf16[24,384]{1,0:T(8,128)(2,1)S(1)}, bf16[24,384]{1,0:T(8,128)(2,1)S(1)}, u32[]{:S(2)}, u32[]{:S(2)}) collective-permute-start(bf16[24,384]{1,0:T(8,128)(2,1)S(1)} %get-tuple-element.25), channel_id=1, source_target_pairs={{0,24},{4,28},{16,0},{20,4},{24,8},{28,12},{1,25},{5,29},{17,1},{2... | collective-permute-start | bytes 55304 | tf_op jit(solution)/shard_map/ppermute | solution.py:275
  24.8 3.6 %collective-permute-start.8 = (bf16[24,384]{1,0:T(8,128)(2,1)S(1)}, bf16[24,384]{1,0:T(8,128)(2,1)S(1)}, u32[]{:S(2)}, u32[]{:S(2)}) collective-permute-start(bf16[24,384]{1,0:T(8,128)(2,1)S(1)} %get-tuple-element.26), channel_id=1, source_target_pairs={{0,8},{4,12},{8,16},{12,20},{16,24},{20,28},{1,9},{5,13},{9,17},{1... | collective-permute-start | bytes 55304 | tf_op jit(solution)/shard_map/ppermute | solution.py:275
  26.1 2.3 %copy-start.1 = (bf16[256,1024]{1,0:T(8,128)(2,1)S(1)}, bf16[256,1024]{1,0:T(8,128)(2,1)}, u32[]{:S(2)}) copy-start(bf16[256,1024]{1,0:T(8,128)(2,1)} %proj.3) | copy-start | bytes 1572868
  26.4 7.8 %collective-permute-start.13 = (bf16[160,256]{1,0:T(8,128)(2,1)S(1)}, bf16[160,256]{1,0:T(8,128)(2,1)S(1)}, u32[]{:S(2)}, u32[]{:S(2)}) collective-permute-start(bf16[160,256]{1,0:T(8,128)(2,1)S(1)} %get-tuple-element.36), channel_id=1, source_target_pairs={{0,2},{1,3},{2,0},{3,1},{4,6},{5,7},{6,4},{7,5},{8,10},{9,11},{10,... | collective-permute-start | bytes 245768 | tf_op jit(solution)/shard_map/ppermute | solution.py:248
  28.3 5.9 %collective-permute-start.14 = (bf16[160,256]{1,0:T(8,128)(2,1)S(1)}, bf16[160,256]{1,0:T(8,128)(2,1)S(1)}, u32[]{:S(2)}, u32[]{:S(2)}) collective-permute-start(bf16[160,256]{1,0:T(8,128)(2,1)S(1)} %get-tuple-element.37), channel_id=1, source_target_pairs={{0,3},{1,2},{2,1},{3,0},{4,7},{5,6},{6,5},{7,4},{8,11},{9,10},{10,... | collective-permute-start | bytes 245768 | tf_op jit(solution)/shard_map/ppermute | solution.py:248
  28.7 5.5 %collective-permute-start.12 = (bf16[152,256]{1,0:T(8,128)(2,1)S(1)}, bf16[152,256]{1,0:T(8,128)(2,1)S(1)}, u32[]{:S(2)}, u32[]{:S(2)}) collective-permute-start(bf16[152,256]{1,0:T(8,128)(2,1)S(1)} %get-tuple-element.34), channel_id=1, source_target_pairs={{0,1},{1,0},{2,3},{3,2},{4,5},{5,4},{6,7},{7,6},{8,9},{9,8},{10,11... | collective-permute-start | bytes 233480 | tf_op jit(solution)/shard_map/ppermute | solution.py:248
  29.0 3.9 %collective-permute-start.10 = (bf16[24,256]{1,0:T(8,128)(2,1)S(1)}, bf16[24,256]{1,0:T(8,128)(2,1)S(1)}, u32[]{:S(2)}, u32[]{:S(2)}) collective-permute-start(bf16[24,256]{1,0:T(8,128)(2,1)S(1)} %get-tuple-element.32), channel_id=1, source_target_pairs={{0,3},{1,2},{2,1},{3,0},{4,7},{5,6},{6,5},{7,4},{8,11},{9,10},{10,... | collective-permute-start | bytes 36872 | tf_op jit(solution)/shard_map/ppermute | solution.py:248
  30.6 3.7 %collective-permute-start.11 = (bf16[24,256]{1,0:T(8,128)(2,1)S(1)}, bf16[24,256]{1,0:T(8,128)(2,1)S(1)}, u32[]{:S(2)}, u32[]{:S(2)}) collective-permute-start(bf16[24,256]{1,0:T(8,128)(2,1)S(1)} %get-tuple-element.33), channel_id=1, source_target_pairs={{0,2},{1,3},{2,0},{3,1},{4,6},{5,7},{6,4},{7,5},{8,10},{9,11},{10,... | collective-permute-start | bytes 36872 | tf_op jit(solution)/shard_map/ppermute | solution.py:248

commit v7 on v6

--- a/solution.py
+++ b/solution.py
@@ -19,16 +19,15 @@
 
 
 GATHER_4 = [
-    {0: 1, 2: 3},
-    {1: 0, 0: 3, 2: 1, 3: 2},
-    {0: 2, 3: 0, 1: 3},
-    {2: 0, 3: 1, 1: 2},
+    {0: 1, 1: 0, 2: 3, 3: 2},
+    {0: 3, 1: 2, 2: 0, 3: 1},
+    {0: 2, 1: 3, 2: 1, 3: 0},
 ]
 SCATTER_4 = [
-    {3: 2, 1: 0},
-    {0: 2, 3: 0, 2: 1, 1: 3},
-    {0: 3, 3: 1, 2: 0},
-    {0: 1, 2: 3, 1: 2},
+    {0: 1, 1: 3, 2: 2, 3: 0},
+    {0: 2, 1: 1, 2: 0, 3: 3},
+    {0: 3, 1: 0, 2: 1, 3: 2},
+    {0: 0, 1: 2, 2: 3, 3: 1},
 ]
 
 
@@ -71,13 +70,12 @@
     return value
 
 
-def sources(step, count):
-    back = {target: source for source, target in step.items()}
-    return [back.get(i, -1) for i in range(count)]
-
-
-def targets(step, count):
-    return [step.get(i, -1) for i in range(count)]
+def sources(step):
+    return sorted(step, key=step.get)
+
+
+def targets(step):
+    return [step[i] for i in sorted(step)]
 
 
 def attend(aud_count, vid_count, gather, scatter, here, *refs):
@@ -87,11 +85,7 @@
     me = here[0]
     blocks[me] = mine[...]
     for step, got in zip(gather, gots):
-        source = lookup(sources(step, vid_count), me)
-
-        @pl.when(source >= 0)
-        def _():
-            blocks[source] = got[...]
+        blocks[lookup(sources(step), me)] = got[...]
 
     width = auds[0].shape[1] // 2
     heads = width // HEAD_DIM
@@ -135,7 +129,7 @@
         rows = slice(i * vid_rows, (i + 1) * vid_rows)
         put_cols(states.at[i], col_mix[rows], logs[rows])
     for step, out in zip(scatter, col_outs):
-        out[...] = states[jnp.maximum(lookup(targets(step, vid_count), me), 0)]
+        out[...] = states[lookup(targets(step), me)]
     col_outs[-1][...] = states[me]
 
 
@@ -201,12 +195,12 @@
     project(mix.T.astype(BF16), proj, me[0], outs)
 
 
-def project_video(vid_count, scatter, me, here, proj, gots, mine, aud_core, outs):
+def project_video(scatter, me, here, proj, gots, mine, aud_core, outs):
     states = [get_cols(mine, proj.shape[0])]
     for step, got in zip(scatter, gots):
         mix, log = get_cols(got, proj.shape[0])
-        sent = lookup(sources(step, vid_count), here[0]) >= 0
-        states.append((mix, log + jnp.where(sent, 0.0, NEVER)))
+        own = lookup(sources(step), here[0]) == here[0]
+        states.append((mix, log + jnp.where(own, NEVER, 0.0)))
     mix = merge(states)
     aud_rows = aud_core.shape[0]
     outs[1][:aud_rows, :] = aud_core[...]
@@ -270,8 +264,7 @@
     pairs = []
     for i in range(lax.axis_size(axis)):
         here = i // stride % count
-        if here in step:
-            pairs.append((i, i + (step[here] - here) * stride))
+        pairs.append((i, i + (step[here] - here) * stride))
     return lax.ppermute(block, axis, pairs)
 
 
@@ -330,7 +323,6 @@
     )
     vid_terms = call(
         lambda me, here, proj, *refs: project_video(
-            vid_count,
             scatter,
             me,
             here,

time: 35.2 us -> 30.8 us (0.88)
  the two profiles are of different devices: /device:TPU:0 before, /device:TPU:10 now
where the time goes in v7:
time: 30.8 us; the launch traced here: 30.5 us
  starting transfers between devices  19.3 us (63%)
  waiting for transfers between devices  7.68 us (25%)
  Pallas kernels  2.87 us (9%)
  between operations  0.73 us (2%)
    ppermute x7, starting transfers between devices, move(): return lax.ppermute(block, axis, pairs)  13.3 us
    ppermute x7, starting transfers between devices, swap(): lax.ppermute(block, axis, [(i, i ^ distance) for i in range(lax.axis_size...  5.93 us
    ppermute x7, waiting for transfers between devices, move(): return lax.ppermute(block, axis, pairs)  4.48 us
    ppermute x7, waiting for transfers between devices, swap(): lax.ppermute(block, axis, [(i, i ^ distance) for i in range(lax.axis_size...  3.2 us
    pallas_call x5, Pallas kernels, call(): pl.pallas_call(body, out_shape=out_shape, in_specs=in_specs or [vmem] * l...  2.87 us
  transfers between devices with their start and end apart: 14, of which 5 were waited for; matrix products, arithmetic and copies ran while one was open for 0% of the time, Pallas kernels for 2%

profile of v7, /device:TPU:10, one launch (start us, length us, event | category | flops | bytes accessed | tf_op | source)
XLA Modules:
  0.0 30.5 jit_solution(9575241068584132306)
XLA Ops:
  0.6 0.9 %shard_map.77 = (bf16[128,512]{1,0:T(8,128)(2,1)S(1)}, bf16[24,512]{1,0:T(8,128)(2,1)S(1)}) custom-call(bf16[128,256]{1,0:T(8,128)(2,1)} %aud_ref.1, bf16[128,256]{1,0:T(8,128)(2,1)} %aud_val.1, bf16[24,256]{1,0:T(8,128)(2,1)} %vid_ref.1, bf16[24,256]{1,0:T(8,128)(2,1)} %vid_val.1), custom_call_target="tpu_custom_call" | custom-call | flops 5000000000 | tf_op jit(solution)/shard_map/pallas_call | solution.py:226
  1.5 0.6 %collective-permute-start = (bf16[128,512]{1,0:T(8,128)(2,1)S(1)}, bf16[128,512]{1,0:T(8,128)(2,1)S(1)}, u32[]{:S(2)}, u32[]{:S(2)}) collective-permute-start(bf16[128,512]{1,0:T(8,128)(2,1)S(1)} %get-tuple-element.21.refs_1_), channel_id=1, source_target_pairs={{0,4},{4,0},{8,12},{12,8},{16,20},{20,16},{24,28},{28,24},{1,5},{5... | collective-permute-start | bytes 393224 | tf_op jit(solution)/shard_map/ppermute | solution.py:242
  2.1 2.6 %collective-permute-start.3 = (bf16[24,512]{1,0:T(8,128)(2,1)S(1)}, bf16[24,512]{1,0:T(8,128)(2,1)S(1)}, u32[]{:S(2)}, u32[]{:S(2)}) collective-permute-start(bf16[24,512]{1,0:T(8,128)(2,1)S(1)} %get-tuple-element.22.refs_5_), channel_id=1, source_target_pairs={{0,16},{4,20},{8,24},{12,28},{16,8},{20,12},{24,0},{28,4},{1,17},{... | collective-permute-start | bytes 73736 | tf_op jit(solution)/shard_map/ppermute | solution.py:268
  4.7 1.5 %collective-permute-start.1 = (bf16[24,512]{1,0:T(8,128)(2,1)S(1)}, bf16[24,512]{1,0:T(8,128)(2,1)S(1)}, u32[]{:S(2)}, u32[]{:S(2)}) collective-permute-start(bf16[24,512]{1,0:T(8,128)(2,1)S(1)} %get-tuple-element.22.refs_5_), channel_id=1, source_target_pairs={{0,8},{4,12},{8,0},{12,4},{16,24},{20,28},{24,16},{28,20},{1,9},{5... | collective-permute-start | bytes 73736 | tf_op jit(solution)/shard_map/ppermute | solution.py:268
  6.2 0.1 collective-permute-done.3.refs_4_
  6.3 3.2 %collective-permute-done.2.refs_3_ = bf16[24,512]{1,0:T(8,128)(2,1)S(1)} collective-permute-done((bf16[24,512]{1,0:T(8,128)(2,1)S(1)}, bf16[24,512]{1,0:T(8,128)(2,1)S(1)}, u32[]{:S(2)}, u32[]{:S(2)}) %collective-permute-start.2) | collective-permute-done | bytes 24608 | tf_op jit(solution)/shard_map/ppermute | solution.py:268
  9.5 0.0 collective-permute-done.1.refs_2_
  9.5 0.7 %shard_map.78 = (bf16[272,128]{1,0:T(8,128)(2,1)S(1)}, bf16[272,128]{1,0:T(8,128)(2,1)S(1)}, bf16[24,384]{1,0:T(8,128)(2,1)S(1)}, bf16[24,384]{1,0:T(8,128)(2,1)...) custom-call(s32[1]{0:T(128)} %bitcast.1.here, ...), custom_call_target="tpu_custom_call" | custom-call | flops 5000000000 | tf_op jit(solution)/shard_map/pallas_call | solution.py:226
  10.1 1.6 %collective-permute-start.8 = (bf16[272,128]{1,0:T(8,128)(2,1)S(1)}, bf16[272,128]{1,0:T(8,128)(2,1)S(1)}, u32[]{:S(2)}, u32[]{:S(2)}) collective-permute-start(bf16[272,128]{1,0:T(8,128)(2,1)S(1)} %get-tuple-element.28), channel_id=1, source_target_pairs={{0,4},{4,0},{8,12},{12,8},{16,20},{20,16},{24,28},{28,24},{1,5},{5... | collective-permute-start | bytes 208904 | tf_op jit(solution)/shard_map/ppermute | solution.py:242
  11.7 3.9 %collective-permute-start.4 = (bf16[24,384]{1,0:T(8,128)(2,1)S(1)}, bf16[24,384]{1,0:T(8,128)(2,1)S(1)}, u32[]{:S(2)}, u32[]{:S(2)}) collective-permute-start(bf16[24,384]{1,0:T(8,128)(2,1)S(1)} %get-tuple-element.23), channel_id=1, source_target_pairs={{0,8},{4,12},{8,24},{12,28},{16,16},{20,20},{24,0},{28,4},{1,9},{5... | collective-permute-start | bytes 55304 | tf_op jit(solution)/shard_map/ppermute | solution.py:268
  15.6 0.7 %collective-permute-start.5 = (bf16[24,384]{1,0:T(8,128)(2,1)S(1)}, bf16[24,384]{1,0:T(8,128)(2,1)S(1)}, u32[]{:S(2)}, u32[]{:S(2)}) collective-permute-start(bf16[24,384]{1,0:T(8,128)(2,1)S(1)} %get-tuple-element.24), channel_id=1, source_target_pairs={{0,16},{4,20},{8,8},{12,12},{16,0},{20,4},{24,24},{28,28},{1,17},{... | collective-permute-start | bytes 55304 | tf_op jit(solution)/shard_map/ppermute | solution.py:268
  16.3 1.3 %collective-permute-start.6 = (bf16[24,384]{1,0:T(8,128)(2,1)S(1)}, bf16[24,384]{1,0:T(8,128)(2,1)S(1)}, u32[]{:S(2)}, u32[]{:S(2)}) collective-permute-start(bf16[24,384]{1,0:T(8,128)(2,1)S(1)} %get-tuple-element.25), channel_id=1, source_target_pairs={{0,24},{4,28},{8,0},{12,4},{16,8},{20,12},{24,16},{28,20},{1,25},{... | collective-permute-start | bytes 55304 | tf_op jit(solution)/shard_map/ppermute | solution.py:268
  17.6 3.4 %collective-permute-start.7 = (bf16[24,384]{1,0:T(8,128)(2,1)S(1)}, bf16[24,384]{1,0:T(8,128)(2,1)S(1)}, u32[]{:S(2)}, u32[]{:S(2)}) collective-permute-start(bf16[24,384]{1,0:T(8,128)(2,1)S(1)} %get-tuple-element.26), channel_id=1, source_target_pairs={{0,0},{4,4},{8,16},{12,20},{16,24},{20,28},{24,8},{28,12},{1,1},{5... | collective-permute-start | bytes 55304 | tf_op jit(solution)/shard_map/ppermute | solution.py:268
  21.0 0.0 copy-start.1
  21.0 0.3 shard_map.79
  21.3 1.6 %collective-permute-start.12 = (bf16[160,256]{1,0:T(8,128)(2,1)S(1)}, bf16[160,256]{1,0:T(8,128)(2,1)S(1)}, u32[]{:S(2)}, u32[]{:S(2)}) collective-permute-start(bf16[160,256]{1,0:T(8,128)(2,1)S(1)} %get-tuple-element.36), channel_id=1, source_target_pairs={{0,2},{1,3},{2,0},{3,1},{4,6},{5,7},{6,4},{7,5},{8,10},{9,11},{10,... | collective-permute-start | bytes 245768 | tf_op jit(solution)/shard_map/ppermute | solution.py:242
  22.9 1.2 %collective-permute-done.7.refs_3_ = bf16[24,384]{1,0:T(8,128)(2,1)S(1)} collective-permute-done((bf16[24,384]{1,0:T(8,128)(2,1)S(1)}, bf16[24,384]{1,0:T(8,128)(2,1)S(1)}, u32[]{:S(2)}, u32[]{:S(2)}) %collective-permute-start.7) | collective-permute-done | bytes 18464 | tf_op jit(solution)/shard_map/ppermute | solution.py:268
  24.1 0.3 %shard_map.80 = (f32[24,256]{1,0:T(8,128)S(1)}, bf16[152,256]{1,0:T(8,128)(2,1)S(1)}, bf16[24,256]{1,0:T(8,128)(2,1)S(1)}, bf16[24,256]{1,0:T(8,128)(2,1)S(1)}) custom-call(s32[1]{0:T(128)} %bitcast.me, s32[1]{0:T(128)} %bitcast.1.here, bf16[256,1024]{1,0:T(8,128)(2,1)S(1)} %copy-done.1, bf16[24,384]{1,0:T(8,128)(2,1)S(1)} %collective-permute-done.4.refs_0_, ...), custom_call_target="tpu_custom_call" | custom-call | flops 5000000000 | tf_op jit(solution)/shard_map/pallas_call | solution.py:226
  24.5 0.0 collective-permute-start.11
  24.5 1.6 %collective-permute-start.9 = (bf16[24,256]{1,0:T(8,128)(2,1)S(1)}, bf16[24,256]{1,0:T(8,128)(2,1)S(1)}, u32[]{:S(2)}, u32[]{:S(2)}) collective-permute-start(bf16[24,256]{1,0:T(8,128)(2,1)S(1)} %get-tuple-element.32), channel_id=1, source_target_pairs={{0,3},{1,2},{2,1},{3,0},{4,7},{5,6},{6,5},{7,4},{8,11},{9,10},{10,... | collective-permute-start | bytes 36872 | tf_op jit(solution)/shard_map/ppermute | solution.py:242
  26.2 0.5 %collective-permute-start.10 = (bf16[24,256]{1,0:T(8,128)(2,1)S(1)}, bf16[24,256]{1,0:T(8,128)(2,1)S(1)}, u32[]{:S(2)}, u32[]{:S(2)}) collective-permute-start(bf16[24,256]{1,0:T(8,128)(2,1)S(1)} %get-tuple-element.33), channel_id=1, source_target_pairs={{0,2},{1,3},{2,0},{3,1},{4,6},{5,7},{6,4},{7,5},{8,10},{9,11},{10,... | collective-permute-start | bytes 36872 | tf_op jit(solution)/shard_map/ppermute | solution.py:242
  26.7 1.0 %collective-permute-done.9.refs_1_ = bf16[24,256]{1,0:T(8,128)(2,1)S(1)} collective-permute-done((bf16[24,256]{1,0:T(8,128)(2,1)S(1)}, bf16[24,256]{1,0:T(8,128)(2,1)S(1)}, u32[]{:S(2)}, u32[]{:S(2)}) %collective-permute-start.9) | collective-permute-done | bytes 12320 | tf_op jit(solution)/shard_map/ppermute | solution.py:242
  27.7 2.1 %collective-permute-done.10.refs_2_ = bf16[24,256]{1,0:T(8,128)(2,1)S(1)} collective-permute-done((bf16[24,256]{1,0:T(8,128)(2,1)S(1)}, bf16[24,256]{1,0:T(8,128)(2,1)S(1)}, u32[]{:S(2)}, u32[]{:S(2)}) %collective-permute-start.10) | collective-permute-done | bytes 12320 | tf_op jit(solution)/shard_map/ppermute | solution.py:242
  29.9 0.7 %shard_map.81 = (bf16[24,256]{1,0:T(8,128)(2,1)}, bf16[128,256]{1,0:T(8,128)(2,1)}) custom-call(f32[24,256]{1,0:T(8,128)S(1)} %get-tuple-element.31.refs_0_, bf16[24,256]{1,0:T(8,128)(2,1)S(1)} %collective-permute-done.9.refs_1_, bf16[24,256]{1,0:T(8,128)(2,1)S(1)} %collective-permute-done.10.refs_2_, bf16[152,256]{1,0:T(8,128)(2,1)S(1)} %collective-permute-done.11.refs_3_, ...), custom_call_target="tpu_custom_call" | custom-call | flops 5000000000 | tf_op jit(solution)/shard_map/pallas_call | solution.py:226
  (13 shorter events, 0.0 us)
Async XLA Ops:
  1.5 7.9 %collective-permute-start = (bf16[128,512]{1,0:T(8,128)(2,1)S(1)}, bf16[128,512]{1,0:T(8,128)(2,1)S(1)}, u32[]{:S(2)}, u32[]{:S(2)}) collective-permute-start(bf16[128,512]{1,0:T(8,128)(2,1)S(1)} %get-tuple-element.21.refs_1_), channel_id=1, source_target_pairs={{0,4},{4,0},{8,12},{12,8},{16,20},{20,16},{24,28},{28,24},{1,5},{5... | collective-permute-start | bytes 393224 | tf_op jit(solution)/shard_map/ppermute | solution.py:242
  2.1 4.1 %collective-permute-start.3 = (bf16[24,512]{1,0:T(8,128)(2,1)S(1)}, bf16[24,512]{1,0:T(8,128)(2,1)S(1)}, u32[]{:S(2)}, u32[]{:S(2)}) collective-permute-start(bf16[24,512]{1,0:T(8,128)(2,1)S(1)} %get-tuple-element.22.refs_5_), channel_id=1, source_target_pairs={{0,16},{4,20},{8,24},{12,28},{16,8},{20,12},{24,0},{28,4},{1,17},{... | collective-permute-start | bytes 73736 | tf_op jit(solution)/shard_map/ppermute | solution.py:268
  4.7 4.7 %collective-permute-start.2 = (bf16[24,512]{1,0:T(8,128)(2,1)S(1)}, bf16[24,512]{1,0:T(8,128)(2,1)S(1)}, u32[]{:S(2)}, u32[]{:S(2)}) collective-permute-start(bf16[24,512]{1,0:T(8,128)(2,1)S(1)} %get-tuple-element.22.refs_5_), channel_id=1, source_target_pairs={{0,24},{4,28},{8,16},{12,20},{16,0},{20,4},{24,8},{28,12},{1,25},{... | collective-permute-start | bytes 73736 | tf_op jit(solution)/shard_map/ppermute | solution.py:268
  4.7 4.7 %collective-permute-start.1 = (bf16[24,512]{1,0:T(8,128)(2,1)S(1)}, bf16[24,512]{1,0:T(8,128)(2,1)S(1)}, u32[]{:S(2)}, u32[]{:S(2)}) collective-permute-start(bf16[24,512]{1,0:T(8,128)(2,1)S(1)} %get-tuple-element.22.refs_5_), channel_id=1, source_target_pairs={{0,8},{4,12},{8,0},{12,4},{16,24},{20,28},{24,16},{28,20},{1,9},{5... | collective-permute-start | bytes 73736 | tf_op jit(solution)/shard_map/ppermute | solution.py:268
  9.5 11.5 %copy-start = (bf16[256,1024]{1,0:T(8,128)(2,1)S(1)}, bf16[256,1024]{1,0:T(8,128)(2,1)}, u32[]{:S(2)}) copy-start(bf16[256,1024]{1,0:T(8,128)(2,1)} %proj.2) | copy-start | bytes 1572868
  10.1 10.9 %collective-permute-start.8 = (bf16[272,128]{1,0:T(8,128)(2,1)S(1)}, bf16[272,128]{1,0:T(8,128)(2,1)S(1)}, u32[]{:S(2)}, u32[]{:S(2)}) collective-permute-start(bf16[272,128]{1,0:T(8,128)(2,1)S(1)} %get-tuple-element.28), channel_id=1, source_target_pairs={{0,4},{4,0},{8,12},{12,8},{16,20},{20,16},{24,28},{28,24},{1,5},{5... | collective-permute-start | bytes 208904 | tf_op jit(solution)/shard_map/ppermute | solution.py:242
  11.7 11.2 %collective-permute-start.4 = (bf16[24,384]{1,0:T(8,128)(2,1)S(1)}, bf16[24,384]{1,0:T(8,128)(2,1)S(1)}, u32[]{:S(2)}, u32[]{:S(2)}) collective-permute-start(bf16[24,384]{1,0:T(8,128)(2,1)S(1)} %get-tuple-element.23), channel_id=1, source_target_pairs={{0,8},{4,12},{8,24},{12,28},{16,16},{20,20},{24,0},{28,4},{1,9},{5... | collective-permute-start | bytes 55304 | tf_op jit(solution)/shard_map/ppermute | solution.py:268
  15.6 7.3 %collective-permute-start.5 = (bf16[24,384]{1,0:T(8,128)(2,1)S(1)}, bf16[24,384]{1,0:T(8,128)(2,1)S(1)}, u32[]{:S(2)}, u32[]{:S(2)}) collective-permute-start(bf16[24,384]{1,0:T(8,128)(2,1)S(1)} %get-tuple-element.24), channel_id=1, source_target_pairs={{0,16},{4,20},{8,8},{12,12},{16,0},{20,4},{24,24},{28,28},{1,17},{... | collective-permute-start | bytes 55304 | tf_op jit(solution)/shard_map/ppermute | solution.py:268
  16.3 6.6 %collective-permute-start.6 = (bf16[24,384]{1,0:T(8,128)(2,1)S(1)}, bf16[24,384]{1,0:T(8,128)(2,1)S(1)}, u32[]{:S(2)}, u32[]{:S(2)}) collective-permute-start(bf16[24,384]{1,0:T(8,128)(2,1)S(1)} %get-tuple-element.25), channel_id=1, source_target_pairs={{0,24},{4,28},{8,0},{12,4},{16,8},{20,12},{24,16},{28,20},{1,25},{... | collective-permute-start | bytes 55304 | tf_op jit(solution)/shard_map/ppermute | solution.py:268
  17.6 6.5 %collective-permute-start.7 = (bf16[24,384]{1,0:T(8,128)(2,1)S(1)}, bf16[24,384]{1,0:T(8,128)(2,1)S(1)}, u32[]{:S(2)}, u32[]{:S(2)}) collective-permute-start(bf16[24,384]{1,0:T(8,128)(2,1)S(1)} %get-tuple-element.26), channel_id=1, source_target_pairs={{0,0},{4,4},{8,16},{12,20},{16,24},{20,28},{24,8},{28,12},{1,1},{5... | collective-permute-start | bytes 55304 | tf_op jit(solution)/shard_map/ppermute | solution.py:268
  21.0 3.1 %copy-start.1 = (bf16[256,1024]{1,0:T(8,128)(2,1)S(1)}, bf16[256,1024]{1,0:T(8,128)(2,1)}, u32[]{:S(2)}) copy-start(bf16[256,1024]{1,0:T(8,128)(2,1)} %proj.3) | copy-start | bytes 1572868
  21.3 8.5 %collective-permute-start.12 = (bf16[160,256]{1,0:T(8,128)(2,1)S(1)}, bf16[160,256]{1,0:T(8,128)(2,1)S(1)}, u32[]{:S(2)}, u32[]{:S(2)}) collective-permute-start(bf16[160,256]{1,0:T(8,128)(2,1)S(1)} %get-tuple-element.36), channel_id=1, source_target_pairs={{0,2},{1,3},{2,0},{3,1},{4,6},{5,7},{6,4},{7,5},{8,10},{9,11},{10,... | collective-permute-start | bytes 245768 | tf_op jit(solution)/shard_map/ppermute | solution.py:242
  22.9 7.0 %collective-permute-start.13 = (bf16[160,256]{1,0:T(8,128)(2,1)S(1)}, bf16[160,256]{1,0:T(8,128)(2,1)S(1)}, u32[]{:S(2)}, u32[]{:S(2)}) collective-permute-start(bf16[160,256]{1,0:T(8,128)(2,1)S(1)} %get-tuple-element.37), channel_id=1, source_target_pairs={{0,3},{1,2},{2,1},{3,0},{4,7},{5,6},{6,5},{7,4},{8,11},{9,10},{10,... | collective-permute-start | bytes 245768 | tf_op jit(solution)/shard_map/ppermute | solution.py:242
  24.5 5.4 %collective-permute-start.11 = (bf16[152,256]{1,0:T(8,128)(2,1)S(1)}, bf16[152,256]{1,0:T(8,128)(2,1)S(1)}, u32[]{:S(2)}, u32[]{:S(2)}) collective-permute-start(bf16[152,256]{1,0:T(8,128)(2,1)S(1)} %get-tuple-element.34), channel_id=1, source_target_pairs={{0,1},{1,0},{2,3},{3,2},{4,5},{5,4},{6,7},{7,6},{8,9},{9,8},{10,11... | collective-permute-start | bytes 233480 | tf_op jit(solution)/shard_map/ppermute | solution.py:242
  24.5 3.2 %collective-permute-start.9 = (bf16[24,256]{1,0:T(8,128)(2,1)S(1)}, bf16[24,256]{1,0:T(8,128)(2,1)S(1)}, u32[]{:S(2)}, u32[]{:S(2)}) collective-permute-start(bf16[24,256]{1,0:T(8,128)(2,1)S(1)} %get-tuple-element.32), channel_id=1, source_target_pairs={{0,3},{1,2},{2,1},{3,0},{4,7},{5,6},{6,5},{7,4},{8,11},{9,10},{10,... | collective-permute-start | bytes 36872 | tf_op jit(solution)/shard_map/ppermute | solution.py:242
  26.2 3.7 %collective-permute-start.10 = (bf16[24,256]{1,0:T(8,128)(2,1)S(1)}, bf16[24,256]{1,0:T(8,128)(2,1)S(1)}, u32[]{:S(2)}, u32[]{:S(2)}) collective-permute-start(bf16[24,256]{1,0:T(8,128)(2,1)S(1)} %get-tuple-element.33), channel_id=1, source_target_pairs={{0,2},{1,3},{2,0},{3,1},{4,6},{5,7},{6,4},{7,5},{8,10},{9,11},{10,... | collective-permute-start | bytes 36872 | tf_op jit(solution)/shard_map/ppermute | solution.py:242

commit v8 on v5

--- a/solution.py
+++ b/solution.py
@@ -168,10 +168,10 @@
     terms, vid_out, aud_out = refs[:-2], refs[-2], refs[-1]
     count = len(terms) // 2 + 1
     aud_rows = aud_out.shape[0]
-    core = terms[1][...].astype(F32)
+    core = terms[count - 1][...].astype(F32)
     vid = terms[0][...] + core[aud_rows:]
     aud = terms[count][...] + core[:aud_rows]
-    for vid_term, aud_term in zip(terms[2:count], terms[count + 1 :]):
+    for vid_term, aud_term in zip(terms[1 : count - 1], terms[count + 1 :]):
         vid += vid_term[...].astype(F32)
         aud += aud_term[:aud_rows].astype(F32)
     vid_out[...] = vid.astype(BF16)
@@ -264,8 +264,12 @@
         [me, video_proj, *cols, aud_terms[1]],
         in_specs=[smem] + [vmem] * (vid_count + 2),
     )
-    vid_got = [vid_terms[0]] + [swap(vid_terms[k], "head", k) for k in range(1, peers)]
-    aud_got = [aud_terms[0]] + [swap(aud_terms[k], "head", k) for k in range(2, peers)]
+    vid_got = [vid_terms[0]] + [
+        swap(vid_terms[k], "head", k) for k in reversed(range(1, peers))
+    ]
+    aud_got = [aud_terms[0]] + [
+        swap(aud_terms[k], "head", k) for k in reversed(range(2, peers))
+    ]
     vid_out, aud_out = call(
         add, [shape(vid_rows, step), shape(aud_rows, step)], vid_got + aud_got
     )

time: 27 us -> 27 us (level)
  no operation moved by 1% of the time
where the time goes in v8:
time: 27 us; the launch traced here: 26.8 us
  starting transfers between devices  16.2 us (60%)
  waiting for transfers between devices  7.08 us (26%)
  Pallas kernels  2.84 us (11%)
  between operations  0.69 us (3%)
    ppermute x13, starting transfers between devices, swap(): lax.ppermute(block, axis, [(i, i ^ distance) for i in range(lax.axis_size...  16.2 us
    ppermute x13, waiting for transfers between devices, swap(): lax.ppermute(block, axis, [(i, i ^ distance) for i in range(lax.axis_size...  7.08 us
    pallas_call x5, Pallas kernels, call(): pl.pallas_call(body, out_shape=out_shape, in_specs=in_specs or [vmem] * l...  2.84 us
  transfers between devices with their start and end apart: 13, of which 4 were waited for; matrix products, arithmetic and copies ran while one was open for 0% of the time, Pallas kernels for 2%

profile of v8, /device:TPU:0, one launch (start us, length us, event | category | flops | bytes accessed | tf_op | source)
XLA Modules:
  0.0 26.8 jit_solution(5262184780812671854)
XLA Ops:
  0.6 0.9 %shard_map.77 = (bf16[128,512]{1,0:T(8,128)(2,1)S(1)}, bf16[24,512]{1,0:T(8,128)(2,1)S(1)}) custom-call(bf16[128,256]{1,0:T(8,128)(2,1)} %aud_ref.1, bf16[128,256]{1,0:T(8,128)(2,1)} %aud_val.1, bf16[24,256]{1,0:T(8,128)(2,1)} %vid_ref.1, bf16[24,256]{1,0:T(8,128)(2,1)} %vid_val.1), custom_call_target="tpu_custom_call" | custom-call | flops 5000000000 | tf_op jit(solution)/shard_map/pallas_call | solution.py:183
  1.5 3.0 %collective-permute-start = (bf16[128,512]{1,0:T(8,128)(2,1)S(1)}, bf16[128,512]{1,0:T(8,128)(2,1)S(1)}, u32[]{:S(2)}, u32[]{:S(2)}) collective-permute-start(bf16[128,512]{1,0:T(8,128)(2,1)S(1)} %get-tuple-element.20.refs_1_), channel_id=1, source_target_pairs={{0,4},{4,0},{8,12},{12,8},{16,20},{20,16},{24,28},{28,24},{1,5},{5... | collective-permute-start | bytes 393224 | tf_op jit(solution)/shard_map/ppermute | solution.py:199
  4.6 3.6 %collective-permute-start.3 = (bf16[24,512]{1,0:T(8,128)(2,1)S(1)}, bf16[24,512]{1,0:T(8,128)(2,1)S(1)}, u32[]{:S(2)}, u32[]{:S(2)}) collective-permute-start(bf16[24,512]{1,0:T(8,128)(2,1)S(1)} %get-tuple-element.21.refs_5_), channel_id=1, source_target_pairs={{0,24},{4,28},{8,16},{12,20},{16,8},{20,12},{24,0},{28,4},{1,25},{... | collective-permute-start | bytes 73736 | tf_op jit(solution)/shard_map/ppermute | solution.py:199
  8.2 0.8 %collective-permute-start.1 = (bf16[24,512]{1,0:T(8,128)(2,1)S(1)}, bf16[24,512]{1,0:T(8,128)(2,1)S(1)}, u32[]{:S(2)}, u32[]{:S(2)}) collective-permute-start(bf16[24,512]{1,0:T(8,128)(2,1)S(1)} %get-tuple-element.21.refs_5_), channel_id=1, source_target_pairs={{0,8},{4,12},{8,0},{12,4},{16,24},{20,28},{24,16},{28,20},{1,9},{5... | collective-permute-start | bytes 73736 | tf_op jit(solution)/shard_map/ppermute | solution.py:199
  8.9 1.5 %collective-permute-done.3.refs_4_ = bf16[24,512]{1,0:T(8,128)(2,1)S(1)} collective-permute-done((bf16[24,512]{1,0:T(8,128)(2,1)S(1)}, bf16[24,512]{1,0:T(8,128)(2,1)S(1)}, u32[]{:S(2)}, u32[]{:S(2)}) %collective-permute-start.3) | collective-permute-done | bytes 24608 | tf_op jit(solution)/shard_map/ppermute | solution.py:199
  10.4 2.4 %collective-permute-done.2.refs_3_ = bf16[24,512]{1,0:T(8,128)(2,1)S(1)} collective-permute-done((bf16[24,512]{1,0:T(8,128)(2,1)S(1)}, bf16[24,512]{1,0:T(8,128)(2,1)S(1)}, u32[]{:S(2)}, u32[]{:S(2)}) %collective-permute-start.2) | collective-permute-done | bytes 24608 | tf_op jit(solution)/shard_map/ppermute | solution.py:199
  12.9 0.0 collective-permute-done.1.refs_2_
  12.9 0.0 collective-permute-done.refs_0_
  12.9 0.6 %shard_map.78 = (bf16[272,128]{1,0:T(8,128)(2,1)S(1)}, bf16[272,128]{1,0:T(8,128)(2,1)S(1)}, bf16[24,384]{1,0:T(8,128)(2,1)S(1)}, bf16[24,384]{1,0:T(8,128)(2,1)...) custom-call(bf16[128,512]{1,0:T(8,128)(2,1)S(1)} %collective-permute-done.refs_0_, ...), custom_call_target="tpu_custom_call" | custom-call | flops 5000000000 | tf_op jit(solution)/shard_map/pallas_call | solution.py:183
  13.5 0.6 %collective-permute-start.7 = (bf16[272,128]{1,0:T(8,128)(2,1)S(1)}, bf16[272,128]{1,0:T(8,128)(2,1)S(1)}, u32[]{:S(2)}, u32[]{:S(2)}) collective-permute-start(bf16[272,128]{1,0:T(8,128)(2,1)S(1)} %get-tuple-element.26), channel_id=1, source_target_pairs={{0,4},{4,0},{8,12},{12,8},{16,20},{20,16},{24,28},{28,24},{1,5},{5... | collective-permute-start | bytes 208904 | tf_op jit(solution)/shard_map/ppermute | solution.py:199
  14.1 1.5 %collective-permute-start.4 = (bf16[24,384]{1,0:T(8,128)(2,1)S(1)}, bf16[24,384]{1,0:T(8,128)(2,1)S(1)}, u32[]{:S(2)}, u32[]{:S(2)}) collective-permute-start(bf16[24,384]{1,0:T(8,128)(2,1)S(1)} %get-tuple-element.22), channel_id=1, source_target_pairs={{0,24},{4,28},{8,16},{12,20},{16,8},{20,12},{24,0},{28,4},{1,25},{... | collective-permute-start | bytes 55304 | tf_op jit(solution)/shard_map/ppermute | solution.py:199
  15.6 0.6 %collective-permute-start.5 = (bf16[24,384]{1,0:T(8,128)(2,1)S(1)}, bf16[24,384]{1,0:T(8,128)(2,1)S(1)}, u32[]{:S(2)}, u32[]{:S(2)}) collective-permute-start(bf16[24,384]{1,0:T(8,128)(2,1)S(1)} %get-tuple-element.23), channel_id=1, source_target_pairs={{0,16},{4,20},{8,24},{12,28},{16,0},{20,4},{24,8},{28,12},{1,17},{... | collective-permute-start | bytes 55304 | tf_op jit(solution)/shard_map/ppermute | solution.py:199
  16.2 2.4 %collective-permute-start.6 = (bf16[24,384]{1,0:T(8,128)(2,1)S(1)}, bf16[24,384]{1,0:T(8,128)(2,1)S(1)}, u32[]{:S(2)}, u32[]{:S(2)}) collective-permute-start(bf16[24,384]{1,0:T(8,128)(2,1)S(1)} %get-tuple-element.24), channel_id=1, source_target_pairs={{0,8},{4,12},{8,0},{12,4},{16,24},{20,28},{24,16},{28,20},{1,9},{5... | collective-permute-start | bytes 55304 | tf_op jit(solution)/shard_map/ppermute | solution.py:199
  18.5 0.0 collective-permute-done.7.refs_0_
  18.5 0.3 %shard_map.79 = (f32[128,256]{1,0:T(8,128)S(1)}, bf16[128,256]{1,0:T(8,128)(2,1)S(1)}, bf16[160,256]{1,0:T(8,128)(2,1)S(1)}, bf16[160,256]{1,0:T(8,128)(2,1)S(1)}) custom-call(s32[1]{0:T(128)} %bitcast.me, bf16[256,1024]{1,0:T(8,128)(2,1)S(1)} %copy-done, bf16[272,128]{1,0:T(8,128)(2,1)S(1)} %collective-permute-done.7.refs_0_, ...), custom_call_target="tpu_custom_call" | custom-call | flops 5000000000 | tf_op jit(solution)/shard_map/pallas_call | solution.py:183
  18.8 0.1 collective-permute-start.11
  18.9 1.6 %collective-permute-start.12 = (bf16[160,256]{1,0:T(8,128)(2,1)S(1)}, bf16[160,256]{1,0:T(8,128)(2,1)S(1)}, u32[]{:S(2)}, u32[]{:S(2)}) collective-permute-start(bf16[160,256]{1,0:T(8,128)(2,1)S(1)} %get-tuple-element.35), channel_id=1, source_target_pairs={{0,2},{1,3},{2,0},{3,1},{4,6},{5,7},{6,4},{7,5},{8,10},{9,11},{10,... | collective-permute-start | bytes 245768 | tf_op jit(solution)/shard_map/ppermute | solution.py:199
  20.5 0.3 %shard_map.80 = (f32[24,256]{1,0:T(8,128)S(1)}, bf16[152,256]{1,0:T(8,128)(2,1)S(1)}, bf16[24,256]{1,0:T(8,128)(2,1)S(1)}, bf16[24,256]{1,0:T(8,128)(2,1)S(1)}) custom-call(s32[1]{0:T(128)} %bitcast.me, bf16[256,1024]{1,0:T(8,128)(2,1)S(1)} %copy-done.1, bf16[24,384]{1,0:T(8,128)(2,1)S(1)} %collective-permute-done.4.refs_0_, ...), custom_call_target="tpu_custom_call" | custom-call | flops 5000000000 | tf_op jit(solution)/shard_map/pallas_call | solution.py:183
  20.8 0.3 %collective-permute-start.10 = (bf16[152,256]{1,0:T(8,128)(2,1)S(1)}, bf16[152,256]{1,0:T(8,128)(2,1)S(1)}, u32[]{:S(2)}, u32[]{:S(2)}) collective-permute-start(bf16[152,256]{1,0:T(8,128)(2,1)S(1)} %get-tuple-element.32), channel_id=1, source_target_pairs={{0,1},{1,0},{2,3},{3,2},{4,5},{5,4},{6,7},{7,6},{8,9},{9,8},{10,11... | collective-permute-start | bytes 233480 | tf_op jit(solution)/shard_map/ppermute | solution.py:199
  21.1 1.3 %collective-permute-start.8 = (bf16[24,256]{1,0:T(8,128)(2,1)S(1)}, bf16[24,256]{1,0:T(8,128)(2,1)S(1)}, u32[]{:S(2)}, u32[]{:S(2)}) collective-permute-start(bf16[24,256]{1,0:T(8,128)(2,1)S(1)} %get-tuple-element.30), channel_id=1, source_target_pairs={{0,3},{1,2},{2,1},{3,0},{4,7},{5,6},{6,5},{7,4},{8,11},{9,10},{10,... | collective-permute-start | bytes 36872 | tf_op jit(solution)/shard_map/ppermute | solution.py:199
  22.4 0.6 %collective-permute-start.9 = (bf16[24,256]{1,0:T(8,128)(2,1)S(1)}, bf16[24,256]{1,0:T(8,128)(2,1)S(1)}, u32[]{:S(2)}, u32[]{:S(2)}) collective-permute-start(bf16[24,256]{1,0:T(8,128)(2,1)S(1)} %get-tuple-element.31), channel_id=1, source_target_pairs={{0,2},{1,3},{2,0},{3,1},{4,6},{5,7},{6,4},{7,5},{8,10},{9,11},{10,... | collective-permute-start | bytes 36872 | tf_op jit(solution)/shard_map/ppermute | solution.py:199
  23.0 2.6 %collective-permute-done.8.refs_1_ = bf16[24,256]{1,0:T(8,128)(2,1)S(1)} collective-permute-done((bf16[24,256]{1,0:T(8,128)(2,1)S(1)}, bf16[24,256]{1,0:T(8,128)(2,1)S(1)}, u32[]{:S(2)}, u32[]{:S(2)}) %collective-permute-start.8) | collective-permute-done | bytes 12320 | tf_op jit(solution)/shard_map/ppermute | solution.py:199
  25.6 0.6 %collective-permute-done.9.refs_2_ = bf16[24,256]{1,0:T(8,128)(2,1)S(1)} collective-permute-done((bf16[24,256]{1,0:T(8,128)(2,1)S(1)}, bf16[24,256]{1,0:T(8,128)(2,1)S(1)}, u32[]{:S(2)}, u32[]{:S(2)}) %collective-permute-start.9) | collective-permute-done | bytes 12320 | tf_op jit(solution)/shard_map/ppermute | solution.py:199
  26.2 0.7 %shard_map.81 = (bf16[24,256]{1,0:T(8,128)(2,1)}, bf16[128,256]{1,0:T(8,128)(2,1)}) custom-call(f32[24,256]{1,0:T(8,128)S(1)} %get-tuple-element.29.refs_0_, bf16[24,256]{1,0:T(8,128)(2,1)S(1)} %collective-permute-done.8.refs_1_, bf16[24,256]{1,0:T(8,128)(2,1)S(1)} %collective-permute-done.9.refs_2_, bf16[152,256]{1,0:T(8,128)(2,1)S(1)} %collective-permute-done.10.refs_3_, ...), custom_call_target="tpu_custom_call" | custom-call | flops 5000000000 | tf_op jit(solution)/shard_map/pallas_call | solution.py:183
  (11 shorter events, 0.0 us)
Async XLA Ops:
  1.5 11.3 %collective-permute-start = (bf16[128,512]{1,0:T(8,128)(2,1)S(1)}, bf16[128,512]{1,0:T(8,128)(2,1)S(1)}, u32[]{:S(2)}, u32[]{:S(2)}) collective-permute-start(bf16[128,512]{1,0:T(8,128)(2,1)S(1)} %get-tuple-element.20.refs_1_), channel_id=1, source_target_pairs={{0,4},{4,0},{8,12},{12,8},{16,20},{20,16},{24,28},{28,24},{1,5},{5... | collective-permute-start | bytes 393224 | tf_op jit(solution)/shard_map/ppermute | solution.py:199
  4.6 14.0 %copy-start = (bf16[256,1024]{1,0:T(8,128)(2,1)S(1)}, bf16[256,1024]{1,0:T(8,128)(2,1)}, u32[]{:S(2)}) copy-start(bf16[256,1024]{1,0:T(8,128)(2,1)} %proj.2) | copy-start | bytes 1572868
  4.6 5.9 %collective-permute-start.3 = (bf16[24,512]{1,0:T(8,128)(2,1)S(1)}, bf16[24,512]{1,0:T(8,128)(2,1)S(1)}, u32[]{:S(2)}, u32[]{:S(2)}) collective-permute-start(bf16[24,512]{1,0:T(8,128)(2,1)S(1)} %get-tuple-element.21.refs_5_), channel_id=1, source_target_pairs={{0,24},{4,28},{8,16},{12,20},{16,8},{20,12},{24,0},{28,4},{1,25},{... | collective-permute-start | bytes 73736 | tf_op jit(solution)/shard_map/ppermute | solution.py:199
  8.2 4.7 %collective-permute-start.2 = (bf16[24,512]{1,0:T(8,128)(2,1)S(1)}, bf16[24,512]{1,0:T(8,128)(2,1)S(1)}, u32[]{:S(2)}, u32[]{:S(2)}) collective-permute-start(bf16[24,512]{1,0:T(8,128)(2,1)S(1)} %get-tuple-element.21.refs_5_), channel_id=1, source_target_pairs={{0,16},{4,20},{8,24},{12,28},{16,0},{20,4},{24,8},{28,12},{1,17},{... | collective-permute-start | bytes 73736 | tf_op jit(solution)/shard_map/ppermute | solution.py:199
  8.2 4.7 %collective-permute-start.1 = (bf16[24,512]{1,0:T(8,128)(2,1)S(1)}, bf16[24,512]{1,0:T(8,128)(2,1)S(1)}, u32[]{:S(2)}, u32[]{:S(2)}) collective-permute-start(bf16[24,512]{1,0:T(8,128)(2,1)S(1)} %get-tuple-element.21.refs_5_), channel_id=1, source_target_pairs={{0,8},{4,12},{8,0},{12,4},{16,24},{20,28},{24,16},{28,20},{1,9},{5... | collective-permute-start | bytes 73736 | tf_op jit(solution)/shard_map/ppermute | solution.py:199
  13.5 5.0 %collective-permute-start.7 = (bf16[272,128]{1,0:T(8,128)(2,1)S(1)}, bf16[272,128]{1,0:T(8,128)(2,1)S(1)}, u32[]{:S(2)}, u32[]{:S(2)}) collective-permute-start(bf16[272,128]{1,0:T(8,128)(2,1)S(1)} %get-tuple-element.26), channel_id=1, source_target_pairs={{0,4},{4,0},{8,12},{12,8},{16,20},{20,16},{24,28},{28,24},{1,5},{5... | collective-permute-start | bytes 208904 | tf_op jit(solution)/shard_map/ppermute | solution.py:199
  14.1 6.4 %collective-permute-start.4 = (bf16[24,384]{1,0:T(8,128)(2,1)S(1)}, bf16[24,384]{1,0:T(8,128)(2,1)S(1)}, u32[]{:S(2)}, u32[]{:S(2)}) collective-permute-start(bf16[24,384]{1,0:T(8,128)(2,1)S(1)} %get-tuple-element.22), channel_id=1, source_target_pairs={{0,24},{4,28},{8,16},{12,20},{16,8},{20,12},{24,0},{28,4},{1,25},{... | collective-permute-start | bytes 55304 | tf_op jit(solution)/shard_map/ppermute | solution.py:199
  15.6 4.9 %collective-permute-start.5 = (bf16[24,384]{1,0:T(8,128)(2,1)S(1)}, bf16[24,384]{1,0:T(8,128)(2,1)S(1)}, u32[]{:S(2)}, u32[]{:S(2)}) collective-permute-start(bf16[24,384]{1,0:T(8,128)(2,1)S(1)} %get-tuple-element.23), channel_id=1, source_target_pairs={{0,16},{4,20},{8,24},{12,28},{16,0},{20,4},{24,8},{28,12},{1,17},{... | collective-permute-start | bytes 55304 | tf_op jit(solution)/shard_map/ppermute | solution.py:199
  16.2 4.3 %collective-permute-start.6 = (bf16[24,384]{1,0:T(8,128)(2,1)S(1)}, bf16[24,384]{1,0:T(8,128)(2,1)S(1)}, u32[]{:S(2)}, u32[]{:S(2)}) collective-permute-start(bf16[24,384]{1,0:T(8,128)(2,1)S(1)} %get-tuple-element.24), channel_id=1, source_target_pairs={{0,8},{4,12},{8,0},{12,4},{16,24},{20,28},{24,16},{28,20},{1,9},{5... | collective-permute-start | bytes 55304 | tf_op jit(solution)/shard_map/ppermute | solution.py:199
  18.5 2.0 %copy-start.1 = (bf16[256,1024]{1,0:T(8,128)(2,1)S(1)}, bf16[256,1024]{1,0:T(8,128)(2,1)}, u32[]{:S(2)}) copy-start(bf16[256,1024]{1,0:T(8,128)(2,1)} %proj.3) | copy-start | bytes 1572868
  18.8 7.3 %collective-permute-start.11 = (bf16[160,256]{1,0:T(8,128)(2,1)S(1)}, bf16[160,256]{1,0:T(8,128)(2,1)S(1)}, u32[]{:S(2)}, u32[]{:S(2)}) collective-permute-start(bf16[160,256]{1,0:T(8,128)(2,1)S(1)} %get-tuple-element.34), channel_id=1, source_target_pairs={{0,3},{1,2},{2,1},{3,0},{4,7},{5,6},{6,5},{7,4},{8,11},{9,10},{10,... | collective-permute-start | bytes 245768 | tf_op jit(solution)/shard_map/ppermute | solution.py:199
  18.9 7.2 %collective-permute-start.12 = (bf16[160,256]{1,0:T(8,128)(2,1)S(1)}, bf16[160,256]{1,0:T(8,128)(2,1)S(1)}, u32[]{:S(2)}, u32[]{:S(2)}) collective-permute-start(bf16[160,256]{1,0:T(8,128)(2,1)S(1)} %get-tuple-element.35), channel_id=1, source_target_pairs={{0,2},{1,3},{2,0},{3,1},{4,6},{5,7},{6,4},{7,5},{8,10},{9,11},{10,... | collective-permute-start | bytes 245768 | tf_op jit(solution)/shard_map/ppermute | solution.py:199
  20.8 5.3 %collective-permute-start.10 = (bf16[152,256]{1,0:T(8,128)(2,1)S(1)}, bf16[152,256]{1,0:T(8,128)(2,1)S(1)}, u32[]{:S(2)}, u32[]{:S(2)}) collective-permute-start(bf16[152,256]{1,0:T(8,128)(2,1)S(1)} %get-tuple-element.32), channel_id=1, source_target_pairs={{0,1},{1,0},{2,3},{3,2},{4,5},{5,4},{6,7},{7,6},{8,9},{9,8},{10,11... | collective-permute-start | bytes 233480 | tf_op jit(solution)/shard_map/ppermute | solution.py:199
  21.1 4.4 %collective-permute-start.8 = (bf16[24,256]{1,0:T(8,128)(2,1)S(1)}, bf16[24,256]{1,0:T(8,128)(2,1)S(1)}, u32[]{:S(2)}, u32[]{:S(2)}) collective-permute-start(bf16[24,256]{1,0:T(8,128)(2,1)S(1)} %get-tuple-element.30), channel_id=1, source_target_pairs={{0,3},{1,2},{2,1},{3,0},{4,7},{5,6},{6,5},{7,4},{8,11},{9,10},{10,... | collective-permute-start | bytes 36872 | tf_op jit(solution)/shard_map/ppermute | solution.py:199
  22.4 3.7 %collective-permute-start.9 = (bf16[24,256]{1,0:T(8,128)(2,1)S(1)}, bf16[24,256]{1,0:T(8,128)(2,1)S(1)}, u32[]{:S(2)}, u32[]{:S(2)}) collective-permute-start(bf16[24,256]{1,0:T(8,128)(2,1)S(1)} %get-tuple-element.31), channel_id=1, source_target_pairs={{0,2},{1,3},{2,0},{3,1},{4,6},{5,7},{6,4},{7,5},{8,10},{9,11},{10,... | collective-permute-start | bytes 36872 | tf_op jit(solution)/shard_map/ppermute | solution.py:199

commit v9 on v8

--- a/solution.py
+++ b/solution.py
@@ -1,4 +1,5 @@
 import functools
+import math
 
 import jax
 import jax.numpy as jnp
@@ -10,7 +11,7 @@
 HEAD_DIM = 64
 LANES = 128
 PIECES = 3
-SCALE = HEAD_DIM ** (-0.5)
+SCALE = HEAD_DIM ** (-0.5) * math.log2(math.e)
 VMEM_LIMIT = 48 * 1024 * 1024
 COST = 5 * 10**9
 BF16 = jnp.bfloat16
@@ -36,13 +37,8 @@
 
 
 def pack(aud_ref, aud_val, vid_ref, vid_val, aud, vid, sems):
-    width = aud_ref.shape[1]
-    copies = [
-        pltpu.make_async_copy(source, target.at[:, start : start + width], sems.at[i])
-        for i, (source, target, start) in enumerate(
-            ((aud_ref, aud, 0), (aud_val, aud, width), (vid_ref, vid, 0), (vid_val, vid, width))
-        )
-    ]
+    pairs = ((aud_ref, aud.at[0]), (aud_val, aud.at[1]), (vid_ref, vid.at[0]), (vid_val, vid.at[1]))
+    copies = [pltpu.make_async_copy(a, b, sems.at[i]) for i, (a, b) in enumerate(pairs)]
     for copy in copies:
         copy.start()
     for copy in copies:
@@ -53,34 +49,40 @@
     auds, vids = refs[:aud_count], refs[aud_count : aud_count + vid_count]
     row_outs = refs[aud_count + vid_count : 2 * aud_count + vid_count]
     col_outs = refs[2 * aud_count + vid_count :]
-    width = auds[0].shape[1] // 2
-    heads = width // HEAD_DIM
-    aud = jnp.concatenate([ref[...] for ref in auds], axis=0)
-    vid = jnp.concatenate([ref[...] for ref in vids], axis=0).astype(F32)
-    queries, aud_vals = aud[:, :width], aud[:, width:]
-    total_aud, total_vid = aud.shape[0], vid.shape[0]
+    width = auds[0].shape[2]
+    heads = width // HEAD_DIM
+    queries, aud_vals = (jnp.concatenate([ref[i] for ref in auds], axis=0) for i in range(2))
+    vid_refs, vid_vals = (
+        jnp.concatenate([ref[i].astype(F32) for ref in vids], axis=0) for i in range(2)
+    )
+    total_aud, total_vid = queries.shape[0], vid_refs.shape[0]
     masks = [head_lanes(total_vid, width, h) for h in range(heads)]
-    keys = jnp.concatenate([jnp.where(m, vid[:, :width], 0.0) for m in masks], axis=0)
-    vals = jnp.concatenate([jnp.where(m, vid[:, width:], 0.0) for m in masks], axis=0)
-    scores = dot(keys.astype(BF16), queries, 1, 1).reshape(heads, total_vid, total_aud)
+    lanes = [head_lanes(1, width, h).astype(F32).astype(BF16) for h in range(heads)]
+    keys = vid_refs.astype(BF16)
+    keys = jnp.concatenate([keys * lane for lane in lanes], axis=0)
+    scores = dot(keys, queries, 1, 1).reshape(heads, total_vid, total_aud)
 
     row_top = jnp.max(scores, axis=1, keepdims=True)
-    row_probs = jnp.exp((scores - row_top) * SCALE)
+    row_probs = jnp.exp2((scores - row_top) * SCALE)
     row_total = jnp.sum(row_probs, axis=1, keepdims=True)
-    row_probs = row_probs.reshape(heads * total_vid, total_aud).astype(BF16)
-    row_mix = dot(vals.astype(BF16), row_probs, 0, 0).reshape(heads, HEAD_DIM, total_aud)
-    row_mix = (row_mix / row_total).reshape(width, total_aud)
-    row_log = (row_top * SCALE + jnp.log(row_total)).reshape(heads, total_aud)
+    row_probs = row_probs.astype(BF16)
+    vals = vid_vals.T.astype(BF16)
+    row_mix = [
+        dot(vals[h * HEAD_DIM : (h + 1) * HEAD_DIM], row_probs[h]) * (1.0 / row_total[h])
+        for h in range(heads)
+    ]
+    row_mix = jnp.concatenate(row_mix, axis=0)
+    row_log = (row_top * SCALE + jnp.log2(row_total)).reshape(heads, total_aud)
     for i, out in enumerate(row_outs):
         cols = slice(i * out.shape[1], (i + 1) * out.shape[1])
         put_rows(out, row_mix[:, cols], row_log[:, cols])
 
     col_top = jnp.max(scores, axis=2, keepdims=True)
-    col_probs = jnp.exp((scores - col_top) * SCALE)
+    col_probs = jnp.exp2((scores - col_top) * SCALE)
     col_total = jnp.sum(col_probs, axis=2, keepdims=True)
     col_probs = col_probs.reshape(heads * total_vid, total_aud).astype(BF16)
     every = dot(col_probs, aud_vals).reshape(heads, total_vid, width)
-    col_log = col_top * SCALE + jnp.log(col_total)
+    col_log = col_top * SCALE + jnp.log2(col_total)
     col_mix, divisor = every[0], jnp.broadcast_to(col_total[0], (total_vid, width))
     for h in range(1, heads):
         col_mix = jnp.where(masks[h], every[h], col_mix)
@@ -138,7 +140,7 @@
         top = jnp.maximum(top, log)
     total, mix = 0.0, 0.0
     for part, log in states:
-        weight = jnp.exp(log - top)
+        weight = jnp.exp2(log - top)
         total += weight
         mix += weight * part
     return mix / total
@@ -214,8 +216,8 @@
     step = audio_proj.shape[1] // peers
     log_rows = -(-PIECES * heads // 16) * 16
 
-    def shape(rows, cols, dtype=BF16):
-        return jax.ShapeDtypeStruct((rows, cols), dtype)
+    def shape(*dims, dtype=BF16):
+        return jax.ShapeDtypeStruct(dims, dtype)
 
     def gather(block, stride, count):
         return [swap(block, "seq", k * stride) for k in range(1, count)] + [block]
@@ -226,7 +228,7 @@
 
     aud, vid = call(
         pack,
-        [shape(aud_rows, 2 * width), shape(vid_rows, 2 * width)],
+        [shape(2, aud_rows, width), shape(2, vid_rows, width)],
         [
             pltpu.with_memory_space_constraint(x, pltpu.HBM)
             for x in (ref_audio, val_audio, ref_video, val_video)
@@ -250,7 +252,7 @@
 
     aud_terms = call(
         lambda me, proj, *refs: project_audio(me, proj, refs[:aud_count], refs[aud_count:]),
-        [shape(aud_rows, step, F32), shape(aud_rows, step)]
+        [shape(aud_rows, step, dtype=F32), shape(aud_rows, step)]
         + [shape(aud_rows + vid_rows + 8, step)] * (peers - 2),
         [me, audio_proj, *rows],
         in_specs=[smem, vmem] + [vmem] * aud_count,
@@ -259,7 +261,7 @@
         lambda me, proj, *refs: project_video(
             me, proj, refs[:vid_count], refs[vid_count], refs[vid_count + 1 :]
         ),
-        [shape(vid_rows, step, F32), shape(aud_rows + vid_rows, step)]
+        [shape(vid_rows, step, dtype=F32), shape(aud_rows + vid_rows, step)]
         + [shape(vid_rows, step)] * (peers - 2),
         [me, video_proj, *cols, aud_terms[1]],
         in_specs=[smem] + [vmem] * (vid_count + 2),

time: 27 us -> 27 us (level)
  no operation moved by 1% of the time
where the time goes in v9:
time: 27 us; the launch traced here: 26.8 us
  starting transfers between devices  16.2 us (60%)
  waiting for transfers between devices  7.08 us (26%)
  Pallas kernels  2.83 us (10%)
  between operations  0.69 us (3%)
    ppermute x13, starting transfers between devices, swap(): lax.ppermute(block, axis, [(i, i ^ distance) for i in range(lax.axis_size...  16.2 us
    ppermute x13, waiting for transfers between devices, swap(): lax.ppermute(block, axis, [(i, i ^ distance) for i in range(lax.axis_size...  7.08 us
    pallas_call x5, Pallas kernels, call(): pl.pallas_call(body, out_shape=out_shape, in_specs=in_specs or [vmem] * l...  2.83 us
  transfers between devices with their start and end apart: 13, of which 4 were waited for; matrix products, arithmetic and copies ran while one was open for 0% of the time, Pallas kernels for 2%

profile of v9, /device:TPU:0, one launch (start us, length us, event | category | flops | bytes accessed | tf_op | source)
XLA Modules:
  0.0 26.8 jit_solution(3729224833062161184)
XLA Ops:
  0.6 0.9 %shard_map.77 = (bf16[2,128,256]{2,1,0:T(8,128)(2,1)S(1)}, bf16[2,24,256]{2,1,0:T(8,128)(2,1)S(1)}) custom-call(bf16[128,256]{1,0:T(8,128)(2,1)} %aud_ref.1, bf16[128,256]{1,0:T(8,128)(2,1)} %aud_val.1, bf16[24,256]{1,0:T(8,128)(2,1)} %vid_ref.1, bf16[24,256]{1,0:T(8,128)(2,1)} %vid_val.1), custom_call_target="tpu_custom_call" | custom-call | flops 5000000000 | tf_op jit(solution)/shard_map/pallas_call | solution.py:185
  1.5 3.0 %collective-permute-start = (bf16[2,128,256]{2,1,0:T(8,128)(2,1)S(1)}, bf16[2,128,256]{2,1,0:T(8,128)(2,1)S(1)}, u32[]{:S(2)}, u32[]{:S(2)}) collective-permute-start(bf16[2,128,256]{2,1,0:T(8,128)(2,1)S(1)} %get-tuple-element.20.refs_1_), channel_id=1, source_target_pairs={{0,4},{4,0},{8,12},{12,8},{16,20},{20,16},{24,28},{28,24},{1,5},{5... | collective-permute-start | bytes 393224 | tf_op jit(solution)/shard_map/ppermute | solution.py:201
  4.6 3.6 %collective-permute-start.3 = (bf16[2,24,256]{2,1,0:T(8,128)(2,1)S(1)}, bf16[2,24,256]{2,1,0:T(8,128)(2,1)S(1)}, u32[]{:S(2)}, u32[]{:S(2)}) collective-permute-start(bf16[2,24,256]{2,1,0:T(8,128)(2,1)S(1)} %get-tuple-element.21.refs_5_), channel_id=1, source_target_pairs={{0,24},{4,28},{8,16},{12,20},{16,8},{20,12},{24,0},{28,4},{1,25},{... | collective-permute-start | bytes 73736 | tf_op jit(solution)/shard_map/ppermute | solution.py:201
  8.2 0.0 collective-permute-start.2
  8.2 0.8 %collective-permute-start.1 = (bf16[2,24,256]{2,1,0:T(8,128)(2,1)S(1)}, bf16[2,24,256]{2,1,0:T(8,128)(2,1)S(1)}, u32[]{:S(2)}, u32[]{:S(2)}) collective-permute-start(bf16[2,24,256]{2,1,0:T(8,128)(2,1)S(1)} %get-tuple-element.21.refs_5_), channel_id=1, source_target_pairs={{0,8},{4,12},{8,0},{12,4},{16,24},{20,28},{24,16},{28,20},{1,9},{5... | collective-permute-start | bytes 73736 | tf_op jit(solution)/shard_map/ppermute | solution.py:201
  8.9 1.5 %collective-permute-done.3.refs_4_ = bf16[2,24,256]{2,1,0:T(8,128)(2,1)S(1)} collective-permute-done((bf16[2,24,256]{2,1,0:T(8,128)(2,1)S(1)}, bf16[2,24,256]{2,1,0:T(8,128)(2,1)S(1)}, u32[]{:S(2)}, u32[]{:S(2)}) %collective-permute-start.3) | collective-permute-done | bytes 24608 | tf_op jit(solution)/shard_map/ppermute | solution.py:201
  10.4 2.4 %collective-permute-done.2.refs_3_ = bf16[2,24,256]{2,1,0:T(8,128)(2,1)S(1)} collective-permute-done((bf16[2,24,256]{2,1,0:T(8,128)(2,1)S(1)}, bf16[2,24,256]{2,1,0:T(8,128)(2,1)S(1)}, u32[]{:S(2)}, u32[]{:S(2)}) %collective-permute-start.2) | collective-permute-done | bytes 24608 | tf_op jit(solution)/shard_map/ppermute | solution.py:201
  12.9 0.6 %shard_map.78 = (bf16[272,128]{1,0:T(8,128)(2,1)S(1)}, bf16[272,128]{1,0:T(8,128)(2,1)S(1)}, bf16[24,384]{1,0:T(8,128)(2,1)S(1)}, bf16[24,384]{1,0:T(8,128)(2,1)...) custom-call(bf16[2,128,256]{2,1,0:T(8,128)(2,1)S(1)} %collective-permute-done.refs_0_, ...), custom_call_target="tpu_custom_call" | custom-call | flops 5000000000 | tf_op jit(solution)/shard_map/pallas_call | solution.py:185
  13.5 0.6 %collective-permute-start.7 = (bf16[272,128]{1,0:T(8,128)(2,1)S(1)}, bf16[272,128]{1,0:T(8,128)(2,1)S(1)}, u32[]{:S(2)}, u32[]{:S(2)}) collective-permute-start(bf16[272,128]{1,0:T(8,128)(2,1)S(1)} %get-tuple-element.26), channel_id=1, source_target_pairs={{0,4},{4,0},{8,12},{12,8},{16,20},{20,16},{24,28},{28,24},{1,5},{5... | collective-permute-start | bytes 208904 | tf_op jit(solution)/shard_map/ppermute | solution.py:201
  14.1 1.5 %collective-permute-start.4 = (bf16[24,384]{1,0:T(8,128)(2,1)S(1)}, bf16[24,384]{1,0:T(8,128)(2,1)S(1)}, u32[]{:S(2)}, u32[]{:S(2)}) collective-permute-start(bf16[24,384]{1,0:T(8,128)(2,1)S(1)} %get-tuple-element.22), channel_id=1, source_target_pairs={{0,24},{4,28},{8,16},{12,20},{16,8},{20,12},{24,0},{28,4},{1,25},{... | collective-permute-start | bytes 55304 | tf_op jit(solution)/shard_map/ppermute | solution.py:201
  15.6 0.6 %collective-permute-start.5 = (bf16[24,384]{1,0:T(8,128)(2,1)S(1)}, bf16[24,384]{1,0:T(8,128)(2,1)S(1)}, u32[]{:S(2)}, u32[]{:S(2)}) collective-permute-start(bf16[24,384]{1,0:T(8,128)(2,1)S(1)} %get-tuple-element.23), channel_id=1, source_target_pairs={{0,16},{4,20},{8,24},{12,28},{16,0},{20,4},{24,8},{28,12},{1,17},{... | collective-permute-start | bytes 55304 | tf_op jit(solution)/shard_map/ppermute | solution.py:201
  16.1 2.4 %collective-permute-start.6 = (bf16[24,384]{1,0:T(8,128)(2,1)S(1)}, bf16[24,384]{1,0:T(8,128)(2,1)S(1)}, u32[]{:S(2)}, u32[]{:S(2)}) collective-permute-start(bf16[24,384]{1,0:T(8,128)(2,1)S(1)} %get-tuple-element.24), channel_id=1, source_target_pairs={{0,8},{4,12},{8,0},{12,4},{16,24},{20,28},{24,16},{28,20},{1,9},{5... | collective-permute-start | bytes 55304 | tf_op jit(solution)/shard_map/ppermute | solution.py:201
  18.5 0.3 %shard_map.79 = (f32[128,256]{1,0:T(8,128)S(1)}, bf16[128,256]{1,0:T(8,128)(2,1)S(1)}, bf16[160,256]{1,0:T(8,128)(2,1)S(1)}, bf16[160,256]{1,0:T(8,128)(2,1)S(1)}) custom-call(s32[1]{0:T(128)} %bitcast.me, bf16[256,1024]{1,0:T(8,128)(2,1)S(1)} %copy-done, bf16[272,128]{1,0:T(8,128)(2,1)S(1)} %collective-permute-done.7.refs_0_, ...), custom_call_target="tpu_custom_call" | custom-call | flops 5000000000 | tf_op jit(solution)/shard_map/pallas_call | solution.py:185
  18.8 0.1 collective-permute-start.11
  18.9 1.6 %collective-permute-start.12 = (bf16[160,256]{1,0:T(8,128)(2,1)S(1)}, bf16[160,256]{1,0:T(8,128)(2,1)S(1)}, u32[]{:S(2)}, u32[]{:S(2)}) collective-permute-start(bf16[160,256]{1,0:T(8,128)(2,1)S(1)} %get-tuple-element.35), channel_id=1, source_target_pairs={{0,2},{1,3},{2,0},{3,1},{4,6},{5,7},{6,4},{7,5},{8,10},{9,11},{10,... | collective-permute-start | bytes 245768 | tf_op jit(solution)/shard_map/ppermute | solution.py:201
  20.5 0.0 collective-permute-done.4.refs_0_
  20.5 0.3 %shard_map.80 = (f32[24,256]{1,0:T(8,128)S(1)}, bf16[152,256]{1,0:T(8,128)(2,1)S(1)}, bf16[24,256]{1,0:T(8,128)(2,1)S(1)}, bf16[24,256]{1,0:T(8,128)(2,1)S(1)}) custom-call(s32[1]{0:T(128)} %bitcast.me, bf16[256,1024]{1,0:T(8,128)(2,1)S(1)} %copy-done.1, bf16[24,384]{1,0:T(8,128)(2,1)S(1)} %collective-permute-done.4.refs_0_, ...), custom_call_target="tpu_custom_call" | custom-call | flops 5000000000 | tf_op jit(solution)/shard_map/pallas_call | solution.py:185
  20.8 0.3 %collective-permute-start.10 = (bf16[152,256]{1,0:T(8,128)(2,1)S(1)}, bf16[152,256]{1,0:T(8,128)(2,1)S(1)}, u32[]{:S(2)}, u32[]{:S(2)}) collective-permute-start(bf16[152,256]{1,0:T(8,128)(2,1)S(1)} %get-tuple-element.32), channel_id=1, source_target_pairs={{0,1},{1,0},{2,3},{3,2},{4,5},{5,4},{6,7},{7,6},{8,9},{9,8},{10,11... | collective-permute-start | bytes 233480 | tf_op jit(solution)/shard_map/ppermute | solution.py:201
  21.1 1.3 %collective-permute-start.8 = (bf16[24,256]{1,0:T(8,128)(2,1)S(1)}, bf16[24,256]{1,0:T(8,128)(2,1)S(1)}, u32[]{:S(2)}, u32[]{:S(2)}) collective-permute-start(bf16[24,256]{1,0:T(8,128)(2,1)S(1)} %get-tuple-element.30), channel_id=1, source_target_pairs={{0,3},{1,2},{2,1},{3,0},{4,7},{5,6},{6,5},{7,4},{8,11},{9,10},{10,... | collective-permute-start | bytes 36872 | tf_op jit(solution)/shard_map/ppermute | solution.py:201
  22.4 0.6 %collective-permute-start.9 = (bf16[24,256]{1,0:T(8,128)(2,1)S(1)}, bf16[24,256]{1,0:T(8,128)(2,1)S(1)}, u32[]{:S(2)}, u32[]{:S(2)}) collective-permute-start(bf16[24,256]{1,0:T(8,128)(2,1)S(1)} %get-tuple-element.31), channel_id=1, source_target_pairs={{0,2},{1,3},{2,0},{3,1},{4,6},{5,7},{6,4},{7,5},{8,10},{9,11},{10,... | collective-permute-start | bytes 36872 | tf_op jit(solution)/shard_map/ppermute | solution.py:201
  23.0 2.6 %collective-permute-done.8.refs_1_ = bf16[24,256]{1,0:T(8,128)(2,1)S(1)} collective-permute-done((bf16[24,256]{1,0:T(8,128)(2,1)S(1)}, bf16[24,256]{1,0:T(8,128)(2,1)S(1)}, u32[]{:S(2)}, u32[]{:S(2)}) %collective-permute-start.8) | collective-permute-done | bytes 12320 | tf_op jit(solution)/shard_map/ppermute | solution.py:201
  25.6 0.6 %collective-permute-done.9.refs_2_ = bf16[24,256]{1,0:T(8,128)(2,1)S(1)} collective-permute-done((bf16[24,256]{1,0:T(8,128)(2,1)S(1)}, bf16[24,256]{1,0:T(8,128)(2,1)S(1)}, u32[]{:S(2)}, u32[]{:S(2)}) %collective-permute-start.9) | collective-permute-done | bytes 12320 | tf_op jit(solution)/shard_map/ppermute | solution.py:201
  26.1 0.0 collective-permute-done.12.refs_6_
  26.1 0.7 %shard_map.81 = (bf16[24,256]{1,0:T(8,128)(2,1)}, bf16[128,256]{1,0:T(8,128)(2,1)}) custom-call(f32[24,256]{1,0:T(8,128)S(1)} %get-tuple-element.29.refs_0_, bf16[24,256]{1,0:T(8,128)(2,1)S(1)} %collective-permute-done.8.refs_1_, bf16[24,256]{1,0:T(8,128)(2,1)S(1)} %collective-permute-done.9.refs_2_, bf16[152,256]{1,0:T(8,128)(2,1)S(1)} %collective-permute-done.10.refs_3_, ...), custom_call_target="tpu_custom_call" | custom-call | flops 5000000000 | tf_op jit(solution)/shard_map/pallas_call | solution.py:185
  (11 shorter events, 0.0 us)
Async XLA Ops:
  1.5 11.3 %collective-permute-start = (bf16[2,128,256]{2,1,0:T(8,128)(2,1)S(1)}, bf16[2,128,256]{2,1,0:T(8,128)(2,1)S(1)}, u32[]{:S(2)}, u32[]{:S(2)}) collective-permute-start(bf16[2,128,256]{2,1,0:T(8,128)(2,1)S(1)} %get-tuple-element.20.refs_1_), channel_id=1, source_target_pairs={{0,4},{4,0},{8,12},{12,8},{16,20},{20,16},{24,28},{28,24},{1,5},{5... | collective-permute-start | bytes 393224 | tf_op jit(solution)/shard_map/ppermute | solution.py:201
  4.6 14.0 %copy-start = (bf16[256,1024]{1,0:T(8,128)(2,1)S(1)}, bf16[256,1024]{1,0:T(8,128)(2,1)}, u32[]{:S(2)}) copy-start(bf16[256,1024]{1,0:T(8,128)(2,1)} %proj.2) | copy-start | bytes 1572868
  4.6 5.9 %collective-permute-start.3 = (bf16[2,24,256]{2,1,0:T(8,128)(2,1)S(1)}, bf16[2,24,256]{2,1,0:T(8,128)(2,1)S(1)}, u32[]{:S(2)}, u32[]{:S(2)}) collective-permute-start(bf16[2,24,256]{2,1,0:T(8,128)(2,1)S(1)} %get-tuple-element.21.refs_5_), channel_id=1, source_target_pairs={{0,24},{4,28},{8,16},{12,20},{16,8},{20,12},{24,0},{28,4},{1,25},{... | collective-permute-start | bytes 73736 | tf_op jit(solution)/shard_map/ppermute | solution.py:201
  8.2 4.7 %collective-permute-start.2 = (bf16[2,24,256]{2,1,0:T(8,128)(2,1)S(1)}, bf16[2,24,256]{2,1,0:T(8,128)(2,1)S(1)}, u32[]{:S(2)}, u32[]{:S(2)}) collective-permute-start(bf16[2,24,256]{2,1,0:T(8,128)(2,1)S(1)} %get-tuple-element.21.refs_5_), channel_id=1, source_target_pairs={{0,16},{4,20},{8,24},{12,28},{16,0},{20,4},{24,8},{28,12},{1,17},{... | collective-permute-start | bytes 73736 | tf_op jit(solution)/shard_map/ppermute | solution.py:201
  8.2 4.7 %collective-permute-start.1 = (bf16[2,24,256]{2,1,0:T(8,128)(2,1)S(1)}, bf16[2,24,256]{2,1,0:T(8,128)(2,1)S(1)}, u32[]{:S(2)}, u32[]{:S(2)}) collective-permute-start(bf16[2,24,256]{2,1,0:T(8,128)(2,1)S(1)} %get-tuple-element.21.refs_5_), channel_id=1, source_target_pairs={{0,8},{4,12},{8,0},{12,4},{16,24},{20,28},{24,16},{28,20},{1,9},{5... | collective-permute-start | bytes 73736 | tf_op jit(solution)/shard_map/ppermute | solution.py:201
  13.5 5.0 %collective-permute-start.7 = (bf16[272,128]{1,0:T(8,128)(2,1)S(1)}, bf16[272,128]{1,0:T(8,128)(2,1)S(1)}, u32[]{:S(2)}, u32[]{:S(2)}) collective-permute-start(bf16[272,128]{1,0:T(8,128)(2,1)S(1)} %get-tuple-element.26), channel_id=1, source_target_pairs={{0,4},{4,0},{8,12},{12,8},{16,20},{20,16},{24,28},{28,24},{1,5},{5... | collective-permute-start | bytes 208904 | tf_op jit(solution)/shard_map/ppermute | solution.py:201
  14.1 6.4 %collective-permute-start.4 = (bf16[24,384]{1,0:T(8,128)(2,1)S(1)}, bf16[24,384]{1,0:T(8,128)(2,1)S(1)}, u32[]{:S(2)}, u32[]{:S(2)}) collective-permute-start(bf16[24,384]{1,0:T(8,128)(2,1)S(1)} %get-tuple-element.22), channel_id=1, source_target_pairs={{0,24},{4,28},{8,16},{12,20},{16,8},{20,12},{24,0},{28,4},{1,25},{... | collective-permute-start | bytes 55304 | tf_op jit(solution)/shard_map/ppermute | solution.py:201
  15.6 4.9 %collective-permute-start.5 = (bf16[24,384]{1,0:T(8,128)(2,1)S(1)}, bf16[24,384]{1,0:T(8,128)(2,1)S(1)}, u32[]{:S(2)}, u32[]{:S(2)}) collective-permute-start(bf16[24,384]{1,0:T(8,128)(2,1)S(1)} %get-tuple-element.23), channel_id=1, source_target_pairs={{0,16},{4,20},{8,24},{12,28},{16,0},{20,4},{24,8},{28,12},{1,17},{... | collective-permute-start | bytes 55304 | tf_op jit(solution)/shard_map/ppermute | solution.py:201
  16.1 4.3 %collective-permute-start.6 = (bf16[24,384]{1,0:T(8,128)(2,1)S(1)}, bf16[24,384]{1,0:T(8,128)(2,1)S(1)}, u32[]{:S(2)}, u32[]{:S(2)}) collective-permute-start(bf16[24,384]{1,0:T(8,128)(2,1)S(1)} %get-tuple-element.24), channel_id=1, source_target_pairs={{0,8},{4,12},{8,0},{12,4},{16,24},{20,28},{24,16},{28,20},{1,9},{5... | collective-permute-start | bytes 55304 | tf_op jit(solution)/shard_map/ppermute | solution.py:201
  18.5 2.0 %copy-start.1 = (bf16[256,1024]{1,0:T(8,128)(2,1)S(1)}, bf16[256,1024]{1,0:T(8,128)(2,1)}, u32[]{:S(2)}) copy-start(bf16[256,1024]{1,0:T(8,128)(2,1)} %proj.3) | copy-start | bytes 1572868
  18.8 7.3 %collective-permute-start.11 = (bf16[160,256]{1,0:T(8,128)(2,1)S(1)}, bf16[160,256]{1,0:T(8,128)(2,1)S(1)}, u32[]{:S(2)}, u32[]{:S(2)}) collective-permute-start(bf16[160,256]{1,0:T(8,128)(2,1)S(1)} %get-tuple-element.34), channel_id=1, source_target_pairs={{0,3},{1,2},{2,1},{3,0},{4,7},{5,6},{6,5},{7,4},{8,11},{9,10},{10,... | collective-permute-start | bytes 245768 | tf_op jit(solution)/shard_map/ppermute | solution.py:201
  18.9 7.2 %collective-permute-start.12 = (bf16[160,256]{1,0:T(8,128)(2,1)S(1)}, bf16[160,256]{1,0:T(8,128)(2,1)S(1)}, u32[]{:S(2)}, u32[]{:S(2)}) collective-permute-start(bf16[160,256]{1,0:T(8,128)(2,1)S(1)} %get-tuple-element.35), channel_id=1, source_target_pairs={{0,2},{1,3},{2,0},{3,1},{4,6},{5,7},{6,4},{7,5},{8,10},{9,11},{10,... | collective-permute-start | bytes 245768 | tf_op jit(solution)/shard_map/ppermute | solution.py:201
  20.8 5.3 %collective-permute-start.10 = (bf16[152,256]{1,0:T(8,128)(2,1)S(1)}, bf16[152,256]{1,0:T(8,128)(2,1)S(1)}, u32[]{:S(2)}, u32[]{:S(2)}) collective-permute-start(bf16[152,256]{1,0:T(8,128)(2,1)S(1)} %get-tuple-element.32), channel_id=1, source_target_pairs={{0,1},{1,0},{2,3},{3,2},{4,5},{5,4},{6,7},{7,6},{8,9},{9,8},{10,11... | collective-permute-start | bytes 233480 | tf_op jit(solution)/shard_map/ppermute | solution.py:201
  21.1 4.4 %collective-permute-start.8 = (bf16[24,256]{1,0:T(8,128)(2,1)S(1)}, bf16[24,256]{1,0:T(8,128)(2,1)S(1)}, u32[]{:S(2)}, u32[]{:S(2)}) collective-permute-start(bf16[24,256]{1,0:T(8,128)(2,1)S(1)} %get-tuple-element.30), channel_id=1, source_target_pairs={{0,3},{1,2},{2,1},{3,0},{4,7},{5,6},{6,5},{7,4},{8,11},{9,10},{10,... | collective-permute-start | bytes 36872 | tf_op jit(solution)/shard_map/ppermute | solution.py:201
  22.4 3.7 %collective-permute-start.9 = (bf16[24,256]{1,0:T(8,128)(2,1)S(1)}, bf16[24,256]{1,0:T(8,128)(2,1)S(1)}, u32[]{:S(2)}, u32[]{:S(2)}) collective-permute-start(bf16[24,256]{1,0:T(8,128)(2,1)S(1)} %get-tuple-element.31), channel_id=1, source_target_pairs={{0,2},{1,3},{2,0},{3,1},{4,6},{5,7},{6,4},{7,5},{8,10},{9,11},{10,... | collective-permute-start | bytes 36872 | tf_op jit(solution)/shard_map/ppermute | solution.py:201

commit v10 on v9

--- a/solution.py
+++ b/solution.py
@@ -14,6 +14,7 @@
 SCALE = HEAD_DIM ** (-0.5) * math.log2(math.e)
 VMEM_LIMIT = 48 * 1024 * 1024
 COST = 5 * 10**9
+COST_A = 10**9
 BF16 = jnp.bfloat16
 F32 = jnp.float32
 
@@ -45,56 +46,76 @@
         copy.wait()
 
 
-def attend(aud_count, vid_count, *refs):
-    auds, vids = refs[:aud_count], refs[aud_count : aud_count + vid_count]
-    row_outs = refs[aud_count + vid_count : 2 * aud_count + vid_count]
-    col_outs = refs[2 * aud_count + vid_count :]
-    width = auds[0].shape[2]
+def tile_scores(queries, vids):
+    total_vid, width = sum(ref.shape[1] for ref in vids), queries.shape[1]
     heads = width // HEAD_DIM
-    queries, aud_vals = (jnp.concatenate([ref[i] for ref in auds], axis=0) for i in range(2))
-    vid_refs, vid_vals = (
-        jnp.concatenate([ref[i].astype(F32) for ref in vids], axis=0) for i in range(2)
-    )
-    total_aud, total_vid = queries.shape[0], vid_refs.shape[0]
-    masks = [head_lanes(total_vid, width, h) for h in range(heads)]
+    keys = jnp.concatenate([ref[0].astype(F32) for ref in vids], axis=0).astype(BF16)
     lanes = [head_lanes(1, width, h).astype(F32).astype(BF16) for h in range(heads)]
-    keys = vid_refs.astype(BF16)
     keys = jnp.concatenate([keys * lane for lane in lanes], axis=0)
-    scores = dot(keys, queries, 1, 1).reshape(heads, total_vid, total_aud)
-
-    row_top = jnp.max(scores, axis=1, keepdims=True)
-    row_probs = jnp.exp2((scores - row_top) * SCALE)
-    row_total = jnp.sum(row_probs, axis=1, keepdims=True)
-    row_probs = row_probs.astype(BF16)
+    return dot(keys, queries, 1, 1).reshape(heads, total_vid, queries.shape[0])
+
+
+def both(auds):
+    return (jnp.concatenate([ref[i] for ref in auds], axis=0) for i in range(2))
+
+
+def column_states(scores, aud_vals, outs):
+    heads, total_vid, total_aud = scores.shape
+    width = heads * HEAD_DIM
+    top = jnp.max(scores, axis=2, keepdims=True)
+    probs = jnp.exp2((scores - top) * SCALE)
+    total = jnp.sum(probs, axis=2, keepdims=True)
+    probs = probs.reshape(heads * total_vid, total_aud).astype(BF16)
+    every = dot(probs, aud_vals).reshape(heads, total_vid, width)
+    log = top * SCALE + jnp.log2(total)
+    lane = lax.broadcasted_iota(jnp.int32, (total_vid, LANES), 1) % heads
+    mix, divisor = every[0], jnp.broadcast_to(total[0], (total_vid, width))
+    logs = jnp.broadcast_to(log[0], (total_vid, LANES))
+    for h in range(1, heads):
+        mask = head_lanes(total_vid, width, h)
+        mix = jnp.where(mask, every[h], mix)
+        divisor = jnp.where(mask, total[h], divisor)
+        logs = jnp.where(lane == h, log[h], logs)
+    mix = mix / divisor
+    for i, out in enumerate(outs):
+        rows = slice(i * out.shape[0], (i + 1) * out.shape[0])
+        put_cols(out, mix[rows], logs[rows])
+
+
+def row_states(scores, vid_vals, outs):
+    heads, _, total_aud = scores.shape
+    top = jnp.max(scores, axis=1, keepdims=True)
+    probs = jnp.exp2((scores - top) * SCALE)
+    total = jnp.sum(probs, axis=1, keepdims=True)
+    probs = probs.astype(BF16)
     vals = vid_vals.T.astype(BF16)
-    row_mix = [
-        dot(vals[h * HEAD_DIM : (h + 1) * HEAD_DIM], row_probs[h]) * (1.0 / row_total[h])
+    mix = [
+        dot(vals[h * HEAD_DIM : (h + 1) * HEAD_DIM], probs[h]) * (1.0 / total[h])
         for h in range(heads)
     ]
-    row_mix = jnp.concatenate(row_mix, axis=0)
-    row_log = (row_top * SCALE + jnp.log2(row_total)).reshape(heads, total_aud)
-    for i, out in enumerate(row_outs):
+    mix = jnp.concatenate(mix, axis=0)
+    log = (top * SCALE + jnp.log2(total)).reshape(heads, total_aud)
+    for i, out in enumerate(outs):
         cols = slice(i * out.shape[1], (i + 1) * out.shape[1])
-        put_rows(out, row_mix[:, cols], row_log[:, cols])
-
-    col_top = jnp.max(scores, axis=2, keepdims=True)
-    col_probs = jnp.exp2((scores - col_top) * SCALE)
-    col_total = jnp.sum(col_probs, axis=2, keepdims=True)
-    col_probs = col_probs.reshape(heads * total_vid, total_aud).astype(BF16)
-    every = dot(col_probs, aud_vals).reshape(heads, total_vid, width)
-    col_log = col_top * SCALE + jnp.log2(col_total)
-    col_mix, divisor = every[0], jnp.broadcast_to(col_total[0], (total_vid, width))
-    for h in range(1, heads):
-        col_mix = jnp.where(masks[h], every[h], col_mix)
-        divisor = jnp.where(masks[h], col_total[h], divisor)
-    col_mix = col_mix / divisor
-    lane = lax.broadcasted_iota(jnp.int32, (total_vid, LANES), 1) % heads
-    logs = jnp.broadcast_to(col_log[0], (total_vid, LANES))
-    for h in range(1, heads):
-        logs = jnp.where(lane == h, col_log[h], logs)
-    for i, out in enumerate(col_outs):
-        rows = slice(i * out.shape[0], (i + 1) * out.shape[0])
-        put_cols(out, col_mix[rows], logs[rows])
+        put_rows(out, mix[:, cols], log[:, cols])
+
+
+def attend_first(*refs):
+    *auds, vid, col_out, scores_out = refs
+    queries, aud_vals = both(auds)
+    scores = tile_scores(queries, [vid])
+    scores_out[...] = scores
+    column_states(scores, aud_vals, [col_out])
+
+
+def attend(aud_count, vid_count, *refs):
+    auds, vids, refs = refs[:aud_count], refs[aud_count : aud_count + vid_count], refs[aud_count + vid_count :]
+    first, first_scores, row_outs, col_outs = refs[0], refs[1], refs[2 : 2 + aud_count], refs[2 + aud_count :]
+    queries, aud_vals = both(auds)
+    scores = tile_scores(queries, vids)
+    column_states(scores, aud_vals, col_outs)
+    vals = jnp.concatenate([ref[1].astype(F32) for ref in (first, *vids)], axis=0)
+    row_states(jnp.concatenate([first_scores[...], scores], axis=1), vals, row_outs)
 
 
 def put_rows(out, mix, log):
@@ -159,8 +180,17 @@
     project(mix.T.astype(BF16), proj, me[0], outs)
 
 
-def project_video(me, proj, states, aud_core, outs):
-    mix = merge([get_cols(ref, proj.shape[0]) for ref in states])
+def merge_first(mine, got, _, mix_out, log_out):
+    states = [get_cols(ref, mix_out.shape[1]) for ref in (mine, got)]
+    top = jnp.maximum(states[0][1], states[1][1])
+    weights = [jnp.exp2(log - top) for _, log in states]
+    total = weights[0] + weights[1]
+    mix_out[...] = (weights[0] * states[0][0] + weights[1] * states[1][0]) / total
+    log_out[...] = top + jnp.log2(total)
+
+
+def project_video(me, proj, mix_log, states, aud_core, outs):
+    mix = merge([tuple(ref[...] for ref in mix_log)] + [get_cols(ref, proj.shape[0]) for ref in states])
     aud_rows = aud_core.shape[0]
     outs[1][:aud_rows, :] = aud_core[...]
     project(mix.astype(BF16), proj, me[0], [outs[0], outs[1].at[aud_rows:, :], *outs[2:]])
@@ -180,7 +210,7 @@
     aud_out[...] = aud.astype(BF16)
 
 
-def call(body, out_shape, args, in_specs=None, scratch=()):
+def call(body, out_shape, args, in_specs=None, scratch=(), cost=COST):
     vmem = pl.BlockSpec(memory_space=pltpu.VMEM)
     return pl.pallas_call(
         body,
@@ -189,7 +219,7 @@
         out_specs=[vmem] * len(out_shape),
         scratch_shapes=scratch,
         compiler_params=pltpu.CompilerParams(vmem_limit_bytes=VMEM_LIMIT),
-        cost_estimate=pl.CostEstimate(flops=COST, bytes_accessed=0, transcendentals=0),
+        cost_estimate=pl.CostEstimate(flops=cost, bytes_accessed=0, transcendentals=0),
     )(*args)
 
 
@@ -218,13 +248,6 @@
 
     def shape(*dims, dtype=BF16):
         return jax.ShapeDtypeStruct(dims, dtype)
-
-    def gather(block, stride, count):
-        return [swap(block, "seq", k * stride) for k in range(1, count)] + [block]
-
-    def scatter(blocks, stride):
-        count = len(blocks)
-        return [swap(blocks[k - 1], "seq", k * stride) for k in reversed(range(1, count))] + [blocks[-1]]
 
     aud, vid = call(
         pack,
@@ -236,38 +259,52 @@
         in_specs=[pl.BlockSpec(memory_space=pltpu.HBM)] * 4,
         scratch=[pltpu.SemaphoreType.DMA((4,))],
     )
-    auds, vids = gather(aud, 1, aud_count), gather(vid, aud_count, vid_count)
+    early = vid_count // 2
+    late = [k for k in reversed(range(1, vid_count)) if k != early]
+    auds = [swap(aud, "seq", k) for k in range(1, aud_count)] + [aud]
+    vids = {k: swap(vid, "seq", k * aud_count) for k in (early, *late)}
+    state = shape(vid_rows, width + LANES)
+    first_state, scores = call(
+        attend_first,
+        [state, shape(heads, vid_rows, aud_count * aud_rows, dtype=F32)],
+        [*auds, vids[early]],
+    )
     states = call(
-        functools.partial(attend, aud_count, vid_count),
-        [shape(width + log_rows, aud_rows)] * aud_count + [shape(vid_rows, width + LANES)] * vid_count,
-        [*auds, *vids],
-    )
-    rows = scatter(states[:aud_count], 1)
-    cols = scatter(states[aud_count:], aud_count)
+        functools.partial(attend, aud_count, len(late) + 1),
+        [shape(width + log_rows, aud_rows)] * aud_count + [state] * (len(late) + 1),
+        [*auds, *(vids[k] for k in late), vid, vids[early], scores],
+    )
+    rows = [swap(states[k - 1], "seq", k) for k in range(1, aud_count)] + [states[aud_count - 1]]
+    states = dict(zip((early, *late, 0), (first_state, *states[aud_count:])))
+    cols = [swap(states[k], "seq", k * aud_count) for k in (early, *late)] + [states[0]]
 
     me = lax.axis_index("head").astype(jnp.int32).reshape(1)
     vmem = pl.BlockSpec(memory_space=pltpu.VMEM)
     smem = pl.BlockSpec(memory_space=pltpu.SMEM)
     hbm = pl.BlockSpec(memory_space=pl.ANY)
 
+    mix_log = call(
+        merge_first, [shape(vid_rows, width, dtype=F32)] * 2, [cols.pop(), cols.pop(0), audio_proj]
+    )
     aud_terms = call(
-        lambda me, proj, *refs: project_audio(me, proj, refs[:aud_count], refs[aud_count:]),
+        lambda me, proj, *refs: project_audio(me, proj, refs[:aud_count], refs[aud_count + 1 :]),
         [shape(aud_rows, step, dtype=F32), shape(aud_rows, step)]
         + [shape(aud_rows + vid_rows + 8, step)] * (peers - 2),
-        [me, audio_proj, *rows],
-        in_specs=[smem, vmem] + [vmem] * aud_count,
+        [me, audio_proj, *rows, mix_log[0]],
+        in_specs=[smem, vmem] + [vmem] * aud_count + [pl.BlockSpec(memory_space=pl.ANY)],
+        cost=COST_A,
     )
     vid_terms = call(
-        lambda me, proj, *refs: project_video(
-            me, proj, refs[:vid_count], refs[vid_count], refs[vid_count + 1 :]
+        lambda me, proj, mix, log, core, *refs: project_video(
+            me, proj, (mix, log), refs[: len(cols)], core, refs[len(cols) :]
         ),
         [shape(vid_rows, step, dtype=F32), shape(aud_rows + vid_rows, step)]
         + [shape(vid_rows, step)] * (peers - 2),
-        [me, video_proj, *cols, aud_terms[1]],
-        in_specs=[smem] + [vmem] * (vid_count + 2),
+        [me, video_proj, *mix_log, aud_terms[1], *cols],
+        in_specs=[smem] + [vmem] * (len(cols) + 4),
     )
     vid_got = [vid_terms[0]] + [
-        swap(vid_terms[k], "head", k) for k in reversed(range(1, peers))
+        swap(vid_terms[k], "head", k) for k in (*range(2, peers), 1)
     ]
     aud_got = [aud_terms[0]] + [
         swap(aud_terms[k], "head", k) for k in reversed(range(2, peers))

time: 27 us -> 25.8 us (0.956)
  waiting for transfers between devices: 7.08 us -> 5.5 us
  Pallas kernels: 2.83 us -> 3.27 us
    ppermute x13, waiting for transfers between devices: 7.08 us -> 5.5 us  [swap(): lax.ppermute(block, axis, [(i, i ^ distance) for i in range(lax.axis_size...]
    pallas_call x5 -> x7, Pallas kernels: 2.83 us -> 3.27 us  [call(): pl.pallas_call(body, out_shape=out_shape, in_specs=in_specs or [vmem] * l...]
  transfers between devices with their start and end apart: 13 -> 13, of which waited for: 4 -> 5; matrix products, arithmetic and copies ran while one was open for 0% -> 0% of each run, Pallas kernels for 2% -> 7%
where the time goes in v10:
time: 25.8 us; the launch traced here: 25.6 us
  starting transfers between devices  16.2 us (63%)
  waiting for transfers between devices  5.5 us (21%)
  Pallas kernels  3.27 us (13%)
  between operations  0.7 us (3%)
    ppermute x13, starting transfers between devices, swap(): lax.ppermute(block, axis, [(i, i ^ distance) for i in range(lax.axis_size...  16.2 us
    ppermute x13, waiting for transfers between devices, swap(): lax.ppermute(block, axis, [(i, i ^ distance) for i in range(lax.axis_size...  5.5 us
    pallas_call x7, Pallas kernels, call(): pl.pallas_call(body, out_shape=out_shape, in_specs=in_specs or [vmem] * l...  3.27 us
  transfers between devices with their start and end apart: 13, of which 5 were waited for; matrix products, arithmetic and copies ran while one was open for 0% of the time, Pallas kernels for 7%

profile of v10, /device:TPU:0, one launch (start us, length us, event | category | flops | bytes accessed | tf_op | source)
XLA Modules:
  0.0 25.6 jit_solution(5275291458849382254)
XLA Ops:
  0.6 0.9 %shard_map.77 = (bf16[2,128,256]{2,1,0:T(8,128)(2,1)S(1)}, bf16[2,24,256]{2,1,0:T(8,128)(2,1)S(1)}) custom-call(bf16[128,256]{1,0:T(8,128)(2,1)} %aud_ref.1, bf16[128,256]{1,0:T(8,128)(2,1)} %aud_val.1, bf16[24,256]{1,0:T(8,128)(2,1)} %vid_ref.1, bf16[24,256]{1,0:T(8,128)(2,1)} %vid_val.1), custom_call_target="tpu_custom_call" | custom-call | flops 5000000000 | tf_op jit(solution)/shard_map/pallas_call | solution.py:215
  1.5 3.0 %collective-permute-start = (bf16[2,128,256]{2,1,0:T(8,128)(2,1)S(1)}, bf16[2,128,256]{2,1,0:T(8,128)(2,1)S(1)}, u32[]{:S(2)}, u32[]{:S(2)}) collective-permute-start(bf16[2,128,256]{2,1,0:T(8,128)(2,1)S(1)} %get-tuple-element.23.refs_1_), channel_id=1, source_target_pairs={{0,4},{4,0},{8,12},{12,8},{16,20},{20,16},{24,28},{28,24},{1,5},{5... | collective-permute-start | bytes 393224 | tf_op jit(solution)/shard_map/ppermute | solution.py:231
  4.6 2.6 %collective-permute-start.3 = (bf16[2,24,256]{2,1,0:T(8,128)(2,1)S(1)}, bf16[2,24,256]{2,1,0:T(8,128)(2,1)S(1)}, u32[]{:S(2)}, u32[]{:S(2)}) collective-permute-start(bf16[2,24,256]{2,1,0:T(8,128)(2,1)S(1)} %get-tuple-element.24.refs_4_), channel_id=1, source_target_pairs={{0,16},{4,20},{8,24},{12,28},{16,0},{20,4},{24,8},{28,12},{1,17},{... | collective-permute-start | bytes 73736 | tf_op jit(solution)/shard_map/ppermute | solution.py:231
  7.1 1.3 %collective-permute-start.1 = (bf16[2,24,256]{2,1,0:T(8,128)(2,1)S(1)}, bf16[2,24,256]{2,1,0:T(8,128)(2,1)S(1)}, u32[]{:S(2)}, u32[]{:S(2)}) collective-permute-start(bf16[2,24,256]{2,1,0:T(8,128)(2,1)S(1)} %get-tuple-element.24.refs_4_), channel_id=1, source_target_pairs={{0,24},{4,28},{8,16},{12,20},{16,8},{20,12},{24,0},{28,4},{1,25},{... | collective-permute-start | bytes 73736 | tf_op jit(solution)/shard_map/ppermute | solution.py:231
  8.5 0.2 collective-permute-start.2
  8.7 0.6 %collective-permute-done.3.refs_2_.refs_5_ = bf16[2,24,256]{2,1,0:T(8,128)(2,1)S(1)} collective-permute-done((bf16[2,24,256]{2,1,0:T(8,128)(2,1)S(1)}, bf16[2,24,256]{2,1,0:T(8,128)(2,1)S(1)}, u32[]{:S(2)}, u32[]{:S(2)}) %collective-permute-start.3) | collective-permute-done | bytes 24608 | tf_op jit(solution)/shard_map/ppermute | solution.py:231
  9.3 0.4 %shard_map.78 = (bf16[24,384]{1,0:T(8,128)(2,1)S(1)}, f32[4,24,256]{2,1,0:T(8,128)S(1)}) custom-call(bf16[2,128,256]{2,1,0:T(8,128)(2,1)S(1)} %collective-permute-done.refs_0_, bf16[2,128,256]{2,1,0:T(8,128)(2,1)S(1)} %get-tuple-element.23.refs_1_, bf16[2,24,256]{2,1,0:T(8,128)(2,1)S(1)} %collective-permute-done.3.refs_2_.refs_5_), custom_call_target="tpu_custom_call" | custom-call | flops 5000000000 | tf_op jit(solution)/shard_map/pallas_call | solution.py:215
  9.7 2.8 %collective-permute-start.4 = (bf16[24,384]{1,0:T(8,128)(2,1)S(1)}, bf16[24,384]{1,0:T(8,128)(2,1)S(1)}, u32[]{:S(2)}, u32[]{:S(2)}) collective-permute-start(bf16[24,384]{1,0:T(8,128)(2,1)S(1)} %get-tuple-element.27), channel_id=1, source_target_pairs={{0,16},{4,20},{8,24},{12,28},{16,0},{20,4},{24,8},{28,12},{1,17},{... | collective-permute-start | bytes 55304 | tf_op jit(solution)/shard_map/ppermute | solution.py:231
  12.5 0.2 collective-permute-done.1.refs_2_
  12.8 0.5 %shard_map.79 = (bf16[272,128]{1,0:T(8,128)(2,1)S(1)}, bf16[272,128]{1,0:T(8,128)(2,1)S(1)}, bf16[24,384]{1,0:T(8,128)(2,1)S(1)}, bf16[24,384]{1,0:T(8,128)(2,1)S(1)}, bf16[24,384]{1,0:T(8,128)(2,1)S(1)}) custom-call(bf16[2,128,256]{2,1,0:T(8,128)(2,1)S(1)} %collective-permute-done.refs_0_, bf16[2,128,256]{2,1,0:T(8,128)(2,1)S(1)} %get-tuple-element.23.refs_1_, ...), custom_call_target="tpu_custom_call" | custom-call | flops 5000000000 | tf_op jit(solution)/shard_map/pallas_call | solution.py:215
  13.3 0.6 %collective-permute-start.5 = (bf16[272,128]{1,0:T(8,128)(2,1)S(1)}, bf16[272,128]{1,0:T(8,128)(2,1)S(1)}, u32[]{:S(2)}, u32[]{:S(2)}) collective-permute-start(bf16[272,128]{1,0:T(8,128)(2,1)S(1)} %get-tuple-element.30), channel_id=1, source_target_pairs={{0,4},{4,0},{8,12},{12,8},{16,20},{20,16},{24,28},{28,24},{1,5},{5... | collective-permute-start | bytes 208904 | tf_op jit(solution)/shard_map/ppermute | solution.py:231
  13.9 2.0 %collective-permute-start.6 = (bf16[24,384]{1,0:T(8,128)(2,1)S(1)}, bf16[24,384]{1,0:T(8,128)(2,1)S(1)}, u32[]{:S(2)}, u32[]{:S(2)}) collective-permute-start(bf16[24,384]{1,0:T(8,128)(2,1)S(1)} %get-tuple-element.33), channel_id=1, source_target_pairs={{0,24},{4,28},{8,16},{12,20},{16,8},{20,12},{24,0},{28,4},{1,25},{... | collective-permute-start | bytes 55304 | tf_op jit(solution)/shard_map/ppermute | solution.py:231
  15.9 0.1 shard_map.80
  16.1 1.6 %collective-permute-done.5.refs_0_ = bf16[272,128]{1,0:T(8,128)(2,1)S(1)} collective-permute-done((bf16[272,128]{1,0:T(8,128)(2,1)S(1)}, bf16[272,128]{1,0:T(8,128)(2,1)S(1)}, u32[]{:S(2)}, u32[]{:S(2)}) %collective-permute-start.5) | collective-permute-done | bytes 69664 | tf_op jit(solution)/shard_map/ppermute | solution.py:231
  17.7 0.3 %shard_map.81 = (f32[128,256]{1,0:T(8,128)S(1)}, bf16[128,256]{1,0:T(8,128)(2,1)S(1)}, bf16[160,256]{1,0:T(8,128)(2,1)S(1)}, bf16[160,256]{1,0:T(8,128)(2,1)S(1)}) custom-call(s32[1]{0:T(128)} %bitcast.me, bf16[256,1024]{1,0:T(8,128)(2,1)S(1)} %copy-done, bf16[272,128]{1,0:T(8,128)(2,1)S(1)} %collective-permute-done.5.refs_0_, ...), custom_call_target="tpu_custom_call" | custom-call | flops 1000000000 | tf_op jit(solution)/shard_map/pallas_call | solution.py:215
  18.0 0.1 collective-permute-start.11
  18.1 1.6 %collective-permute-start.12 = (bf16[160,256]{1,0:T(8,128)(2,1)S(1)}, bf16[160,256]{1,0:T(8,128)(2,1)S(1)}, u32[]{:S(2)}, u32[]{:S(2)}) collective-permute-start(bf16[160,256]{1,0:T(8,128)(2,1)S(1)} %get-tuple-element.41), channel_id=1, source_target_pairs={{0,2},{1,3},{2,0},{3,1},{4,6},{5,7},{6,4},{7,5},{8,10},{9,11},{10,... | collective-permute-start | bytes 245768 | tf_op jit(solution)/shard_map/ppermute | solution.py:231
  19.7 0.3 %shard_map.82 = (f32[24,256]{1,0:T(8,128)S(1)}, bf16[152,256]{1,0:T(8,128)(2,1)S(1)}, bf16[24,256]{1,0:T(8,128)(2,1)S(1)}, bf16[24,256]{1,0:T(8,128)(2,1)S(1)}) custom-call(s32[1]{0:T(128)} %bitcast.me, bf16[256,1024]{1,0:T(8,128)(2,1)S(1)} %copy-done.1, f32[24,256]{1,0:T(8,128)S(1)} %get-tuple-element.28.refs_2_.mix, f32[24,256]{1,0:T(8,128)S(1)} %get-tuple-element.29.log, ...), custom_call_target="tpu_custom_call" | custom-call | flops 5000000000 | tf_op jit(solution)/shard_map/pallas_call | solution.py:215
  20.0 0.3 %collective-permute-start.10 = (bf16[152,256]{1,0:T(8,128)(2,1)S(1)}, bf16[152,256]{1,0:T(8,128)(2,1)S(1)}, u32[]{:S(2)}, u32[]{:S(2)}) collective-permute-start(bf16[152,256]{1,0:T(8,128)(2,1)S(1)} %get-tuple-element.38), channel_id=1, source_target_pairs={{0,1},{1,0},{2,3},{3,2},{4,5},{5,4},{6,7},{7,6},{8,9},{9,8},{10,11... | collective-permute-start | bytes 233480 | tf_op jit(solution)/shard_map/ppermute | solution.py:231
  20.3 1.5 %collective-permute-start.8 = (bf16[24,256]{1,0:T(8,128)(2,1)S(1)}, bf16[24,256]{1,0:T(8,128)(2,1)S(1)}, u32[]{:S(2)}, u32[]{:S(2)}) collective-permute-start(bf16[24,256]{1,0:T(8,128)(2,1)S(1)} %get-tuple-element.36), channel_id=1, source_target_pairs={{0,2},{1,3},{2,0},{3,1},{4,6},{5,7},{6,4},{7,5},{8,10},{9,11},{10,... | collective-permute-start | bytes 36872 | tf_op jit(solution)/shard_map/ppermute | solution.py:231
  21.8 0.1 collective-permute-start.9
  21.9 2.9 %collective-permute-done.8.refs_1_ = bf16[24,256]{1,0:T(8,128)(2,1)S(1)} collective-permute-done((bf16[24,256]{1,0:T(8,128)(2,1)S(1)}, bf16[24,256]{1,0:T(8,128)(2,1)S(1)}, u32[]{:S(2)}, u32[]{:S(2)}) %collective-permute-start.8) | collective-permute-done | bytes 12320 | tf_op jit(solution)/shard_map/ppermute | solution.py:231
  24.8 0.1 collective-permute-done.9.refs_2_
  25.0 0.7 %shard_map.83 = (bf16[24,256]{1,0:T(8,128)(2,1)}, bf16[128,256]{1,0:T(8,128)(2,1)}) custom-call(f32[24,256]{1,0:T(8,128)S(1)} %get-tuple-element.35.refs_0_, bf16[24,256]{1,0:T(8,128)(2,1)S(1)} %collective-permute-done.8.refs_1_, bf16[24,256]{1,0:T(8,128)(2,1)S(1)} %collective-permute-done.9.refs_2_, bf16[152,256]{1,0:T(8,128)(2,1)S(1)} %collective-permute-done.10.refs_3_, ...), custom_call_target="tpu_custom_call" | custom-call | flops 5000000000 | tf_op jit(solution)/shard_map/pallas_call | solution.py:215
  (13 shorter events, 0.1 us)
Async XLA Ops:
  1.5 7.7 %collective-permute-start = (bf16[2,128,256]{2,1,0:T(8,128)(2,1)S(1)}, bf16[2,128,256]{2,1,0:T(8,128)(2,1)S(1)}, u32[]{:S(2)}, u32[]{:S(2)}) collective-permute-start(bf16[2,128,256]{2,1,0:T(8,128)(2,1)S(1)} %get-tuple-element.23.refs_1_), channel_id=1, source_target_pairs={{0,4},{4,0},{8,12},{12,8},{16,20},{20,16},{24,28},{28,24},{1,5},{5... | collective-permute-start | bytes 393224 | tf_op jit(solution)/shard_map/ppermute | solution.py:231
  4.6 4.7 %collective-permute-start.3 = (bf16[2,24,256]{2,1,0:T(8,128)(2,1)S(1)}, bf16[2,24,256]{2,1,0:T(8,128)(2,1)S(1)}, u32[]{:S(2)}, u32[]{:S(2)}) collective-permute-start(bf16[2,24,256]{2,1,0:T(8,128)(2,1)S(1)} %get-tuple-element.24.refs_4_), channel_id=1, source_target_pairs={{0,16},{4,20},{8,24},{12,28},{16,0},{20,4},{24,8},{28,12},{1,17},{... | collective-permute-start | bytes 73736 | tf_op jit(solution)/shard_map/ppermute | solution.py:231
  7.1 5.6 %collective-permute-start.1 = (bf16[2,24,256]{2,1,0:T(8,128)(2,1)S(1)}, bf16[2,24,256]{2,1,0:T(8,128)(2,1)S(1)}, u32[]{:S(2)}, u32[]{:S(2)}) collective-permute-start(bf16[2,24,256]{2,1,0:T(8,128)(2,1)S(1)} %get-tuple-element.24.refs_4_), channel_id=1, source_target_pairs={{0,24},{4,28},{8,16},{12,20},{16,8},{20,12},{24,0},{28,4},{1,25},{... | collective-permute-start | bytes 73736 | tf_op jit(solution)/shard_map/ppermute | solution.py:231
  8.5 4.3 %collective-permute-start.2 = (bf16[2,24,256]{2,1,0:T(8,128)(2,1)S(1)}, bf16[2,24,256]{2,1,0:T(8,128)(2,1)S(1)}, u32[]{:S(2)}, u32[]{:S(2)}) collective-permute-start(bf16[2,24,256]{2,1,0:T(8,128)(2,1)S(1)} %get-tuple-element.24.refs_4_), channel_id=1, source_target_pairs={{0,8},{4,12},{8,0},{12,4},{16,24},{20,28},{24,16},{28,20},{1,9},{5... | collective-permute-start | bytes 73736 | tf_op jit(solution)/shard_map/ppermute | solution.py:231
  9.7 6.2 %collective-permute-start.4 = (bf16[24,384]{1,0:T(8,128)(2,1)S(1)}, bf16[24,384]{1,0:T(8,128)(2,1)S(1)}, u32[]{:S(2)}, u32[]{:S(2)}) collective-permute-start(bf16[24,384]{1,0:T(8,128)(2,1)S(1)} %get-tuple-element.27), channel_id=1, source_target_pairs={{0,16},{4,20},{8,24},{12,28},{16,0},{20,4},{24,8},{28,12},{1,17},{... | collective-permute-start | bytes 55304 | tf_op jit(solution)/shard_map/ppermute | solution.py:231
  12.8 3.2 %copy-start = (bf16[256,1024]{1,0:T(8,128)(2,1)S(1)}, bf16[256,1024]{1,0:T(8,128)(2,1)}, u32[]{:S(2)}) copy-start(bf16[256,1024]{1,0:T(8,128)(2,1)} %proj.2) | copy-start | bytes 1572868
  13.3 4.4 %collective-permute-start.5 = (bf16[272,128]{1,0:T(8,128)(2,1)S(1)}, bf16[272,128]{1,0:T(8,128)(2,1)S(1)}, u32[]{:S(2)}, u32[]{:S(2)}) collective-permute-start(bf16[272,128]{1,0:T(8,128)(2,1)S(1)} %get-tuple-element.30), channel_id=1, source_target_pairs={{0,4},{4,0},{8,12},{12,8},{16,20},{20,16},{24,28},{28,24},{1,5},{5... | collective-permute-start | bytes 208904 | tf_op jit(solution)/shard_map/ppermute | solution.py:231
  13.9 5.7 %collective-permute-start.6 = (bf16[24,384]{1,0:T(8,128)(2,1)S(1)}, bf16[24,384]{1,0:T(8,128)(2,1)S(1)}, u32[]{:S(2)}, u32[]{:S(2)}) collective-permute-start(bf16[24,384]{1,0:T(8,128)(2,1)S(1)} %get-tuple-element.33), channel_id=1, source_target_pairs={{0,24},{4,28},{8,16},{12,20},{16,8},{20,12},{24,0},{28,4},{1,25},{... | collective-permute-start | bytes 55304 | tf_op jit(solution)/shard_map/ppermute | solution.py:231
  15.9 3.8 %collective-permute-start.7 = (bf16[24,384]{1,0:T(8,128)(2,1)S(1)}, bf16[24,384]{1,0:T(8,128)(2,1)S(1)}, u32[]{:S(2)}, u32[]{:S(2)}) collective-permute-start(bf16[24,384]{1,0:T(8,128)(2,1)S(1)} %get-tuple-element.34), channel_id=1, source_target_pairs={{0,8},{4,12},{8,0},{12,4},{16,24},{20,28},{24,16},{28,20},{1,9},{5... | collective-permute-start | bytes 55304 | tf_op jit(solution)/shard_map/ppermute | solution.py:231
  17.7 2.0 %copy-start.1 = (bf16[256,1024]{1,0:T(8,128)(2,1)S(1)}, bf16[256,1024]{1,0:T(8,128)(2,1)}, u32[]{:S(2)}) copy-start(bf16[256,1024]{1,0:T(8,128)(2,1)} %proj.3) | copy-start | bytes 1572868
  18.0 7.0 %collective-permute-start.11 = (bf16[160,256]{1,0:T(8,128)(2,1)S(1)}, bf16[160,256]{1,0:T(8,128)(2,1)S(1)}, u32[]{:S(2)}, u32[]{:S(2)}) collective-permute-start(bf16[160,256]{1,0:T(8,128)(2,1)S(1)} %get-tuple-element.40), channel_id=1, source_target_pairs={{0,3},{1,2},{2,1},{3,0},{4,7},{5,6},{6,5},{7,4},{8,11},{9,10},{10,... | collective-permute-start | bytes 245768 | tf_op jit(solution)/shard_map/ppermute | solution.py:231
  18.1 6.9 %collective-permute-start.12 = (bf16[160,256]{1,0:T(8,128)(2,1)S(1)}, bf16[160,256]{1,0:T(8,128)(2,1)S(1)}, u32[]{:S(2)}, u32[]{:S(2)}) collective-permute-start(bf16[160,256]{1,0:T(8,128)(2,1)S(1)} %get-tuple-element.41), channel_id=1, source_target_pairs={{0,2},{1,3},{2,0},{3,1},{4,6},{5,7},{6,4},{7,5},{8,10},{9,11},{10,... | collective-permute-start | bytes 245768 | tf_op jit(solution)/shard_map/ppermute | solution.py:231
  20.0 5.0 %collective-permute-start.10 = (bf16[152,256]{1,0:T(8,128)(2,1)S(1)}, bf16[152,256]{1,0:T(8,128)(2,1)S(1)}, u32[]{:S(2)}, u32[]{:S(2)}) collective-permute-start(bf16[152,256]{1,0:T(8,128)(2,1)S(1)} %get-tuple-element.38), channel_id=1, source_target_pairs={{0,1},{1,0},{2,3},{3,2},{4,5},{5,4},{6,7},{7,6},{8,9},{9,8},{10,11... | collective-permute-start | bytes 233480 | tf_op jit(solution)/shard_map/ppermute | solution.py:231
  20.3 4.5 %collective-permute-start.8 = (bf16[24,256]{1,0:T(8,128)(2,1)S(1)}, bf16[24,256]{1,0:T(8,128)(2,1)S(1)}, u32[]{:S(2)}, u32[]{:S(2)}) collective-permute-start(bf16[24,256]{1,0:T(8,128)(2,1)S(1)} %get-tuple-element.36), channel_id=1, source_target_pairs={{0,2},{1,3},{2,0},{3,1},{4,6},{5,7},{6,4},{7,5},{8,10},{9,11},{10,... | collective-permute-start | bytes 36872 | tf_op jit(solution)/shard_map/ppermute | solution.py:231
  21.8 3.2 %collective-permute-start.9 = (bf16[24,256]{1,0:T(8,128)(2,1)S(1)}, bf16[24,256]{1,0:T(8,128)(2,1)S(1)}, u32[]{:S(2)}, u32[]{:S(2)}) collective-permute-start(bf16[24,256]{1,0:T(8,128)(2,1)S(1)} %get-tuple-element.37), channel_id=1, source_target_pairs={{0,3},{1,2},{2,1},{3,0},{4,7},{5,6},{6,5},{7,4},{8,11},{9,10},{10,... | collective-permute-start | bytes 36872 | tf_op jit(solution)/shard_map/ppermute | solution.py:231

commit v11 on v10

--- a/solution.py
+++ b/solution.py
@@ -171,7 +171,7 @@
     step = outs[0].shape[1]
     for i, out in enumerate(outs):
         block = pl.ds(pl.multiple_of(partner(me, i, len(outs)) * step, step), step)
-        out[: mix.shape[0], :] = dot(mix, proj[:, block]).astype(out.dtype)
+        out[...] = dot(mix, proj[:, block]).astype(out.dtype)
 
 
 def project_audio(me, proj, states, outs):
@@ -196,18 +196,22 @@
     project(mix.astype(BF16), proj, me[0], [outs[0], outs[1].at[aud_rows:, :], *outs[2:]])
 
 
-def add(*refs):
-    terms, vid_out, aud_out = refs[:-2], refs[-2], refs[-1]
-    count = len(terms) // 2 + 1
+def add_audio(*refs):
+    *terms, out = refs
+    total = terms[0][...]
+    for term in terms[1:]:
+        total += term[...].astype(F32)
+    out[...] = total
+
+
+def add(aud_part, core, *refs):
+    *vid_terms, aud_out, vid_out = refs
     aud_rows = aud_out.shape[0]
-    core = terms[count - 1][...].astype(F32)
-    vid = terms[0][...] + core[aud_rows:]
-    aud = terms[count][...] + core[:aud_rows]
-    for vid_term, aud_term in zip(terms[1 : count - 1], terms[count + 1 :]):
-        vid += vid_term[...].astype(F32)
-        aud += aud_term[:aud_rows].astype(F32)
+    aud_out[...] = (aud_part[...] + core[:aud_rows].astype(F32)).astype(BF16)
+    vid = vid_terms[0][...] + core[aud_rows:].astype(F32)
+    for term in vid_terms[1:]:
+        vid += term[...].astype(F32)
     vid_out[...] = vid.astype(BF16)
-    aud_out[...] = aud.astype(BF16)
 
 
 def call(body, out_shape, args, in_specs=None, scratch=(), cost=COST):
@@ -288,8 +292,7 @@
     )
     aud_terms = call(
         lambda me, proj, *refs: project_audio(me, proj, refs[:aud_count], refs[aud_count + 1 :]),
-        [shape(aud_rows, step, dtype=F32), shape(aud_rows, step)]
-        + [shape(aud_rows + vid_rows + 8, step)] * (peers - 2),
+        [shape(aud_rows, step, dtype=F32)] + [shape(aud_rows, step)] * (peers - 1),
         [me, audio_proj, *rows, mix_log[0]],
         in_specs=[smem, vmem] + [vmem] * aud_count + [pl.BlockSpec(memory_space=pl.ANY)],
         cost=COST_A,
@@ -303,16 +306,17 @@
         [me, video_proj, *mix_log, aud_terms[1], *cols],
         in_specs=[smem] + [vmem] * (len(cols) + 4),
     )
-    vid_got = [vid_terms[0]] + [
-        swap(vid_terms[k], "head", k) for k in (*range(2, peers), 1)
-    ]
-    aud_got = [aud_terms[0]] + [
-        swap(aud_terms[k], "head", k) for k in reversed(range(2, peers))
-    ]
-    vid_out, aud_out = call(
-        add, [shape(vid_rows, step), shape(aud_rows, step)], vid_got + aud_got
-    )
-    return aud_out, vid_out
+    vid_got = [swap(vid_terms[k], "head", k) for k in range(2, peers)]
+    core_got = swap(vid_terms[1], "head", 1)
+    aud_got = [swap(aud_terms[k], "head", k) for k in reversed(range(2, peers))]
+    aud_part = call(add_audio, [shape(aud_rows, step, dtype=F32)], [aud_terms[0], *aud_got])[0]
+    return tuple(
+        call(
+            add,
+            [shape(aud_rows, step), shape(vid_rows, step)],
+            [aud_part, core_got, vid_terms[0], *vid_got],
+        )
+    )
 
 
 def solution(mesh):

time: 25.8 us -> 25.8 us (level)
    pallas_call x7 -> x8, Pallas kernels: 3.27 us -> 3.27 us  [call(): pl.pallas_call(body, out_shape=out_shape, in_specs=in_specs or [vmem] * l...]
  transfers between devices with their start and end apart: 13 -> 13, of which waited for: 5 -> 7; matrix products, arithmetic and copies ran while one was open for 0% -> 0% of each run, Pallas kernels for 7% -> 7%
where the time goes in v11:
time: 25.8 us; the launch traced here: 25.6 us
  starting transfers between devices  16.2 us (63%)
  waiting for transfers between devices  5.43 us (21%)
  Pallas kernels  3.27 us (13%)
  between operations  0.69 us (3%)
    ppermute x13, starting transfers between devices, swap(): lax.ppermute(block, axis, [(i, i ^ distance) for i in range(lax.axis_size...  16.2 us
    ppermute x13, waiting for transfers between devices, swap(): lax.ppermute(block, axis, [(i, i ^ distance) for i in range(lax.axis_size...  5.43 us
    pallas_call x8, Pallas kernels, call(): pl.pallas_call(body, out_shape=out_shape, in_specs=in_specs or [vmem] * l...  3.27 us
  transfers between devices with their start and end apart: 13, of which 7 were waited for; matrix products, arithmetic and copies ran while one was open for 0% of the time, Pallas kernels for 7%

profile of v11, /device:TPU:0, one launch (start us, length us, event | category | flops | bytes accessed | tf_op | source)
XLA Modules:
  0.0 25.6 jit_solution(14279509762872942658)
XLA Ops:
  0.6 0.9 %shard_map.77 = (bf16[2,128,256]{2,1,0:T(8,128)(2,1)S(1)}, bf16[2,24,256]{2,1,0:T(8,128)(2,1)S(1)}) custom-call(bf16[128,256]{1,0:T(8,128)(2,1)} %aud_ref.1, bf16[128,256]{1,0:T(8,128)(2,1)} %aud_val.1, bf16[24,256]{1,0:T(8,128)(2,1)} %vid_ref.1, bf16[24,256]{1,0:T(8,128)(2,1)} %vid_val.1), custom_call_target="tpu_custom_call" | custom-call | flops 5000000000 | tf_op jit(solution)/shard_map/pallas_call | solution.py:219
  1.5 3.0 %collective-permute-start = (bf16[2,128,256]{2,1,0:T(8,128)(2,1)S(1)}, bf16[2,128,256]{2,1,0:T(8,128)(2,1)S(1)}, u32[]{:S(2)}, u32[]{:S(2)}) collective-permute-start(bf16[2,128,256]{2,1,0:T(8,128)(2,1)S(1)} %get-tuple-element.21.refs_1_), channel_id=1, source_target_pairs={{0,4},{4,0},{8,12},{12,8},{16,20},{20,16},{24,28},{28,24},{1,5},{5... | collective-permute-start | bytes 393224 | tf_op jit(solution)/shard_map/ppermute | solution.py:235
  4.6 2.6 %collective-permute-start.3 = (bf16[2,24,256]{2,1,0:T(8,128)(2,1)S(1)}, bf16[2,24,256]{2,1,0:T(8,128)(2,1)S(1)}, u32[]{:S(2)}, u32[]{:S(2)}) collective-permute-start(bf16[2,24,256]{2,1,0:T(8,128)(2,1)S(1)} %get-tuple-element.22.refs_4_), channel_id=1, source_target_pairs={{0,16},{4,20},{8,24},{12,28},{16,0},{20,4},{24,8},{28,12},{1,17},{... | collective-permute-start | bytes 73736 | tf_op jit(solution)/shard_map/ppermute | solution.py:235
  7.1 1.3 %collective-permute-start.1 = (bf16[2,24,256]{2,1,0:T(8,128)(2,1)S(1)}, bf16[2,24,256]{2,1,0:T(8,128)(2,1)S(1)}, u32[]{:S(2)}, u32[]{:S(2)}) collective-permute-start(bf16[2,24,256]{2,1,0:T(8,128)(2,1)S(1)} %get-tuple-element.22.refs_4_), channel_id=1, source_target_pairs={{0,24},{4,28},{8,16},{12,20},{16,8},{20,12},{24,0},{28,4},{1,25},{... | collective-permute-start | bytes 73736 | tf_op jit(solution)/shard_map/ppermute | solution.py:235
  8.5 0.2 collective-permute-start.2
  8.7 0.6 %collective-permute-done.3.refs_2_.refs_5_ = bf16[2,24,256]{2,1,0:T(8,128)(2,1)S(1)} collective-permute-done((bf16[2,24,256]{2,1,0:T(8,128)(2,1)S(1)}, bf16[2,24,256]{2,1,0:T(8,128)(2,1)S(1)}, u32[]{:S(2)}, u32[]{:S(2)}) %collective-permute-start.3) | collective-permute-done | bytes 24608 | tf_op jit(solution)/shard_map/ppermute | solution.py:235
  9.3 0.4 %shard_map.78 = (bf16[24,384]{1,0:T(8,128)(2,1)S(1)}, f32[4,24,256]{2,1,0:T(8,128)S(1)}) custom-call(bf16[2,128,256]{2,1,0:T(8,128)(2,1)S(1)} %collective-permute-done.refs_0_, bf16[2,128,256]{2,1,0:T(8,128)(2,1)S(1)} %get-tuple-element.21.refs_1_, bf16[2,24,256]{2,1,0:T(8,128)(2,1)S(1)} %collective-permute-done.3.refs_2_.refs_5_), custom_call_target="tpu_custom_call" | custom-call | flops 5000000000 | tf_op jit(solution)/shard_map/pallas_call | solution.py:219
  9.7 2.8 %collective-permute-start.5 = (bf16[24,384]{1,0:T(8,128)(2,1)S(1)}, bf16[24,384]{1,0:T(8,128)(2,1)S(1)}, u32[]{:S(2)}, u32[]{:S(2)}) collective-permute-start(bf16[24,384]{1,0:T(8,128)(2,1)S(1)} %get-tuple-element.27), channel_id=1, source_target_pairs={{0,16},{4,20},{8,24},{12,28},{16,0},{20,4},{24,8},{28,12},{1,17},{... | collective-permute-start | bytes 55304 | tf_op jit(solution)/shard_map/ppermute | solution.py:235
  12.5 0.2 collective-permute-done.1.refs_2_
  12.8 0.5 %shard_map.79 = (bf16[272,128]{1,0:T(8,128)(2,1)S(1)}, bf16[272,128]{1,0:T(8,128)(2,1)S(1)}, bf16[24,384]{1,0:T(8,128)(2,1)S(1)}, bf16[24,384]{1,0:T(8,128)(2,1)S(1)}, bf16[24,384]{1,0:T(8,128)(2,1)S(1)}) custom-call(bf16[2,128,256]{2,1,0:T(8,128)(2,1)S(1)} %collective-permute-done.refs_0_, bf16[2,128,256]{2,1,0:T(8,128)(2,1)S(1)} %get-tuple-element.21.refs_1_, ...), custom_call_target="tpu_custom_call" | custom-call | flops 5000000000 | tf_op jit(solution)/shard_map/pallas_call | solution.py:219
  13.3 0.6 %collective-permute-start.4 = (bf16[272,128]{1,0:T(8,128)(2,1)S(1)}, bf16[272,128]{1,0:T(8,128)(2,1)S(1)}, u32[]{:S(2)}, u32[]{:S(2)}) collective-permute-start(bf16[272,128]{1,0:T(8,128)(2,1)S(1)} %get-tuple-element.24), channel_id=1, source_target_pairs={{0,4},{4,0},{8,12},{12,8},{16,20},{20,16},{24,28},{28,24},{1,5},{5... | collective-permute-start | bytes 208904 | tf_op jit(solution)/shard_map/ppermute | solution.py:235
  13.9 2.0 %collective-permute-start.8 = (bf16[24,384]{1,0:T(8,128)(2,1)S(1)}, bf16[24,384]{1,0:T(8,128)(2,1)S(1)}, u32[]{:S(2)}, u32[]{:S(2)}) collective-permute-start(bf16[24,384]{1,0:T(8,128)(2,1)S(1)} %get-tuple-element.34), channel_id=1, source_target_pairs={{0,24},{4,28},{8,16},{12,20},{16,8},{20,12},{24,0},{28,4},{1,25},{... | collective-permute-start | bytes 55304 | tf_op jit(solution)/shard_map/ppermute | solution.py:235
  15.9 0.1 shard_map.80
  16.1 1.6 %collective-permute-done.4.refs_0_ = bf16[272,128]{1,0:T(8,128)(2,1)S(1)} collective-permute-done((bf16[272,128]{1,0:T(8,128)(2,1)S(1)}, bf16[272,128]{1,0:T(8,128)(2,1)S(1)}, u32[]{:S(2)}, u32[]{:S(2)}) %collective-permute-start.4) | collective-permute-done | bytes 69664 | tf_op jit(solution)/shard_map/ppermute | solution.py:235
  17.7 0.3 %shard_map.81 = (f32[128,256]{1,0:T(8,128)S(1)}, bf16[128,256]{1,0:T(8,128)(2,1)S(1)}, bf16[128,256]{1,0:T(8,128)(2,1)S(1)}, bf16[128,256]{1,0:T(8,128)(2,1)S(1)}) custom-call(s32[1]{0:T(128)} %bitcast.me, bf16[256,1024]{1,0:T(8,128)(2,1)S(1)} %copy-done, bf16[272,128]{1,0:T(8,128)(2,1)S(1)} %collective-permute-done.4.refs_0_, ...), custom_call_target="tpu_custom_call" | custom-call | flops 1000000000 | tf_op jit(solution)/shard_map/pallas_call | solution.py:219
  18.1 1.6 %collective-permute-start.7 = (bf16[128,256]{1,0:T(8,128)(2,1)S(1)}, bf16[128,256]{1,0:T(8,128)(2,1)S(1)}, u32[]{:S(2)}, u32[]{:S(2)}) collective-permute-start(bf16[128,256]{1,0:T(8,128)(2,1)S(1)} %get-tuple-element.31), channel_id=1, source_target_pairs={{0,2},{1,3},{2,0},{3,1},{4,6},{5,7},{6,4},{7,5},{8,10},{9,11},{10,... | collective-permute-start | bytes 196616 | tf_op jit(solution)/shard_map/ppermute | solution.py:235
  19.7 0.3 %shard_map.83 = (f32[24,256]{1,0:T(8,128)S(1)}, bf16[152,256]{1,0:T(8,128)(2,1)S(1)}, bf16[24,256]{1,0:T(8,128)(2,1)S(1)}, bf16[24,256]{1,0:T(8,128)(2,1)S(1)}) custom-call(s32[1]{0:T(128)} %bitcast.me, bf16[256,1024]{1,0:T(8,128)(2,1)S(1)} %copy-done.1, f32[24,256]{1,0:T(8,128)S(1)} %get-tuple-element.28.refs_2_.mix, f32[24,256]{1,0:T(8,128)S(1)} %get-tuple-element.32.log, ...), custom_call_target="tpu_custom_call" | custom-call | flops 5000000000 | tf_op jit(solution)/shard_map/pallas_call | solution.py:219
  20.0 0.3 %collective-permute-start.10 = (bf16[152,256]{1,0:T(8,128)(2,1)S(1)}, bf16[152,256]{1,0:T(8,128)(2,1)S(1)}, u32[]{:S(2)}, u32[]{:S(2)}) collective-permute-start(bf16[152,256]{1,0:T(8,128)(2,1)S(1)} %get-tuple-element.36), channel_id=1, source_target_pairs={{0,1},{1,0},{2,3},{3,2},{4,5},{5,4},{6,7},{7,6},{8,9},{9,8},{10,11... | collective-permute-start | bytes 233480 | tf_op jit(solution)/shard_map/ppermute | solution.py:235
  20.3 1.5 %collective-permute-start.11 = (bf16[24,256]{1,0:T(8,128)(2,1)S(1)}, bf16[24,256]{1,0:T(8,128)(2,1)S(1)}, u32[]{:S(2)}, u32[]{:S(2)}) collective-permute-start(bf16[24,256]{1,0:T(8,128)(2,1)S(1)} %get-tuple-element.38), channel_id=1, source_target_pairs={{0,2},{1,3},{2,0},{3,1},{4,6},{5,7},{6,4},{7,5},{8,10},{9,11},{10,... | collective-permute-start | bytes 36872 | tf_op jit(solution)/shard_map/ppermute | solution.py:235
  21.9 0.5 %collective-permute-done.6.refs_1_ = bf16[128,256]{1,0:T(8,128)(2,1)S(1)} collective-permute-done((bf16[128,256]{1,0:T(8,128)(2,1)S(1)}, bf16[128,256]{1,0:T(8,128)(2,1)S(1)}, u32[]{:S(2)}, u32[]{:S(2)}) %collective-permute-start.6) | collective-permute-done | bytes 65568 | tf_op jit(solution)/shard_map/ppermute | solution.py:235
  22.4 1.6 %collective-permute-done.7.refs_2_ = bf16[128,256]{1,0:T(8,128)(2,1)S(1)} collective-permute-done((bf16[128,256]{1,0:T(8,128)(2,1)S(1)}, bf16[128,256]{1,0:T(8,128)(2,1)S(1)}, u32[]{:S(2)}, u32[]{:S(2)}) %collective-permute-start.7) | collective-permute-done | bytes 65568 | tf_op jit(solution)/shard_map/ppermute | solution.py:235
  24.0 0.2 collective-permute-done.11.refs_1_
  24.1 0.8 %collective-permute-done.12.refs_2_ = bf16[24,256]{1,0:T(8,128)(2,1)S(1)} collective-permute-done((bf16[24,256]{1,0:T(8,128)(2,1)S(1)}, bf16[24,256]{1,0:T(8,128)(2,1)S(1)}, u32[]{:S(2)}, u32[]{:S(2)}) %collective-permute-start.12) | collective-permute-done | bytes 12320 | tf_op jit(solution)/shard_map/ppermute | solution.py:235
  24.9 0.6 %shard_map.84 = (bf16[128,256]{1,0:T(8,128)(2,1)}, bf16[24,256]{1,0:T(8,128)(2,1)}) custom-call(f32[128,256]{1,0:T(8,128)S(1)} %shard_map.82.aud_part, bf16[152,256]{1,0:T(8,128)(2,1)S(1)} %collective-permute-done.10.core, f32[24,256]{1,0:T(8,128)S(1)} %get-tuple-element.37.refs_0_, bf16[24,256]{1,0:T(8,128)(2,1)S(1)} %collective-permute-done.11.refs_1_, ...), custom_call_target="tpu_custom_call" | custom-call | flops 5000000000 | tf_op jit(solution)/shard_map/pallas_call | solution.py:219
  (14 shorter events, 0.3 us)
Async XLA Ops:
  1.5 7.7 %collective-permute-start = (bf16[2,128,256]{2,1,0:T(8,128)(2,1)S(1)}, bf16[2,128,256]{2,1,0:T(8,128)(2,1)S(1)}, u32[]{:S(2)}, u32[]{:S(2)}) collective-permute-start(bf16[2,128,256]{2,1,0:T(8,128)(2,1)S(1)} %get-tuple-element.21.refs_1_), channel_id=1, source_target_pairs={{0,4},{4,0},{8,12},{12,8},{16,20},{20,16},{24,28},{28,24},{1,5},{5... | collective-permute-start | bytes 393224 | tf_op jit(solution)/shard_map/ppermute | solution.py:235
  4.6 4.7 %collective-permute-start.3 = (bf16[2,24,256]{2,1,0:T(8,128)(2,1)S(1)}, bf16[2,24,256]{2,1,0:T(8,128)(2,1)S(1)}, u32[]{:S(2)}, u32[]{:S(2)}) collective-permute-start(bf16[2,24,256]{2,1,0:T(8,128)(2,1)S(1)} %get-tuple-element.22.refs_4_), channel_id=1, source_target_pairs={{0,16},{4,20},{8,24},{12,28},{16,0},{20,4},{24,8},{28,12},{1,17},{... | collective-permute-start | bytes 73736 | tf_op jit(solution)/shard_map/ppermute | solution.py:235
  7.1 5.6 %collective-permute-start.1 = (bf16[2,24,256]{2,1,0:T(8,128)(2,1)S(1)}, bf16[2,24,256]{2,1,0:T(8,128)(2,1)S(1)}, u32[]{:S(2)}, u32[]{:S(2)}) collective-permute-start(bf16[2,24,256]{2,1,0:T(8,128)(2,1)S(1)} %get-tuple-element.22.refs_4_), channel_id=1, source_target_pairs={{0,24},{4,28},{8,16},{12,20},{16,8},{20,12},{24,0},{28,4},{1,25},{... | collective-permute-start | bytes 73736 | tf_op jit(solution)/shard_map/ppermute | solution.py:235
  8.5 4.3 %collective-permute-start.2 = (bf16[2,24,256]{2,1,0:T(8,128)(2,1)S(1)}, bf16[2,24,256]{2,1,0:T(8,128)(2,1)S(1)}, u32[]{:S(2)}, u32[]{:S(2)}) collective-permute-start(bf16[2,24,256]{2,1,0:T(8,128)(2,1)S(1)} %get-tuple-element.22.refs_4_), channel_id=1, source_target_pairs={{0,8},{4,12},{8,0},{12,4},{16,24},{20,28},{24,16},{28,20},{1,9},{5... | collective-permute-start | bytes 73736 | tf_op jit(solution)/shard_map/ppermute | solution.py:235
  9.7 6.2 %collective-permute-start.5 = (bf16[24,384]{1,0:T(8,128)(2,1)S(1)}, bf16[24,384]{1,0:T(8,128)(2,1)S(1)}, u32[]{:S(2)}, u32[]{:S(2)}) collective-permute-start(bf16[24,384]{1,0:T(8,128)(2,1)S(1)} %get-tuple-element.27), channel_id=1, source_target_pairs={{0,16},{4,20},{8,24},{12,28},{16,0},{20,4},{24,8},{28,12},{1,17},{... | collective-permute-start | bytes 55304 | tf_op jit(solution)/shard_map/ppermute | solution.py:235
  12.8 3.2 %copy-start = (bf16[256,1024]{1,0:T(8,128)(2,1)S(1)}, bf16[256,1024]{1,0:T(8,128)(2,1)}, u32[]{:S(2)}) copy-start(bf16[256,1024]{1,0:T(8,128)(2,1)} %proj.2) | copy-start | bytes 1572868
  13.3 4.4 %collective-permute-start.4 = (bf16[272,128]{1,0:T(8,128)(2,1)S(1)}, bf16[272,128]{1,0:T(8,128)(2,1)S(1)}, u32[]{:S(2)}, u32[]{:S(2)}) collective-permute-start(bf16[272,128]{1,0:T(8,128)(2,1)S(1)} %get-tuple-element.24), channel_id=1, source_target_pairs={{0,4},{4,0},{8,12},{12,8},{16,20},{20,16},{24,28},{28,24},{1,5},{5... | collective-permute-start | bytes 208904 | tf_op jit(solution)/shard_map/ppermute | solution.py:235
  13.9 5.7 %collective-permute-start.8 = (bf16[24,384]{1,0:T(8,128)(2,1)S(1)}, bf16[24,384]{1,0:T(8,128)(2,1)S(1)}, u32[]{:S(2)}, u32[]{:S(2)}) collective-permute-start(bf16[24,384]{1,0:T(8,128)(2,1)S(1)} %get-tuple-element.34), channel_id=1, source_target_pairs={{0,24},{4,28},{8,16},{12,20},{16,8},{20,12},{24,0},{28,4},{1,25},{... | collective-permute-start | bytes 55304 | tf_op jit(solution)/shard_map/ppermute | solution.py:235
  15.9 3.8 %collective-permute-start.9 = (bf16[24,384]{1,0:T(8,128)(2,1)S(1)}, bf16[24,384]{1,0:T(8,128)(2,1)S(1)}, u32[]{:S(2)}, u32[]{:S(2)}) collective-permute-start(bf16[24,384]{1,0:T(8,128)(2,1)S(1)} %get-tuple-element.35), channel_id=1, source_target_pairs={{0,8},{4,12},{8,0},{12,4},{16,24},{20,28},{24,16},{28,20},{1,9},{5... | collective-permute-start | bytes 55304 | tf_op jit(solution)/shard_map/ppermute | solution.py:235
  17.7 2.0 %copy-start.1 = (bf16[256,1024]{1,0:T(8,128)(2,1)S(1)}, bf16[256,1024]{1,0:T(8,128)(2,1)}, u32[]{:S(2)}) copy-start(bf16[256,1024]{1,0:T(8,128)(2,1)} %proj.3) | copy-start | bytes 1572868
  18.0 4.4 %collective-permute-start.6 = (bf16[128,256]{1,0:T(8,128)(2,1)S(1)}, bf16[128,256]{1,0:T(8,128)(2,1)S(1)}, u32[]{:S(2)}, u32[]{:S(2)}) collective-permute-start(bf16[128,256]{1,0:T(8,128)(2,1)S(1)} %get-tuple-element.30), channel_id=1, source_target_pairs={{0,3},{1,2},{2,1},{3,0},{4,7},{5,6},{6,5},{7,4},{8,11},{9,10},{10,... | collective-permute-start | bytes 196616 | tf_op jit(solution)/shard_map/ppermute | solution.py:235
  18.1 5.9 %collective-permute-start.7 = (bf16[128,256]{1,0:T(8,128)(2,1)S(1)}, bf16[128,256]{1,0:T(8,128)(2,1)S(1)}, u32[]{:S(2)}, u32[]{:S(2)}) collective-permute-start(bf16[128,256]{1,0:T(8,128)(2,1)S(1)} %get-tuple-element.31), channel_id=1, source_target_pairs={{0,2},{1,3},{2,0},{3,1},{4,6},{5,7},{6,4},{7,5},{8,10},{9,11},{10,... | collective-permute-start | bytes 196616 | tf_op jit(solution)/shard_map/ppermute | solution.py:235
  20.0 4.9 %collective-permute-start.10 = (bf16[152,256]{1,0:T(8,128)(2,1)S(1)}, bf16[152,256]{1,0:T(8,128)(2,1)S(1)}, u32[]{:S(2)}, u32[]{:S(2)}) collective-permute-start(bf16[152,256]{1,0:T(8,128)(2,1)S(1)} %get-tuple-element.36), channel_id=1, source_target_pairs={{0,1},{1,0},{2,3},{3,2},{4,5},{5,4},{6,7},{7,6},{8,9},{9,8},{10,11... | collective-permute-start | bytes 233480 | tf_op jit(solution)/shard_map/ppermute | solution.py:235
  20.3 3.8 %collective-permute-start.11 = (bf16[24,256]{1,0:T(8,128)(2,1)S(1)}, bf16[24,256]{1,0:T(8,128)(2,1)S(1)}, u32[]{:S(2)}, u32[]{:S(2)}) collective-permute-start(bf16[24,256]{1,0:T(8,128)(2,1)S(1)} %get-tuple-element.38), channel_id=1, source_target_pairs={{0,2},{1,3},{2,0},{3,1},{4,6},{5,7},{6,4},{7,5},{8,10},{9,11},{10,... | collective-permute-start | bytes 36872 | tf_op jit(solution)/shard_map/ppermute | solution.py:235
  21.8 3.1 %collective-permute-start.12 = (bf16[24,256]{1,0:T(8,128)(2,1)S(1)}, bf16[24,256]{1,0:T(8,128)(2,1)S(1)}, u32[]{:S(2)}, u32[]{:S(2)}) collective-permute-start(bf16[24,256]{1,0:T(8,128)(2,1)S(1)} %get-tuple-element.39), channel_id=1, source_target_pairs={{0,3},{1,2},{2,1},{3,0},{4,7},{5,6},{6,5},{7,4},{8,11},{9,10},{10,... | collective-permute-start | bytes 36872 | tf_op jit(solution)/shard_map/ppermute | solution.py:235

commit v12 on v11

--- a/solution.py
+++ b/solution.py
@@ -100,21 +100,21 @@
         put_rows(out, mix[:, cols], log[:, cols])
 
 
-def attend_first(*refs):
-    *auds, vid, col_out, scores_out = refs
+def attend_first(aud_count, *refs):
+    auds, vids, (scores_out, *col_outs) = refs[:aud_count], refs[aud_count : aud_count + 2], refs[aud_count + 2 :]
     queries, aud_vals = both(auds)
-    scores = tile_scores(queries, [vid])
+    scores = tile_scores(queries, vids)
     scores_out[...] = scores
-    column_states(scores, aud_vals, [col_out])
+    column_states(scores, aud_vals, col_outs)
 
 
 def attend(aud_count, vid_count, *refs):
     auds, vids, refs = refs[:aud_count], refs[aud_count : aud_count + vid_count], refs[aud_count + vid_count :]
-    first, first_scores, row_outs, col_outs = refs[0], refs[1], refs[2 : 2 + aud_count], refs[2 + aud_count :]
+    firsts, first_scores, row_outs, col_outs = refs[:2], refs[2], refs[3 : 3 + aud_count], refs[3 + aud_count :]
     queries, aud_vals = both(auds)
     scores = tile_scores(queries, vids)
     column_states(scores, aud_vals, col_outs)
-    vals = jnp.concatenate([ref[1].astype(F32) for ref in (first, *vids)], axis=0)
+    vals = jnp.concatenate([ref[1].astype(F32) for ref in (*firsts, *vids)], axis=0)
     row_states(jnp.concatenate([first_scores[...], scores], axis=1), vals, row_outs)
 
 
@@ -268,18 +268,18 @@
     auds = [swap(aud, "seq", k) for k in range(1, aud_count)] + [aud]
     vids = {k: swap(vid, "seq", k * aud_count) for k in (early, *late)}
     state = shape(vid_rows, width + LANES)
-    first_state, scores = call(
-        attend_first,
-        [state, shape(heads, vid_rows, aud_count * aud_rows, dtype=F32)],
-        [*auds, vids[early]],
+    scores, first_state, own_state = call(
+        functools.partial(attend_first, aud_count),
+        [shape(heads, 2 * vid_rows, aud_count * aud_rows, dtype=F32), state, state],
+        [*auds, vids[early], vid],
     )
     states = call(
-        functools.partial(attend, aud_count, len(late) + 1),
-        [shape(width + log_rows, aud_rows)] * aud_count + [state] * (len(late) + 1),
-        [*auds, *(vids[k] for k in late), vid, vids[early], scores],
+        functools.partial(attend, aud_count, len(late)),
+        [shape(width + log_rows, aud_rows)] * aud_count + [state] * len(late),
+        [*auds, *(vids[k] for k in late), vids[early], vid, scores],
     )
     rows = [swap(states[k - 1], "seq", k) for k in range(1, aud_count)] + [states[aud_count - 1]]
-    states = dict(zip((early, *late, 0), (first_state, *states[aud_count:])))
+    states = dict(zip((early, 0, *late), (first_state, own_state, *states[aud_count:])))
     cols = [swap(states[k], "seq", k * aud_count) for k in (early, *late)] + [states[0]]
 
     me = lax.axis_index("head").astype(jnp.int32).reshape(1)

time: 25.8 us -> 25.7 us (level)
  no operation moved by 1% of the time
where the time goes in v12:
time: 25.7 us; the launch traced here: 25.5 us
  starting transfers between devices  16.2 us (63%)
  waiting for transfers between devices  5.4 us (21%)
  Pallas kernels  3.26 us (13%)
  between operations  0.7 us (3%)
    ppermute x13, starting transfers between devices, swap(): lax.ppermute(block, axis, [(i, i ^ distance) for i in range(lax.axis_size...  16.2 us
    ppermute x13, waiting for transfers between devices, swap(): lax.ppermute(block, axis, [(i, i ^ distance) for i in range(lax.axis_size...  5.4 us
    pallas_call x8, Pallas kernels, call(): pl.pallas_call(body, out_shape=out_shape, in_specs=in_specs or [vmem] * l...  3.26 us
  transfers between devices with their start and end apart: 13, of which 7 were waited for; matrix products, arithmetic and copies ran while one was open for 0% of the time, Pallas kernels for 7%

profile of v12, /device:TPU:0, one launch (start us, length us, event | category | flops | bytes accessed | tf_op | source)
XLA Modules:
  0.0 25.5 jit_solution(7566765463283235713)
XLA Ops:
  0.6 0.9 %shard_map.77 = (bf16[2,128,256]{2,1,0:T(8,128)(2,1)S(1)}, bf16[2,24,256]{2,1,0:T(8,128)(2,1)S(1)}) custom-call(bf16[128,256]{1,0:T(8,128)(2,1)} %aud_ref.1, bf16[128,256]{1,0:T(8,128)(2,1)} %aud_val.1, bf16[24,256]{1,0:T(8,128)(2,1)} %vid_ref.1, bf16[24,256]{1,0:T(8,128)(2,1)} %vid_val.1), custom_call_target="tpu_custom_call" | custom-call | flops 5000000000 | tf_op jit(solution)/shard_map/pallas_call | solution.py:219
  1.5 3.0 %collective-permute-start = (bf16[2,128,256]{2,1,0:T(8,128)(2,1)S(1)}, bf16[2,128,256]{2,1,0:T(8,128)(2,1)S(1)}, u32[]{:S(2)}, u32[]{:S(2)}) collective-permute-start(bf16[2,128,256]{2,1,0:T(8,128)(2,1)S(1)} %get-tuple-element.21.refs_1_), channel_id=1, source_target_pairs={{0,4},{4,0},{8,12},{12,8},{16,20},{20,16},{24,28},{28,24},{1,5},{5... | collective-permute-start | bytes 393224 | tf_op jit(solution)/shard_map/ppermute | solution.py:235
  4.6 2.6 %collective-permute-start.3 = (bf16[2,24,256]{2,1,0:T(8,128)(2,1)S(1)}, bf16[2,24,256]{2,1,0:T(8,128)(2,1)S(1)}, u32[]{:S(2)}, u32[]{:S(2)}) collective-permute-start(bf16[2,24,256]{2,1,0:T(8,128)(2,1)S(1)} %get-tuple-element.22.refs_3_.refs_5_), channel_id=1, source_target_pairs={{0,16},{4,20},{8,24},{12,28},{16,0},{20,4},{24,8},{28,12},{1,17},{... | collective-permute-start | bytes 73736 | tf_op jit(solution)/shard_map/ppermute | solution.py:235
  7.1 1.3 %collective-permute-start.1 = (bf16[2,24,256]{2,1,0:T(8,128)(2,1)S(1)}, bf16[2,24,256]{2,1,0:T(8,128)(2,1)S(1)}, u32[]{:S(2)}, u32[]{:S(2)}) collective-permute-start(bf16[2,24,256]{2,1,0:T(8,128)(2,1)S(1)} %get-tuple-element.22.refs_3_.refs_5_), channel_id=1, source_target_pairs={{0,24},{4,28},{8,16},{12,20},{16,8},{20,12},{24,0},{28,4},{1,25},{... | collective-permute-start | bytes 73736 | tf_op jit(solution)/shard_map/ppermute | solution.py:235
  8.5 0.2 collective-permute-start.2
  8.7 0.6 %collective-permute-done.3.refs_2_.refs_4_ = bf16[2,24,256]{2,1,0:T(8,128)(2,1)S(1)} collective-permute-done((bf16[2,24,256]{2,1,0:T(8,128)(2,1)S(1)}, bf16[2,24,256]{2,1,0:T(8,128)(2,1)S(1)}, u32[]{:S(2)}, u32[]{:S(2)}) %collective-permute-start.3) | collective-permute-done | bytes 24608 | tf_op jit(solution)/shard_map/ppermute | solution.py:235
  9.3 0.4 %shard_map.78 = (f32[4,48,256]{2,1,0:T(8,128)S(1)}, bf16[24,384]{1,0:T(8,128)(2,1)S(1)}, bf16[24,384]{1,0:T(8,128)(2,1)S(1)}) custom-call(bf16[2,128,256]{2,1,0:T(8,128)(2,1)S(1)} %collective-permute-done.refs_0_, bf16[2,128,256]{2,1,0:T(8,128)(2,1)S(1)} %get-tuple-element.21.refs_1_, bf16[2,24,256]{2,1,0:T(8,128)(2,1)S(1)} %collective-permute-done.3.refs_2_.refs_4_, ...), custom_call_target="tpu_custom_call" | custom-call | flops 5000000000 | tf_op jit(solution)/shard_map/pallas_call | solution.py:219
  9.7 2.8 %collective-permute-start.5 = (bf16[24,384]{1,0:T(8,128)(2,1)S(1)}, bf16[24,384]{1,0:T(8,128)(2,1)S(1)}, u32[]{:S(2)}, u32[]{:S(2)}) collective-permute-start(bf16[24,384]{1,0:T(8,128)(2,1)S(1)} %get-tuple-element.27), channel_id=1, source_target_pairs={{0,16},{4,20},{8,24},{12,28},{16,0},{20,4},{24,8},{28,12},{1,17},{... | collective-permute-start | bytes 55304 | tf_op jit(solution)/shard_map/ppermute | solution.py:235
  12.5 0.2 collective-permute-done.1.refs_2_
  12.8 0.5 %shard_map.79 = (bf16[272,128]{1,0:T(8,128)(2,1)S(1)}, bf16[272,128]{1,0:T(8,128)(2,1)S(1)}, bf16[24,384]{1,0:T(8,128)(2,1)S(1)}, bf16[24,384]{1,0:T(8,128)(2,1)S(1)}) custom-call(bf16[2,128,256]{2,1,0:T(8,128)(2,1)S(1)} %collective-permute-done.refs_0_, bf16[2,128,256]{2,1,0:T(8,128)(2,1)S(1)} %get-tuple-element.21.refs_1_, ...), custom_call_target="tpu_custom_call" | custom-call | flops 5000000000 | tf_op jit(solution)/shard_map/pallas_call | solution.py:219
  13.3 0.6 %collective-permute-start.4 = (bf16[272,128]{1,0:T(8,128)(2,1)S(1)}, bf16[272,128]{1,0:T(8,128)(2,1)S(1)}, u32[]{:S(2)}, u32[]{:S(2)}) collective-permute-start(bf16[272,128]{1,0:T(8,128)(2,1)S(1)} %get-tuple-element.24), channel_id=1, source_target_pairs={{0,4},{4,0},{8,12},{12,8},{16,20},{20,16},{24,28},{28,24},{1,5},{5... | collective-permute-start | bytes 208904 | tf_op jit(solution)/shard_map/ppermute | solution.py:235
  13.9 2.0 %collective-permute-start.8 = (bf16[24,384]{1,0:T(8,128)(2,1)S(1)}, bf16[24,384]{1,0:T(8,128)(2,1)S(1)}, u32[]{:S(2)}, u32[]{:S(2)}) collective-permute-start(bf16[24,384]{1,0:T(8,128)(2,1)S(1)} %get-tuple-element.34), channel_id=1, source_target_pairs={{0,24},{4,28},{8,16},{12,20},{16,8},{20,12},{24,0},{28,4},{1,25},{... | collective-permute-start | bytes 55304 | tf_op jit(solution)/shard_map/ppermute | solution.py:235
  15.9 0.1 shard_map.80
  16.1 1.6 %collective-permute-done.4.refs_0_ = bf16[272,128]{1,0:T(8,128)(2,1)S(1)} collective-permute-done((bf16[272,128]{1,0:T(8,128)(2,1)S(1)}, bf16[272,128]{1,0:T(8,128)(2,1)S(1)}, u32[]{:S(2)}, u32[]{:S(2)}) %collective-permute-start.4) | collective-permute-done | bytes 69664 | tf_op jit(solution)/shard_map/ppermute | solution.py:235
  17.7 0.3 %shard_map.81 = (f32[128,256]{1,0:T(8,128)S(1)}, bf16[128,256]{1,0:T(8,128)(2,1)S(1)}, bf16[128,256]{1,0:T(8,128)(2,1)S(1)}, bf16[128,256]{1,0:T(8,128)(2,1)S(1)}) custom-call(s32[1]{0:T(128)} %bitcast.me, bf16[256,1024]{1,0:T(8,128)(2,1)S(1)} %copy-done, bf16[272,128]{1,0:T(8,128)(2,1)S(1)} %collective-permute-done.4.refs_0_, ...), custom_call_target="tpu_custom_call" | custom-call | flops 1000000000 | tf_op jit(solution)/shard_map/pallas_call | solution.py:219
  18.0 1.6 %collective-permute-start.7 = (bf16[128,256]{1,0:T(8,128)(2,1)S(1)}, bf16[128,256]{1,0:T(8,128)(2,1)S(1)}, u32[]{:S(2)}, u32[]{:S(2)}) collective-permute-start(bf16[128,256]{1,0:T(8,128)(2,1)S(1)} %get-tuple-element.31), channel_id=1, source_target_pairs={{0,2},{1,3},{2,0},{3,1},{4,6},{5,7},{6,4},{7,5},{8,10},{9,11},{10,... | collective-permute-start | bytes 196616 | tf_op jit(solution)/shard_map/ppermute | solution.py:235
  19.7 0.3 %shard_map.83 = (f32[24,256]{1,0:T(8,128)S(1)}, bf16[152,256]{1,0:T(8,128)(2,1)S(1)}, bf16[24,256]{1,0:T(8,128)(2,1)S(1)}, bf16[24,256]{1,0:T(8,128)(2,1)S(1)}) custom-call(s32[1]{0:T(128)} %bitcast.me, bf16[256,1024]{1,0:T(8,128)(2,1)S(1)} %copy-done.1, f32[24,256]{1,0:T(8,128)S(1)} %get-tuple-element.28.refs_2_.mix, f32[24,256]{1,0:T(8,128)S(1)} %get-tuple-element.32.log, ...), custom_call_target="tpu_custom_call" | custom-call | flops 5000000000 | tf_op jit(solution)/shard_map/pallas_call | solution.py:219
  20.0 0.3 %collective-permute-start.10 = (bf16[152,256]{1,0:T(8,128)(2,1)S(1)}, bf16[152,256]{1,0:T(8,128)(2,1)S(1)}, u32[]{:S(2)}, u32[]{:S(2)}) collective-permute-start(bf16[152,256]{1,0:T(8,128)(2,1)S(1)} %get-tuple-element.36), channel_id=1, source_target_pairs={{0,1},{1,0},{2,3},{3,2},{4,5},{5,4},{6,7},{7,6},{8,9},{9,8},{10,11... | collective-permute-start | bytes 233480 | tf_op jit(solution)/shard_map/ppermute | solution.py:235
  20.2 1.5 %collective-permute-start.11 = (bf16[24,256]{1,0:T(8,128)(2,1)S(1)}, bf16[24,256]{1,0:T(8,128)(2,1)S(1)}, u32[]{:S(2)}, u32[]{:S(2)}) collective-permute-start(bf16[24,256]{1,0:T(8,128)(2,1)S(1)} %get-tuple-element.38), channel_id=1, source_target_pairs={{0,2},{1,3},{2,0},{3,1},{4,6},{5,7},{6,4},{7,5},{8,10},{9,11},{10,... | collective-permute-start | bytes 36872 | tf_op jit(solution)/shard_map/ppermute | solution.py:235
  21.9 0.5 %collective-permute-done.6.refs_1_ = bf16[128,256]{1,0:T(8,128)(2,1)S(1)} collective-permute-done((bf16[128,256]{1,0:T(8,128)(2,1)S(1)}, bf16[128,256]{1,0:T(8,128)(2,1)S(1)}, u32[]{:S(2)}, u32[]{:S(2)}) %collective-permute-start.6) | collective-permute-done | bytes 65568 | tf_op jit(solution)/shard_map/ppermute | solution.py:235
  22.3 1.6 %collective-permute-done.7.refs_2_ = bf16[128,256]{1,0:T(8,128)(2,1)S(1)} collective-permute-done((bf16[128,256]{1,0:T(8,128)(2,1)S(1)}, bf16[128,256]{1,0:T(8,128)(2,1)S(1)}, u32[]{:S(2)}, u32[]{:S(2)}) %collective-permute-start.7) | collective-permute-done | bytes 65568 | tf_op jit(solution)/shard_map/ppermute | solution.py:235
  23.9 0.2 collective-permute-done.11.refs_1_
  24.1 0.8 %collective-permute-done.12.refs_2_ = bf16[24,256]{1,0:T(8,128)(2,1)S(1)} collective-permute-done((bf16[24,256]{1,0:T(8,128)(2,1)S(1)}, bf16[24,256]{1,0:T(8,128)(2,1)S(1)}, u32[]{:S(2)}, u32[]{:S(2)}) %collective-permute-start.12) | collective-permute-done | bytes 12320 | tf_op jit(solution)/shard_map/ppermute | solution.py:235
  24.9 0.6 %shard_map.84 = (bf16[128,256]{1,0:T(8,128)(2,1)}, bf16[24,256]{1,0:T(8,128)(2,1)}) custom-call(f32[128,256]{1,0:T(8,128)S(1)} %shard_map.82.aud_part, bf16[152,256]{1,0:T(8,128)(2,1)S(1)} %collective-permute-done.10.core, f32[24,256]{1,0:T(8,128)S(1)} %get-tuple-element.37.refs_0_, bf16[24,256]{1,0:T(8,128)(2,1)S(1)} %collective-permute-done.11.refs_1_, ...), custom_call_target="tpu_custom_call" | custom-call | flops 5000000000 | tf_op jit(solution)/shard_map/pallas_call | solution.py:219
  (14 shorter events, 0.3 us)
Async XLA Ops:
  1.5 7.7 %collective-permute-start = (bf16[2,128,256]{2,1,0:T(8,128)(2,1)S(1)}, bf16[2,128,256]{2,1,0:T(8,128)(2,1)S(1)}, u32[]{:S(2)}, u32[]{:S(2)}) collective-permute-start(bf16[2,128,256]{2,1,0:T(8,128)(2,1)S(1)} %get-tuple-element.21.refs_1_), channel_id=1, source_target_pairs={{0,4},{4,0},{8,12},{12,8},{16,20},{20,16},{24,28},{28,24},{1,5},{5... | collective-permute-start | bytes 393224 | tf_op jit(solution)/shard_map/ppermute | solution.py:235
  4.6 4.7 %collective-permute-start.3 = (bf16[2,24,256]{2,1,0:T(8,128)(2,1)S(1)}, bf16[2,24,256]{2,1,0:T(8,128)(2,1)S(1)}, u32[]{:S(2)}, u32[]{:S(2)}) collective-permute-start(bf16[2,24,256]{2,1,0:T(8,128)(2,1)S(1)} %get-tuple-element.22.refs_3_.refs_5_), channel_id=1, source_target_pairs={{0,16},{4,20},{8,24},{12,28},{16,0},{20,4},{24,8},{28,12},{1,17},{... | collective-permute-start | bytes 73736 | tf_op jit(solution)/shard_map/ppermute | solution.py:235
  7.1 5.6 %collective-permute-start.1 = (bf16[2,24,256]{2,1,0:T(8,128)(2,1)S(1)}, bf16[2,24,256]{2,1,0:T(8,128)(2,1)S(1)}, u32[]{:S(2)}, u32[]{:S(2)}) collective-permute-start(bf16[2,24,256]{2,1,0:T(8,128)(2,1)S(1)} %get-tuple-element.22.refs_3_.refs_5_), channel_id=1, source_target_pairs={{0,24},{4,28},{8,16},{12,20},{16,8},{20,12},{24,0},{28,4},{1,25},{... | collective-permute-start | bytes 73736 | tf_op jit(solution)/shard_map/ppermute | solution.py:235
  8.5 4.3 %collective-permute-start.2 = (bf16[2,24,256]{2,1,0:T(8,128)(2,1)S(1)}, bf16[2,24,256]{2,1,0:T(8,128)(2,1)S(1)}, u32[]{:S(2)}, u32[]{:S(2)}) collective-permute-start(bf16[2,24,256]{2,1,0:T(8,128)(2,1)S(1)} %get-tuple-element.22.refs_3_.refs_5_), channel_id=1, source_target_pairs={{0,8},{4,12},{8,0},{12,4},{16,24},{20,28},{24,16},{28,20},{1,9},{5... | collective-permute-start | bytes 73736 | tf_op jit(solution)/shard_map/ppermute | solution.py:235
  9.7 6.2 %collective-permute-start.5 = (bf16[24,384]{1,0:T(8,128)(2,1)S(1)}, bf16[24,384]{1,0:T(8,128)(2,1)S(1)}, u32[]{:S(2)}, u32[]{:S(2)}) collective-permute-start(bf16[24,384]{1,0:T(8,128)(2,1)S(1)} %get-tuple-element.27), channel_id=1, source_target_pairs={{0,16},{4,20},{8,24},{12,28},{16,0},{20,4},{24,8},{28,12},{1,17},{... | collective-permute-start | bytes 55304 | tf_op jit(solution)/shard_map/ppermute | solution.py:235
  12.8 3.1 %copy-start = (bf16[256,1024]{1,0:T(8,128)(2,1)S(1)}, bf16[256,1024]{1,0:T(8,128)(2,1)}, u32[]{:S(2)}) copy-start(bf16[256,1024]{1,0:T(8,128)(2,1)} %proj.2) | copy-start | bytes 1572868
  13.3 4.4 %collective-permute-start.4 = (bf16[272,128]{1,0:T(8,128)(2,1)S(1)}, bf16[272,128]{1,0:T(8,128)(2,1)S(1)}, u32[]{:S(2)}, u32[]{:S(2)}) collective-permute-start(bf16[272,128]{1,0:T(8,128)(2,1)S(1)} %get-tuple-element.24), channel_id=1, source_target_pairs={{0,4},{4,0},{8,12},{12,8},{16,20},{20,16},{24,28},{28,24},{1,5},{5... | collective-permute-start | bytes 208904 | tf_op jit(solution)/shard_map/ppermute | solution.py:235
  13.9 5.7 %collective-permute-start.8 = (bf16[24,384]{1,0:T(8,128)(2,1)S(1)}, bf16[24,384]{1,0:T(8,128)(2,1)S(1)}, u32[]{:S(2)}, u32[]{:S(2)}) collective-permute-start(bf16[24,384]{1,0:T(8,128)(2,1)S(1)} %get-tuple-element.34), channel_id=1, source_target_pairs={{0,24},{4,28},{8,16},{12,20},{16,8},{20,12},{24,0},{28,4},{1,25},{... | collective-permute-start | bytes 55304 | tf_op jit(solution)/shard_map/ppermute | solution.py:235
  15.9 3.8 %collective-permute-start.9 = (bf16[24,384]{1,0:T(8,128)(2,1)S(1)}, bf16[24,384]{1,0:T(8,128)(2,1)S(1)}, u32[]{:S(2)}, u32[]{:S(2)}) collective-permute-start(bf16[24,384]{1,0:T(8,128)(2,1)S(1)} %get-tuple-element.35), channel_id=1, source_target_pairs={{0,8},{4,12},{8,0},{12,4},{16,24},{20,28},{24,16},{28,20},{1,9},{5... | collective-permute-start | bytes 55304 | tf_op jit(solution)/shard_map/ppermute | solution.py:235
  17.7 2.0 %copy-start.1 = (bf16[256,1024]{1,0:T(8,128)(2,1)S(1)}, bf16[256,1024]{1,0:T(8,128)(2,1)}, u32[]{:S(2)}) copy-start(bf16[256,1024]{1,0:T(8,128)(2,1)} %proj.3) | copy-start | bytes 1572868
  18.0 4.4 %collective-permute-start.6 = (bf16[128,256]{1,0:T(8,128)(2,1)S(1)}, bf16[128,256]{1,0:T(8,128)(2,1)S(1)}, u32[]{:S(2)}, u32[]{:S(2)}) collective-permute-start(bf16[128,256]{1,0:T(8,128)(2,1)S(1)} %get-tuple-element.30), channel_id=1, source_target_pairs={{0,3},{1,2},{2,1},{3,0},{4,7},{5,6},{6,5},{7,4},{8,11},{9,10},{10,... | collective-permute-start | bytes 196616 | tf_op jit(solution)/shard_map/ppermute | solution.py:235
  18.0 5.9 %collective-permute-start.7 = (bf16[128,256]{1,0:T(8,128)(2,1)S(1)}, bf16[128,256]{1,0:T(8,128)(2,1)S(1)}, u32[]{:S(2)}, u32[]{:S(2)}) collective-permute-start(bf16[128,256]{1,0:T(8,128)(2,1)S(1)} %get-tuple-element.31), channel_id=1, source_target_pairs={{0,2},{1,3},{2,0},{3,1},{4,6},{5,7},{6,4},{7,5},{8,10},{9,11},{10,... | collective-permute-start | bytes 196616 | tf_op jit(solution)/shard_map/ppermute | solution.py:235
  20.0 4.9 %collective-permute-start.10 = (bf16[152,256]{1,0:T(8,128)(2,1)S(1)}, bf16[152,256]{1,0:T(8,128)(2,1)S(1)}, u32[]{:S(2)}, u32[]{:S(2)}) collective-permute-start(bf16[152,256]{1,0:T(8,128)(2,1)S(1)} %get-tuple-element.36), channel_id=1, source_target_pairs={{0,1},{1,0},{2,3},{3,2},{4,5},{5,4},{6,7},{7,6},{8,9},{9,8},{10,11... | collective-permute-start | bytes 233480 | tf_op jit(solution)/shard_map/ppermute | solution.py:235
  20.2 3.8 %collective-permute-start.11 = (bf16[24,256]{1,0:T(8,128)(2,1)S(1)}, bf16[24,256]{1,0:T(8,128)(2,1)S(1)}, u32[]{:S(2)}, u32[]{:S(2)}) collective-permute-start(bf16[24,256]{1,0:T(8,128)(2,1)S(1)} %get-tuple-element.38), channel_id=1, source_target_pairs={{0,2},{1,3},{2,0},{3,1},{4,6},{5,7},{6,4},{7,5},{8,10},{9,11},{10,... | collective-permute-start | bytes 36872 | tf_op jit(solution)/shard_map/ppermute | solution.py:235
  21.8 3.1 %collective-permute-start.12 = (bf16[24,256]{1,0:T(8,128)(2,1)S(1)}, bf16[24,256]{1,0:T(8,128)(2,1)S(1)}, u32[]{:S(2)}, u32[]{:S(2)}) collective-permute-start(bf16[24,256]{1,0:T(8,128)(2,1)S(1)} %get-tuple-element.39), channel_id=1, source_target_pairs={{0,3},{1,2},{2,1},{3,0},{4,7},{5,6},{6,5},{7,4},{8,11},{9,10},{10,... | collective-permute-start | bytes 36872 | tf_op jit(solution)/shard_map/ppermute | solution.py:235

commit v13 on v12

--- a/solution.py
+++ b/solution.py
@@ -46,17 +46,17 @@
         copy.wait()
 
 
-def tile_scores(queries, vids):
-    total_vid, width = sum(ref.shape[1] for ref in vids), queries.shape[1]
+def tile_scores(queries_t, vids):
+    total_vid, width = sum(ref.shape[1] for ref in vids), queries_t.shape[0]
     heads = width // HEAD_DIM
     keys = jnp.concatenate([ref[0].astype(F32) for ref in vids], axis=0).astype(BF16)
     lanes = [head_lanes(1, width, h).astype(F32).astype(BF16) for h in range(heads)]
     keys = jnp.concatenate([keys * lane for lane in lanes], axis=0)
-    return dot(keys, queries, 1, 1).reshape(heads, total_vid, queries.shape[0])
-
-
-def both(auds):
-    return (jnp.concatenate([ref[i] for ref in auds], axis=0) for i in range(2))
+    return dot(keys, queries_t).reshape(heads, total_vid, queries_t.shape[1])
+
+
+def values_t(vids):
+    return jnp.concatenate([ref[1].astype(F32) for ref in vids], axis=0).T.astype(BF16)
 
 
 def column_states(scores, aud_vals, outs):
@@ -82,18 +82,19 @@
         put_cols(out, mix[rows], logs[rows])
 
 
-def row_states(scores, vid_vals, outs):
-    heads, _, total_aud = scores.shape
-    top = jnp.max(scores, axis=1, keepdims=True)
-    probs = jnp.exp2((scores - top) * SCALE)
-    total = jnp.sum(probs, axis=1, keepdims=True)
-    probs = probs.astype(BF16)
-    vals = vid_vals.T.astype(BF16)
-    mix = [
-        dot(vals[h * HEAD_DIM : (h + 1) * HEAD_DIM], probs[h]) * (1.0 / total[h])
-        for h in range(heads)
-    ]
-    mix = jnp.concatenate(mix, axis=0)
+def row_states(parts, outs):
+    heads, _, total_aud = parts[0][0].shape
+    top = jnp.max(parts[0][0], axis=1, keepdims=True)
+    for scores, _ in parts[1:]:
+        top = jnp.maximum(top, jnp.max(scores, axis=1, keepdims=True))
+    total, mix = 0.0, [0.0] * heads
+    for scores, vals in parts:
+        probs = jnp.exp2((scores - top) * SCALE)
+        total += jnp.sum(probs, axis=1, keepdims=True)
+        probs = probs.astype(BF16)
+        for h in range(heads):
+            mix[h] += dot(vals[h * HEAD_DIM : (h + 1) * HEAD_DIM], probs[h])
+    mix = jnp.concatenate([mix[h] * (1.0 / total[h]) for h in range(heads)], axis=0)
     log = (top * SCALE + jnp.log2(total)).reshape(heads, total_aud)
     for i, out in enumerate(outs):
         cols = slice(i * out.shape[1], (i + 1) * out.shape[1])
@@ -101,21 +102,24 @@
 
 
 def attend_first(aud_count, *refs):
-    auds, vids, (scores_out, *col_outs) = refs[:aud_count], refs[aud_count : aud_count + 2], refs[aud_count + 2 :]
-    queries, aud_vals = both(auds)
-    scores = tile_scores(queries, vids)
+    auds, vids, outs = refs[:aud_count], refs[aud_count : aud_count + 2], refs[aud_count + 2 :]
+    scores_out, queries_out, aud_vals_out, vals_out, *col_outs = outs
+    queries, aud_vals = (jnp.concatenate([ref[i] for ref in auds], axis=0) for i in range(2))
+    queries_t = queries.astype(F32).T.astype(BF16)
+    queries_out[...] = queries_t
+    aud_vals_out[...] = aud_vals
+    scores = tile_scores(queries_t, vids)
     scores_out[...] = scores
+    vals_out[...] = values_t(vids)
     column_states(scores, aud_vals, col_outs)
 
 
-def attend(aud_count, vid_count, *refs):
-    auds, vids, refs = refs[:aud_count], refs[aud_count : aud_count + vid_count], refs[aud_count + vid_count :]
-    firsts, first_scores, row_outs, col_outs = refs[:2], refs[2], refs[3 : 3 + aud_count], refs[3 + aud_count :]
-    queries, aud_vals = both(auds)
-    scores = tile_scores(queries, vids)
-    column_states(scores, aud_vals, col_outs)
-    vals = jnp.concatenate([ref[1].astype(F32) for ref in (*firsts, *vids)], axis=0)
-    row_states(jnp.concatenate([first_scores[...], scores], axis=1), vals, row_outs)
+def attend(aud_count, vid_count, queries, aud_vals, first_scores, first_vals, *refs):
+    vids, refs = refs[:vid_count], refs[vid_count:]
+    row_outs, col_outs = refs[:aud_count], refs[aud_count:]
+    scores = tile_scores(queries[...], vids)
+    column_states(scores, aud_vals[...], col_outs)
+    row_states([(first_scores[...], first_vals[...]), (scores, values_t(vids))], row_outs)
 
 
 def put_rows(out, mix, log):
@@ -268,15 +272,24 @@
     auds = [swap(aud, "seq", k) for k in range(1, aud_count)] + [aud]
     vids = {k: swap(vid, "seq", k * aud_count) for k in (early, *late)}
     state = shape(vid_rows, width + LANES)
-    scores, first_state, own_state = call(
+    total_aud = aud_count * aud_rows
+    *shared, first_state, own_state = call(
         functools.partial(attend_first, aud_count),
-        [shape(heads, 2 * vid_rows, aud_count * aud_rows, dtype=F32), state, state],
+        [
+            shape(heads, 2 * vid_rows, total_aud, dtype=F32),
+            shape(width, total_aud),
+            shape(total_aud, width),
+            shape(width, 2 * vid_rows),
+            state,
+            state,
+        ],
         [*auds, vids[early], vid],
     )
+    scores, queries_t, aud_vals, vals_t = shared
     states = call(
         functools.partial(attend, aud_count, len(late)),
         [shape(width + log_rows, aud_rows)] * aud_count + [state] * len(late),
-        [*auds, *(vids[k] for k in late), vids[early], vid, scores],
+        [queries_t, aud_vals, scores, vals_t, *(vids[k] for k in late)],
     )
     rows = [swap(states[k - 1], "seq", k) for k in range(1, aud_count)] + [states[aud_count - 1]]
     states = dict(zip((early, 0, *late), (first_state, own_state, *states[aud_count:])))

time: 25.7 us -> 25.7 us (level)
  no operation moved by 1% of the time
where the time goes in v13:
time: 25.7 us; the launch traced here: 25.5 us
  starting transfers between devices  16.2 us (63%)
  waiting for transfers between devices  5.34 us (21%)
  Pallas kernels  3.32 us (13%)
  between operations  0.7 us (3%)
    ppermute x13, starting transfers between devices, swap(): lax.ppermute(block, axis, [(i, i ^ distance) for i in range(lax.axis_size...  16.2 us
    ppermute x13, waiting for transfers between devices, swap(): lax.ppermute(block, axis, [(i, i ^ distance) for i in range(lax.axis_size...  5.34 us
    pallas_call x8, Pallas kernels, call(): pl.pallas_call(body, out_shape=out_shape, in_specs=in_specs or [vmem] * l...  3.32 us
  transfers between devices with their start and end apart: 13, of which 7 were waited for; matrix products, arithmetic and copies ran while one was open for 0% of the time, Pallas kernels for 7%

profile of v13, /device:TPU:0, one launch (start us, length us, event | category | flops | bytes accessed | tf_op | source)
XLA Modules:
  0.0 25.5 jit_solution(5740766922307539875)
XLA Ops:
  0.6 0.9 %shard_map.77 = (bf16[2,128,256]{2,1,0:T(8,128)(2,1)S(1)}, bf16[2,24,256]{2,1,0:T(8,128)(2,1)S(1)}) custom-call(bf16[128,256]{1,0:T(8,128)(2,1)} %aud_ref.1, bf16[128,256]{1,0:T(8,128)(2,1)} %aud_val.1, bf16[24,256]{1,0:T(8,128)(2,1)} %vid_ref.1, bf16[24,256]{1,0:T(8,128)(2,1)} %vid_val.1), custom_call_target="tpu_custom_call" | custom-call | flops 5000000000 | tf_op jit(solution)/shard_map/pallas_call | solution.py:223
  1.5 3.0 %collective-permute-start = (bf16[2,128,256]{2,1,0:T(8,128)(2,1)S(1)}, bf16[2,128,256]{2,1,0:T(8,128)(2,1)S(1)}, u32[]{:S(2)}, u32[]{:S(2)}) collective-permute-start(bf16[2,128,256]{2,1,0:T(8,128)(2,1)S(1)} %get-tuple-element.24.refs_1_), channel_id=1, source_target_pairs={{0,4},{4,0},{8,12},{12,8},{16,20},{20,16},{24,28},{28,24},{1,5},{5... | collective-permute-start | bytes 393224 | tf_op jit(solution)/shard_map/ppermute | solution.py:239
  4.6 2.6 %collective-permute-start.1 = (bf16[2,24,256]{2,1,0:T(8,128)(2,1)S(1)}, bf16[2,24,256]{2,1,0:T(8,128)(2,1)S(1)}, u32[]{:S(2)}, u32[]{:S(2)}) collective-permute-start(bf16[2,24,256]{2,1,0:T(8,128)(2,1)S(1)} %get-tuple-element.25.refs_3_), channel_id=1, source_target_pairs={{0,16},{4,20},{8,24},{12,28},{16,0},{20,4},{24,8},{28,12},{1,17},{... | collective-permute-start | bytes 73736 | tf_op jit(solution)/shard_map/ppermute | solution.py:239
  7.1 1.3 %collective-permute-start.2 = (bf16[2,24,256]{2,1,0:T(8,128)(2,1)S(1)}, bf16[2,24,256]{2,1,0:T(8,128)(2,1)S(1)}, u32[]{:S(2)}, u32[]{:S(2)}) collective-permute-start(bf16[2,24,256]{2,1,0:T(8,128)(2,1)S(1)} %get-tuple-element.25.refs_3_), channel_id=1, source_target_pairs={{0,24},{4,28},{8,16},{12,20},{16,8},{20,12},{24,0},{28,4},{1,25},{... | collective-permute-start | bytes 73736 | tf_op jit(solution)/shard_map/ppermute | solution.py:239
  8.5 0.2 collective-permute-start.3
  8.7 0.6 %collective-permute-done.1.refs_2_ = bf16[2,24,256]{2,1,0:T(8,128)(2,1)S(1)} collective-permute-done((bf16[2,24,256]{2,1,0:T(8,128)(2,1)S(1)}, bf16[2,24,256]{2,1,0:T(8,128)(2,1)S(1)}, u32[]{:S(2)}, u32[]{:S(2)}) %collective-permute-start.1) | collective-permute-done | bytes 24608 | tf_op jit(solution)/shard_map/ppermute | solution.py:239
  9.3 0.5 %shard_map.78 = (f32[4,48,256]{2,1,0:T(8,128)S(1)}, bf16[256,256]{1,0:T(8,128)(2,1)S(1)}, bf16[256,256]{1,0:T(8,128)(2,1)S(1)}, bf16[256,48]{1,0:T(8,128)(2,1)S(...) custom-call(bf16[2,128,256]{2,1,0:T(8,128)(2,1)S(1)} %collective-permute-done.refs_0_, ...), custom_call_target="tpu_custom_call" | custom-call | flops 5000000000 | tf_op jit(solution)/shard_map/pallas_call | solution.py:223
  9.8 2.8 %collective-permute-start.5 = (bf16[24,384]{1,0:T(8,128)(2,1)S(1)}, bf16[24,384]{1,0:T(8,128)(2,1)S(1)}, u32[]{:S(2)}, u32[]{:S(2)}) collective-permute-start(bf16[24,384]{1,0:T(8,128)(2,1)S(1)} %get-tuple-element.33), channel_id=1, source_target_pairs={{0,16},{4,20},{8,24},{12,28},{16,0},{20,4},{24,8},{28,12},{1,17},{... | collective-permute-start | bytes 55304 | tf_op jit(solution)/shard_map/ppermute | solution.py:239
  12.6 0.2 collective-permute-done.2.refs_0_
  12.8 0.5 %shard_map.79 = (bf16[272,128]{1,0:T(8,128)(2,1)S(1)}, bf16[272,128]{1,0:T(8,128)(2,1)S(1)}, bf16[24,384]{1,0:T(8,128)(2,1)S(1)}, bf16[24,384]{1,0:T(8,128)(2,1)S(1)}) custom-call(bf16[256,256]{1,0:T(8,128)(2,1)S(1)} %get-tuple-element.26.queries, bf16[256,256]{1,0:T(8,128)(2,1)S(1)} %get-tuple-element.27.aud_vals, ...), custom_call_target="tpu_custom_call" | custom-call | flops 5000000000 | tf_op jit(solution)/shard_map/pallas_call | solution.py:223
  13.3 0.6 %collective-permute-start.4 = (bf16[272,128]{1,0:T(8,128)(2,1)S(1)}, bf16[272,128]{1,0:T(8,128)(2,1)S(1)}, u32[]{:S(2)}, u32[]{:S(2)}) collective-permute-start(bf16[272,128]{1,0:T(8,128)(2,1)S(1)} %get-tuple-element.30), channel_id=1, source_target_pairs={{0,4},{4,0},{8,12},{12,8},{16,20},{20,16},{24,28},{28,24},{1,5},{5... | collective-permute-start | bytes 208904 | tf_op jit(solution)/shard_map/ppermute | solution.py:239
  13.9 2.0 %collective-permute-start.8 = (bf16[24,384]{1,0:T(8,128)(2,1)S(1)}, bf16[24,384]{1,0:T(8,128)(2,1)S(1)}, u32[]{:S(2)}, u32[]{:S(2)}) collective-permute-start(bf16[24,384]{1,0:T(8,128)(2,1)S(1)} %get-tuple-element.40), channel_id=1, source_target_pairs={{0,24},{4,28},{8,16},{12,20},{16,8},{20,12},{24,0},{28,4},{1,25},{... | collective-permute-start | bytes 55304 | tf_op jit(solution)/shard_map/ppermute | solution.py:239
  15.9 0.1 shard_map.80
  16.1 1.6 %collective-permute-done.4.refs_0_ = bf16[272,128]{1,0:T(8,128)(2,1)S(1)} collective-permute-done((bf16[272,128]{1,0:T(8,128)(2,1)S(1)}, bf16[272,128]{1,0:T(8,128)(2,1)S(1)}, u32[]{:S(2)}, u32[]{:S(2)}) %collective-permute-start.4) | collective-permute-done | bytes 69664 | tf_op jit(solution)/shard_map/ppermute | solution.py:239
  17.7 0.3 %shard_map.81 = (f32[128,256]{1,0:T(8,128)S(1)}, bf16[128,256]{1,0:T(8,128)(2,1)S(1)}, bf16[128,256]{1,0:T(8,128)(2,1)S(1)}, bf16[128,256]{1,0:T(8,128)(2,1)S(1)}) custom-call(s32[1]{0:T(128)} %bitcast.me, bf16[256,1024]{1,0:T(8,128)(2,1)S(1)} %copy-done, bf16[272,128]{1,0:T(8,128)(2,1)S(1)} %collective-permute-done.4.refs_0_, ...), custom_call_target="tpu_custom_call" | custom-call | flops 1000000000 | tf_op jit(solution)/shard_map/pallas_call | solution.py:223
  18.0 1.6 %collective-permute-start.7 = (bf16[128,256]{1,0:T(8,128)(2,1)S(1)}, bf16[128,256]{1,0:T(8,128)(2,1)S(1)}, u32[]{:S(2)}, u32[]{:S(2)}) collective-permute-start(bf16[128,256]{1,0:T(8,128)(2,1)S(1)} %get-tuple-element.37), channel_id=1, source_target_pairs={{0,2},{1,3},{2,0},{3,1},{4,6},{5,7},{6,4},{7,5},{8,10},{9,11},{10,... | collective-permute-start | bytes 196616 | tf_op jit(solution)/shard_map/ppermute | solution.py:239
  19.7 0.3 %shard_map.83 = (f32[24,256]{1,0:T(8,128)S(1)}, bf16[152,256]{1,0:T(8,128)(2,1)S(1)}, bf16[24,256]{1,0:T(8,128)(2,1)S(1)}, bf16[24,256]{1,0:T(8,128)(2,1)S(1)}) custom-call(s32[1]{0:T(128)} %bitcast.me, bf16[256,1024]{1,0:T(8,128)(2,1)S(1)} %copy-done.1, f32[24,256]{1,0:T(8,128)S(1)} %get-tuple-element.34.refs_2_.mix, f32[24,256]{1,0:T(8,128)S(1)} %get-tuple-element.38.log, ...), custom_call_target="tpu_custom_call" | custom-call | flops 5000000000 | tf_op jit(solution)/shard_map/pallas_call | solution.py:223
  20.0 0.3 %collective-permute-start.10 = (bf16[152,256]{1,0:T(8,128)(2,1)S(1)}, bf16[152,256]{1,0:T(8,128)(2,1)S(1)}, u32[]{:S(2)}, u32[]{:S(2)}) collective-permute-start(bf16[152,256]{1,0:T(8,128)(2,1)S(1)} %get-tuple-element.42), channel_id=1, source_target_pairs={{0,1},{1,0},{2,3},{3,2},{4,5},{5,4},{6,7},{7,6},{8,9},{9,8},{10,11... | collective-permute-start | bytes 233480 | tf_op jit(solution)/shard_map/ppermute | solution.py:239
  20.2 1.5 %collective-permute-start.11 = (bf16[24,256]{1,0:T(8,128)(2,1)S(1)}, bf16[24,256]{1,0:T(8,128)(2,1)S(1)}, u32[]{:S(2)}, u32[]{:S(2)}) collective-permute-start(bf16[24,256]{1,0:T(8,128)(2,1)S(1)} %get-tuple-element.44), channel_id=1, source_target_pairs={{0,2},{1,3},{2,0},{3,1},{4,6},{5,7},{6,4},{7,5},{8,10},{9,11},{10,... | collective-permute-start | bytes 36872 | tf_op jit(solution)/shard_map/ppermute | solution.py:239
  21.9 0.5 %collective-permute-done.6.refs_1_ = bf16[128,256]{1,0:T(8,128)(2,1)S(1)} collective-permute-done((bf16[128,256]{1,0:T(8,128)(2,1)S(1)}, bf16[128,256]{1,0:T(8,128)(2,1)S(1)}, u32[]{:S(2)}, u32[]{:S(2)}) %collective-permute-start.6) | collective-permute-done | bytes 65568 | tf_op jit(solution)/shard_map/ppermute | solution.py:239
  22.3 1.6 %collective-permute-done.7.refs_2_ = bf16[128,256]{1,0:T(8,128)(2,1)S(1)} collective-permute-done((bf16[128,256]{1,0:T(8,128)(2,1)S(1)}, bf16[128,256]{1,0:T(8,128)(2,1)S(1)}, u32[]{:S(2)}, u32[]{:S(2)}) %collective-permute-start.7) | collective-permute-done | bytes 65568 | tf_op jit(solution)/shard_map/ppermute | solution.py:239
  23.9 0.2 collective-permute-done.11.refs_1_
  24.1 0.8 %collective-permute-done.12.refs_2_ = bf16[24,256]{1,0:T(8,128)(2,1)S(1)} collective-permute-done((bf16[24,256]{1,0:T(8,128)(2,1)S(1)}, bf16[24,256]{1,0:T(8,128)(2,1)S(1)}, u32[]{:S(2)}, u32[]{:S(2)}) %collective-permute-start.12) | collective-permute-done | bytes 12320 | tf_op jit(solution)/shard_map/ppermute | solution.py:239
  24.9 0.6 %shard_map.84 = (bf16[128,256]{1,0:T(8,128)(2,1)}, bf16[24,256]{1,0:T(8,128)(2,1)}) custom-call(f32[128,256]{1,0:T(8,128)S(1)} %shard_map.82.aud_part, bf16[152,256]{1,0:T(8,128)(2,1)S(1)} %collective-permute-done.10.core, f32[24,256]{1,0:T(8,128)S(1)} %get-tuple-element.43.refs_0_, bf16[24,256]{1,0:T(8,128)(2,1)S(1)} %collective-permute-done.11.refs_1_, ...), custom_call_target="tpu_custom_call" | custom-call | flops 5000000000 | tf_op jit(solution)/shard_map/pallas_call | solution.py:223
  (14 shorter events, 0.3 us)
Async XLA Ops:
  1.5 7.7 %collective-permute-start = (bf16[2,128,256]{2,1,0:T(8,128)(2,1)S(1)}, bf16[2,128,256]{2,1,0:T(8,128)(2,1)S(1)}, u32[]{:S(2)}, u32[]{:S(2)}) collective-permute-start(bf16[2,128,256]{2,1,0:T(8,128)(2,1)S(1)} %get-tuple-element.24.refs_1_), channel_id=1, source_target_pairs={{0,4},{4,0},{8,12},{12,8},{16,20},{20,16},{24,28},{28,24},{1,5},{5... | collective-permute-start | bytes 393224 | tf_op jit(solution)/shard_map/ppermute | solution.py:239
  4.6 4.7 %collective-permute-start.1 = (bf16[2,24,256]{2,1,0:T(8,128)(2,1)S(1)}, bf16[2,24,256]{2,1,0:T(8,128)(2,1)S(1)}, u32[]{:S(2)}, u32[]{:S(2)}) collective-permute-start(bf16[2,24,256]{2,1,0:T(8,128)(2,1)S(1)} %get-tuple-element.25.refs_3_), channel_id=1, source_target_pairs={{0,16},{4,20},{8,24},{12,28},{16,0},{20,4},{24,8},{28,12},{1,17},{... | collective-permute-start | bytes 73736 | tf_op jit(solution)/shard_map/ppermute | solution.py:239
  7.1 5.6 %collective-permute-start.2 = (bf16[2,24,256]{2,1,0:T(8,128)(2,1)S(1)}, bf16[2,24,256]{2,1,0:T(8,128)(2,1)S(1)}, u32[]{:S(2)}, u32[]{:S(2)}) collective-permute-start(bf16[2,24,256]{2,1,0:T(8,128)(2,1)S(1)} %get-tuple-element.25.refs_3_), channel_id=1, source_target_pairs={{0,24},{4,28},{8,16},{12,20},{16,8},{20,12},{24,0},{28,4},{1,25},{... | collective-permute-start | bytes 73736 | tf_op jit(solution)/shard_map/ppermute | solution.py:239
  8.5 4.3 %collective-permute-start.3 = (bf16[2,24,256]{2,1,0:T(8,128)(2,1)S(1)}, bf16[2,24,256]{2,1,0:T(8,128)(2,1)S(1)}, u32[]{:S(2)}, u32[]{:S(2)}) collective-permute-start(bf16[2,24,256]{2,1,0:T(8,128)(2,1)S(1)} %get-tuple-element.25.refs_3_), channel_id=1, source_target_pairs={{0,8},{4,12},{8,0},{12,4},{16,24},{20,28},{24,16},{28,20},{1,9},{5... | collective-permute-start | bytes 73736 | tf_op jit(solution)/shard_map/ppermute | solution.py:239
  9.8 6.1 %collective-permute-start.5 = (bf16[24,384]{1,0:T(8,128)(2,1)S(1)}, bf16[24,384]{1,0:T(8,128)(2,1)S(1)}, u32[]{:S(2)}, u32[]{:S(2)}) collective-permute-start(bf16[24,384]{1,0:T(8,128)(2,1)S(1)} %get-tuple-element.33), channel_id=1, source_target_pairs={{0,16},{4,20},{8,24},{12,28},{16,0},{20,4},{24,8},{28,12},{1,17},{... | collective-permute-start | bytes 55304 | tf_op jit(solution)/shard_map/ppermute | solution.py:239
  12.8 3.1 %copy-start = (bf16[256,1024]{1,0:T(8,128)(2,1)S(1)}, bf16[256,1024]{1,0:T(8,128)(2,1)}, u32[]{:S(2)}) copy-start(bf16[256,1024]{1,0:T(8,128)(2,1)} %proj.2) | copy-start | bytes 1572868
  13.3 4.4 %collective-permute-start.4 = (bf16[272,128]{1,0:T(8,128)(2,1)S(1)}, bf16[272,128]{1,0:T(8,128)(2,1)S(1)}, u32[]{:S(2)}, u32[]{:S(2)}) collective-permute-start(bf16[272,128]{1,0:T(8,128)(2,1)S(1)} %get-tuple-element.30), channel_id=1, source_target_pairs={{0,4},{4,0},{8,12},{12,8},{16,20},{20,16},{24,28},{28,24},{1,5},{5... | collective-permute-start | bytes 208904 | tf_op jit(solution)/shard_map/ppermute | solution.py:239
  13.9 5.7 %collective-permute-start.8 = (bf16[24,384]{1,0:T(8,128)(2,1)S(1)}, bf16[24,384]{1,0:T(8,128)(2,1)S(1)}, u32[]{:S(2)}, u32[]{:S(2)}) collective-permute-start(bf16[24,384]{1,0:T(8,128)(2,1)S(1)} %get-tuple-element.40), channel_id=1, source_target_pairs={{0,24},{4,28},{8,16},{12,20},{16,8},{20,12},{24,0},{28,4},{1,25},{... | collective-permute-start | bytes 55304 | tf_op jit(solution)/shard_map/ppermute | solution.py:239
  15.9 3.8 %collective-permute-start.9 = (bf16[24,384]{1,0:T(8,128)(2,1)S(1)}, bf16[24,384]{1,0:T(8,128)(2,1)S(1)}, u32[]{:S(2)}, u32[]{:S(2)}) collective-permute-start(bf16[24,384]{1,0:T(8,128)(2,1)S(1)} %get-tuple-element.41), channel_id=1, source_target_pairs={{0,8},{4,12},{8,0},{12,4},{16,24},{20,28},{24,16},{28,20},{1,9},{5... | collective-permute-start | bytes 55304 | tf_op jit(solution)/shard_map/ppermute | solution.py:239
  17.7 2.0 %copy-start.1 = (bf16[256,1024]{1,0:T(8,128)(2,1)S(1)}, bf16[256,1024]{1,0:T(8,128)(2,1)}, u32[]{:S(2)}) copy-start(bf16[256,1024]{1,0:T(8,128)(2,1)} %proj.3) | copy-start | bytes 1572868
  18.0 4.4 %collective-permute-start.6 = (bf16[128,256]{1,0:T(8,128)(2,1)S(1)}, bf16[128,256]{1,0:T(8,128)(2,1)S(1)}, u32[]{:S(2)}, u32[]{:S(2)}) collective-permute-start(bf16[128,256]{1,0:T(8,128)(2,1)S(1)} %get-tuple-element.36), channel_id=1, source_target_pairs={{0,3},{1,2},{2,1},{3,0},{4,7},{5,6},{6,5},{7,4},{8,11},{9,10},{10,... | collective-permute-start | bytes 196616 | tf_op jit(solution)/shard_map/ppermute | solution.py:239
  18.0 5.9 %collective-permute-start.7 = (bf16[128,256]{1,0:T(8,128)(2,1)S(1)}, bf16[128,256]{1,0:T(8,128)(2,1)S(1)}, u32[]{:S(2)}, u32[]{:S(2)}) collective-permute-start(bf16[128,256]{1,0:T(8,128)(2,1)S(1)} %get-tuple-element.37), channel_id=1, source_target_pairs={{0,2},{1,3},{2,0},{3,1},{4,6},{5,7},{6,4},{7,5},{8,10},{9,11},{10,... | collective-permute-start | bytes 196616 | tf_op jit(solution)/shard_map/ppermute | solution.py:239
  20.0 4.9 %collective-permute-start.10 = (bf16[152,256]{1,0:T(8,128)(2,1)S(1)}, bf16[152,256]{1,0:T(8,128)(2,1)S(1)}, u32[]{:S(2)}, u32[]{:S(2)}) collective-permute-start(bf16[152,256]{1,0:T(8,128)(2,1)S(1)} %get-tuple-element.42), channel_id=1, source_target_pairs={{0,1},{1,0},{2,3},{3,2},{4,5},{5,4},{6,7},{7,6},{8,9},{9,8},{10,11... | collective-permute-start | bytes 233480 | tf_op jit(solution)/shard_map/ppermute | solution.py:239
  20.2 3.8 %collective-permute-start.11 = (bf16[24,256]{1,0:T(8,128)(2,1)S(1)}, bf16[24,256]{1,0:T(8,128)(2,1)S(1)}, u32[]{:S(2)}, u32[]{:S(2)}) collective-permute-start(bf16[24,256]{1,0:T(8,128)(2,1)S(1)} %get-tuple-element.44), channel_id=1, source_target_pairs={{0,2},{1,3},{2,0},{3,1},{4,6},{5,7},{6,4},{7,5},{8,10},{9,11},{10,... | collective-permute-start | bytes 36872 | tf_op jit(solution)/shard_map/ppermute | solution.py:239
  21.8 3.1 %collective-permute-start.12 = (bf16[24,256]{1,0:T(8,128)(2,1)S(1)}, bf16[24,256]{1,0:T(8,128)(2,1)S(1)}, u32[]{:S(2)}, u32[]{:S(2)}) collective-permute-start(bf16[24,256]{1,0:T(8,128)(2,1)S(1)} %get-tuple-element.45), channel_id=1, source_target_pairs={{0,3},{1,2},{2,1},{3,0},{4,7},{5,6},{6,5},{7,4},{8,11},{9,10},{10,... | collective-permute-start | bytes 36872 | tf_op jit(solution)/shard_map/ppermute | solution.py:239

commit v14 on v13

--- a/solution.py
+++ b/solution.py
@@ -14,7 +14,7 @@
 SCALE = HEAD_DIM ** (-0.5) * math.log2(math.e)
 VMEM_LIMIT = 48 * 1024 * 1024
 COST = 5 * 10**9
-COST_A = 10**9
+COST_ADD = 10**3
 BF16 = jnp.bfloat16
 F32 = jnp.float32
 
@@ -200,7 +200,7 @@
     project(mix.astype(BF16), proj, me[0], [outs[0], outs[1].at[aud_rows:, :], *outs[2:]])
 
 
-def add_audio(*refs):
+def add_terms(*refs):
     *terms, out = refs
     total = terms[0][...]
     for term in terms[1:]:
@@ -208,14 +208,10 @@
     out[...] = total
 
 
-def add(aud_part, core, *refs):
-    *vid_terms, aud_out, vid_out = refs
+def add_core(aud_sum, vid_sum, core, aud_out, vid_out):
     aud_rows = aud_out.shape[0]
-    aud_out[...] = (aud_part[...] + core[:aud_rows].astype(F32)).astype(BF16)
-    vid = vid_terms[0][...] + core[aud_rows:].astype(F32)
-    for term in vid_terms[1:]:
-        vid += term[...].astype(F32)
-    vid_out[...] = vid.astype(BF16)
+    aud_out[...] = (aud_sum[...] + core[:aud_rows].astype(F32)).astype(BF16)
+    vid_out[...] = (vid_sum[...] + core[aud_rows:].astype(F32)).astype(BF16)
 
 
 def call(body, out_shape, args, in_specs=None, scratch=(), cost=COST):
@@ -308,7 +304,6 @@
         [shape(aud_rows, step, dtype=F32)] + [shape(aud_rows, step)] * (peers - 1),
         [me, audio_proj, *rows, mix_log[0]],
         in_specs=[smem, vmem] + [vmem] * aud_count + [pl.BlockSpec(memory_space=pl.ANY)],
-        cost=COST_A,
     )
     vid_terms = call(
         lambda me, proj, mix, log, core, *refs: project_video(
@@ -322,13 +317,12 @@
     vid_got = [swap(vid_terms[k], "head", k) for k in range(2, peers)]
     core_got = swap(vid_terms[1], "head", 1)
     aud_got = [swap(aud_terms[k], "head", k) for k in reversed(range(2, peers))]
-    aud_part = call(add_audio, [shape(aud_rows, step, dtype=F32)], [aud_terms[0], *aud_got])[0]
+    aud_sum = call(add_terms, [shape(aud_rows, step, dtype=F32)], [aud_terms[0], *aud_got])[0]
+    vid_sum = call(
+        add_terms, [shape(vid_rows, step, dtype=F32)], [vid_terms[0], *vid_got], cost=COST_ADD
+    )[0]
     return tuple(
-        call(
-            add,
-            [shape(aud_rows, step), shape(vid_rows, step)],
-            [aud_part, core_got, vid_terms[0], *vid_got],
-        )
+        call(add_core, [shape(aud_rows, step), shape(vid_rows, step)], [aud_sum, vid_sum, core_got])
     )
 
 

time: 25.7 us -> 25.5 us (level)
  waiting for transfers between devices: 5.34 us -> 4.86 us
  starting transfers between devices: 16.2 us -> 16.5 us
    ppermute x13, waiting for transfers between devices: 5.34 us -> 4.86 us  [swap(): lax.ppermute(block, axis, [(i, i ^ distance) for i in range(lax.axis_size...]
    ppermute x13, starting transfers between devices: 16.2 us -> 16.5 us  [swap(): lax.ppermute(block, axis, [(i, i ^ distance) for i in range(lax.axis_size...]
    pallas_call x8 -> x9, Pallas kernels: 3.32 us -> 3.33 us  [call(): pl.pallas_call(body, out_shape=out_shape, in_specs=in_specs or [vmem] * l...]
  transfers between devices with their start and end apart: 13 -> 13, of which waited for: 7 -> 5; matrix products, arithmetic and copies ran while one was open for 0% -> 0% of each run, Pallas kernels for 7% -> 7%
where the time goes in v14:
time: 25.5 us; the launch traced here: 25.4 us
  starting transfers between devices  16.5 us (65%)
  waiting for transfers between devices  4.86 us (19%)
  Pallas kernels  3.33 us (13%)
  between operations  0.71 us (3%)
    ppermute x13, starting transfers between devices, swap(): lax.ppermute(block, axis, [(i, i ^ distance) for i in range(lax.axis_size...  16.5 us
    ppermute x13, waiting for transfers between devices, swap(): lax.ppermute(block, axis, [(i, i ^ distance) for i in range(lax.axis_size...  4.86 us
    pallas_call x9, Pallas kernels, call(): pl.pallas_call(body, out_shape=out_shape, in_specs=in_specs or [vmem] * l...  3.33 us
  transfers between devices with their start and end apart: 13, of which 5 were waited for; matrix products, arithmetic and copies ran while one was open for 0% of the time, Pallas kernels for 7%

profile of v14, /device:TPU:0, one launch (start us, length us, event | category | flops | bytes accessed | tf_op | source)
XLA Modules:
  0.0 25.4 jit_solution(1282084543557700601)
XLA Ops:
  0.6 0.9 %shard_map.77 = (bf16[2,128,256]{2,1,0:T(8,128)(2,1)S(1)}, bf16[2,24,256]{2,1,0:T(8,128)(2,1)S(1)}) custom-call(bf16[128,256]{1,0:T(8,128)(2,1)} %aud_ref.1, bf16[128,256]{1,0:T(8,128)(2,1)} %aud_val.1, bf16[24,256]{1,0:T(8,128)(2,1)} %vid_ref.1, bf16[24,256]{1,0:T(8,128)(2,1)} %vid_val.1), custom_call_target="tpu_custom_call" | custom-call | flops 5000000000 | tf_op jit(solution)/shard_map/pallas_call | solution.py:219
  1.5 3.0 %collective-permute-start = (bf16[2,128,256]{2,1,0:T(8,128)(2,1)S(1)}, bf16[2,128,256]{2,1,0:T(8,128)(2,1)S(1)}, u32[]{:S(2)}, u32[]{:S(2)}) collective-permute-start(bf16[2,128,256]{2,1,0:T(8,128)(2,1)S(1)} %get-tuple-element.24.refs_1_), channel_id=1, source_target_pairs={{0,4},{4,0},{8,12},{12,8},{16,20},{20,16},{24,28},{28,24},{1,5},{5... | collective-permute-start | bytes 393224 | tf_op jit(solution)/shard_map/ppermute | solution.py:235
  4.6 2.6 %collective-permute-start.1 = (bf16[2,24,256]{2,1,0:T(8,128)(2,1)S(1)}, bf16[2,24,256]{2,1,0:T(8,128)(2,1)S(1)}, u32[]{:S(2)}, u32[]{:S(2)}) collective-permute-start(bf16[2,24,256]{2,1,0:T(8,128)(2,1)S(1)} %get-tuple-element.25.refs_3_), channel_id=1, source_target_pairs={{0,16},{4,20},{8,24},{12,28},{16,0},{20,4},{24,8},{28,12},{1,17},{... | collective-permute-start | bytes 73736 | tf_op jit(solution)/shard_map/ppermute | solution.py:235
  7.1 1.3 %collective-permute-start.2 = (bf16[2,24,256]{2,1,0:T(8,128)(2,1)S(1)}, bf16[2,24,256]{2,1,0:T(8,128)(2,1)S(1)}, u32[]{:S(2)}, u32[]{:S(2)}) collective-permute-start(bf16[2,24,256]{2,1,0:T(8,128)(2,1)S(1)} %get-tuple-element.25.refs_3_), channel_id=1, source_target_pairs={{0,24},{4,28},{8,16},{12,20},{16,8},{20,12},{24,0},{28,4},{1,25},{... | collective-permute-start | bytes 73736 | tf_op jit(solution)/shard_map/ppermute | solution.py:235
  8.5 0.2 collective-permute-start.3
  8.7 0.6 %collective-permute-done.1.refs_2_ = bf16[2,24,256]{2,1,0:T(8,128)(2,1)S(1)} collective-permute-done((bf16[2,24,256]{2,1,0:T(8,128)(2,1)S(1)}, bf16[2,24,256]{2,1,0:T(8,128)(2,1)S(1)}, u32[]{:S(2)}, u32[]{:S(2)}) %collective-permute-start.1) | collective-permute-done | bytes 24608 | tf_op jit(solution)/shard_map/ppermute | solution.py:235
  9.3 0.5 %shard_map.78 = (f32[4,48,256]{2,1,0:T(8,128)S(1)}, bf16[256,256]{1,0:T(8,128)(2,1)S(1)}, bf16[256,256]{1,0:T(8,128)(2,1)S(1)}, bf16[256,48]{1,0:T(8,128)(2,1)S(...) custom-call(bf16[2,128,256]{2,1,0:T(8,128)(2,1)S(1)} %collective-permute-done.refs_0_, ...), custom_call_target="tpu_custom_call" | custom-call | flops 5000000000 | tf_op jit(solution)/shard_map/pallas_call | solution.py:219
  9.8 2.8 %collective-permute-start.5 = (bf16[24,384]{1,0:T(8,128)(2,1)S(1)}, bf16[24,384]{1,0:T(8,128)(2,1)S(1)}, u32[]{:S(2)}, u32[]{:S(2)}) collective-permute-start(bf16[24,384]{1,0:T(8,128)(2,1)S(1)} %get-tuple-element.33), channel_id=1, source_target_pairs={{0,16},{4,20},{8,24},{12,28},{16,0},{20,4},{24,8},{28,12},{1,17},{... | collective-permute-start | bytes 55304 | tf_op jit(solution)/shard_map/ppermute | solution.py:235
  12.6 0.2 collective-permute-done.2.refs_0_
  12.8 0.5 %shard_map.79 = (bf16[272,128]{1,0:T(8,128)(2,1)S(1)}, bf16[272,128]{1,0:T(8,128)(2,1)S(1)}, bf16[24,384]{1,0:T(8,128)(2,1)S(1)}, bf16[24,384]{1,0:T(8,128)(2,1)S(1)}) custom-call(bf16[256,256]{1,0:T(8,128)(2,1)S(1)} %get-tuple-element.26.queries, bf16[256,256]{1,0:T(8,128)(2,1)S(1)} %get-tuple-element.27.aud_vals, ...), custom_call_target="tpu_custom_call" | custom-call | flops 5000000000 | tf_op jit(solution)/shard_map/pallas_call | solution.py:219
  13.3 0.6 %collective-permute-start.4 = (bf16[272,128]{1,0:T(8,128)(2,1)S(1)}, bf16[272,128]{1,0:T(8,128)(2,1)S(1)}, u32[]{:S(2)}, u32[]{:S(2)}) collective-permute-start(bf16[272,128]{1,0:T(8,128)(2,1)S(1)} %get-tuple-element.30), channel_id=1, source_target_pairs={{0,4},{4,0},{8,12},{12,8},{16,20},{20,16},{24,28},{28,24},{1,5},{5... | collective-permute-start | bytes 208904 | tf_op jit(solution)/shard_map/ppermute | solution.py:235
  13.9 2.0 %collective-permute-start.8 = (bf16[24,384]{1,0:T(8,128)(2,1)S(1)}, bf16[24,384]{1,0:T(8,128)(2,1)S(1)}, u32[]{:S(2)}, u32[]{:S(2)}) collective-permute-start(bf16[24,384]{1,0:T(8,128)(2,1)S(1)} %get-tuple-element.40), channel_id=1, source_target_pairs={{0,24},{4,28},{8,16},{12,20},{16,8},{20,12},{24,0},{28,4},{1,25},{... | collective-permute-start | bytes 55304 | tf_op jit(solution)/shard_map/ppermute | solution.py:235
  15.9 0.1 shard_map.80
  16.1 1.6 %collective-permute-done.4.refs_0_ = bf16[272,128]{1,0:T(8,128)(2,1)S(1)} collective-permute-done((bf16[272,128]{1,0:T(8,128)(2,1)S(1)}, bf16[272,128]{1,0:T(8,128)(2,1)S(1)}, u32[]{:S(2)}, u32[]{:S(2)}) %collective-permute-start.4) | collective-permute-done | bytes 69664 | tf_op jit(solution)/shard_map/ppermute | solution.py:235
  17.7 0.3 %shard_map.81 = (f32[128,256]{1,0:T(8,128)S(1)}, bf16[128,256]{1,0:T(8,128)(2,1)S(1)}, bf16[128,256]{1,0:T(8,128)(2,1)S(1)}, bf16[128,256]{1,0:T(8,128)(2,1)S(1)}) custom-call(s32[1]{0:T(128)} %bitcast.me, bf16[256,1024]{1,0:T(8,128)(2,1)S(1)} %copy-done, bf16[272,128]{1,0:T(8,128)(2,1)S(1)} %collective-permute-done.4.refs_0_, ...), custom_call_target="tpu_custom_call" | custom-call | flops 5000000000 | tf_op jit(solution)/shard_map/pallas_call | solution.py:219
  18.0 0.1 collective-permute-start.6
  18.0 1.6 %collective-permute-start.7 = (bf16[128,256]{1,0:T(8,128)(2,1)S(1)}, bf16[128,256]{1,0:T(8,128)(2,1)S(1)}, u32[]{:S(2)}, u32[]{:S(2)}) collective-permute-start(bf16[128,256]{1,0:T(8,128)(2,1)S(1)} %get-tuple-element.37), channel_id=1, source_target_pairs={{0,2},{1,3},{2,0},{3,1},{4,6},{5,7},{6,4},{7,5},{8,10},{9,11},{10,... | collective-permute-start | bytes 196616 | tf_op jit(solution)/shard_map/ppermute | solution.py:235
  19.7 0.3 %shard_map.83 = (f32[24,256]{1,0:T(8,128)S(1)}, bf16[152,256]{1,0:T(8,128)(2,1)S(1)}, bf16[24,256]{1,0:T(8,128)(2,1)S(1)}, bf16[24,256]{1,0:T(8,128)(2,1)S(1)}) custom-call(s32[1]{0:T(128)} %bitcast.me, bf16[256,1024]{1,0:T(8,128)(2,1)S(1)} %copy-done.1, f32[24,256]{1,0:T(8,128)S(1)} %get-tuple-element.34.refs_2_.mix, f32[24,256]{1,0:T(8,128)S(1)} %get-tuple-element.38.log, ...), custom_call_target="tpu_custom_call" | custom-call | flops 5000000000 | tf_op jit(solution)/shard_map/pallas_call | solution.py:219
  20.0 1.6 %collective-permute-start.10 = (bf16[24,256]{1,0:T(8,128)(2,1)S(1)}, bf16[24,256]{1,0:T(8,128)(2,1)S(1)}, u32[]{:S(2)}, u32[]{:S(2)}) collective-permute-start(bf16[24,256]{1,0:T(8,128)(2,1)S(1)} %get-tuple-element.43), channel_id=1, source_target_pairs={{0,2},{1,3},{2,0},{3,1},{4,6},{5,7},{6,4},{7,5},{8,10},{9,11},{10,... | collective-permute-start | bytes 36872 | tf_op jit(solution)/shard_map/ppermute | solution.py:235
  21.5 0.1 collective-permute-start.11
  21.6 0.6 %collective-permute-start.12 = (bf16[152,256]{1,0:T(8,128)(2,1)S(1)}, bf16[152,256]{1,0:T(8,128)(2,1)S(1)}, u32[]{:S(2)}, u32[]{:S(2)}) collective-permute-start(bf16[152,256]{1,0:T(8,128)(2,1)S(1)} %get-tuple-element.45), channel_id=1, source_target_pairs={{0,1},{1,0},{2,3},{3,2},{4,5},{5,4},{6,7},{7,6},{8,9},{9,8},{10,11... | collective-permute-start | bytes 233480 | tf_op jit(solution)/shard_map/ppermute | solution.py:235
  22.1 1.9 %collective-permute-done.10.refs_1_ = bf16[24,256]{1,0:T(8,128)(2,1)S(1)} collective-permute-done((bf16[24,256]{1,0:T(8,128)(2,1)S(1)}, bf16[24,256]{1,0:T(8,128)(2,1)S(1)}, u32[]{:S(2)}, u32[]{:S(2)}) %collective-permute-start.10) | collective-permute-done | bytes 12320 | tf_op jit(solution)/shard_map/ppermute | solution.py:235
  24.1 0.6 %collective-permute-done.11.refs_2_ = bf16[24,256]{1,0:T(8,128)(2,1)S(1)} collective-permute-done((bf16[24,256]{1,0:T(8,128)(2,1)S(1)}, bf16[24,256]{1,0:T(8,128)(2,1)S(1)}, u32[]{:S(2)}, u32[]{:S(2)}) %collective-permute-start.11) | collective-permute-done | bytes 12320 | tf_op jit(solution)/shard_map/ppermute | solution.py:235
  24.7 0.7 %shard_map.85 = (bf16[128,256]{1,0:T(8,128)(2,1)}, bf16[24,256]{1,0:T(8,128)(2,1)}) custom-call(f32[128,256]{1,0:T(8,128)S(1)} %shard_map.82.aud_sum, f32[24,256]{1,0:T(8,128)S(1)} %shard_map.84.vid_sum, bf16[152,256]{1,0:T(8,128)(2,1)S(1)} %collective-permute-done.12.core), custom_call_target="tpu_custom_call" | custom-call | flops 5000000000 | tf_op jit(solution)/shard_map/pallas_call | solution.py:219
  (15 shorter events, 0.1 us)
Async XLA Ops:
  1.5 7.7 %collective-permute-start = (bf16[2,128,256]{2,1,0:T(8,128)(2,1)S(1)}, bf16[2,128,256]{2,1,0:T(8,128)(2,1)S(1)}, u32[]{:S(2)}, u32[]{:S(2)}) collective-permute-start(bf16[2,128,256]{2,1,0:T(8,128)(2,1)S(1)} %get-tuple-element.24.refs_1_), channel_id=1, source_target_pairs={{0,4},{4,0},{8,12},{12,8},{16,20},{20,16},{24,28},{28,24},{1,5},{5... | collective-permute-start | bytes 393224 | tf_op jit(solution)/shard_map/ppermute | solution.py:235
  4.6 4.7 %collective-permute-start.1 = (bf16[2,24,256]{2,1,0:T(8,128)(2,1)S(1)}, bf16[2,24,256]{2,1,0:T(8,128)(2,1)S(1)}, u32[]{:S(2)}, u32[]{:S(2)}) collective-permute-start(bf16[2,24,256]{2,1,0:T(8,128)(2,1)S(1)} %get-tuple-element.25.refs_3_), channel_id=1, source_target_pairs={{0,16},{4,20},{8,24},{12,28},{16,0},{20,4},{24,8},{28,12},{1,17},{... | collective-permute-start | bytes 73736 | tf_op jit(solution)/shard_map/ppermute | solution.py:235
  7.1 5.6 %collective-permute-start.2 = (bf16[2,24,256]{2,1,0:T(8,128)(2,1)S(1)}, bf16[2,24,256]{2,1,0:T(8,128)(2,1)S(1)}, u32[]{:S(2)}, u32[]{:S(2)}) collective-permute-start(bf16[2,24,256]{2,1,0:T(8,128)(2,1)S(1)} %get-tuple-element.25.refs_3_), channel_id=1, source_target_pairs={{0,24},{4,28},{8,16},{12,20},{16,8},{20,12},{24,0},{28,4},{1,25},{... | collective-permute-start | bytes 73736 | tf_op jit(solution)/shard_map/ppermute | solution.py:235
  8.5 4.3 %collective-permute-start.3 = (bf16[2,24,256]{2,1,0:T(8,128)(2,1)S(1)}, bf16[2,24,256]{2,1,0:T(8,128)(2,1)S(1)}, u32[]{:S(2)}, u32[]{:S(2)}) collective-permute-start(bf16[2,24,256]{2,1,0:T(8,128)(2,1)S(1)} %get-tuple-element.25.refs_3_), channel_id=1, source_target_pairs={{0,8},{4,12},{8,0},{12,4},{16,24},{20,28},{24,16},{28,20},{1,9},{5... | collective-permute-start | bytes 73736 | tf_op jit(solution)/shard_map/ppermute | solution.py:235
  9.8 6.1 %collective-permute-start.5 = (bf16[24,384]{1,0:T(8,128)(2,1)S(1)}, bf16[24,384]{1,0:T(8,128)(2,1)S(1)}, u32[]{:S(2)}, u32[]{:S(2)}) collective-permute-start(bf16[24,384]{1,0:T(8,128)(2,1)S(1)} %get-tuple-element.33), channel_id=1, source_target_pairs={{0,16},{4,20},{8,24},{12,28},{16,0},{20,4},{24,8},{28,12},{1,17},{... | collective-permute-start | bytes 55304 | tf_op jit(solution)/shard_map/ppermute | solution.py:235
  12.8 3.1 %copy-start = (bf16[256,1024]{1,0:T(8,128)(2,1)S(1)}, bf16[256,1024]{1,0:T(8,128)(2,1)}, u32[]{:S(2)}) copy-start(bf16[256,1024]{1,0:T(8,128)(2,1)} %proj.2) | copy-start | bytes 1572868
  13.3 4.4 %collective-permute-start.4 = (bf16[272,128]{1,0:T(8,128)(2,1)S(1)}, bf16[272,128]{1,0:T(8,128)(2,1)S(1)}, u32[]{:S(2)}, u32[]{:S(2)}) collective-permute-start(bf16[272,128]{1,0:T(8,128)(2,1)S(1)} %get-tuple-element.30), channel_id=1, source_target_pairs={{0,4},{4,0},{8,12},{12,8},{16,20},{20,16},{24,28},{28,24},{1,5},{5... | collective-permute-start | bytes 208904 | tf_op jit(solution)/shard_map/ppermute | solution.py:235
  13.9 5.7 %collective-permute-start.8 = (bf16[24,384]{1,0:T(8,128)(2,1)S(1)}, bf16[24,384]{1,0:T(8,128)(2,1)S(1)}, u32[]{:S(2)}, u32[]{:S(2)}) collective-permute-start(bf16[24,384]{1,0:T(8,128)(2,1)S(1)} %get-tuple-element.40), channel_id=1, source_target_pairs={{0,24},{4,28},{8,16},{12,20},{16,8},{20,12},{24,0},{28,4},{1,25},{... | collective-permute-start | bytes 55304 | tf_op jit(solution)/shard_map/ppermute | solution.py:235
  15.9 3.8 %collective-permute-start.9 = (bf16[24,384]{1,0:T(8,128)(2,1)S(1)}, bf16[24,384]{1,0:T(8,128)(2,1)S(1)}, u32[]{:S(2)}, u32[]{:S(2)}) collective-permute-start(bf16[24,384]{1,0:T(8,128)(2,1)S(1)} %get-tuple-element.41), channel_id=1, source_target_pairs={{0,8},{4,12},{8,0},{12,4},{16,24},{20,28},{24,16},{28,20},{1,9},{5... | collective-permute-start | bytes 55304 | tf_op jit(solution)/shard_map/ppermute | solution.py:235
  17.7 2.0 %copy-start.1 = (bf16[256,1024]{1,0:T(8,128)(2,1)S(1)}, bf16[256,1024]{1,0:T(8,128)(2,1)}, u32[]{:S(2)}) copy-start(bf16[256,1024]{1,0:T(8,128)(2,1)} %proj.3) | copy-start | bytes 1572868
  18.0 6.7 %collective-permute-start.6 = (bf16[128,256]{1,0:T(8,128)(2,1)S(1)}, bf16[128,256]{1,0:T(8,128)(2,1)S(1)}, u32[]{:S(2)}, u32[]{:S(2)}) collective-permute-start(bf16[128,256]{1,0:T(8,128)(2,1)S(1)} %get-tuple-element.36), channel_id=1, source_target_pairs={{0,3},{1,2},{2,1},{3,0},{4,7},{5,6},{6,5},{7,4},{8,11},{9,10},{10,... | collective-permute-start | bytes 196616 | tf_op jit(solution)/shard_map/ppermute | solution.py:235
  18.0 6.6 %collective-permute-start.7 = (bf16[128,256]{1,0:T(8,128)(2,1)S(1)}, bf16[128,256]{1,0:T(8,128)(2,1)S(1)}, u32[]{:S(2)}, u32[]{:S(2)}) collective-permute-start(bf16[128,256]{1,0:T(8,128)(2,1)S(1)} %get-tuple-element.37), channel_id=1, source_target_pairs={{0,2},{1,3},{2,0},{3,1},{4,6},{5,7},{6,4},{7,5},{8,10},{9,11},{10,... | collective-permute-start | bytes 196616 | tf_op jit(solution)/shard_map/ppermute | solution.py:235
  20.0 4.1 %collective-permute-start.10 = (bf16[24,256]{1,0:T(8,128)(2,1)S(1)}, bf16[24,256]{1,0:T(8,128)(2,1)S(1)}, u32[]{:S(2)}, u32[]{:S(2)}) collective-permute-start(bf16[24,256]{1,0:T(8,128)(2,1)S(1)} %get-tuple-element.43), channel_id=1, source_target_pairs={{0,2},{1,3},{2,0},{3,1},{4,6},{5,7},{6,4},{7,5},{8,10},{9,11},{10,... | collective-permute-start | bytes 36872 | tf_op jit(solution)/shard_map/ppermute | solution.py:235
  21.5 3.1 %collective-permute-start.11 = (bf16[24,256]{1,0:T(8,128)(2,1)S(1)}, bf16[24,256]{1,0:T(8,128)(2,1)S(1)}, u32[]{:S(2)}, u32[]{:S(2)}) collective-permute-start(bf16[24,256]{1,0:T(8,128)(2,1)S(1)} %get-tuple-element.44), channel_id=1, source_target_pairs={{0,3},{1,2},{2,1},{3,0},{4,7},{5,6},{6,5},{7,4},{8,11},{9,10},{10,... | collective-permute-start | bytes 36872 | tf_op jit(solution)/shard_map/ppermute | solution.py:235
  21.6 3.1 %collective-permute-start.12 = (bf16[152,256]{1,0:T(8,128)(2,1)S(1)}, bf16[152,256]{1,0:T(8,128)(2,1)S(1)}, u32[]{:S(2)}, u32[]{:S(2)}) collective-permute-start(bf16[152,256]{1,0:T(8,128)(2,1)S(1)} %get-tuple-element.45), channel_id=1, source_target_pairs={{0,1},{1,0},{2,3},{3,2},{4,5},{5,4},{6,7},{7,6},{8,9},{9,8},{10,11... | collective-permute-start | bytes 233480 | tf_op jit(solution)/shard_map/ppermute | solution.py:235

commit v15 on v14

--- a/solution.py
+++ b/solution.py
@@ -14,7 +14,7 @@
 SCALE = HEAD_DIM ** (-0.5) * math.log2(math.e)
 VMEM_LIMIT = 48 * 1024 * 1024
 COST = 5 * 10**9
-COST_ADD = 10**3
+COST_LOW = 10**3
 BF16 = jnp.bfloat16
 F32 = jnp.float32
 
@@ -171,17 +171,18 @@
     return mix / total
 
 
-def project(mix, proj, me, outs):
-    step = outs[0].shape[1]
-    for i, out in enumerate(outs):
-        block = pl.ds(pl.multiple_of(partner(me, i, len(outs)) * step, step), step)
-        out[...] = dot(mix, proj[:, block]).astype(out.dtype)
-
-
-def project_audio(me, proj, states, outs):
+def project(mix, proj, me, k, out):
+    step = out.shape[1]
+    block = pl.ds(pl.multiple_of((me ^ k) * step, step), step)
+    out[...] = dot(mix, proj[:, block]).astype(out.dtype)
+
+
+def project_audio(me, proj, states, mix_out, outs):
     width = proj.shape[0]
-    mix = merge([get_rows(ref, width) for ref in states]).reshape(width, -1)
-    project(mix.T.astype(BF16), proj, me[0], outs)
+    mix = merge([get_rows(ref, width) for ref in states]).reshape(width, -1).T.astype(BF16)
+    mix_out[...] = mix
+    for k, out in enumerate(outs, 2):
+        project(mix, proj, me[0], k, out)
 
 
 def merge_first(mine, got, _, mix_out, log_out):
@@ -193,11 +194,22 @@
     log_out[...] = top + jnp.log2(total)
 
 
-def project_video(me, proj, mix_log, states, aud_core, outs):
+def project_video(me, proj, mix_log, states, mix_out, outs):
     mix = merge([tuple(ref[...] for ref in mix_log)] + [get_cols(ref, proj.shape[0]) for ref in states])
-    aud_rows = aud_core.shape[0]
-    outs[1][:aud_rows, :] = aud_core[...]
-    project(mix.astype(BF16), proj, me[0], [outs[0], outs[1].at[aud_rows:, :], *outs[2:]])
+    mix = mix.astype(BF16)
+    mix_out[...] = mix
+    for k, out in enumerate(outs, 2):
+        project(mix, proj, me[0], k, out)
+
+
+def project_chip(me, aud_mix, vid_mix, aud_proj, vid_proj, aud_own, vid_own, core):
+    aud_rows = aud_mix.shape[0]
+    for mix, proj, own, rows in (
+        (aud_mix, aud_proj, aud_own, slice(0, aud_rows)),
+        (vid_mix, vid_proj, vid_own, slice(aud_rows, None)),
+    ):
+        project(mix[...], proj, me[0], 0, own)
+        project(mix[...], proj, me[0], 1, core.at[rows, :])
 
 
 def add_terms(*refs):
@@ -225,10 +237,6 @@
         compiler_params=pltpu.CompilerParams(vmem_limit_bytes=VMEM_LIMIT),
         cost_estimate=pl.CostEstimate(flops=cost, bytes_accessed=0, transcendentals=0),
     )(*args)
-
-
-def partner(index, k, size):
-    return index ^ k
 
 
 def swap(block, axis, distance):
@@ -299,30 +307,43 @@
     mix_log = call(
         merge_first, [shape(vid_rows, width, dtype=F32)] * 2, [cols.pop(), cols.pop(0), audio_proj]
     )
-    aud_terms = call(
-        lambda me, proj, *refs: project_audio(me, proj, refs[:aud_count], refs[aud_count + 1 :]),
-        [shape(aud_rows, step, dtype=F32)] + [shape(aud_rows, step)] * (peers - 1),
+    aud_mix, *aud_terms = call(
+        lambda me, proj, *refs: project_audio(
+            me, proj, refs[:aud_count], refs[aud_count + 1], refs[aud_count + 2 :]
+        ),
+        [shape(aud_rows, width)] + [shape(aud_rows, step)] * (peers - 2),
         [me, audio_proj, *rows, mix_log[0]],
         in_specs=[smem, vmem] + [vmem] * aud_count + [pl.BlockSpec(memory_space=pl.ANY)],
-    )
-    vid_terms = call(
-        lambda me, proj, mix, log, core, *refs: project_video(
-            me, proj, (mix, log), refs[: len(cols)], core, refs[len(cols) :]
+        cost=COST_LOW,
+    )
+    vid_mix, *vid_terms = call(
+        lambda me, proj, mix, log, _, *refs: project_video(
+            me, proj, (mix, log), refs[: len(cols)], refs[len(cols)], refs[len(cols) + 1 :]
         ),
-        [shape(vid_rows, step, dtype=F32), shape(aud_rows + vid_rows, step)]
-        + [shape(vid_rows, step)] * (peers - 2),
-        [me, video_proj, *mix_log, aud_terms[1], *cols],
-        in_specs=[smem] + [vmem] * (len(cols) + 4),
-    )
-    vid_got = [swap(vid_terms[k], "head", k) for k in range(2, peers)]
-    core_got = swap(vid_terms[1], "head", 1)
-    aud_got = [swap(aud_terms[k], "head", k) for k in reversed(range(2, peers))]
-    aud_sum = call(add_terms, [shape(aud_rows, step, dtype=F32)], [aud_terms[0], *aud_got])[0]
+        [shape(vid_rows, width)] + [shape(vid_rows, step)] * (peers - 2),
+        [me, video_proj, *mix_log, aud_mix, *cols],
+        in_specs=[smem] + [vmem] * 3 + [pl.BlockSpec(memory_space=pl.ANY)] + [vmem] * len(cols),
+    )
+    aud_own, vid_own, core = call(
+        project_chip,
+        [
+            shape(aud_rows, step, dtype=F32),
+            shape(vid_rows, step, dtype=F32),
+            shape(aud_rows + vid_rows, step),
+        ],
+        [me, aud_mix, vid_mix, audio_proj, video_proj],
+        in_specs=[smem] + [vmem] * 4,
+        cost=COST_LOW,
+    )
+    vid_got = [swap(term, "head", k) for k, term in enumerate(vid_terms, 2)]
+    core_got = swap(core, "head", 1)
+    aud_got = [swap(term, "head", k) for k, term in reversed([*enumerate(aud_terms, 2)])]
+    aud_sum = call(add_terms, [shape(aud_rows, step, dtype=F32)], [aud_own, *aud_got])[0]
     vid_sum = call(
-        add_terms, [shape(vid_rows, step, dtype=F32)], [vid_terms[0], *vid_got], cost=COST_ADD
+        add_terms, [shape(vid_rows, step, dtype=F32)], [vid_own, *vid_got], cost=COST_LOW
     )[0]
     return tuple(
-        call(add_core, [shape(aud_rows, step), shape(vid_rows, step)], [aud_sum, vid_sum, core_got])
+        call(add_core, [shape(aud_rows, step), shape(vid_rows, step)], [aud_sum, vid_sum, core_got], cost=COST_LOW)
     )
 
 

time: 25.5 us -> 25.5 us (level)
    pallas_call x9 -> x10, Pallas kernels: 3.33 us -> 3.46 us  [call(): pl.pallas_call(body, out_shape=out_shape, in_specs=in_specs or [vmem] * l...]
  transfers between devices with their start and end apart: 13 -> 13, of which waited for: 5 -> 6; matrix products, arithmetic and copies ran while one was open for 0% -> 0% of each run, Pallas kernels for 7% -> 7%
where the time goes in v15:
time: 25.5 us; the launch traced here: 25.3 us
  starting transfers between devices  16.5 us (65%)
  waiting for transfers between devices  4.64 us (18%)
  Pallas kernels  3.46 us (14%)
  between operations  0.73 us (3%)
    ppermute x13, starting transfers between devices, swap(): lax.ppermute(block, axis, [(i, i ^ distance) for i in range(lax.axis_size...  16.5 us
    ppermute x13, waiting for transfers between devices, swap(): lax.ppermute(block, axis, [(i, i ^ distance) for i in range(lax.axis_size...  4.64 us
    pallas_call x10, Pallas kernels, call(): pl.pallas_call(body, out_shape=out_shape, in_specs=in_specs or [vmem] * l...  3.46 us
  transfers between devices with their start and end apart: 13, of which 6 were waited for; matrix products, arithmetic and copies ran while one was open for 0% of the time, Pallas kernels for 7%

profile of v15, /device:TPU:0, one launch (start us, length us, event | category | flops | bytes accessed | tf_op | source)
XLA Modules:
  0.0 25.3 jit_solution(7522183508632634338)
XLA Ops:
  0.6 0.9 %shard_map.77 = (bf16[2,128,256]{2,1,0:T(8,128)(2,1)S(1)}, bf16[2,24,256]{2,1,0:T(8,128)(2,1)S(1)}) custom-call(bf16[128,256]{1,0:T(8,128)(2,1)} %aud_ref.1, bf16[128,256]{1,0:T(8,128)(2,1)} %aud_val.1, bf16[24,256]{1,0:T(8,128)(2,1)} %vid_ref.1, bf16[24,256]{1,0:T(8,128)(2,1)} %vid_val.1), custom_call_target="tpu_custom_call" | custom-call | flops 5000000000 | tf_op jit(solution)/shard_map/pallas_call | solution.py:231
  1.5 3.0 %collective-permute-start = (bf16[2,128,256]{2,1,0:T(8,128)(2,1)S(1)}, bf16[2,128,256]{2,1,0:T(8,128)(2,1)S(1)}, u32[]{:S(2)}, u32[]{:S(2)}) collective-permute-start(bf16[2,128,256]{2,1,0:T(8,128)(2,1)S(1)} %get-tuple-element.25.refs_1_), channel_id=1, source_target_pairs={{0,4},{4,0},{8,12},{12,8},{16,20},{20,16},{24,28},{28,24},{1,5},{5... | collective-permute-start | bytes 393224 | tf_op jit(solution)/shard_map/ppermute | solution.py:243
  4.6 2.6 %collective-permute-start.1 = (bf16[2,24,256]{2,1,0:T(8,128)(2,1)S(1)}, bf16[2,24,256]{2,1,0:T(8,128)(2,1)S(1)}, u32[]{:S(2)}, u32[]{:S(2)}) collective-permute-start(bf16[2,24,256]{2,1,0:T(8,128)(2,1)S(1)} %get-tuple-element.26.refs_3_), channel_id=1, source_target_pairs={{0,16},{4,20},{8,24},{12,28},{16,0},{20,4},{24,8},{28,12},{1,17},{... | collective-permute-start | bytes 73736 | tf_op jit(solution)/shard_map/ppermute | solution.py:243
  7.1 1.3 %collective-permute-start.2 = (bf16[2,24,256]{2,1,0:T(8,128)(2,1)S(1)}, bf16[2,24,256]{2,1,0:T(8,128)(2,1)S(1)}, u32[]{:S(2)}, u32[]{:S(2)}) collective-permute-start(bf16[2,24,256]{2,1,0:T(8,128)(2,1)S(1)} %get-tuple-element.26.refs_3_), channel_id=1, source_target_pairs={{0,24},{4,28},{8,16},{12,20},{16,8},{20,12},{24,0},{28,4},{1,25},{... | collective-permute-start | bytes 73736 | tf_op jit(solution)/shard_map/ppermute | solution.py:243
  8.5 0.2 collective-permute-start.3
  8.7 0.6 %collective-permute-done.1.refs_2_ = bf16[2,24,256]{2,1,0:T(8,128)(2,1)S(1)} collective-permute-done((bf16[2,24,256]{2,1,0:T(8,128)(2,1)S(1)}, bf16[2,24,256]{2,1,0:T(8,128)(2,1)S(1)}, u32[]{:S(2)}, u32[]{:S(2)}) %collective-permute-start.1) | collective-permute-done | bytes 24608 | tf_op jit(solution)/shard_map/ppermute | solution.py:243
  9.3 0.5 %shard_map.78 = (f32[4,48,256]{2,1,0:T(8,128)S(1)}, bf16[256,256]{1,0:T(8,128)(2,1)S(1)}, bf16[256,256]{1,0:T(8,128)(2,1)S(1)}, bf16[256,48]{1,0:T(8,128)(2,1)S(...) custom-call(bf16[2,128,256]{2,1,0:T(8,128)(2,1)S(1)} %collective-permute-done.refs_0_, ...), custom_call_target="tpu_custom_call" | custom-call | flops 5000000000 | tf_op jit(solution)/shard_map/pallas_call | solution.py:231
  9.8 2.8 %collective-permute-start.5 = (bf16[24,384]{1,0:T(8,128)(2,1)S(1)}, bf16[24,384]{1,0:T(8,128)(2,1)S(1)}, u32[]{:S(2)}, u32[]{:S(2)}) collective-permute-start(bf16[24,384]{1,0:T(8,128)(2,1)S(1)} %get-tuple-element.34), channel_id=1, source_target_pairs={{0,16},{4,20},{8,24},{12,28},{16,0},{20,4},{24,8},{28,12},{1,17},{... | collective-permute-start | bytes 55304 | tf_op jit(solution)/shard_map/ppermute | solution.py:243
  12.6 0.2 collective-permute-done.2.refs_0_
  12.8 0.5 %shard_map.79 = (bf16[272,128]{1,0:T(8,128)(2,1)S(1)}, bf16[272,128]{1,0:T(8,128)(2,1)S(1)}, bf16[24,384]{1,0:T(8,128)(2,1)S(1)}, bf16[24,384]{1,0:T(8,128)(2,1)S(1)}) custom-call(bf16[256,256]{1,0:T(8,128)(2,1)S(1)} %get-tuple-element.27.queries, bf16[256,256]{1,0:T(8,128)(2,1)S(1)} %get-tuple-element.28.aud_vals, ...), custom_call_target="tpu_custom_call" | custom-call | flops 5000000000 | tf_op jit(solution)/shard_map/pallas_call | solution.py:231
  13.3 0.6 %collective-permute-start.4 = (bf16[272,128]{1,0:T(8,128)(2,1)S(1)}, bf16[272,128]{1,0:T(8,128)(2,1)S(1)}, u32[]{:S(2)}, u32[]{:S(2)}) collective-permute-start(bf16[272,128]{1,0:T(8,128)(2,1)S(1)} %get-tuple-element.31), channel_id=1, source_target_pairs={{0,4},{4,0},{8,12},{12,8},{16,20},{20,16},{24,28},{28,24},{1,5},{5... | collective-permute-start | bytes 208904 | tf_op jit(solution)/shard_map/ppermute | solution.py:243
  13.9 2.0 %collective-permute-start.6 = (bf16[24,384]{1,0:T(8,128)(2,1)S(1)}, bf16[24,384]{1,0:T(8,128)(2,1)S(1)}, u32[]{:S(2)}, u32[]{:S(2)}) collective-permute-start(bf16[24,384]{1,0:T(8,128)(2,1)S(1)} %get-tuple-element.38), channel_id=1, source_target_pairs={{0,24},{4,28},{8,16},{12,20},{16,8},{20,12},{24,0},{28,4},{1,25},{... | collective-permute-start | bytes 55304 | tf_op jit(solution)/shard_map/ppermute | solution.py:243
  15.9 0.1 shard_map.80
  16.1 1.6 %collective-permute-done.4.refs_0_ = bf16[272,128]{1,0:T(8,128)(2,1)S(1)} collective-permute-done((bf16[272,128]{1,0:T(8,128)(2,1)S(1)}, bf16[272,128]{1,0:T(8,128)(2,1)S(1)}, u32[]{:S(2)}, u32[]{:S(2)}) %collective-permute-start.4) | collective-permute-done | bytes 69664 | tf_op jit(solution)/shard_map/ppermute | solution.py:243
  17.7 0.3 %shard_map.81 = (bf16[128,256]{1,0:T(8,128)(2,1)S(1)}, bf16[128,256]{1,0:T(8,128)(2,1)S(1)}, bf16[128,256]{1,0:T(8,128)(2,1)S(1)}) custom-call(s32[1]{0:T(128)} %bitcast.me, bf16[256,1024]{1,0:T(8,128)(2,1)S(1)} %copy-done, bf16[272,128]{1,0:T(8,128)(2,1)S(1)} %collective-permute-done.4.refs_0_, bf16[272,128]{1,0:T(8,128)(2,1)S(1)} %get-tuple-element.32.refs_1_, ...), custom_call_target="tpu_custom_call" | custom-call | flops 1000 | tf_op jit(solution)/shard_map/pallas_call | solution.py:231
  18.0 1.6 %collective-permute-start.9 = (bf16[128,256]{1,0:T(8,128)(2,1)S(1)}, bf16[128,256]{1,0:T(8,128)(2,1)S(1)}, u32[]{:S(2)}, u32[]{:S(2)}) collective-permute-start(bf16[128,256]{1,0:T(8,128)(2,1)S(1)} %get-tuple-element.43), channel_id=1, source_target_pairs={{0,2},{1,3},{2,0},{3,1},{4,6},{5,7},{6,4},{7,5},{8,10},{9,11},{10,... | collective-permute-start | bytes 196616 | tf_op jit(solution)/shard_map/ppermute | solution.py:243
  19.6 0.1 collective-permute-done.7.refs_1_
  19.7 0.3 %shard_map.82 = (bf16[24,256]{1,0:T(8,128)(2,1)S(1)}, bf16[24,256]{1,0:T(8,128)(2,1)S(1)}, bf16[24,256]{1,0:T(8,128)(2,1)S(1)}) custom-call(s32[1]{0:T(128)} %bitcast.me, bf16[256,1024]{1,0:T(8,128)(2,1)S(1)} %copy-done.1, f32[24,256]{1,0:T(8,128)S(1)} %get-tuple-element.35.refs_2_.mix, f32[24,256]{1,0:T(8,128)S(1)} %get-tuple-element.37.log, ...), custom_call_target="tpu_custom_call" | custom-call | flops 5000000000 | tf_op jit(solution)/shard_map/pallas_call | solution.py:231
  19.9 1.5 %collective-permute-start.10 = (bf16[24,256]{1,0:T(8,128)(2,1)S(1)}, bf16[24,256]{1,0:T(8,128)(2,1)S(1)}, u32[]{:S(2)}, u32[]{:S(2)}) collective-permute-start(bf16[24,256]{1,0:T(8,128)(2,1)S(1)} %get-tuple-element.45), channel_id=1, source_target_pairs={{0,2},{1,3},{2,0},{3,1},{4,6},{5,7},{6,4},{7,5},{8,10},{9,11},{10,... | collective-permute-start | bytes 36872 | tf_op jit(solution)/shard_map/ppermute | solution.py:243
  21.5 0.2 shard_map.83
  21.7 0.6 %collective-permute-start.12 = (bf16[152,256]{1,0:T(8,128)(2,1)S(1)}, bf16[152,256]{1,0:T(8,128)(2,1)S(1)}, u32[]{:S(2)}, u32[]{:S(2)}) collective-permute-start(bf16[152,256]{1,0:T(8,128)(2,1)S(1)} %get-tuple-element.47), channel_id=1, source_target_pairs={{0,1},{1,0},{2,3},{3,2},{4,5},{5,4},{6,7},{7,6},{8,9},{9,8},{10,11... | collective-permute-start | bytes 233480 | tf_op jit(solution)/shard_map/ppermute | solution.py:243
  22.4 1.7 %collective-permute-done.10.refs_1_ = bf16[24,256]{1,0:T(8,128)(2,1)S(1)} collective-permute-done((bf16[24,256]{1,0:T(8,128)(2,1)S(1)}, bf16[24,256]{1,0:T(8,128)(2,1)S(1)}, u32[]{:S(2)}, u32[]{:S(2)}) %collective-permute-start.10) | collective-permute-done | bytes 12320 | tf_op jit(solution)/shard_map/ppermute | solution.py:243
  24.0 0.6 %collective-permute-done.11.refs_2_ = bf16[24,256]{1,0:T(8,128)(2,1)S(1)} collective-permute-done((bf16[24,256]{1,0:T(8,128)(2,1)S(1)}, bf16[24,256]{1,0:T(8,128)(2,1)S(1)}, u32[]{:S(2)}, u32[]{:S(2)}) %collective-permute-start.11) | collective-permute-done | bytes 12320 | tf_op jit(solution)/shard_map/ppermute | solution.py:243
  24.7 0.7 %shard_map.86 = (bf16[128,256]{1,0:T(8,128)(2,1)}, bf16[24,256]{1,0:T(8,128)(2,1)}) custom-call(f32[128,256]{1,0:T(8,128)S(1)} %shard_map.84.aud_sum, f32[24,256]{1,0:T(8,128)S(1)} %shard_map.85.vid_sum, bf16[152,256]{1,0:T(8,128)(2,1)S(1)} %collective-permute-done.12.core), custom_call_target="tpu_custom_call" | custom-call | flops 1000 | tf_op jit(solution)/shard_map/pallas_call | solution.py:231
  (16 shorter events, 0.2 us)
Async XLA Ops:
  1.5 7.7 %collective-permute-start = (bf16[2,128,256]{2,1,0:T(8,128)(2,1)S(1)}, bf16[2,128,256]{2,1,0:T(8,128)(2,1)S(1)}, u32[]{:S(2)}, u32[]{:S(2)}) collective-permute-start(bf16[2,128,256]{2,1,0:T(8,128)(2,1)S(1)} %get-tuple-element.25.refs_1_), channel_id=1, source_target_pairs={{0,4},{4,0},{8,12},{12,8},{16,20},{20,16},{24,28},{28,24},{1,5},{5... | collective-permute-start | bytes 393224 | tf_op jit(solution)/shard_map/ppermute | solution.py:243
  4.6 4.7 %collective-permute-start.1 = (bf16[2,24,256]{2,1,0:T(8,128)(2,1)S(1)}, bf16[2,24,256]{2,1,0:T(8,128)(2,1)S(1)}, u32[]{:S(2)}, u32[]{:S(2)}) collective-permute-start(bf16[2,24,256]{2,1,0:T(8,128)(2,1)S(1)} %get-tuple-element.26.refs_3_), channel_id=1, source_target_pairs={{0,16},{4,20},{8,24},{12,28},{16,0},{20,4},{24,8},{28,12},{1,17},{... | collective-permute-start | bytes 73736 | tf_op jit(solution)/shard_map/ppermute | solution.py:243
  7.1 5.6 %collective-permute-start.2 = (bf16[2,24,256]{2,1,0:T(8,128)(2,1)S(1)}, bf16[2,24,256]{2,1,0:T(8,128)(2,1)S(1)}, u32[]{:S(2)}, u32[]{:S(2)}) collective-permute-start(bf16[2,24,256]{2,1,0:T(8,128)(2,1)S(1)} %get-tuple-element.26.refs_3_), channel_id=1, source_target_pairs={{0,24},{4,28},{8,16},{12,20},{16,8},{20,12},{24,0},{28,4},{1,25},{... | collective-permute-start | bytes 73736 | tf_op jit(solution)/shard_map/ppermute | solution.py:243
  8.5 4.3 %collective-permute-start.3 = (bf16[2,24,256]{2,1,0:T(8,128)(2,1)S(1)}, bf16[2,24,256]{2,1,0:T(8,128)(2,1)S(1)}, u32[]{:S(2)}, u32[]{:S(2)}) collective-permute-start(bf16[2,24,256]{2,1,0:T(8,128)(2,1)S(1)} %get-tuple-element.26.refs_3_), channel_id=1, source_target_pairs={{0,8},{4,12},{8,0},{12,4},{16,24},{20,28},{24,16},{28,20},{1,9},{5... | collective-permute-start | bytes 73736 | tf_op jit(solution)/shard_map/ppermute | solution.py:243
  9.8 6.1 %collective-permute-start.5 = (bf16[24,384]{1,0:T(8,128)(2,1)S(1)}, bf16[24,384]{1,0:T(8,128)(2,1)S(1)}, u32[]{:S(2)}, u32[]{:S(2)}) collective-permute-start(bf16[24,384]{1,0:T(8,128)(2,1)S(1)} %get-tuple-element.34), channel_id=1, source_target_pairs={{0,16},{4,20},{8,24},{12,28},{16,0},{20,4},{24,8},{28,12},{1,17},{... | collective-permute-start | bytes 55304 | tf_op jit(solution)/shard_map/ppermute | solution.py:243
  12.8 3.1 %copy-start = (bf16[256,1024]{1,0:T(8,128)(2,1)S(1)}, bf16[256,1024]{1,0:T(8,128)(2,1)}, u32[]{:S(2)}) copy-start(bf16[256,1024]{1,0:T(8,128)(2,1)} %aud_proj.1) | copy-start | bytes 1572868
  13.3 4.4 %collective-permute-start.4 = (bf16[272,128]{1,0:T(8,128)(2,1)S(1)}, bf16[272,128]{1,0:T(8,128)(2,1)S(1)}, u32[]{:S(2)}, u32[]{:S(2)}) collective-permute-start(bf16[272,128]{1,0:T(8,128)(2,1)S(1)} %get-tuple-element.31), channel_id=1, source_target_pairs={{0,4},{4,0},{8,12},{12,8},{16,20},{20,16},{24,28},{28,24},{1,5},{5... | collective-permute-start | bytes 208904 | tf_op jit(solution)/shard_map/ppermute | solution.py:243
  13.9 5.7 %collective-permute-start.6 = (bf16[24,384]{1,0:T(8,128)(2,1)S(1)}, bf16[24,384]{1,0:T(8,128)(2,1)S(1)}, u32[]{:S(2)}, u32[]{:S(2)}) collective-permute-start(bf16[24,384]{1,0:T(8,128)(2,1)S(1)} %get-tuple-element.38), channel_id=1, source_target_pairs={{0,24},{4,28},{8,16},{12,20},{16,8},{20,12},{24,0},{28,4},{1,25},{... | collective-permute-start | bytes 55304 | tf_op jit(solution)/shard_map/ppermute | solution.py:243
  15.9 3.8 %collective-permute-start.7 = (bf16[24,384]{1,0:T(8,128)(2,1)S(1)}, bf16[24,384]{1,0:T(8,128)(2,1)S(1)}, u32[]{:S(2)}, u32[]{:S(2)}) collective-permute-start(bf16[24,384]{1,0:T(8,128)(2,1)S(1)} %get-tuple-element.39), channel_id=1, source_target_pairs={{0,8},{4,12},{8,0},{12,4},{16,24},{20,28},{24,16},{28,20},{1,9},{5... | collective-permute-start | bytes 55304 | tf_op jit(solution)/shard_map/ppermute | solution.py:243
  16.1 3.6 %copy-start.1 = (bf16[256,1024]{1,0:T(8,128)(2,1)S(1)}, bf16[256,1024]{1,0:T(8,128)(2,1)}, u32[]{:S(2)}) copy-start(bf16[256,1024]{1,0:T(8,128)(2,1)} %vid_proj.1) | copy-start | bytes 1572868
  17.9 6.7 %collective-permute-start.8 = (bf16[128,256]{1,0:T(8,128)(2,1)S(1)}, bf16[128,256]{1,0:T(8,128)(2,1)S(1)}, u32[]{:S(2)}, u32[]{:S(2)}) collective-permute-start(bf16[128,256]{1,0:T(8,128)(2,1)S(1)} %get-tuple-element.42), channel_id=1, source_target_pairs={{0,3},{1,2},{2,1},{3,0},{4,7},{5,6},{6,5},{7,4},{8,11},{9,10},{10,... | collective-permute-start | bytes 196616 | tf_op jit(solution)/shard_map/ppermute | solution.py:243
  18.0 6.6 %collective-permute-start.9 = (bf16[128,256]{1,0:T(8,128)(2,1)S(1)}, bf16[128,256]{1,0:T(8,128)(2,1)S(1)}, u32[]{:S(2)}, u32[]{:S(2)}) collective-permute-start(bf16[128,256]{1,0:T(8,128)(2,1)S(1)} %get-tuple-element.43), channel_id=1, source_target_pairs={{0,2},{1,3},{2,0},{3,1},{4,6},{5,7},{6,4},{7,5},{8,10},{9,11},{10,... | collective-permute-start | bytes 196616 | tf_op jit(solution)/shard_map/ppermute | solution.py:243
  19.9 4.1 %collective-permute-start.10 = (bf16[24,256]{1,0:T(8,128)(2,1)S(1)}, bf16[24,256]{1,0:T(8,128)(2,1)S(1)}, u32[]{:S(2)}, u32[]{:S(2)}) collective-permute-start(bf16[24,256]{1,0:T(8,128)(2,1)S(1)} %get-tuple-element.45), channel_id=1, source_target_pairs={{0,2},{1,3},{2,0},{3,1},{4,6},{5,7},{6,4},{7,5},{8,10},{9,11},{10,... | collective-permute-start | bytes 36872 | tf_op jit(solution)/shard_map/ppermute | solution.py:243
  21.5 3.2 %collective-permute-start.11 = (bf16[24,256]{1,0:T(8,128)(2,1)S(1)}, bf16[24,256]{1,0:T(8,128)(2,1)S(1)}, u32[]{:S(2)}, u32[]{:S(2)}) collective-permute-start(bf16[24,256]{1,0:T(8,128)(2,1)S(1)} %get-tuple-element.46), channel_id=1, source_target_pairs={{0,3},{1,2},{2,1},{3,0},{4,7},{5,6},{6,5},{7,4},{8,11},{9,10},{10,... | collective-permute-start | bytes 36872 | tf_op jit(solution)/shard_map/ppermute | solution.py:243
  21.7 3.0 %collective-permute-start.12 = (bf16[152,256]{1,0:T(8,128)(2,1)S(1)}, bf16[152,256]{1,0:T(8,128)(2,1)S(1)}, u32[]{:S(2)}, u32[]{:S(2)}) collective-permute-start(bf16[152,256]{1,0:T(8,128)(2,1)S(1)} %get-tuple-element.47), channel_id=1, source_target_pairs={{0,1},{1,0},{2,3},{3,2},{4,5},{5,4},{6,7},{7,6},{8,9},{9,8},{10,11... | collective-permute-start | bytes 233480 | tf_op jit(solution)/shard_map/ppermute | solution.py:243

commit v16 on v14

--- a/solution.py
+++ b/solution.py
@@ -314,7 +314,7 @@
         [me, video_proj, *mix_log, aud_terms[1], *cols],
         in_specs=[smem] + [vmem] * (len(cols) + 4),
     )
-    vid_got = [swap(vid_terms[k], "head", k) for k in range(2, peers)]
+    vid_got = [swap(vid_terms[k], "head", k) for k in reversed(range(2, peers))]
     core_got = swap(vid_terms[1], "head", 1)
     aud_got = [swap(aud_terms[k], "head", k) for k in reversed(range(2, peers))]
     aud_sum = call(add_terms, [shape(aud_rows, step, dtype=F32)], [aud_terms[0], *aud_got])[0]

time: 25.5 us -> 26 us (1.020)
  waiting for transfers between devices: 4.86 us -> 5.54 us
  starting transfers between devices: 16.5 us -> 16.2 us
    ppermute x13, waiting for transfers between devices: 4.86 us -> 5.54 us  [swap(): lax.ppermute(block, axis, [(i, i ^ distance) for i in range(lax.axis_size...]
    ppermute x13, starting transfers between devices: 16.5 us -> 16.2 us  [swap(): lax.ppermute(block, axis, [(i, i ^ distance) for i in range(lax.axis_size...]
where the time goes in v16:
time: 26 us; the launch traced here: 25.8 us
  starting transfers between devices  16.2 us (62%)
  waiting for transfers between devices  5.54 us (21%)
  Pallas kernels  3.33 us (13%)
  between operations  0.71 us (3%)
    ppermute x13, starting transfers between devices, swap(): lax.ppermute(block, axis, [(i, i ^ distance) for i in range(lax.axis_size...  16.2 us
    ppermute x13, waiting for transfers between devices, swap(): lax.ppermute(block, axis, [(i, i ^ distance) for i in range(lax.axis_size...  5.54 us
    pallas_call x9, Pallas kernels, call(): pl.pallas_call(body, out_shape=out_shape, in_specs=in_specs or [vmem] * l...  3.33 us
  transfers between devices with their start and end apart: 13, of which 5 were waited for; matrix products, arithmetic and copies ran while one was open for 0% of the time, Pallas kernels for 7%

profile of v16, /device:TPU:0, one launch (start us, length us, event | category | flops | bytes accessed | tf_op | source)
XLA Modules:
  0.0 25.8 jit_solution(9137021025414454297)
XLA Ops:
  0.6 0.9 %shard_map.77 = (bf16[2,128,256]{2,1,0:T(8,128)(2,1)S(1)}, bf16[2,24,256]{2,1,0:T(8,128)(2,1)S(1)}) custom-call(bf16[128,256]{1,0:T(8,128)(2,1)} %aud_ref.1, bf16[128,256]{1,0:T(8,128)(2,1)} %aud_val.1, bf16[24,256]{1,0:T(8,128)(2,1)} %vid_ref.1, bf16[24,256]{1,0:T(8,128)(2,1)} %vid_val.1), custom_call_target="tpu_custom_call" | custom-call | flops 5000000000 | tf_op jit(solution)/shard_map/pallas_call | solution.py:219
  1.5 3.0 %collective-permute-start = (bf16[2,128,256]{2,1,0:T(8,128)(2,1)S(1)}, bf16[2,128,256]{2,1,0:T(8,128)(2,1)S(1)}, u32[]{:S(2)}, u32[]{:S(2)}) collective-permute-start(bf16[2,128,256]{2,1,0:T(8,128)(2,1)S(1)} %get-tuple-element.24.refs_1_), channel_id=1, source_target_pairs={{0,4},{4,0},{8,12},{12,8},{16,20},{20,16},{24,28},{28,24},{1,5},{5... | collective-permute-start | bytes 393224 | tf_op jit(solution)/shard_map/ppermute | solution.py:235
  4.6 2.6 %collective-permute-start.1 = (bf16[2,24,256]{2,1,0:T(8,128)(2,1)S(1)}, bf16[2,24,256]{2,1,0:T(8,128)(2,1)S(1)}, u32[]{:S(2)}, u32[]{:S(2)}) collective-permute-start(bf16[2,24,256]{2,1,0:T(8,128)(2,1)S(1)} %get-tuple-element.25.refs_3_), channel_id=1, source_target_pairs={{0,16},{4,20},{8,24},{12,28},{16,0},{20,4},{24,8},{28,12},{1,17},{... | collective-permute-start | bytes 73736 | tf_op jit(solution)/shard_map/ppermute | solution.py:235
  7.1 1.3 %collective-permute-start.2 = (bf16[2,24,256]{2,1,0:T(8,128)(2,1)S(1)}, bf16[2,24,256]{2,1,0:T(8,128)(2,1)S(1)}, u32[]{:S(2)}, u32[]{:S(2)}) collective-permute-start(bf16[2,24,256]{2,1,0:T(8,128)(2,1)S(1)} %get-tuple-element.25.refs_3_), channel_id=1, source_target_pairs={{0,24},{4,28},{8,16},{12,20},{16,8},{20,12},{24,0},{28,4},{1,25},{... | collective-permute-start | bytes 73736 | tf_op jit(solution)/shard_map/ppermute | solution.py:235
  8.5 0.2 collective-permute-start.3
  8.7 0.6 %collective-permute-done.1.refs_2_ = bf16[2,24,256]{2,1,0:T(8,128)(2,1)S(1)} collective-permute-done((bf16[2,24,256]{2,1,0:T(8,128)(2,1)S(1)}, bf16[2,24,256]{2,1,0:T(8,128)(2,1)S(1)}, u32[]{:S(2)}, u32[]{:S(2)}) %collective-permute-start.1) | collective-permute-done | bytes 24608 | tf_op jit(solution)/shard_map/ppermute | solution.py:235
  9.3 0.5 %shard_map.78 = (f32[4,48,256]{2,1,0:T(8,128)S(1)}, bf16[256,256]{1,0:T(8,128)(2,1)S(1)}, bf16[256,256]{1,0:T(8,128)(2,1)S(1)}, bf16[256,48]{1,0:T(8,128)(2,1)S(...) custom-call(bf16[2,128,256]{2,1,0:T(8,128)(2,1)S(1)} %collective-permute-done.refs_0_, ...), custom_call_target="tpu_custom_call" | custom-call | flops 5000000000 | tf_op jit(solution)/shard_map/pallas_call | solution.py:219
  9.8 2.8 %collective-permute-start.5 = (bf16[24,384]{1,0:T(8,128)(2,1)S(1)}, bf16[24,384]{1,0:T(8,128)(2,1)S(1)}, u32[]{:S(2)}, u32[]{:S(2)}) collective-permute-start(bf16[24,384]{1,0:T(8,128)(2,1)S(1)} %get-tuple-element.33), channel_id=1, source_target_pairs={{0,16},{4,20},{8,24},{12,28},{16,0},{20,4},{24,8},{28,12},{1,17},{... | collective-permute-start | bytes 55304 | tf_op jit(solution)/shard_map/ppermute | solution.py:235
  12.6 0.2 collective-permute-done.2.refs_0_
  12.8 0.5 %shard_map.79 = (bf16[272,128]{1,0:T(8,128)(2,1)S(1)}, bf16[272,128]{1,0:T(8,128)(2,1)S(1)}, bf16[24,384]{1,0:T(8,128)(2,1)S(1)}, bf16[24,384]{1,0:T(8,128)(2,1)S(1)}) custom-call(bf16[256,256]{1,0:T(8,128)(2,1)S(1)} %get-tuple-element.26.queries, bf16[256,256]{1,0:T(8,128)(2,1)S(1)} %get-tuple-element.27.aud_vals, ...), custom_call_target="tpu_custom_call" | custom-call | flops 5000000000 | tf_op jit(solution)/shard_map/pallas_call | solution.py:219
  13.3 0.6 %collective-permute-start.4 = (bf16[272,128]{1,0:T(8,128)(2,1)S(1)}, bf16[272,128]{1,0:T(8,128)(2,1)S(1)}, u32[]{:S(2)}, u32[]{:S(2)}) collective-permute-start(bf16[272,128]{1,0:T(8,128)(2,1)S(1)} %get-tuple-element.30), channel_id=1, source_target_pairs={{0,4},{4,0},{8,12},{12,8},{16,20},{20,16},{24,28},{28,24},{1,5},{5... | collective-permute-start | bytes 208904 | tf_op jit(solution)/shard_map/ppermute | solution.py:235
  13.9 2.0 %collective-permute-start.8 = (bf16[24,384]{1,0:T(8,128)(2,1)S(1)}, bf16[24,384]{1,0:T(8,128)(2,1)S(1)}, u32[]{:S(2)}, u32[]{:S(2)}) collective-permute-start(bf16[24,384]{1,0:T(8,128)(2,1)S(1)} %get-tuple-element.40), channel_id=1, source_target_pairs={{0,24},{4,28},{8,16},{12,20},{16,8},{20,12},{24,0},{28,4},{1,25},{... | collective-permute-start | bytes 55304 | tf_op jit(solution)/shard_map/ppermute | solution.py:235
  15.9 0.1 shard_map.80
  16.1 1.6 %collective-permute-done.4.refs_0_ = bf16[272,128]{1,0:T(8,128)(2,1)S(1)} collective-permute-done((bf16[272,128]{1,0:T(8,128)(2,1)S(1)}, bf16[272,128]{1,0:T(8,128)(2,1)S(1)}, u32[]{:S(2)}, u32[]{:S(2)}) %collective-permute-start.4) | collective-permute-done | bytes 69664 | tf_op jit(solution)/shard_map/ppermute | solution.py:235
  17.7 0.3 %shard_map.81 = (f32[128,256]{1,0:T(8,128)S(1)}, bf16[128,256]{1,0:T(8,128)(2,1)S(1)}, bf16[128,256]{1,0:T(8,128)(2,1)S(1)}, bf16[128,256]{1,0:T(8,128)(2,1)S(1)}) custom-call(s32[1]{0:T(128)} %bitcast.me, bf16[256,1024]{1,0:T(8,128)(2,1)S(1)} %copy-done, bf16[272,128]{1,0:T(8,128)(2,1)S(1)} %collective-permute-done.4.refs_0_, ...), custom_call_target="tpu_custom_call" | custom-call | flops 5000000000 | tf_op jit(solution)/shard_map/pallas_call | solution.py:219
  18.0 0.1 collective-permute-start.6
  18.0 1.6 %collective-permute-start.7 = (bf16[128,256]{1,0:T(8,128)(2,1)S(1)}, bf16[128,256]{1,0:T(8,128)(2,1)S(1)}, u32[]{:S(2)}, u32[]{:S(2)}) collective-permute-start(bf16[128,256]{1,0:T(8,128)(2,1)S(1)} %get-tuple-element.37), channel_id=1, source_target_pairs={{0,2},{1,3},{2,0},{3,1},{4,6},{5,7},{6,4},{7,5},{8,10},{9,11},{10,... | collective-permute-start | bytes 196616 | tf_op jit(solution)/shard_map/ppermute | solution.py:235
  19.6 0.0 collective-permute-done.9.refs_1_
  19.7 0.3 %shard_map.83 = (f32[24,256]{1,0:T(8,128)S(1)}, bf16[152,256]{1,0:T(8,128)(2,1)S(1)}, bf16[24,256]{1,0:T(8,128)(2,1)S(1)}, bf16[24,256]{1,0:T(8,128)(2,1)S(1)}) custom-call(s32[1]{0:T(128)} %bitcast.me, bf16[256,1024]{1,0:T(8,128)(2,1)S(1)} %copy-done.1, f32[24,256]{1,0:T(8,128)S(1)} %get-tuple-element.34.refs_2_.mix, f32[24,256]{1,0:T(8,128)S(1)} %get-tuple-element.38.log, ...), custom_call_target="tpu_custom_call" | custom-call | flops 5000000000 | tf_op jit(solution)/shard_map/pallas_call | solution.py:219
  20.0 1.4 %collective-permute-start.10 = (bf16[24,256]{1,0:T(8,128)(2,1)S(1)}, bf16[24,256]{1,0:T(8,128)(2,1)S(1)}, u32[]{:S(2)}, u32[]{:S(2)}) collective-permute-start(bf16[24,256]{1,0:T(8,128)(2,1)S(1)} %get-tuple-element.43), channel_id=1, source_target_pairs={{0,3},{1,2},{2,1},{3,0},{4,7},{5,6},{6,5},{7,4},{8,11},{9,10},{10,... | collective-permute-start | bytes 36872 | tf_op jit(solution)/shard_map/ppermute | solution.py:235
  21.4 0.5 %collective-permute-start.11 = (bf16[24,256]{1,0:T(8,128)(2,1)S(1)}, bf16[24,256]{1,0:T(8,128)(2,1)S(1)}, u32[]{:S(2)}, u32[]{:S(2)}) collective-permute-start(bf16[24,256]{1,0:T(8,128)(2,1)S(1)} %get-tuple-element.44), channel_id=1, source_target_pairs={{0,2},{1,3},{2,0},{3,1},{4,6},{5,7},{6,4},{7,5},{8,10},{9,11},{10,... | collective-permute-start | bytes 36872 | tf_op jit(solution)/shard_map/ppermute | solution.py:235
  21.9 2.1 %collective-permute-done.10.refs_1_ = bf16[24,256]{1,0:T(8,128)(2,1)S(1)} collective-permute-done((bf16[24,256]{1,0:T(8,128)(2,1)S(1)}, bf16[24,256]{1,0:T(8,128)(2,1)S(1)}, u32[]{:S(2)}, u32[]{:S(2)}) %collective-permute-start.10) | collective-permute-done | bytes 12320 | tf_op jit(solution)/shard_map/ppermute | solution.py:235
  24.0 1.1 %collective-permute-done.11.refs_2_ = bf16[24,256]{1,0:T(8,128)(2,1)S(1)} collective-permute-done((bf16[24,256]{1,0:T(8,128)(2,1)S(1)}, bf16[24,256]{1,0:T(8,128)(2,1)S(1)}, u32[]{:S(2)}, u32[]{:S(2)}) %collective-permute-start.11) | collective-permute-done | bytes 12320 | tf_op jit(solution)/shard_map/ppermute | solution.py:235
  25.1 0.7 %shard_map.85 = (bf16[128,256]{1,0:T(8,128)(2,1)}, bf16[24,256]{1,0:T(8,128)(2,1)}) custom-call(f32[128,256]{1,0:T(8,128)S(1)} %shard_map.82.aud_sum, f32[24,256]{1,0:T(8,128)S(1)} %shard_map.84.vid_sum, bf16[152,256]{1,0:T(8,128)(2,1)S(1)} %collective-permute-done.12.core), custom_call_target="tpu_custom_call" | custom-call | flops 5000000000 | tf_op jit(solution)/shard_map/pallas_call | solution.py:219
  (15 shorter events, 0.1 us)
Async XLA Ops:
  1.5 7.7 %collective-permute-start = (bf16[2,128,256]{2,1,0:T(8,128)(2,1)S(1)}, bf16[2,128,256]{2,1,0:T(8,128)(2,1)S(1)}, u32[]{:S(2)}, u32[]{:S(2)}) collective-permute-start(bf16[2,128,256]{2,1,0:T(8,128)(2,1)S(1)} %get-tuple-element.24.refs_1_), channel_id=1, source_target_pairs={{0,4},{4,0},{8,12},{12,8},{16,20},{20,16},{24,28},{28,24},{1,5},{5... | collective-permute-start | bytes 393224 | tf_op jit(solution)/shard_map/ppermute | solution.py:235
  4.6 4.7 %collective-permute-start.1 = (bf16[2,24,256]{2,1,0:T(8,128)(2,1)S(1)}, bf16[2,24,256]{2,1,0:T(8,128)(2,1)S(1)}, u32[]{:S(2)}, u32[]{:S(2)}) collective-permute-start(bf16[2,24,256]{2,1,0:T(8,128)(2,1)S(1)} %get-tuple-element.25.refs_3_), channel_id=1, source_target_pairs={{0,16},{4,20},{8,24},{12,28},{16,0},{20,4},{24,8},{28,12},{1,17},{... | collective-permute-start | bytes 73736 | tf_op jit(solution)/shard_map/ppermute | solution.py:235
  7.1 5.6 %collective-permute-start.2 = (bf16[2,24,256]{2,1,0:T(8,128)(2,1)S(1)}, bf16[2,24,256]{2,1,0:T(8,128)(2,1)S(1)}, u32[]{:S(2)}, u32[]{:S(2)}) collective-permute-start(bf16[2,24,256]{2,1,0:T(8,128)(2,1)S(1)} %get-tuple-element.25.refs_3_), channel_id=1, source_target_pairs={{0,24},{4,28},{8,16},{12,20},{16,8},{20,12},{24,0},{28,4},{1,25},{... | collective-permute-start | bytes 73736 | tf_op jit(solution)/shard_map/ppermute | solution.py:235
  8.5 4.3 %collective-permute-start.3 = (bf16[2,24,256]{2,1,0:T(8,128)(2,1)S(1)}, bf16[2,24,256]{2,1,0:T(8,128)(2,1)S(1)}, u32[]{:S(2)}, u32[]{:S(2)}) collective-permute-start(bf16[2,24,256]{2,1,0:T(8,128)(2,1)S(1)} %get-tuple-element.25.refs_3_), channel_id=1, source_target_pairs={{0,8},{4,12},{8,0},{12,4},{16,24},{20,28},{24,16},{28,20},{1,9},{5... | collective-permute-start | bytes 73736 | tf_op jit(solution)/shard_map/ppermute | solution.py:235
  9.8 6.1 %collective-permute-start.5 = (bf16[24,384]{1,0:T(8,128)(2,1)S(1)}, bf16[24,384]{1,0:T(8,128)(2,1)S(1)}, u32[]{:S(2)}, u32[]{:S(2)}) collective-permute-start(bf16[24,384]{1,0:T(8,128)(2,1)S(1)} %get-tuple-element.33), channel_id=1, source_target_pairs={{0,16},{4,20},{8,24},{12,28},{16,0},{20,4},{24,8},{28,12},{1,17},{... | collective-permute-start | bytes 55304 | tf_op jit(solution)/shard_map/ppermute | solution.py:235
  12.8 3.1 %copy-start = (bf16[256,1024]{1,0:T(8,128)(2,1)S(1)}, bf16[256,1024]{1,0:T(8,128)(2,1)}, u32[]{:S(2)}) copy-start(bf16[256,1024]{1,0:T(8,128)(2,1)} %proj.2) | copy-start | bytes 1572868
  13.3 4.4 %collective-permute-start.4 = (bf16[272,128]{1,0:T(8,128)(2,1)S(1)}, bf16[272,128]{1,0:T(8,128)(2,1)S(1)}, u32[]{:S(2)}, u32[]{:S(2)}) collective-permute-start(bf16[272,128]{1,0:T(8,128)(2,1)S(1)} %get-tuple-element.30), channel_id=1, source_target_pairs={{0,4},{4,0},{8,12},{12,8},{16,20},{20,16},{24,28},{28,24},{1,5},{5... | collective-permute-start | bytes 208904 | tf_op jit(solution)/shard_map/ppermute | solution.py:235
  13.9 5.7 %collective-permute-start.8 = (bf16[24,384]{1,0:T(8,128)(2,1)S(1)}, bf16[24,384]{1,0:T(8,128)(2,1)S(1)}, u32[]{:S(2)}, u32[]{:S(2)}) collective-permute-start(bf16[24,384]{1,0:T(8,128)(2,1)S(1)} %get-tuple-element.40), channel_id=1, source_target_pairs={{0,24},{4,28},{8,16},{12,20},{16,8},{20,12},{24,0},{28,4},{1,25},{... | collective-permute-start | bytes 55304 | tf_op jit(solution)/shard_map/ppermute | solution.py:235
  15.9 3.8 %collective-permute-start.9 = (bf16[24,384]{1,0:T(8,128)(2,1)S(1)}, bf16[24,384]{1,0:T(8,128)(2,1)S(1)}, u32[]{:S(2)}, u32[]{:S(2)}) collective-permute-start(bf16[24,384]{1,0:T(8,128)(2,1)S(1)} %get-tuple-element.41), channel_id=1, source_target_pairs={{0,8},{4,12},{8,0},{12,4},{16,24},{20,28},{24,16},{28,20},{1,9},{5... | collective-permute-start | bytes 55304 | tf_op jit(solution)/shard_map/ppermute | solution.py:235
  17.7 2.0 %copy-start.1 = (bf16[256,1024]{1,0:T(8,128)(2,1)S(1)}, bf16[256,1024]{1,0:T(8,128)(2,1)}, u32[]{:S(2)}) copy-start(bf16[256,1024]{1,0:T(8,128)(2,1)} %proj.3) | copy-start | bytes 1572868
  18.0 7.1 %collective-permute-start.6 = (bf16[128,256]{1,0:T(8,128)(2,1)S(1)}, bf16[128,256]{1,0:T(8,128)(2,1)S(1)}, u32[]{:S(2)}, u32[]{:S(2)}) collective-permute-start(bf16[128,256]{1,0:T(8,128)(2,1)S(1)} %get-tuple-element.36), channel_id=1, source_target_pairs={{0,3},{1,2},{2,1},{3,0},{4,7},{5,6},{6,5},{7,4},{8,11},{9,10},{10,... | collective-permute-start | bytes 196616 | tf_op jit(solution)/shard_map/ppermute | solution.py:235
  18.0 7.0 %collective-permute-start.7 = (bf16[128,256]{1,0:T(8,128)(2,1)S(1)}, bf16[128,256]{1,0:T(8,128)(2,1)S(1)}, u32[]{:S(2)}, u32[]{:S(2)}) collective-permute-start(bf16[128,256]{1,0:T(8,128)(2,1)S(1)} %get-tuple-element.37), channel_id=1, source_target_pairs={{0,2},{1,3},{2,0},{3,1},{4,6},{5,7},{6,4},{7,5},{8,10},{9,11},{10,... | collective-permute-start | bytes 196616 | tf_op jit(solution)/shard_map/ppermute | solution.py:235
  20.0 4.0 %collective-permute-start.10 = (bf16[24,256]{1,0:T(8,128)(2,1)S(1)}, bf16[24,256]{1,0:T(8,128)(2,1)S(1)}, u32[]{:S(2)}, u32[]{:S(2)}) collective-permute-start(bf16[24,256]{1,0:T(8,128)(2,1)S(1)} %get-tuple-element.43), channel_id=1, source_target_pairs={{0,3},{1,2},{2,1},{3,0},{4,7},{5,6},{6,5},{7,4},{8,11},{9,10},{10,... | collective-permute-start | bytes 36872 | tf_op jit(solution)/shard_map/ppermute | solution.py:235
  21.4 3.7 %collective-permute-start.11 = (bf16[24,256]{1,0:T(8,128)(2,1)S(1)}, bf16[24,256]{1,0:T(8,128)(2,1)S(1)}, u32[]{:S(2)}, u32[]{:S(2)}) collective-permute-start(bf16[24,256]{1,0:T(8,128)(2,1)S(1)} %get-tuple-element.44), channel_id=1, source_target_pairs={{0,2},{1,3},{2,0},{3,1},{4,6},{5,7},{6,4},{7,5},{8,10},{9,11},{10,... | collective-permute-start | bytes 36872 | tf_op jit(solution)/shard_map/ppermute | solution.py:235
  21.9 3.2 %collective-permute-start.12 = (bf16[152,256]{1,0:T(8,128)(2,1)S(1)}, bf16[152,256]{1,0:T(8,128)(2,1)S(1)}, u32[]{:S(2)}, u32[]{:S(2)}) collective-permute-start(bf16[152,256]{1,0:T(8,128)(2,1)S(1)} %get-tuple-element.45), channel_id=1, source_target_pairs={{0,1},{1,0},{2,3},{3,2},{4,5},{5,4},{6,7},{7,6},{8,9},{9,8},{10,11... | collective-permute-start | bytes 233480 | tf_op jit(solution)/shard_map/ppermute | solution.py:235
